TPU v7x, 32 devices: a whole 2x2x4 slice. The times are simulated.
32 devices in a mesh: branch: 4 (over x, core), col: 8 (over z, y).
Axes of the slice: x: 2, y: 2, z: 4, core: 2. Of those that a mesh axis runs over, the one named last changes fastest.
Arguments:
- child_fronts: float32 [4, 4096, 4096], P('branch', None, 'col'), as said below
- extend_map: int32 [4, 14], P('branch'), may hold values from 0 to 15, as said below
- parent_front: float32 [4096, 4096], P('branch', 'col'), as said below
Outputs:
- child_factor: float32 [4, 512, 4096], P('branch', None, 'col')
- parent_factor: float32 [512, 4096], P(None, 'col')
- parent_update: float32 [4096, 4096], P('branch', 'col')
Inputs may be any that keep to these rules, and one draw needn't show every extreme that they name: Each row of extend_map names 14 different parent blocks; some row names block 0 and some row names block 15. `child_fronts`: each child front is symmetric and positive definite. `parent_front`: the parent front is symmetric and positive definite.
All inputs are finite; a program needn't handle non-finite values.
Results may differ from a plain program's by a relative error of at most 0.0003.
Values sent between devices are 32-bit elements; how exact they have to be, the bound alone decides.
No kernel may reach another device: no remote copies, remote signals or barrier semaphores. Data moves between devices by JAX's collectives and lax.ppermute only.
A program may use at most 128 MiB of HBM per device.

v0:
```python
import jax
import jax.numpy as jnp
from jax import lax
from jax.sharding import PartitionSpec as P

BS = 256
P_SIZE = 512
NP = 4096
PP = 512


def from_root(x, axis, root):
    mine = lax.axis_index(axis) == root
    return lax.psum(jnp.where(mine, x, jnp.zeros_like(x)), axis)


def outer_rows(left, right):
    return lax.dot_general(left, right, (((0,), (0,)), ((), ())), precision=lax.Precision.HIGHEST)


def solve_lower(lower_factor, rhs):
    return lax.linalg.triangular_solve(lower_factor, rhs, left_side=True, lower=True)


def source_table(blocks):
    hit = blocks[:, None] == jnp.arange(NP // BS, dtype=jnp.int32)[None, :]
    present = jnp.any(hit, axis=0)
    child_block = jnp.sum(
        jnp.where(hit, jnp.arange(blocks.shape[0], dtype=jnp.int32)[:, None], 0), axis=0
    )
    positions = jnp.arange(NP, dtype=jnp.int32)
    source = P_SIZE + child_block[positions // BS] * BS + positions % BS
    keep = present[positions // BS].astype(jnp.float32)
    return (source, keep)


def on_device(child_fronts, extend_map, parent_front):
    front = child_fronts[0]
    ncols = front.shape[1]
    col_start = lax.axis_index("col") * ncols
    top = lax.all_gather(front[:P_SIZE], "col", axis=1, tiled=True)
    lower_factor = jnp.linalg.cholesky(top[:, :P_SIZE])
    factor = solve_lower(lower_factor, top)
    child_mine = lax.dynamic_slice_in_dim(factor, col_start, ncols, 1)
    update = front - outer_rows(factor, child_mine)
    source, keep = source_table(extend_map[0])
    sent = jnp.take(update, source, axis=0) * keep[:, None]
    received = lax.all_to_all(sent, "col", split_axis=0, concat_axis=1, tiled=True)
    spread = jnp.take(received, source, axis=1) * keep[None, :]
    summed = lax.psum_scatter(spread, "branch", scatter_dimension=1, tiled=True)
    assembled = parent_front + summed.T
    nrows, pcols = parent_front.shape
    row_start = lax.axis_index("branch") * nrows
    pcol_start = lax.axis_index("col") * pcols
    top_mine = from_root(assembled[:PP], "branch", 0)
    ptop = lax.all_gather(top_mine, "col", axis=1, tiled=True)
    plower = jnp.linalg.cholesky(ptop[:, :PP])
    pfactor = solve_lower(plower, ptop)
    parent_mine = lax.dynamic_slice_in_dim(pfactor, pcol_start, pcols, 1)
    row_factor = lax.dynamic_slice_in_dim(pfactor, row_start, nrows, 1)
    result = assembled - outer_rows(row_factor, parent_mine)
    return (child_mine[None], parent_mine, result)


def solution(mesh):
    in_specs = (P("branch", None, "col"), P("branch", None), P("branch", "col"))
    out_specs = (P("branch", None, "col"), P(None, "col"), P("branch", "col"))
    return jax.shard_map(
        on_device, mesh=mesh, in_specs=in_specs, out_specs=out_specs, check_vma=False
    )
```

profile of v0, /device:TPU:0, one launch (start us, length us, event | category | flops | bytes accessed | tf_op | source)
XLA Modules:
  0.0 1031.6 jit_solution(9791690633762173020)
XLA Ops:
  11.1 4.5 select_reduce_fusion.8
  15.6 5.6 select_convert_fusion
  22.0 4.5 compare_select_fusion.4
  26.5 5.5 compare_and_fusion.1
  32.1 106.3 %all-gather.6.cloned.1.call-done = f32[1,512,4096]{1,2,0:T(8,128)} async-done(((f32[1,512,512]{1,2,0:T(8,128)}), f32[1,512,4096]{1,2,0:T(8,128)}) %all-gather.6.cloned.1.call-update) | async-done | bytes 8388624 | tf_op jit(solution)/shard_map/all_gather | solution.py:41
  140.0 1.4 fusion.34
  141.5 11.7 %cholesky.286 = f32[128,128]{1,0:T(8,128)S(1)} custom-call(f32[128,128]{1,0:T(8,128)S(1)} %cholesky.426), custom_call_target="Cholesky" | custom-call | tf_op jit(solution)/shard_map/jit(cholesky)/cholesky | solution.py:42
  153.2 9.8 custom-call.27
  163.9 11.7 %cholesky.305 = f32[128,128]{1,0:T(8,128)S(1)} custom-call(f32[128,128]{1,0:T(8,128)S(1)} %cholesky.430), custom_call_target="Cholesky" | custom-call | tf_op jit(solution)/shard_map/jit(cholesky)/cholesky | solution.py:42
  175.6 10.0 custom-call.28
  186.3 11.7 %cholesky.326 = f32[128,128]{1,0:T(8,128)S(1)} custom-call(f32[128,128]{1,0:T(8,128)S(1)} %cholesky.435), custom_call_target="Cholesky" | custom-call | tf_op jit(solution)/shard_map/jit(cholesky)/cholesky | solution.py:42
  198.7 9.8 custom-call.29
  209.1 22.3 %cholesky.343 = f32[128,128]{1,0:T(8,128)S(1)} custom-call(f32[128,128]{1,0:T(8,128)S(1)} %convolution_subtract_fusion.9), custom_call_target="Cholesky" | custom-call | tf_op jit(solution)/shard_map/jit(cholesky)/cholesky | solution.py:42
  235.3 8.0 while.4
  236.0 1.4 bitcast_dynamic-update-slice_fusion.4
  238.0 1.4 bitcast_dynamic-update-slice_fusion.4
  240.0 1.4 bitcast_dynamic-update-slice_fusion.4
  243.4 39.3 %custom-call.30 = f32[4,128,128]{1,2,0:T(8,128)S(1)} custom-call(f32[4,128,128]{2,1,0:T(8,128)S(1)} %get-tuple-element.19), custom_call_target="InvertDiagBlocksLowerTriangular" | custom-call | tf_op jit(solution)/shard_map/triangular_solve/custom-call.3 | solution.py:22
  282.7 3.5 fusion.26
  286.2 5.0 convolution_subtract_fusion.3
  291.2 1.9 fusion.61
  293.2 8.7 convolution_subtract_fusion.2
  301.9 1.9 fusion.59
  303.8 11.8 %fusion.15 = f32[128,4096]{0,1:T(8,128)S(1)} fusion(f32[128,4096]{1,0:T(8,128)S(1)} %fusion.59, f32[128,4096]{1,0:T(8,128)S(1)} %fusion.61, f32[128,4096]{1,0:T(8,128)S(1)} %fusion.26, f32[512,4096]{0,1:T(8,128)} %bitcast.156, f32[512,512]{1,0:T(8,128)S(1)} %get-tuple-element.211), kind=kOutput, calls=%fused_computation.28 | convolution fusion | flops 2419589120 | bytes 10682368 | tf_op jit(solution)/shard_map/triangular_solve/dot.12 | solution.py:22
  315.6 1.9 fusion.58
  318.6 3.2 copy-done
  321.8 15.4 %bitcast_subtract_fusion = f32[4096,512]{1,0:T(8,128)} fusion(f32[1,4096,512]{2,1,0:T(8,128)S(1)} %bitcast.150, f32[512,4096]{1,0:T(8,128)S(1)} %pad_maximum_fusion, s32[]{:T(128)S(6)} %select_n.100), kind=kOutput, calls=%fused_computation.8 | convolution fusion | flops 12886999040 | bytes 26214404 | tf_op jit(solution)/shard_map/dot_general | solution.py:18
  337.3 21.4 %gather_fusion = f32[4096,512]{1,0:T(8,128)} fusion(f32[4096,512]{1,0:T(8,128)} %bitcast_subtract_fusion, s32[4096]{0:T(1024)S(1)} %broadcast_clamp_fusion), kind=kCustom, calls=%fused_computation | custom fusion | bytes 16793600 | tf_op jit(solution)/shard_map/jit(_take)/gather | solution.py:47
  358.7 4.7 select_multiply_fusion
  363.4 186.4 %all_to_all.16 = f32[8,512,512]{2,1,0:T(8,128)} all-to-all(f32[8,512,512]{2,1,0:T(8,128)S(1)} %select_multiply_fusion), channel_id=1, replica_groups=mesh['branch'=4,'col'=8] {'col'}, dimensions={0} | all-to-all | bytes 16777216 | tf_op jit(solution)/shard_map/all_to_all | solution.py:48
  549.7 9.1 copy.27
  558.9 21.4 %gather_fusion.1 = f32[4096,512]{1,0:T(8,128)} fusion(f32[512,4096]{0,1:T(8,128)} %bitcast.146, s32[4096]{0:T(1024)S(1)} %broadcast_clamp_fusion), kind=kCustom, calls=%fused_computation.1 | custom fusion | bytes 16793600 | tf_op jit(solution)/shard_map/jit(_take)/gather | solution.py:49
  580.3 8.9 copy.28
  589.2 8.1 multiply_bitcast_fusion
  597.4 1.5 copy-done.3
  598.9 1.8 copy.29
  600.7 67.5 %reduce-scatter.2.cloned.1.call-done = f32[512,1024]{1,0:T(8,128)} async-done(((f32[512,4096]{1,0:T(8,128)}), f32[512,1024]{1,0:T(8,128)}) %reduce-scatter.2.cloned.1.call-update) | async-done | bytes 2097168 | tf_op jit(solution)/shard_map/reduce_scatter | solution.py:50
  668.2 2.6 bitcast_add_fusion
  672.4 35.8 %all-reduce.3.cloned.1.call-done = f32[512,512]{0,1:T(8,128)} async-done(((f32[512,512]{0,1:T(8,128)}), f32[512,512]{0,1:T(8,128)}) %all-reduce.3.cloned.1.call-update) | async-done | bytes 1048592 | tf_op jit(solution)/shard_map/psum | solution.py:14
  708.2 2.3 dynamic-slice_bitcast_fusion
  710.5 125.0 %all-gather.4.cloned.1.call-done = f32[512,4096]{0,1:T(8,128)} async-done(((f32[512,512]{0,1:T(8,128)}), f32[512,4096]{0,1:T(8,128)}) %all-gather.4.cloned.1.call-update) | async-done | bytes 8388624 | tf_op jit(solution)/shard_map/all_gather | solution.py:56
  838.1 1.8 fusion.33
  840.8 11.7 %cholesky.358 = f32[128,128]{1,0:T(8,128)S(1)} custom-call(f32[128,128]{1,0:T(8,128)S(1)} %cholesky.439), custom_call_target="Cholesky" | custom-call | tf_op jit(solution)/shard_map/jit(cholesky)/cholesky | solution.py:57
  853.2 9.8 custom-call.31
  865.7 11.7 %cholesky.377 = f32[128,128]{1,0:T(8,128)S(1)} custom-call(f32[128,128]{1,0:T(8,128)S(1)} %cholesky.443), custom_call_target="Cholesky" | custom-call | tf_op jit(solution)/shard_map/jit(cholesky)/cholesky | solution.py:57
  878.1 10.0 custom-call.32
  889.7 11.7 %cholesky.398 = f32[128,128]{1,0:T(8,128)S(1)} custom-call(f32[128,128]{1,0:T(8,128)S(1)} %cholesky.448), custom_call_target="Cholesky" | custom-call | tf_op jit(solution)/shard_map/jit(cholesky)/cholesky | solution.py:57
  902.1 9.8 custom-call.33
  913.3 11.7 %cholesky.415 = f32[128,128]{1,0:T(8,128)S(1)} custom-call(f32[128,128]{1,0:T(8,128)S(1)} %convolution_subtract_fusion.8), custom_call_target="Cholesky" | custom-call | tf_op jit(solution)/shard_map/jit(cholesky)/cholesky | solution.py:57
  929.8 12.0 %while.5 = (s32[]{:T(128)}, f32[512,512]{1,0:T(8,128)}, s32[4,2]{0,1:T(2,128)S(1)}, f32[4,128,128]{2,1,0:T(8,128)S(1)}, s32[]{:T(128)}) while((s32[]{:T(128)}, f32[512,512]{1,0:T(8,128)}, s32[4,2]{0,1:T(2,128)S(1)}, f32[4,128,128]{2,1,0:T(8,128)S(1)}, s32[]{:T(128)}) %tuple.103), condition=%wide.while_cond.clone, body=%wide.while_body.clone.sunk | while | flops 2 | bytes 131189 | solution.py:22
  930.5 2.3 bitcast_dynamic-update-slice_fusion.5
  933.5 2.3 bitcast_dynamic-update-slice_fusion.5
  936.5 2.3 bitcast_dynamic-update-slice_fusion.5
  939.5 2.3 bitcast_dynamic-update-slice_fusion.5
  941.8 39.3 %custom-call.34 = f32[4,128,128]{1,2,0:T(8,128)S(1)} custom-call(f32[4,128,128]{2,1,0:T(8,128)S(1)} %get-tuple-element.20), custom_call_target="InvertDiagBlocksLowerTriangular" | custom-call | tf_op jit(solution)/shard_map/triangular_solve/custom-call.3 | solution.py:22
  981.1 3.5 fusion.24
  984.7 5.2 convolution_subtract_fusion.1
  989.9 1.9 fusion.55
  991.8 8.9 convolution_subtract_fusion
  1000.8 2.0 fusion.53
  1002.8 11.2 %fusion.12 = f32[128,4096]{0,1:T(8,128)S(1)} fusion(f32[128,4096]{1,0:T(8,128)S(1)} %fusion.53, f32[128,4096]{1,0:T(8,128)S(1)} %fusion.55, f32[128,4096]{1,0:T(8,128)S(1)} %fusion.24, f32[512,4096]{0,1:T(8,128)S(1)} %bitcast.158, f32[512,512]{1,0:T(8,128)} %get-tuple-element.210), kind=kOutput, calls=%fused_computation.27 | convolution fusion | flops 2419589120 | bytes 10682368 | tf_op jit(solution)/shard_map/triangular_solve/dot.12 | solution.py:22
  1014.0 1.9 fusion.52
  1017.1 4.9 fusion.30
  1022.0 2.9 copy.35
  (114 shorter events, 34.3 us)
Async XLA Ops:
  7.2 1.2 slice-start.2
  7.2 131.2 %all-gather.6.cloned.1.call-start = ((), (), s32[]{:S(2)}) async-start(), calls=%async_computation.5 | async-start | bytes 9437184 | tf_op jit(solution)/shard_map/all_gather | solution.py:41
  8.4 1.9 copy-start.4
  9.7 658.5 %reduce-scatter.2.cloned.1.call-start = ((), (), s32[]{:S(2)}) async-start(), calls=%async_computation.2 | async-start | bytes 10485760 | tf_op jit(solution)/shard_map/reduce_scatter | solution.py:50
  315.6 6.2 slice-start
  317.6 4.3 slice-start.1
  318.6 3.2 copy-start
  597.3 1.6 copy-start.3
  597.4 110.8 %all-reduce.3.cloned.1.call-start = ((), (), s32[]{:S(2)}) async-start(), calls=%async_computation.3 | async-start | bytes 2097152 | tf_op jit(solution)/shard_map/psum | solution.py:14
  671.9 163.6 %all-gather.4.cloned.1.call-start = ((), (), s32[]{:S(2)}) async-start(), calls=%async_computation.4 | async-start | bytes 9437184 | tf_op jit(solution)/shard_map/all_gather | solution.py:56
  835.5 1.2 slice-start.5
  839.8 1.0 copy-start.2
  989.8 12.9 %slice-start.3 = ((s8[8388608]{0:T(1024)(128)(4,1)}), s8[4194304]{0:T(1024)(128)(4,1)S(1)}, s32[]{:S(2)}) async-start(s8[8388608]{0:T(1024)(128)(4,1)} %bitcast.157), calls=%async_computation.9 | async-start | bytes 8388608
  991.8 10.9 %slice-start.4 = ((s8[8388608]{0:T(1024)(128)(4,1)}), s8[4194304]{0:T(1024)(128)(4,1)S(1)}, s32[]{:S(2)}) async-start(s8[8388608]{0:T(1024)(128)(4,1)} %bitcast.157), calls=%async_computation.10 | async-start | bytes 8388608
  1017.1 4.9 copy-start.1
Sparse Core Ops, SparseCore 0:
  10.7 127.6 all-gather.5
  597.5 70.6 reduce-scatter.1
  672.1 36.0 all-reduce.2
  710.2 125.3 all-gather.3
where the time goes:
time: 1040 us; the launch traced here: 1030 us
  waiting for transfers between devices  335 us (32%)
  other arithmetic  291 us (28%)
  blocking collectives  186 us (18%)
  local copies, waits for them, and re-layouts  102 us (10%)
  matrix products  97.2 us (9%)
  between operations  19.6 us (2%)
    all_to_all x1, blocking collectives, on_device(): lax.all_to_all(sent, 'col', split_axis=0, concat_axis=1, tiled=True)  186 us
    all_gather x1, waiting for transfers between devices, on_device(): ptop = lax.all_gather(top_mine, 'col', axis=1, tiled=True)  125 us
    all_gather x1, waiting for transfers between devices, on_device(): top = lax.all_gather(front[:P_SIZE], 'col', axis=1, tiled=True)  106 us
    another operation x14, other arithmetic, on_device(): lower_factor = jnp.linalg.cholesky(top[:, :P_SIZE])  89.1 us
    another operation x7, other arithmetic, solve_lower(): lax.linalg.triangular_solve(lower_factor, rhs, left_side=True, lower=True)  81.9 us
    another operation x15, other arithmetic, on_device(): plower = jnp.linalg.cholesky(ptop[:, :PP])  79.6 us
    another operation x14, matrix products, solve_lower(): lax.linalg.triangular_solve(lower_factor, rhs, left_side=True, lower=True)  69.5 us
    reduce_scatter x1, waiting for transfers between devices, on_device(): summed = lax.psum_scatter(spread, 'branch', scatter_dimension=1, tiled=True)  67.5 us
  transfers between devices with their start and end apart: 4, of which 4 were waited for; matrix products, arithmetic and copies ran while one was open for 3% of the time, Pallas kernels for 0%

commit v1 on v0

v1 whole, which is shorter than its diff:
```python
import jax
import jax.numpy as jnp
from jax import lax
from jax.experimental import pallas as pl
from jax.experimental.pallas import tpu as pltpu
from jax.sharding import PartitionSpec as P

BS = 256
P_SIZE = 512
NP = 4096
PP = 512

SUB = 8
LANES = 128
F32 = jnp.float32


def mm(a, b, ca, cb):
    return lax.dot_general(
        a, b, (((ca,), (cb,)), ((), ())),
        precision=lax.Precision.HIGHEST, preferred_element_type=F32,
    )


def factor_tile(rows):
    sub = lax.broadcasted_iota(jnp.int32, (SUB, LANES), 0)
    lane = lax.broadcasted_iota(jnp.int32, (SUB, LANES), 1)
    rows = list(rows)
    count = len(rows)
    spread = lambda column: jnp.broadcast_to(column, (SUB, LANES))
    for g in range(count):
        base = g * SUB
        inside = (lane >= base) & (lane < base + SUB)
        cols = [spread(rows[g][:, base + j:base + j + 1]) for j in range(SUB)]
        panel = jnp.where(inside, jnp.where(lane - base == sub, 1.0, 0.0), rows[g])
        kept = panel
        pivots = cols[0]
        for j in range(SUB):
            here = sub == j
            pivot = spread(cols[j][j:j + 1, :])
            inverse = 1.0 / pivot
            scaled = cols[j] * inverse
            row = spread(panel[j:j + 1, :])
            kept = jnp.where(here, panel, kept)
            pivots = jnp.where(here, pivot, pivots)
            panel = jnp.where(here, row * inverse, panel - scaled * row)
            for m in range(j + 1, SUB):
                across = spread(cols[m][j:j + 1, :])
                cols[m] = jnp.where(here, across * inverse, cols[m] - scaled * across)
        rows[g] = kept * lax.rsqrt(pivots)
        panel_rows = [spread(panel[j:j + 1, :]) for j in range(SUB)]
        for i in range(g + 1, count):
            terms = [spread(rows[i][:, base + j:base + j + 1]) * panel_rows[j] for j in range(SUB)]
            while len(terms) > 1:
                terms = [terms[t] + terms[t + 1] for t in range(0, len(terms), 2)]
            rows[i] = jnp.where(inside, 0.0, rows[i]) - terms[0]
    return rows


def inverse_factor_kernel(a_ref, w_ref):
    n = a_ref.shape[0]
    steps = n // LANES
    tri = (lax.broadcasted_iota(jnp.int32, (LANES, LANES), 0)
           >= lax.broadcasted_iota(jnp.int32, (LANES, LANES), 1))
    work = [[a_ref[i * LANES:(i + 1) * LANES, j * LANES:(j + 1) * LANES]
             for j in range(steps)] for i in range(steps)]
    for k in range(steps):
        tile = work[k][k]
        done = factor_tile([tile[g * SUB:(g + 1) * SUB, :] for g in range(LANES // SUB)])
        inv = jnp.where(tri, jnp.concatenate(done, axis=0), 0.0)
        work[k] = [inv if j == k else mm(inv, work[k][j], 1, 0) for j in range(steps)]
        for i in range(k + 1, steps):
            left = work[k][i]
            for j in range(steps):
                product = mm(left, work[k][j], 0, 0)
                work[i][j] = -product if j == k else work[i][j] - product
    for i in range(steps):
        for j in range(steps):
            value = work[i][j] if j <= i else jnp.zeros((LANES, LANES), F32)
            w_ref[i * LANES:(i + 1) * LANES, j * LANES:(j + 1) * LANES] = value


def inverse_factor(a):
    n = a.shape[0]
    return pl.pallas_call(
        inverse_factor_kernel,
        out_shape=jax.ShapeDtypeStruct((n, n), F32),
        in_specs=[pl.BlockSpec(memory_space=pltpu.VMEM)],
        out_specs=pl.BlockSpec(memory_space=pltpu.VMEM),
        compiler_params=pltpu.CompilerParams(vmem_limit_bytes=32 * 1024 * 1024),
        cost_estimate=pl.CostEstimate(flops=n * n * n, bytes_accessed=8 * n * n, transcendentals=0),
    )(a)


def split(x):
    high = x.astype(jnp.bfloat16)
    return high, (x - high.astype(F32)).astype(jnp.bfloat16)


def spread_kernel(unit_ref, slot_ref, part_ref, keep_ref, high_ref, low_ref, factor_ref, piece_ref, out_ref):
    t = pl.program_id(0)
    high, low = split(factor_ref[...])
    dims = (((1,), (0,)), ((), ()))
    dot = lambda a, b: lax.dot_general(a, b, dims, preferred_element_type=F32)
    product = dot(high_ref[...], high) + dot(high_ref[...], low) + dot(low_ref[...], high)
    value = piece_ref[0] - product
    out_ref[0] = jnp.where(keep_ref[t] > 0, value, 0.0)


def spread_update(units, slots, parts, keeps, mine_t, factor, pieces, width):
    high, low = split(mine_t)
    count = units.shape[0]
    q, depth = mine_t.shape
    whole = lambda t, *refs: (0, 0)
    return pl.pallas_call(
        spread_kernel,
        grid_spec=pltpu.PrefetchScalarGridSpec(
            num_scalar_prefetch=4,
            grid=(count,),
            in_specs=[
                pl.BlockSpec((q, depth), whole),
                pl.BlockSpec((q, depth), whole),
                pl.BlockSpec((depth, width), lambda t, u, s, h, k: (0, u[t])),
                pl.BlockSpec((1, q, width), lambda t, u, s, h, k: (s[t], 0, h[t])),
            ],
            out_specs=pl.BlockSpec((1, q, width), lambda t, u, s, h, k: (t, 0, 0)),
        ),
        out_shape=jax.ShapeDtypeStruct((count, q, width), F32),
        compiler_params=pltpu.CompilerParams(vmem_limit_bytes=32 * 1024 * 1024),
        cost_estimate=pl.CostEstimate(
            flops=6 * count * q * depth * width,
            bytes_accessed=4 * count * width * (2 * q + depth), transcendentals=0),
    )(units, slots, parts, keeps, high, low, factor, pieces)


def product(a, b, ca, cb, precision=lax.Precision.HIGH):
    return lax.dot_general(a, b, (((ca,), (cb,)), ((), ())), precision=precision)


def on_device(child_fronts, extend_map, parent_front):
    front = child_fronts[0]
    order, ncols = front.shape
    nrows, pcols = parent_front.shape
    groups = lax.axis_size("col")
    width = min(BS, ncols)
    per = ncols // width
    ratio = BS // width
    units_total = NP // width
    col = lax.axis_index("col")
    branch = lax.axis_index("branch")
    pivot_devices = P_SIZE // ncols

    blocks = extend_map[0]
    hit = blocks[:, None] == jnp.arange(NP // BS, dtype=jnp.int32)[None, :]
    present = jnp.any(hit, axis=0).astype(jnp.int32)
    child_block = jnp.sum(
        jnp.where(hit, jnp.arange(blocks.shape[0], dtype=jnp.int32)[:, None], 0), axis=0
    ).astype(jnp.int32)
    t = jnp.arange(units_total, dtype=jnp.int32)
    units = P_SIZE // width + child_block[t // ratio] * ratio + t % ratio
    keeps = present[t // ratio]

    def rows_of(target):
        parts = [
            lax.dynamic_slice_in_dim(front, units[target * per + a] * width, width, 0)
            for a in range(per)
        ]
        return jnp.concatenate(parts, axis=0) if per > 1 else parts[0]

    def placed(x):
        if pivot_devices == 1:
            return jnp.where(col == 0, x, 0.0)
        wide = jnp.zeros((x.shape[0], P_SIZE), F32)
        wide = lax.dynamic_update_slice_in_dim(wide, x, jnp.minimum(col, pivot_devices - 1) * ncols, 1)
        return jnp.where(col < pivot_devices, wide, 0.0)

    pivots = lax.psum(placed(front[:P_SIZE]), "col")

    pivot_units = PP // width

    def pivot_column(b):
        local = units[b] - col * per
        ok = (local >= 0) & (local < per) & (keeps[b] > 0)
        column = lax.dynamic_slice_in_dim(front, jnp.clip(local, 0, per - 1) * width, width, 1)
        head = column[:P_SIZE]
        body = [
            jnp.where(keeps[a] > 0, lax.dynamic_slice_in_dim(column, units[a] * width, width, 0), 0.0)
            for a in range(pivot_units)
        ]
        return jnp.where(ok, jnp.concatenate([head] + body, axis=0), 0.0)

    corner = jnp.concatenate([pivot_column(b) for b in range(pivot_units)], axis=1)
    own = jnp.where(branch == 0, placed(parent_front[:PP]), 0.0)
    corner = corner + jnp.concatenate([jnp.zeros((P_SIZE, PP), F32), own], axis=0)
    corner = lax.psum(corner, "col")

    received = [rows_of(col)]
    for shift in range(1, groups):
        pairs = [(c, (c + shift) % groups) for c in range(groups) if c >= pivot_devices]
        received.append(lax.ppermute(rows_of((col + shift) % groups), "col", pairs))
    pieces = jnp.stack(received)

    top = lax.all_gather(front[:P_SIZE], "col", axis=1, tiled=True)

    inverse = inverse_factor(pivots)
    child_mine = product(inverse, front[:P_SIZE], 1, 0)

    gpiv = product(inverse, corner[:P_SIZE], 1, 0)
    pblock = corner[P_SIZE:] - product(gpiv, gpiv, 0, 0)
    pblock = lax.psum(pblock, "branch")

    factor = product(inverse, top, 1, 0)
    mine = [
        jnp.where(
            keeps[col * per + a] > 0,
            lax.dynamic_slice_in_dim(factor, units[col * per + a] * width, width, 1), 0.0)
        for a in range(per)
    ]
    mine_t = jnp.concatenate(mine, axis=1).T
    mine_keep = jnp.repeat(lax.dynamic_slice_in_dim(keeps, col * per, per), width)
    pieces = jnp.where((mine_keep > 0)[None, :, None], pieces, 0.0)
    source = units // per
    slots = (col - source + groups) % groups
    spread = spread_update(units, slots, units % per, keeps, mine_t, factor, pieces, width)
    summed = lax.psum_scatter(spread, "branch", scatter_dimension=0, tiled=True)
    summed, _ = lax.optimization_barrier((summed, pblock))
    assembled = parent_front + jnp.transpose(summed, (0, 2, 1)).reshape(nrows, pcols)

    top_mine = lax.psum(jnp.where(branch == 0, assembled[:PP], 0.0), "branch")
    side = lax.psum(placed(assembled), "col")

    pinverse = inverse_factor(pblock)
    parent_mine = product(pinverse, top_mine, 1, 0)
    row_factor = product(side, pinverse, 1, 1)
    result = assembled - product(row_factor, parent_mine, 1, 0)
    return (child_mine[None], parent_mine, result)


def solution(mesh):
    in_specs = (P("branch", None, "col"), P("branch", None), P("branch", "col"))
    out_specs = (P("branch", None, "col"), P(None, "col"), P("branch", "col"))
    return jax.shard_map(
        on_device, mesh=mesh, in_specs=in_specs, out_specs=out_specs, check_vma=False
    )
```

time: 1040 us -> 715 us (0.69)
  other arithmetic: 291 us -> 24.1 us
  waiting for transfers between devices: 335 us -> 525 us
  blocking collectives: 186 us -> 0 us
  local copies, waits for them, and re-layouts: 102 us -> 33.4 us
  matrix products: 97.2 us -> 29.3 us
  Pallas kernels: 0 us -> 58.1 us
    another operation x36 -> x0, other arithmetic: 251 us -> none  [the longest x14 89.1 us: on_device(): lower_factor = jnp.linalg.cholesky(top[:, :P_SIZE])]
    all_to_all x1 -> x0, blocking collectives: 186 us -> none  [on_device(): lax.all_to_all(sent, 'col', split_axis=0, concat_axis=1, tiled=True)]
    psum x1 -> x4, waiting for transfers between devices: 35.8 us -> 221 us  [the longest x1 105 us: on_device(): pivots = lax.psum(placed(front[:P_SIZE]), 'col')]
    ppermute x0 -> x7, waiting for transfers between devices: none -> 129 us  [on_device(): received.append(lax.ppermute(rows_of((col + shift) % groups), 'col', pairs))]
    all_gather x1 -> x0, waiting for transfers between devices: 125 us -> none  [on_device(): ptop = lax.all_gather(top_mine, 'col', axis=1, tiled=True)]
    another operation x26 -> x0, matrix products: 76.9 us -> none  [the longest x14 69.5 us: solve_lower(): lax.linalg.triangular_solve(lower_factor, rhs, left_side=True, lower=True)]
    pallas_call x0 -> x3, Pallas kernels: none -> 58.1 us  [the longest x2 42.9 us: inverse_factor(): pl.pallas_call(inverse_factor_kernel, out_shape=jax.ShapeDtypeStruct((n,...]
    gather x5 -> x2, local copies, waits for them, and re-layouts: 53.2 us -> 1.31 us  [the longest x1 0.66 us: on_device(): units = P_SIZE // width + child_block[t // ratio] * ratio + t % ratio]
  transfers between devices with their start and end apart: 4 -> 13, of which waited for: 4 -> 9; matrix products, arithmetic and copies ran while one was open for 3% -> 6% of each run, Pallas kernels for 0% -> 8%
where the time goes in v1:
time: 715 us; the launch traced here: 710 us
  waiting for transfers between devices  525 us (73%)
  Pallas kernels  58.1 us (8%)
  local copies, waits for them, and re-layouts  33.4 us (5%)
  between operations  30 us (4%)
  matrix products  29.3 us (4%)
  other arithmetic  24.1 us (3%)
  starting transfers between devices  9.78 us (1%)
    ppermute x7, waiting for transfers between devices, on_device(): received.append(lax.ppermute(rows_of((col + shift) % groups), 'col', pairs))  129 us
    psum x1, waiting for transfers between devices, on_device(): pivots = lax.psum(placed(front[:P_SIZE]), 'col')  105 us
    psum x1, waiting for transfers between devices, on_device(): side = lax.psum(placed(assembled), 'col')  103 us
    all_gather x1, waiting for transfers between devices, on_device(): top = lax.all_gather(front[:P_SIZE], 'col', axis=1, tiled=True)  101 us
    reduce_scatter x1, waiting for transfers between devices, on_device(): summed = lax.psum_scatter(spread, 'branch', scatter_dimension=0, tiled=True)  74.6 us
    pallas_call x2, Pallas kernels, inverse_factor(): pl.pallas_call(inverse_factor_kernel, out_shape=jax.ShapeDtypeStruct((n,...  42.9 us
    dot_general x7, matrix products, product(): lax.dot_general(a, b, (((ca,), (cb,)), ((), ())), precision=precision)  29.3 us
    unnamed x22, local copies, waits for them, and re-layouts  19.4 us
  transfers between devices with their start and end apart: 13, of which 9 were waited for; matrix products, arithmetic and copies ran while one was open for 6% of the time, Pallas kernels for 8%

profile of v1, /device:TPU:0, one launch (start us, length us, event | category | flops | bytes accessed | tf_op | source)
XLA Modules:
  0.0 710.2 jit_solution(1141592096670010421)
XLA Ops:
  7.3 0.7 select_reduce_fusion
  8.1 0.7 fusion.7
  8.9 0.7 gather_fusion
  9.6 0.8 fusion.10
  13.1 0.7 gather_fusion.1
  13.7 1.4 dynamic-slice_bitcast_fusion.1
  15.1 0.6 fusion.11
  17.1 2.3 bitcast_select_fusion
  19.4 1.3 select_select_fusion
  20.7 1.6 select_bitcast_fusion.3
  22.3 0.1 maximum_select_fusion
  22.4 1.6 maximum_add_fusion
  24.1 2.3 slice.52
  36.4 4.5 dynamic-slice_bitcast_fusion.3
  40.9 1.0 pad_maximum_fusion
  41.9 1.3 collective-permute-start
  43.2 1.1 pad_maximum_fusion.2
  44.3 1.3 collective-permute-start.2
  45.6 1.1 pad_maximum_fusion.1
  46.7 1.3 collective-permute-start.1
  48.0 1.1 pad_maximum_fusion.3
  49.1 1.3 collective-permute-start.3
  50.4 1.1 pad_maximum_fusion.4
  51.4 1.3 collective-permute-start.4
  54.3 39.6 %collective-permute-done = f32[512,512]{1,0:T(8,128)} collective-permute-done((f32[512,512]{1,0:T(8,128)}, f32[512,512]{1,0:T(8,128)}, u32[]{:S(2)}, u32[]{:S(2)}) %collective-permute-start) | collective-permute-done | bytes 1048608 | tf_op jit(solution)/shard_map/ppermute | solution.py:200
  93.9 1.3 collective-permute-start.5
  95.2 1.3 bitcast_dynamic-update-slice_fusion.6
  96.5 19.2 %collective-permute-done.1 = f32[512,512]{1,0:T(8,128)} collective-permute-done((f32[512,512]{1,0:T(8,128)}, f32[512,512]{1,0:T(8,128)}, u32[]{:S(2)}, u32[]{:S(2)}) %collective-permute-start.1) | collective-permute-done | bytes 1048608 | tf_op jit(solution)/shard_map/ppermute | solution.py:200
  115.7 1.5 collective-permute-start.6
  117.2 1.3 bitcast_dynamic-update-slice_fusion.5
  118.5 69.7 %collective-permute-done.2 = f32[512,512]{1,0:T(8,128)} collective-permute-done((f32[512,512]{1,0:T(8,128)}, f32[512,512]{1,0:T(8,128)}, u32[]{:S(2)}, u32[]{:S(2)}) %collective-permute-start.2) | collective-permute-done | bytes 1048608 | tf_op jit(solution)/shard_map/ppermute | solution.py:200
  188.2 1.3 bitcast_dynamic-update-slice_fusion.4
  189.5 1.3 bitcast_dynamic-update-slice_fusion.3
  190.8 1.3 bitcast_dynamic-update-slice_fusion.2
  192.3 4.4 broadcast_select_fusion.piece_ref
  196.7 105.3 %all-reduce.13.cloned.1.call-done = (f32[512,512]{1,0:T(8,128)}, f32[1024,512]{1,0:T(8,128)}) async-done(((f32[512,512]{1,0:T(8,128)}, f32[1024,512]{1,0:T(8,128)}), (f32[512,512]{1,0:T(8,128)}, f32[1024,512]{1,0:T(8,128)})) %all-reduce.13.cloned.1.call-update) | async-done | bytes 3145744 | tf_op jit(solution)/shard_map/psum | solution.py:177
  302.0 1.2 copy-done.3
  303.2 21.5 %shard_map.58 = f32[512,512]{1,0:T(8,128)S(1)} custom-call(f32[512,512]{1,0:T(8,128)S(1)} %copy-done.3), custom_call_target="tpu_custom_call" | custom-call | flops 134217728 | bytes 2097152 | tf_op jit(solution)/shard_map/pallas_call | solution.py:85
  324.7 2.2 fusion.2
  326.9 3.3 convolution_subtract_fusion.1
  330.3 101.4 %all-gather.3.cloned.1.call-done = f32[1,512,4096]{2,1,0:T(8,128)} async-done(((f32[1,512,512]{2,1,0:T(8,128)}), f32[1,512,4096]{2,1,0:T(8,128)}) %all-gather.3.cloned.1.call-update) | async-done | bytes 8388624 | tf_op jit(solution)/shard_map/all_gather | solution.py:203
  431.7 9.5 %fusion.factor_ref = f32[512,4096]{1,0:T(8,128)S(1)} fusion(f32[512,512]{1,0:T(8,128)S(1)} %shard_map.58, f32[1,512,4096]{2,1,0:T(8,128)} %all-gather.3.cloned.1.call-done), kind=kOutput, calls=%fused_computation.2 | convolution fusion | flops 6442450944 | bytes 17825792 | tf_op jit(solution)/shard_map/dot_general | solution.py:137
  441.4 3.2 copy-done
  444.6 0.2 copy.14
  444.8 0.2 copy.15
  445.1 0.1 subtract_convert_fusion.low_ref
  445.3 3.4 copy-done.1
  448.8 15.2 %shard_map.60 = f32[16,512,256]{2,1,0:T(8,128)S(1)} custom-call(s32[16]{0:T(128)S(1)} %get-tuple-element.57.unit_ref, s32[16]{0:T(128)S(1)} %get-tuple-element.56.slot_ref, s32[16]{0:T(128)S(1)} %get-tuple-element.55.part_ref, s32[16]{0:T(128)S(1)} %gather_fusion.1, bf16[512,512]{1,0:T(8,128)(2,1)S(1)} %fusion.6.high_ref, ...), custom_call_target="tpu_custom_call" | custom-call | flops 6442450944 | bytes 25165824 | tf_op jit(solution)/shard_map/pallas_call | solution.py:115
  463.9 3.2 copy-done.2
  467.3 1.9 all-reduce.7.cloned.1.call-done.a_ref
  469.1 74.6 %reduce-scatter.2.cloned.1.call-done = f32[4,512,256]{2,1,0:T(8,128)} async-done(((f32[16,512,256]{2,1,0:T(8,128)}), f32[4,512,256]{2,1,0:T(8,128)}) %reduce-scatter.2.cloned.1.call-update) | async-done | bytes 2097168 | tf_op jit(solution)/shard_map/reduce_scatter | solution.py:225
  543.7 2.9 copy.13
  546.6 4.3 broadcast_select_fusion.1
  550.8 1.3 copy-done.5
  552.2 1.1 slice_select_fusion
  553.3 0.4 all-reduce.11.cloned.1.call-start
  553.7 0.1 all-reduce.11.cloned.1.call-update
  553.8 3.2 convolution_bitcast_fusion
  557.0 21.4 %shard_map.59 = f32[512,512]{1,0:T(8,128)S(1)} custom-call(f32[512,512]{1,0:T(8,128)S(1)} %copy-done.4), custom_call_target="tpu_custom_call" | custom-call | flops 134217728 | bytes 2097152 | tf_op jit(solution)/shard_map/pallas_call | solution.py:85
  578.5 11.0 %all-reduce.9.cloned.1.call-done = f32[512,512]{1,0:T(8,128)} async-done(((f32[512,512]{1,0:T(8,128)}), f32[512,512]{1,0:T(8,128)}) %all-reduce.9.cloned.1.call-update) | async-done | bytes 1048592 | tf_op jit(solution)/shard_map/psum | solution.py:229
  589.5 3.2 fusion.12
  592.7 102.5 %all-reduce.11.cloned.1.call-done = f32[1024,512]{1,0:T(8,128)} async-done(((f32[1024,512]{1,0:T(8,128)}), f32[1024,512]{1,0:T(8,128)}) %all-reduce.11.cloned.1.call-update) | async-done | bytes 2097168 | tf_op jit(solution)/shard_map/psum | solution.py:230
  695.2 3.5 fusion.13
  698.7 4.4 convolution_subtract_fusion
  (39 shorter events, 1.1 us)
Async XLA Ops:
  7.2 294.8 %all-reduce.13.cloned.1.call-start = ((), (), s32[]{:S(2)}) async-start(), calls=%async_computation.6 | async-start | bytes 6291456 | tf_op jit(solution)/shard_map/psum | solution.py:177
  24.1 407.7 %all-gather.3.cloned.1.call-start = ((), (), s32[]{:S(2)}) async-start(), calls=%async_computation.5 | async-start | bytes 9437184 | tf_op jit(solution)/shard_map/all_gather | solution.py:203
  26.4 442.7 %all-reduce.7.cloned.1.call-start = ((), (), s32[]{:S(2)}) async-start(), calls=%async_computation.1 | async-start | bytes 2097152 | tf_op jit(solution)/shard_map/psum | solution.py:210
  41.9 52.0 %collective-permute-start = (f32[512,512]{1,0:T(8,128)}, f32[512,512]{1,0:T(8,128)}, u32[]{:S(2)}, u32[]{:S(2)}) collective-permute-start(f32[512,512]{1,0:T(8,128)} %pad_maximum_fusion), channel_id=1, source_target_pairs={{1,2},{2,3},{3,4},{4,5},{5,6},{6,7},{7,0},{9,10},{10,11},{11,12},{... | collective-permute-start | bytes 3145736 | tf_op jit(solution)/shard_map/ppermute | solution.py:200
  44.3 143.8 %collective-permute-start.2 = (f32[512,512]{1,0:T(8,128)}, f32[512,512]{1,0:T(8,128)}, u32[]{:S(2)}, u32[]{:S(2)}) collective-permute-start(f32[512,512]{1,0:T(8,128)} %pad_maximum_fusion.2), channel_id=1, source_target_pairs={{1,4},{2,5},{3,6},{4,7},{5,0},{6,1},{7,2},{9,12},{10,13},{11,14},{... | collective-permute-start | bytes 3145736 | tf_op jit(solution)/shard_map/ppermute | solution.py:200
  46.7 69.0 %collective-permute-start.1 = (f32[512,512]{1,0:T(8,128)}, f32[512,512]{1,0:T(8,128)}, u32[]{:S(2)}, u32[]{:S(2)}) collective-permute-start(f32[512,512]{1,0:T(8,128)} %pad_maximum_fusion.1), channel_id=1, source_target_pairs={{1,3},{2,4},{3,5},{4,6},{5,7},{6,0},{7,1},{9,11},{10,12},{11,13},{... | collective-permute-start | bytes 3145736 | tf_op jit(solution)/shard_map/ppermute | solution.py:200
  49.1 140.4 %collective-permute-start.3 = (f32[512,512]{1,0:T(8,128)}, f32[512,512]{1,0:T(8,128)}, u32[]{:S(2)}, u32[]{:S(2)}) collective-permute-start(f32[512,512]{1,0:T(8,128)} %pad_maximum_fusion.3), channel_id=1, source_target_pairs={{1,5},{2,6},{3,7},{4,0},{5,1},{6,2},{7,3},{9,13},{10,14},{11,15},{... | collective-permute-start | bytes 3145736 | tf_op jit(solution)/shard_map/ppermute | solution.py:200
  51.4 139.4 %collective-permute-start.4 = (f32[512,512]{1,0:T(8,128)}, f32[512,512]{1,0:T(8,128)}, u32[]{:S(2)}, u32[]{:S(2)}) collective-permute-start(f32[512,512]{1,0:T(8,128)} %pad_maximum_fusion.4), channel_id=1, source_target_pairs={{1,6},{2,7},{3,0},{4,1},{5,2},{6,3},{7,4},{9,14},{10,15},{11,8},{1... | collective-permute-start | bytes 3145736 | tf_op jit(solution)/shard_map/ppermute | solution.py:200
  93.9 98.2 %collective-permute-start.5 = (f32[512,512]{1,0:T(8,128)S(1)}, f32[512,512]{1,0:T(8,128)S(1)}, u32[]{:S(2)}, u32[]{:S(2)}) collective-permute-start(f32[512,512]{1,0:T(8,128)S(1)} %pad_maximum_fusion.5), channel_id=1, source_target_pairs={{1,7},{2,0},{3,1},{4,2},{5,3},{6,4},{7,5},{9,15},{10,8},{11,9},{12... | collective-permute-start | bytes 3145736 | tf_op jit(solution)/shard_map/ppermute | solution.py:200
  115.7 76.5 %collective-permute-start.6 = (f32[512,512]{1,0:T(8,128)S(1)}, f32[512,512]{1,0:T(8,128)S(1)}, u32[]{:S(2)}, u32[]{:S(2)}) collective-permute-start(f32[512,512]{1,0:T(8,128)S(1)} %pad_maximum_fusion.6), channel_id=1, source_target_pairs={{1,0},{2,1},{3,2},{4,3},{5,4},{6,5},{7,6},{9,8},{10,9},{11,10},{12... | collective-permute-start | bytes 3145736 | tf_op jit(solution)/shard_map/ppermute | solution.py:200
  302.0 1.2 copy-start.3
  330.2 213.5 %reduce-scatter.2.cloned.1.call-start = ((), (), s32[]{:S(2)}) async-start(), calls=%async_computation.2 | async-start | bytes 10485760 | tf_op jit(solution)/shard_map/reduce_scatter | solution.py:225
  441.4 3.3 copy-start
  445.3 3.4 copy-start.1
  463.9 3.3 copy-start.2
  467.2 122.3 %all-reduce.9.cloned.1.call-start = ((), (), s32[]{:S(2)}) async-start(), calls=%async_computation.3 | async-start | bytes 2097152 | tf_op jit(solution)/shard_map/psum | solution.py:229
  546.6 10.4 %copy-start.4 = (f32[512,512]{1,0:T(8,128)S(1)}, f32[512,512]{1,0:T(8,128)}, u32[]{:S(2)}) copy-start(f32[512,512]{1,0:T(8,128)} %all-reduce.7.cloned.1.call-done.a_ref) | copy-start | bytes 3145732
  550.8 1.3 copy-start.5
  553.3 142.0 %all-reduce.11.cloned.1.call-start = ((), (), s32[]{:S(2)}) async-start(), calls=%async_computation.4 | async-start | bytes 4194304 | tf_op jit(solution)/shard_map/psum | solution.py:230
  578.5 120.2 %copy-start.6 = (f32[1024,512]{1,0:T(8,128)S(1)}, f32[1024,512]{1,0:T(8,128)}, u32[]{:S(2)}) copy-start(f32[1024,512]{1,0:T(8,128)} %copy-done.5) | copy-start | bytes 6291460
Sparse Core Ops, SparseCore 0:
  24.2 277.7 all-reduce.12
  305.0 126.6 all-gather.2
  434.8 34.2 all-reduce.6
  471.6 72.1 reduce-scatter.1
  553.4 36.0 all-reduce.8
  593.0 102.2 all-reduce.10

commit v2 on v1

--- a/solution.py
+++ b/solution.py
@@ -97,44 +97,106 @@
     return high, (x - high.astype(F32)).astype(jnp.bfloat16)
 
 
-def spread_kernel(unit_ref, slot_ref, part_ref, keep_ref, high_ref, low_ref, factor_ref, piece_ref, out_ref):
+def spread_kernel(slot_ref, place_ref, part_ref, keep_ref, start_ref, high_ref, low_ref, factor_ref, piece_ref, *rest):
     t = pl.program_id(0)
-    high, low = split(factor_ref[...])
+    high, low = split(factor_ref[0])
     dims = (((1,), (0,)), ((), ()))
     dot = lambda a, b: lax.dot_general(a, b, dims, preferred_element_type=F32)
-    product = dot(high_ref[...], high) + dot(high_ref[...], low) + dot(low_ref[...], high)
-    value = piece_ref[0] - product
-    out_ref[0] = jnp.where(keep_ref[t] > 0, value, 0.0)
-
-
-def spread_update(units, slots, parts, keeps, mine_t, factor, pieces, width):
-    high, low = split(mine_t)
-    count = units.shape[0]
-    q, depth = mine_t.shape
+    value = dot(high_ref[...], high) + dot(high_ref[...], low) + dot(low_ref[...], high)
+    out_ref = rest[-1]
+    out_ref[0] = jnp.where(keep_ref[t] > 0, piece_ref[0] - value, 0.0)
+    if len(rest) == 2:
+        extra = rest[0][0]
+        rows = pl.ds(pl.multiple_of(start_ref[0], 8), extra.shape[0])
+        out_ref[0, rows, :] += extra
+
+
+def spread_update(slots, places, parts, keeps, mine, factor, pieces, width, start, extra=None):
+    high, low = split(mine.T)
+    count = slots.shape[0]
+    q, depth = high.shape
     whole = lambda t, *refs: (0, 0)
+    block = lambda t, s, p, h, *refs: (s[t], 0, h[t])
+    piece = lambda t, s, p, h, *refs: (p[t], 0, h[t])
+    more = []
+    if extra is not None:
+        per = extra.shape[2] // width
+        more = [pl.BlockSpec((1, extra.shape[1], width), lambda t, *refs: (t // per, 0, t % per))]
     return pl.pallas_call(
         spread_kernel,
         grid_spec=pltpu.PrefetchScalarGridSpec(
-            num_scalar_prefetch=4,
+            num_scalar_prefetch=5,
             grid=(count,),
             in_specs=[
                 pl.BlockSpec((q, depth), whole),
                 pl.BlockSpec((q, depth), whole),
-                pl.BlockSpec((depth, width), lambda t, u, s, h, k: (0, u[t])),
-                pl.BlockSpec((1, q, width), lambda t, u, s, h, k: (s[t], 0, h[t])),
-            ],
-            out_specs=pl.BlockSpec((1, q, width), lambda t, u, s, h, k: (t, 0, 0)),
+                pl.BlockSpec((1, depth, width), block),
+                pl.BlockSpec((1, q, width), piece),
+            ] + more,
+            out_specs=pl.BlockSpec((1, q, width), lambda t, *refs: (t, 0, 0)),
         ),
         out_shape=jax.ShapeDtypeStruct((count, q, width), F32),
         compiler_params=pltpu.CompilerParams(vmem_limit_bytes=32 * 1024 * 1024),
         cost_estimate=pl.CostEstimate(
             flops=6 * count * q * depth * width,
             bytes_accessed=4 * count * width * (2 * q + depth), transcendentals=0),
-    )(units, slots, parts, keeps, high, low, factor, pieces)
-
-
-def product(a, b, ca, cb, precision=lax.Precision.HIGH):
+    )(slots, places, parts, keeps, start, high, low, factor, pieces, *([] if extra is None else [extra]))
+
+
+def product(a, b, ca, cb, precision=lax.Precision.HIGHEST):
     return lax.dot_general(a, b, (((ca,), (cb,)), ((), ())), precision=precision)
+
+
+def flip(x, axis, bit):
+    n = lax.axis_size(axis)
+    return lax.ppermute(x, axis, [(i, i ^ bit) for i in range(n)])
+
+
+def sum_scatter(x, axis):
+    n = lax.axis_size(axis)
+    me = lax.axis_index(axis)
+    bit = 1
+    while bit < n:
+        pairs = x.reshape((x.shape[0] // 2, 2) + x.shape[1:])
+        mine = (me // bit) % 2
+        away = lax.dynamic_index_in_dim(pairs, 1 - mine, 1, keepdims=False)
+        home = lax.dynamic_index_in_dim(pairs, mine, 1, keepdims=False)
+        x = home + flip(away, axis, bit)
+        bit *= 2
+    return x[0]
+
+
+def sum_all(x, axis):
+    n = lax.axis_size(axis)
+    low = lax.axis_index(axis) % 2
+    half = x.shape[0] // 2
+    away = lax.dynamic_slice_in_dim(x, (1 - low) * half, half, 0)
+    part = lax.dynamic_slice_in_dim(x, low * half, half, 0) + flip(away, axis, 1)
+    bit = 2
+    while bit < n:
+        part = part + flip(part, axis, bit)
+        bit *= 2
+    other = flip(part, axis, 1)
+    return jnp.concatenate([jnp.where(low == 0, part, other), jnp.where(low == 0, other, part)], axis=0)
+
+
+def line_gather(x, axis, ny):
+    n = lax.axis_size(axis)
+    nz = n // ny
+    z = lax.axis_index(axis) // ny
+    slots = [x]
+    up, down = [x], [x]
+    for step in range(1, nz):
+        up.append(lax.ppermute(up[-1], axis, [(c, c + ny) for c in range(n) if step - 1 <= c // ny < nz - 1]))
+        down.append(lax.ppermute(down[-1], axis, [(c, c - ny) for c in range(n) if 0 < c // ny <= nz - step]))
+    for k in range(1, nz):
+        slots.append(jnp.where(z >= k, up[k], down[nz - k]))
+    beside = []
+    for k in range(nz):
+        for j in range(1, ny):
+            pairs = [(c, c // ny * ny + (c % ny - j) % ny) for c in range(n)]
+            beside.append(lax.ppermute(slots[k], axis, pairs))
+    return slots + beside
 
 
 def on_device(child_fronts, extend_map, parent_front):
@@ -142,6 +204,11 @@
     order, ncols = front.shape
     nrows, pcols = parent_front.shape
     groups = lax.axis_size("col")
+    branches = lax.axis_size("branch")
+    ny = 1
+    while 4 * ny * ny <= groups:
+        ny *= 2
+    nz = groups // ny
     width = min(BS, ncols)
     per = ncols // width
     ratio = BS // width
@@ -159,13 +226,11 @@
     t = jnp.arange(units_total, dtype=jnp.int32)
     units = P_SIZE // width + child_block[t // ratio] * ratio + t % ratio
     keeps = present[t // ratio]
-
-    def rows_of(target):
-        parts = [
-            lax.dynamic_slice_in_dim(front, units[target * per + a] * width, width, 0)
-            for a in range(per)
-        ]
-        return jnp.concatenate(parts, axis=0) if per > 1 else parts[0]
+    source = units // per
+    parts = units % per
+
+    def unit_rows(u):
+        return lax.dynamic_slice_in_dim(front, units[u] * width, width, 0)
 
     def placed(x):
         if pivot_devices == 1:
@@ -177,63 +242,64 @@
     pivots = lax.psum(placed(front[:P_SIZE]), "col")
 
     pivot_units = PP // width
-
-    def pivot_column(b):
-        local = units[b] - col * per
-        ok = (local >= 0) & (local < per) & (keeps[b] > 0)
-        column = lax.dynamic_slice_in_dim(front, jnp.clip(local, 0, per - 1) * width, width, 1)
-        head = column[:P_SIZE]
-        body = [
-            jnp.where(keeps[a] > 0, lax.dynamic_slice_in_dim(column, units[a] * width, width, 0), 0.0)
-            for a in range(pivot_units)
-        ]
-        return jnp.where(ok, jnp.concatenate([head] + body, axis=0), 0.0)
-
-    corner = jnp.concatenate([pivot_column(b) for b in range(pivot_units)], axis=1)
-    own = jnp.where(branch == 0, placed(parent_front[:PP]), 0.0)
-    corner = corner + jnp.concatenate([jnp.zeros((P_SIZE, PP), F32), own], axis=0)
-    corner = lax.psum(corner, "col")
-
-    received = [rows_of(col)]
-    for shift in range(1, groups):
-        pairs = [(c, (c + shift) % groups) for c in range(groups) if c >= pivot_devices]
-        received.append(lax.ppermute(rows_of((col + shift) % groups), "col", pairs))
-    pieces = jnp.stack(received)
-
-    top = lax.all_gather(front[:P_SIZE], "col", axis=1, tiled=True)
+    lead = jnp.concatenate(
+        [front[:P_SIZE]] + [jnp.where(keeps[u] > 0, unit_rows(u), 0.0) for u in range(pivot_units)], axis=0)
+    gathered = line_gather(lead, "col", ny)
+    back = (col // ny - source // ny) % nz
+    aside = (source % ny - col % ny) % ny
+    slots = jnp.where(aside == 0, back, nz + back * (ny - 1) + aside - 1)
+
+    share = PP // branches
+    ours = jnp.where(branch == 0, parent_front[:PP], 0.0).reshape(branches, share, pcols)
+    ours = lax.all_gather(sum_scatter(ours, "branch"), "col")
+    start = jnp.reshape(branch * share, (1,)).astype(jnp.int32)
+
+    moved = []
+    for a in range(per):
+        received = [unit_rows(col * per + a)]
+        for shift in range(1, groups):
+            pairs = [(c, (c + shift) % groups) for c in range(groups) if c >= pivot_devices]
+            received.append(lax.ppermute(unit_rows((col + shift) % groups * per + a), "col", pairs))
+        moved.append(jnp.stack(received))
+    shifts = (col - source) % groups
 
     inverse = inverse_factor(pivots)
     child_mine = product(inverse, front[:P_SIZE], 1, 0)
-
-    gpiv = product(inverse, corner[:P_SIZE], 1, 0)
-    pblock = corner[P_SIZE:] - product(gpiv, gpiv, 0, 0)
-    pblock = lax.psum(pblock, "branch")
-
-    factor = product(inverse, top, 1, 0)
-    mine = [
-        jnp.where(
-            keeps[col * per + a] > 0,
-            lax.dynamic_slice_in_dim(factor, units[col * per + a] * width, width, 1), 0.0)
-        for a in range(per)
-    ]
-    mine_t = jnp.concatenate(mine, axis=1).T
-    mine_keep = jnp.repeat(lax.dynamic_slice_in_dim(keeps, col * per, per), width)
-    pieces = jnp.where((mine_keep > 0)[None, :, None], pieces, 0.0)
-    source = units // per
-    slots = (col - source + groups) % groups
-    spread = spread_update(units, slots, units % per, keeps, mine_t, factor, pieces, width)
-    summed = lax.psum_scatter(spread, "branch", scatter_dimension=0, tiled=True)
-    summed, _ = lax.optimization_barrier((summed, pblock))
-    assembled = parent_front + jnp.transpose(summed, (0, 2, 1)).reshape(nrows, pcols)
-
-    top_mine = lax.psum(jnp.where(branch == 0, assembled[:PP], 0.0), "branch")
-    side = lax.psum(placed(assembled), "col")
-
-    pinverse = inverse_factor(pblock)
-    parent_mine = product(pinverse, top_mine, 1, 0)
-    row_factor = product(side, pinverse, 1, 1)
-    result = assembled - product(row_factor, parent_mine, 1, 0)
-    return (child_mine[None], parent_mine, result)
+    factor = jnp.stack([product(inverse, x[:P_SIZE], 1, 0) for x in gathered])
+
+    def factor_columns(u):
+        block = lax.dynamic_slice(factor, (slots[u], 0, parts[u] * width), (1, P_SIZE, width))
+        return jnp.where(keeps[u] > 0, block[0], 0.0)
+
+    head = jnp.concatenate([factor_columns(u) for u in range(pivot_units)], axis=1)
+    head_rows = jnp.stack([x[P_SIZE:] for x in gathered])
+    first = spread_update(slots, slots, parts, keeps, head, factor, head_rows, width, start, ours)
+
+    def first_columns(begin, count):
+        wide = lax.dynamic_slice_in_dim(first, begin, count, 0)
+        return jnp.transpose(wide, (1, 0, 2)).reshape(PP, count * width)
+
+    corner = sum_all(first_columns(0, pivot_units), "branch")
+    top_mine = sum_all(first_columns(col * per, per), "branch")
+    side = sum_scatter(first.reshape((branches, units_total // branches) + first.shape[1:]), "branch")
+    side = jnp.transpose(side, (1, 0, 2)).reshape(PP, nrows)
+
+    parent_inverse = inverse_factor(corner)
+    parent_mine = product(parent_inverse, top_mine, 1, 0)
+    row_factor = product(parent_inverse, side, 1, 0)
+
+    results = []
+    for a in range(per):
+        unit = col * per + a
+        spread = spread_update(
+            slots, shifts, parts, keeps * keeps[unit], factor_columns(unit), factor, moved[a], width, start)
+        spread = spread.reshape((branches, units_total // branches) + spread.shape[1:])
+        added = jnp.transpose(sum_scatter(spread, "branch"), (0, 2, 1)).reshape(nrows, width)
+        columns = slice(a * width, (a + 1) * width)
+        results.append(
+            parent_front[:, columns] + added
+            - product(row_factor, parent_mine[:, columns], 0, 0, lax.Precision.HIGH))
+    return (child_mine[None], parent_mine, jnp.concatenate(results, axis=1))
 
 
 def solution(mesh):

time: 715 us -> 778 us (1.088)
  waiting for transfers between devices: 525 us -> 428 us
  local copies, waits for them, and re-layouts: 33.4 us -> 93 us
  starting transfers between devices: 9.78 us -> 67.6 us
  Pallas kernels: 58.1 us -> 78.6 us
  other arithmetic: 24.1 us -> 39 us
  between operations: 30 us -> 38.7 us
    ppermute x7 -> x38, waiting for transfers between devices: 129 us -> 428 us  [the longest x14 167 us: on_device(): lax.ppermute(unit_rows((col + shift) % groups * per + a), 'col', pairs)]
    psum x3 -> x0, waiting for transfers between devices: 115 us -> none  [the longest x1 103 us: on_device(): side = lax.psum(placed(assembled), 'col')]
    psum x1, waiting for transfers between devices: 105 us -> 0.02 us  [on_device(): pivots = lax.psum(placed(front[:P_SIZE]), 'col')]
    all_gather x1, waiting for transfers between devices: 101 us -> 0.01 us  [on_device(): ours = lax.all_gather(sum_scatter(ours, 'branch'), 'col')]
    reduce_scatter x1 -> x0, waiting for transfers between devices: 74.6 us -> none  [on_device(): summed = lax.psum_scatter(spread, 'branch', scatter_dimension=0, tiled=True)]
    ppermute x7 -> x38, starting transfers between devices: 9.13 us -> 67.5 us  [the longest x4 24.9 us: line_gather(): beside.append(lax.ppermute(slots[k], axis, pairs))]
    unnamed x22 -> x78, local copies, waits for them, and re-layouts: 19.4 us -> 54.2 us
    pallas_call x1 -> x3, Pallas kernels: 15.2 us -> 35.7 us  [spread_update(): pl.pallas_call(spread_kernel, grid_spec=pltpu.PrefetchScalarGridSpec(num_...]
  transfers between devices with their start and end apart: 13 -> 40, of which waited for: 9 -> 12; matrix products, arithmetic and copies ran while one was open for 6% -> 14% of each run, Pallas kernels for 8% -> 10%
where the time goes in v2:
time: 778 us; the launch traced here: 771 us
  waiting for transfers between devices  428 us (55%)
  local copies, waits for them, and re-layouts  93 us (12%)
  Pallas kernels  78.6 us (10%)
  starting transfers between devices  67.6 us (9%)
  other arithmetic  39 us (5%)
  between operations  38.7 us (5%)
  matrix products  25.8 us (3%)
    ppermute x14, waiting for transfers between devices, on_device(): lax.ppermute(unit_rows((col + shift) % groups * per + a), 'col', pairs)  167 us
    ppermute x4, waiting for transfers between devices, line_gather(): beside.append(lax.ppermute(slots[k], axis, pairs))  136 us
    ppermute x14, waiting for transfers between devices, flip(): return lax.ppermute(x, axis, [(i, i ^ bit) for i in range(n)])  75.6 us
    unnamed x78, local copies, waits for them, and re-layouts  54.2 us
    ppermute x3, waiting for transfers between devices, line_gather(): lax.ppermute(down[-1], axis, [(c, c - ny) for c in range(n) if 0 < c // n...  48.8 us
    pallas_call x2, Pallas kernels, inverse_factor(): pl.pallas_call(inverse_factor_kernel, out_shape=jax.ShapeDtypeStruct((n,...  42.9 us
    pallas_call x3, Pallas kernels, spread_update(): pl.pallas_call(spread_kernel, grid_spec=pltpu.PrefetchScalarGridSpec(num_...  35.7 us
    dot_general x12, matrix products, product(): lax.dot_general(a, b, (((ca,), (cb,)), ((), ())), precision=precision)  25.8 us
  transfers between devices with their start and end apart: 40, of which 12 were waited for; matrix products, arithmetic and copies ran while one was open for 14% of the time, Pallas kernels for 10%

profile of v2, /device:TPU:0, one launch (start us, length us, event | category | flops | bytes accessed | tf_op | source)
XLA Modules:
  0.0 770.5 jit_solution(14000197382673795440)
XLA Ops:
  23.1 2.3 slice_bitcast_fusion.8
  25.4 6.5 dynamic-slice_bitcast_fusion.10
  34.8 7.0 collective-permute-start
  43.7 2.4 broadcast_select_fusion.3
  50.2 48.8 %collective-permute-done.1 = f32[1024,512]{1,0:T(8,128)} collective-permute-done((f32[1024,512]{1,0:T(8,128)}, f32[1024,512]{1,0:T(8,128)}, u32[]{:S(2)}, u32[]{:S(2)}) %collective-permute-start.1) | collective-permute-done | bytes 2097184 | tf_op jit(solution)/shard_map/ppermute | solution.py:191
  101.5 2.1 collective-permute-start.4
  105.5 2.3 dynamic-slice_bitcast_fusion.3
  121.6 5.7 collective-permute-done.29
  128.7 1.9 bitcast_dynamic-update-slice_fusion.6
  131.9 1.9 bitcast_dynamic-update-slice_fusion.5
  133.7 83.5 %collective-permute-done.31 = f32[256,512]{1,0:T(8,128)S(1)} collective-permute-done((f32[256,512]{1,0:T(8,128)}, f32[256,512]{1,0:T(8,128)S(1)}, u32[]{:S(2)}, u32[]{:S(2)}) %collective-permute-start.31) | collective-permute-done | bytes 524320 | tf_op jit(solution)/shard_map/ppermute | solution.py:262
  225.0 13.7 %collective-permute-done.34 = f32[256,512]{1,0:T(8,128)S(1)} collective-permute-done((f32[256,512]{1,0:T(8,128)}, f32[256,512]{1,0:T(8,128)S(1)}, u32[]{:S(2)}, u32[]{:S(2)}) %collective-permute-start.34) | collective-permute-done | bytes 524320 | tf_op jit(solution)/shard_map/ppermute | solution.py:262
  240.9 2.0 collective-permute-start.5
  242.8 54.8 %collective-permute-done.18 = f32[256,512]{1,0:T(8,128)S(1)} collective-permute-done((f32[256,512]{1,0:T(8,128)S(1)}, f32[256,512]{1,0:T(8,128)S(1)}, u32[]{:S(2)}, u32[]{:S(2)}) %collective-permute-start.18) | collective-permute-done | bytes 524320 | tf_op jit(solution)/shard_map/ppermute | solution.py:262
  300.8 9.7 %collective-permute-done.20 = f32[256,512]{1,0:T(8,128)S(1)} collective-permute-done((f32[256,512]{1,0:T(8,128)}, f32[256,512]{1,0:T(8,128)S(1)}, u32[]{:S(2)}, u32[]{:S(2)}) %collective-permute-start.20) | collective-permute-done | bytes 524320 | tf_op jit(solution)/shard_map/ppermute | solution.py:262
  312.6 1.7 collective-permute-start.24
  316.4 21.4 %shard_map.58 = f32[512,512]{1,0:T(8,128)S(1)} custom-call(f32[512,512]{1,0:T(8,128)S(1)} %copy-done.10), custom_call_target="tpu_custom_call" | custom-call | flops 134217728 | bytes 2097152 | tf_op jit(solution)/shard_map/pallas_call | solution.py:85
  337.8 4.0 constant_dynamic-update-slice_fusion
  341.9 2.1 broadcast_select_fusion.1
  344.0 22.8 %collective-permute-start.8 = (f32[1024,512]{1,0:T(8,128)S(1)}, f32[1024,512]{1,0:T(8,128)S(1)}, u32[]{:S(2)}, u32[]{:S(2)}) collective-permute-start(f32[1024,512]{1,0:T(8,128)S(1)} %broadcast_select_fusion.1), channel_id=1, source_target_pairs={{0,1},{1,0},{2,3},{3,2},{4,5},{5,4},{6,7},{7,6},{8,9},{9,8},{10,11... | collective-permute-start | bytes 6291464 | tf_op jit(solution)/shard_map/ppermute | solution.py:198
  367.4 2.1 broadcast_select_fusion
  372.6 2.0 collective-permute-start.9
  374.6 2.3 fusion.10
  376.9 1.8 fusion.6
  378.8 1.8 fusion.5
  380.6 1.8 fusion.4
  382.5 3.1 fusion.3
  385.6 90.9 %collective-permute-done.7 = f32[1024,512]{1,0:T(8,128)S(1)} collective-permute-done((f32[1024,512]{1,0:T(8,128)S(1)}, f32[1024,512]{1,0:T(8,128)S(1)}, u32[]{:S(2)}, u32[]{:S(2)}) %collective-permute-start.7) | collective-permute-done | bytes 2097184 | tf_op jit(solution)/shard_map/ppermute | solution.py:198
  477.9 1.8 fusion.2
  481.1 1.8 fusion.1
  483.0 45.1 %collective-permute-done.9 = f32[1024,512]{1,0:T(8,128)S(1)} collective-permute-done((f32[1024,512]{1,0:T(8,128)S(1)}, f32[1024,512]{1,0:T(8,128)S(1)}, u32[]{:S(2)}, u32[]{:S(2)}) %collective-permute-start.9) | collective-permute-done | bytes 2097184 | tf_op jit(solution)/shard_map/ppermute | solution.py:198
  529.4 1.8 fusion.factor_ref
  531.4 3.3 copy-done
  537.2 2.3 fusion.9
  539.5 2.3 fusion.8
  543.0 3.4 copy-done.1
  548.0 15.3 %shard_map.59 = f32[16,512,256]{2,1,0:T(8,128)S(1)} custom-call(s32[16]{0:T(128)S(1)} %compare_select_fusion.6.slot_ref.place_ref, s32[16]{0:T(128)S(1)} %compare_select_fusion.6.slot_ref.place_ref, s32[16]{0:T(128)S(1)} %and_select_fusion.1.part_ref, s32[16]{0:T(128)S(1)} %gather_fusion.1, s32[1]{0:T(128)} %bitcast.3.start_ref, ...), custom_call_target="tpu_custom_call" | custom-call | flops 6442450944 | bytes 25165824 | tf_op jit(solution)/shard_map/pallas_call | solution.py:125
  563.3 4.3 constant_dynamic-slice_fusion.3
  569.3 5.3 copy.102
  574.7 1.9 bitcast_dynamic-update-slice_fusion.10
  576.5 1.9 bitcast_dynamic-update-slice_fusion.9
  578.4 1.9 bitcast_dynamic-update-slice_fusion.8
  580.3 1.9 bitcast_dynamic-update-slice_fusion.7.piece_ref
  582.2 1.8 fusion.32
  584.3 3.4 copy-done.2
  587.6 12.4 %shard_map.61 = f32[16,256,256]{2,1,0:T(8,128)S(1)} custom-call(s32[16]{0:T(128)S(1)} %compare_select_fusion.6.slot_ref.place_ref, s32[16]{0:T(128)S(1)} %get-tuple-element.19.place_ref, s32[16]{0:T(128)S(1)} %and_select_fusion.1.part_ref, s32[16]{0:T(128)S(1)} %get-tuple-element.80.keep_ref, s32[1]{0:T(128)} %bitcast.3.start_ref, ...), custom_call_target="tpu_custom_call" | custom-call | flops 3221225472 | bytes 16777216 | tf_op jit(solution)/shard_map/pallas_call | solution.py:125
  602.2 1.9 bitcast_dynamic-update-slice_fusion.piece_ref
  608.7 3.4 copy-done.3
  612.1 2.2 copy-done.8
  614.3 8.0 %shard_map.62 = f32[16,256,256]{2,1,0:T(8,128)S(1)} custom-call(s32[16]{0:T(128)S(1)} %compare_select_fusion.6.slot_ref.place_ref, s32[16]{0:T(128)S(1)} %get-tuple-element.19.place_ref, s32[16]{0:T(128)S(1)} %and_select_fusion.1.part_ref, s32[16]{0:T(128)S(1)} %get-tuple-element.81.keep_ref, s32[1]{0:T(128)} %bitcast.3.start_ref, ...), custom_call_target="tpu_custom_call" | custom-call | flops 3221225472 | bytes 16777216 | tf_op jit(solution)/shard_map/pallas_call | solution.py:125
  622.2 2.1 copy-done.6
  626.2 2.0 dynamic-slice_add_fusion.1
  634.1 5.7 copy.101
  639.8 3.4 collective-permute-done.16
  644.7 9.0 %collective-permute-done.13 = f32[256,512]{1,0:T(8,128)} collective-permute-done((f32[256,512]{1,0:T(8,128)}, f32[256,512]{1,0:T(8,128)}, u32[]{:S(2)}, u32[]{:S(2)}) %collective-permute-start.13) | collective-permute-done | bytes 524320 | tf_op jit(solution)/shard_map/ppermute | solution.py:152
  655.0 2.5 bitcast_add_fusion.2
  657.6 3.2 bitcast_add_fusion
  663.2 2.0 bitcast_add_fusion.1
  667.1 21.5 %shard_map.60 = f32[512,512]{1,0:T(8,128)S(1)} custom-call(f32[512,512]{1,0:T(8,128)S(1)} %pad_maximum_fusion.2.a_ref), custom_call_target="tpu_custom_call" | custom-call | flops 134217728 | bytes 2097152 | tf_op jit(solution)/shard_map/pallas_call | solution.py:85
  688.7 1.8 fusion.22
  690.6 41.3 %collective-permute-done.26 = f32[1,4,256,256]{3,2,1,0:T(8,128)S(1)} collective-permute-done((f32[1,4,256,256]{3,2,1,0:T(8,128)S(1)}, f32[1,4,256,256]{3,2,1,0:T(8,128)S(1)}, u32[]{:S(2)}, u32[]{:S(2)}) %collective-permute-start.26) | collective-permute-done | bytes 1048608 | tf_op jit(solution)/shard_map/ppermute | solution.py:152
  732.2 21.8 %collective-permute-done.37 = f32[1,4,256,256]{3,2,1,0:T(8,128)S(1)} collective-permute-done((f32[1,4,256,256]{3,2,1,0:T(8,128)S(1)}, f32[1,4,256,256]{3,2,1,0:T(8,128)S(1)}, u32[]{:S(2)}, u32[]{:S(2)}) %collective-permute-start.37) | collective-permute-done | bytes 1048608 | tf_op jit(solution)/shard_map/ppermute | solution.py:152
  754.8 3.6 fusion.44
  761.7 1.8 copy.109
  (185 shorter events, 80.2 us)
Async XLA Ops:
  7.2 308.0 %all-reduce.2.cloned.1.call-start = ((), (), s32[]{:S(2)}) async-start(), calls=%async_computation | async-start | bytes 2097152 | tf_op jit(solution)/shard_map/psum | solution.py:242
  25.4 6.5 copy-start.19
  31.9 9.9 %copy-start.12 = (f32[1024,512]{1,0:T(8,128)S(1)}, f32[1024,512]{1,0:T(8,128)}, u32[]{:S(2)}) copy-start(f32[1024,512]{1,0:T(8,128)} %param.5) | copy-start | bytes 6291460
  33.5 65.6 %collective-permute-start.1 = (f32[1024,512]{1,0:T(8,128)}, f32[1024,512]{1,0:T(8,128)}, u32[]{:S(2)}, u32[]{:S(2)}) collective-permute-start(f32[1024,512]{1,0:T(8,128)} %pad_maximum_fusion), channel_id=1, source_target_pairs={{2,0},{3,1},{4,2},{5,3},{6,4},{7,5},{10,8},{11,9},{12,10},{13,11},... | collective-permute-start | bytes 6291464 | tf_op jit(solution)/shard_map/ppermute | solution.py:191
  34.8 66.7 %collective-permute-start = (f32[1024,512]{1,0:T(8,128)}, f32[1024,512]{1,0:T(8,128)}, u32[]{:S(2)}, u32[]{:S(2)}) collective-permute-start(f32[1024,512]{1,0:T(8,128)} %pad_maximum_fusion), channel_id=1, source_target_pairs={{0,2},{1,3},{2,4},{3,5},{4,6},{5,7},{8,10},{9,11},{10,12},{11,13},... | collective-permute-start | bytes 6291464 | tf_op jit(solution)/shard_map/ppermute | solution.py:190
  43.7 76.8 %copy-start.16 = (f32[512,512]{1,0:T(8,128)S(1)}, f32[512,512]{1,0:T(8,128)}, u32[]{:S(2)}) copy-start(f32[512,512]{1,0:T(8,128)} %copy-done.15) | copy-start | bytes 3145732
  43.7 75.5 %collective-permute-start.10 = (f32[2,128,512]{2,1,0:T(8,128)}, f32[2,128,512]{2,1,0:T(8,128)}, u32[]{:S(2)}, u32[]{:S(2)}) collective-permute-start(f32[2,128,512]{2,1,0:T(8,128)} %dynamic-slice_bitcast_fusion.17), channel_id=1, source_target_pairs={{0,8},{8,0},{16,24},{24,16},{1,9},{9,1},{17,25},{25,17},{2,10},{10... | collective-permute-start | bytes 1572872 | tf_op jit(solution)/shard_map/ppermute | solution.py:152
  43.7 83.7 %copy-start.27 = (f32[256,512]{1,0:T(8,128)S(1)}, f32[256,512]{1,0:T(8,128)}, u32[]{:S(2)}) copy-start(f32[256,512]{1,0:T(8,128)} %get-tuple-element.24) | copy-start | bytes 1572868
  46.1 84.5 %copy-start.26 = (f32[256,512]{1,0:T(8,128)S(1)}, f32[256,512]{1,0:T(8,128)}, u32[]{:S(2)}) copy-start(f32[256,512]{1,0:T(8,128)} %get-tuple-element.23) | copy-start | bytes 1572868
  46.1 496.9 %all-gather.2.cloned.1.call-start = ((), (), s32[]{:S(2)}) async-start(), calls=%async_computation.1 | async-start | bytes 2359296 | tf_op jit(solution)/shard_map/all_gather | solution.py:254
  46.2 84.4 %collective-permute-start.30 = (f32[256,512]{1,0:T(8,128)}, f32[256,512]{1,0:T(8,128)}, u32[]{:S(2)}, u32[]{:S(2)}) collective-permute-start(f32[256,512]{1,0:T(8,128)} %get-tuple-element.26), channel_id=1, source_target_pairs={{1,3},{2,4},{3,5},{4,6},{5,7},{6,0},{7,1},{9,11},{10,12},{11,13},{... | collective-permute-start | bytes 1572872 | tf_op jit(solution)/shard_map/ppermute | solution.py:262
  47.6 79.8 %collective-permute-start.29 = (f32[256,512]{1,0:T(8,128)}, f32[256,512]{1,0:T(8,128)}, u32[]{:S(2)}, u32[]{:S(2)}) collective-permute-start(f32[256,512]{1,0:T(8,128)} %get-tuple-element.27), channel_id=1, source_target_pairs={{1,2},{2,3},{3,4},{4,5},{5,6},{6,7},{7,0},{9,10},{10,11},{11,12},{... | collective-permute-start | bytes 1572872 | tf_op jit(solution)/shard_map/ppermute | solution.py:262
  99.1 123.7 %collective-permute-start.2 = (f32[1024,512]{1,0:T(8,128)}, f32[1024,512]{1,0:T(8,128)}, u32[]{:S(2)}, u32[]{:S(2)}) collective-permute-start(f32[1024,512]{1,0:T(8,128)} %collective-permute-done.1), channel_id=1, source_target_pairs={{2,0},{3,1},{4,2},{5,3},{10,8},{11,9},{12,10},{13,11},{18,16},{19,... | collective-permute-start | bytes 6291464 | tf_op jit(solution)/shard_map/ppermute | solution.py:191
  101.5 120.1 %copy-start.25 = (f32[256,512]{1,0:T(8,128)S(1)}, f32[256,512]{1,0:T(8,128)}, u32[]{:S(2)}) copy-start(f32[256,512]{1,0:T(8,128)} %get-tuple-element.34) | copy-start | bytes 1572868
  101.5 139.4 %collective-permute-start.4 = (f32[1024,512]{1,0:T(8,128)}, f32[1024,512]{1,0:T(8,128)}, u32[]{:S(2)}, u32[]{:S(2)}) collective-permute-start(f32[1024,512]{1,0:T(8,128)} %collective-permute-done), channel_id=1, source_target_pairs={{2,4},{3,5},{4,6},{5,7},{10,12},{11,13},{12,14},{13,15},{18,20},{1... | collective-permute-start | bytes 6291464 | tf_op jit(solution)/shard_map/ppermute | solution.py:190
  105.5 133.2 %copy-start.24 = (f32[256,512]{1,0:T(8,128)S(1)}, f32[256,512]{1,0:T(8,128)}, u32[]{:S(2)}) copy-start(f32[256,512]{1,0:T(8,128)} %get-tuple-element.33) | copy-start | bytes 1572868
  119.2 98.1 %collective-permute-start.31 = (f32[256,512]{1,0:T(8,128)}, f32[256,512]{1,0:T(8,128)S(1)}, u32[]{:S(2)}, u32[]{:S(2)}) collective-permute-start(f32[256,512]{1,0:T(8,128)} %get-tuple-element.25), channel_id=1, source_target_pairs={{1,4},{2,5},{3,6},{4,7},{5,0},{6,1},{7,2},{9,12},{10,13},{11,14},{... | collective-permute-start | bytes 1572872 | tf_op jit(solution)/shard_map/ppermute | solution.py:262
  127.4 92.0 %collective-permute-start.32 = (f32[256,512]{1,0:T(8,128)S(1)}, f32[256,512]{1,0:T(8,128)S(1)}, u32[]{:S(2)}, u32[]{:S(2)}) collective-permute-start(f32[256,512]{1,0:T(8,128)S(1)} %copy-done.27), channel_id=1, source_target_pairs={{1,5},{2,6},{3,7},{4,0},{5,1},{6,2},{7,3},{9,13},{10,14},{11,15},{... | collective-permute-start | bytes 1572872 | tf_op jit(solution)/shard_map/ppermute | solution.py:262
  130.6 90.9 %collective-permute-start.33 = (f32[256,512]{1,0:T(8,128)S(1)}, f32[256,512]{1,0:T(8,128)S(1)}, u32[]{:S(2)}, u32[]{:S(2)}) collective-permute-start(f32[256,512]{1,0:T(8,128)S(1)} %copy-done.26), channel_id=1, source_target_pairs={{1,6},{2,7},{3,0},{4,1},{5,2},{6,3},{7,4},{9,14},{10,15},{11,8},{1... | collective-permute-start | bytes 1572872 | tf_op jit(solution)/shard_map/ppermute | solution.py:262
  217.3 21.4 %collective-permute-start.34 = (f32[256,512]{1,0:T(8,128)}, f32[256,512]{1,0:T(8,128)S(1)}, u32[]{:S(2)}, u32[]{:S(2)}) collective-permute-start(f32[256,512]{1,0:T(8,128)} %get-tuple-element.41), channel_id=1, source_target_pairs={{1,7},{2,0},{3,1},{4,2},{5,3},{6,4},{7,5},{9,15},{10,8},{11,9},{12... | collective-permute-start | bytes 1572872 | tf_op jit(solution)/shard_map/ppermute | solution.py:262
  219.4 91.1 %collective-permute-start.20 = (f32[256,512]{1,0:T(8,128)}, f32[256,512]{1,0:T(8,128)S(1)}, u32[]{:S(2)}, u32[]{:S(2)}) collective-permute-start(f32[256,512]{1,0:T(8,128)} %get-tuple-element.32), channel_id=1, source_target_pairs={{1,4},{2,5},{3,6},{4,7},{5,0},{6,1},{7,2},{9,12},{10,13},{11,14},{... | collective-permute-start | bytes 1572872 | tf_op jit(solution)/shard_map/ppermute | solution.py:262
  221.5 76.1 %collective-permute-start.18 = (f32[256,512]{1,0:T(8,128)S(1)}, f32[256,512]{1,0:T(8,128)S(1)}, u32[]{:S(2)}, u32[]{:S(2)}) collective-permute-start(f32[256,512]{1,0:T(8,128)S(1)} %copy-done.25), channel_id=1, source_target_pairs={{1,2},{2,3},{3,4},{4,5},{5,6},{6,7},{7,0},{9,10},{10,11},{11,12},{... | collective-permute-start | bytes 1572872 | tf_op jit(solution)/shard_map/ppermute | solution.py:262
  222.8 121.1 %collective-permute-start.3 = (f32[1024,512]{1,0:T(8,128)}, f32[1024,512]{1,0:T(8,128)S(1)}, u32[]{:S(2)}, u32[]{:S(2)}) collective-permute-start(f32[1024,512]{1,0:T(8,128)} %collective-permute-done.2), channel_id=1, source_target_pairs={{2,0},{3,1},{10,8},{11,9},{18,16},{19,17},{26,24},{27,25}} | collective-permute-start | bytes 6291464 | tf_op jit(solution)/shard_map/ppermute | solution.py:191
  238.7 59.8 %collective-permute-start.19 = (f32[256,512]{1,0:T(8,128)S(1)}, f32[256,512]{1,0:T(8,128)S(1)}, u32[]{:S(2)}, u32[]{:S(2)}) collective-permute-start(f32[256,512]{1,0:T(8,128)S(1)} %copy-done.24), channel_id=1, source_target_pairs={{1,3},{2,4},{3,5},{4,6},{5,7},{6,0},{7,1},{9,11},{10,12},{11,13},{... | collective-permute-start | bytes 1572872 | tf_op jit(solution)/shard_map/ppermute | solution.py:262
  240.9 126.4 %collective-permute-start.5 = (f32[1024,512]{1,0:T(8,128)}, f32[1024,512]{1,0:T(8,128)}, u32[]{:S(2)}, u32[]{:S(2)}) collective-permute-start(f32[1024,512]{1,0:T(8,128)} %collective-permute-done.4), channel_id=1, source_target_pairs={{4,6},{5,7},{12,14},{13,15},{20,22},{21,23},{28,30},{29,31}} | collective-permute-start | bytes 6291464 | tf_op jit(solution)/shard_map/ppermute | solution.py:190
  297.6 75.0 %collective-permute-start.6 = (f32[1024,512]{1,0:T(8,128)}, f32[1024,512]{1,0:T(8,128)}, u32[]{:S(2)}, u32[]{:S(2)}) collective-permute-start(f32[1024,512]{1,0:T(8,128)} %pad_maximum_fusion), channel_id=1, source_target_pairs={{0,1},{1,0},{2,3},{3,2},{4,5},{5,4},{6,7},{7,6},{8,9},{9,8},{10,11... | collective-permute-start | bytes 6291464 | tf_op jit(solution)/shard_map/ppermute | solution.py:198
  298.5 14.2 %collective-permute-start.11 = (f32[1,128,512]{2,1,0:T(8,128)S(1)}, f32[1,128,512]{2,1,0:T(8,128)S(1)}, u32[]{:S(2)}, u32[]{:S(2)}) collective-permute-start(f32[1,128,512]{2,1,0:T(8,128)S(1)} %constant_dynamic-slice_fusion.7), channel_id=1, source_target_pairs={{0,16},{8,24},{16,0},{24,8},{1,17},{9,25},{17,1},{25,9},{2,18},{10... | collective-permute-start | bytes 786440 | tf_op jit(solution)/shard_map/ppermute | solution.py:152
  310.5 291.7 %collective-permute-start.35 = (f32[256,512]{1,0:T(8,128)}, f32[256,512]{1,0:T(8,128)}, u32[]{:S(2)}, u32[]{:S(2)}) collective-permute-start(f32[256,512]{1,0:T(8,128)} %get-tuple-element.40), channel_id=1, source_target_pairs={{1,0},{2,1},{3,2},{4,3},{5,4},{6,5},{7,6},{9,8},{10,9},{11,10},{12... | collective-permute-start | bytes 1572872 | tf_op jit(solution)/shard_map/ppermute | solution.py:262
  312.6 267.7 %collective-permute-start.24 = (f32[256,512]{1,0:T(8,128)}, f32[256,512]{1,0:T(8,128)}, u32[]{:S(2)}, u32[]{:S(2)}) collective-permute-start(f32[256,512]{1,0:T(8,128)} %get-tuple-element.22), channel_id=1, source_target_pairs={{1,0},{2,1},{3,2},{4,3},{5,4},{6,5},{7,6},{9,8},{10,9},{11,10},{12... | collective-permute-start | bytes 1572872 | tf_op jit(solution)/shard_map/ppermute | solution.py:262
  344.0 135.8 %collective-permute-start.8 = (f32[1024,512]{1,0:T(8,128)S(1)}, f32[1024,512]{1,0:T(8,128)S(1)}, u32[]{:S(2)}, u32[]{:S(2)}) collective-permute-start(f32[1024,512]{1,0:T(8,128)S(1)} %broadcast_select_fusion.1), channel_id=1, source_target_pairs={{0,1},{1,0},{2,3},{3,2},{4,5},{5,4},{6,7},{7,6},{8,9},{9,8},{10,11... | collective-permute-start | bytes 6291464 | tf_op jit(solution)/shard_map/ppermute | solution.py:198
  367.3 109.1 %collective-permute-start.7 = (f32[1024,512]{1,0:T(8,128)S(1)}, f32[1024,512]{1,0:T(8,128)S(1)}, u32[]{:S(2)}, u32[]{:S(2)}) collective-permute-start(f32[1024,512]{1,0:T(8,128)S(1)} %broadcast_select_fusion.2), channel_id=1, source_target_pairs={{0,1},{1,0},{2,3},{3,2},{4,5},{5,4},{6,7},{7,6},{8,9},{9,8},{10,11... | collective-permute-start | bytes 6291464 | tf_op jit(solution)/shard_map/ppermute | solution.py:198
  372.6 155.4 %collective-permute-start.9 = (f32[1024,512]{1,0:T(8,128)S(1)}, f32[1024,512]{1,0:T(8,128)S(1)}, u32[]{:S(2)}, u32[]{:S(2)}) collective-permute-start(f32[1024,512]{1,0:T(8,128)S(1)} %broadcast_select_fusion), channel_id=1, source_target_pairs={{0,1},{1,0},{2,3},{3,2},{4,5},{5,4},{6,7},{7,6},{8,9},{9,8},{10,11... | collective-permute-start | bytes 6291464 | tf_op jit(solution)/shard_map/ppermute | solution.py:198
  476.4 54.8 %copy-start.21 = (f32[1024,512]{1,0:T(8,128)}, f32[1024,512]{1,0:T(8,128)S(1)}, u32[]{:S(2)}) copy-start(f32[1024,512]{1,0:T(8,128)S(1)} %collective-permute-done.7) | copy-start | bytes 6291460
  476.4 102.0 %collective-permute-start.23 = (f32[256,512]{1,0:T(8,128)}, f32[256,512]{1,0:T(8,128)}, u32[]{:S(2)}, u32[]{:S(2)}) collective-permute-start(f32[256,512]{1,0:T(8,128)} %get-tuple-element.29), channel_id=1, source_target_pairs={{1,7},{2,0},{3,1},{4,2},{5,3},{6,4},{7,5},{9,15},{10,8},{11,9},{12... | collective-permute-start | bytes 1572872 | tf_op jit(solution)/shard_map/ppermute | solution.py:262
  479.8 51.6 %copy-start.20 = (f32[1024,512]{1,0:T(8,128)}, f32[1024,512]{1,0:T(8,128)S(1)}, u32[]{:S(2)}) copy-start(f32[1024,512]{1,0:T(8,128)S(1)} %collective-permute-done.8) | copy-start | bytes 6291460
  479.8 96.7 %collective-permute-start.22 = (f32[256,512]{1,0:T(8,128)}, f32[256,512]{1,0:T(8,128)}, u32[]{:S(2)}, u32[]{:S(2)}) collective-permute-start(f32[256,512]{1,0:T(8,128)} %get-tuple-element.30), channel_id=1, source_target_pairs={{1,6},{2,7},{3,0},{4,1},{5,2},{6,3},{7,4},{9,14},{10,15},{11,8},{1... | collective-permute-start | bytes 1572872 | tf_op jit(solution)/shard_map/ppermute | solution.py:262
  528.1 6.6 copy-start.22
  528.1 46.6 %collective-permute-start.21 = (f32[256,512]{1,0:T(8,128)}, f32[256,512]{1,0:T(8,128)}, u32[]{:S(2)}, u32[]{:S(2)}) collective-permute-start(f32[256,512]{1,0:T(8,128)} %get-tuple-element.31), channel_id=1, source_target_pairs={{1,5},{2,6},{3,7},{4,0},{5,1},{6,2},{7,3},{9,13},{10,14},{11,15},{... | collective-permute-start | bytes 1572872 | tf_op jit(solution)/shard_map/ppermute | solution.py:262
  531.4 3.3 copy-start
  535.8 6.0 copy-start.23
  543.0 3.4 copy-start.1
  563.3 6.0 copy-start.4
  574.7 82.9 %collective-permute-start.27 = (f32[2,4,512,256]{2,3,1,0:T(8,128)}, f32[2,4,512,256]{2,3,1,0:T(8,128)}, u32[]{:S(2)}, u32[]{:S(2)}) collective-permute-start(f32[2,4,512,256]{2,3,1,0:T(8,128)} %bitcast.260), channel_id=1, source_target_pairs={{0,8},{8,0},{16,24},{24,16},{1,9},{9,1},{17,25},{25,17},{2,10},{10... | collective-permute-start | bytes 12582920 | tf_op jit(solution)/shard_map/ppermute | solution.py:152
  584.2 3.4 copy-start.2
  600.0 5.7 copy-start.5
  601.7 53.3 %collective-permute-start.25 = (f32[2,4,256,256]{3,2,1,0:T(8,128)}, f32[2,4,256,256]{3,2,1,0:T(8,128)}, u32[]{:S(2)}, u32[]{:S(2)}) collective-permute-start(f32[2,4,256,256]{3,2,1,0:T(8,128)} %dynamic-slice_bitcast_fusion.1), channel_id=1, source_target_pairs={{0,8},{8,0},{16,24},{24,16},{1,9},{9,1},{17,25},{25,17},{2,10},{10... | collective-permute-start | bytes 6291464 | tf_op jit(solution)/shard_map/ppermute | solution.py:152
  605.9 2.3 copy-start.17
  606.8 19.4 %collective-permute-start.15 = (f32[256,512]{1,0:T(8,128)}, f32[256,512]{1,0:T(8,128)}, u32[]{:S(2)}, u32[]{:S(2)}) collective-permute-start(f32[256,512]{1,0:T(8,128)} %constant_dynamic-slice_fusion.5), channel_id=1, source_target_pairs={{0,8},{8,0},{16,24},{24,16},{1,9},{9,1},{17,25},{25,17},{2,10},{10... | collective-permute-start | bytes 1572872 | tf_op jit(solution)/shard_map/ppermute | solution.py:152
  608.5 21.2 %collective-permute-start.12 = (f32[256,512]{1,0:T(8,128)}, f32[256,512]{1,0:T(8,128)S(1)}, u32[]{:S(2)}, u32[]{:S(2)}) collective-permute-start(f32[256,512]{1,0:T(8,128)} %constant_dynamic-slice_fusion.6), channel_id=1, source_target_pairs={{0,8},{8,0},{16,24},{24,16},{1,9},{9,1},{17,25},{25,17},{2,10},{10... | collective-permute-start | bytes 1572872 | tf_op jit(solution)/shard_map/ppermute | solution.py:152
  608.7 3.4 copy-start.3
  612.1 2.2 copy-start.8
  622.2 4.0 copy-start.18
  622.2 8.9 %copy-start.13 = (f32[1024,512]{1,0:T(8,128)S(1)}, f32[1024,512]{1,0:T(8,128)}, u32[]{:S(2)}) copy-start(f32[1024,512]{1,0:T(8,128)} %param.5) | copy-start | bytes 6291460
  625.8 37.4 %collective-permute-start.36 = (f32[2,4,256,256]{3,2,1,0:T(8,128)}, f32[2,4,256,256]{3,2,1,0:T(8,128)}, u32[]{:S(2)}, u32[]{:S(2)}) collective-permute-start(f32[2,4,256,256]{3,2,1,0:T(8,128)} %dynamic-slice_bitcast_fusion), channel_id=1, source_target_pairs={{0,8},{8,0},{16,24},{24,16},{1,9},{9,1},{17,25},{25,17},{2,10},{10... | collective-permute-start | bytes 6291464 | tf_op jit(solution)/shard_map/ppermute | solution.py:152
  628.2 15.1 %collective-permute-start.16 = (f32[256,512]{1,0:T(8,128)}, f32[256,512]{1,0:T(8,128)}, u32[]{:S(2)}, u32[]{:S(2)}) collective-permute-start(f32[256,512]{1,0:T(8,128)} %dynamic-slice_add_fusion.1), channel_id=1, source_target_pairs={{0,16},{8,24},{16,0},{24,8},{1,17},{9,25},{17,1},{25,9},{2,18},{10... | collective-permute-start | bytes 1572872 | tf_op jit(solution)/shard_map/ppermute | solution.py:152
  630.6 23.0 %collective-permute-start.13 = (f32[256,512]{1,0:T(8,128)}, f32[256,512]{1,0:T(8,128)}, u32[]{:S(2)}, u32[]{:S(2)}) collective-permute-start(f32[256,512]{1,0:T(8,128)} %dynamic-slice_add_fusion.2), channel_id=1, source_target_pairs={{0,16},{8,24},{16,0},{24,8},{1,17},{9,25},{17,1},{25,9},{2,18},{10... | collective-permute-start | bytes 1572872 | tf_op jit(solution)/shard_map/ppermute | solution.py:152
  644.6 13.0 %copy-start.11 = (f32[2,1,4,512,256]{3,4,2,0,1:T(8,128)S(1)}, f32[2,1,4,512,256]{3,4,2,0,1:T(8,128)}, u32[]{:S(2)}) copy-start(f32[2,1,4,512,256]{3,4,2,0,1:T(8,128)} %copy.101) | copy-start | bytes 12582916
  644.6 44.0 %collective-permute-start.17 = (f32[256,512]{1,0:T(8,128)S(1)}, f32[256,512]{1,0:T(8,128)S(1)}, u32[]{:S(2)}, u32[]{:S(2)}) collective-permute-start(f32[256,512]{1,0:T(8,128)S(1)} %add.407), channel_id=1, source_target_pairs={{0,8},{8,0},{16,24},{24,16},{1,9},{9,1},{17,25},{25,17},{2,10},{10... | collective-permute-start | bytes 1572872 | tf_op jit(solution)/shard_map/ppermute | solution.py:152
  654.9 12.0 %collective-permute-start.14 = (f32[256,512]{1,0:T(8,128)S(1)}, f32[256,512]{1,0:T(8,128)S(1)}, u32[]{:S(2)}, u32[]{:S(2)}) collective-permute-start(f32[256,512]{1,0:T(8,128)S(1)} %add.404), channel_id=1, source_target_pairs={{0,8},{8,0},{16,24},{24,16},{1,9},{9,1},{17,25},{25,17},{2,10},{10... | collective-permute-start | bytes 1572872 | tf_op jit(solution)/shard_map/ppermute | solution.py:152
  660.8 2.4 copy-start.7
  661.0 93.3 %collective-permute-start.28 = (f32[1,4,512,256]{2,3,1,0:T(8,128)S(1)}, f32[1,4,512,256]{2,3,1,0:T(8,128)S(1)}, u32[]{:S(2)}, u32[]{:S(2)}) collective-permute-start(f32[1,4,512,256]{2,3,1,0:T(8,128)S(1)} %constant_dynamic-slice_fusion.1), channel_id=1, source_target_pairs={{0,16},{8,24},{16,0},{24,8},{1,17},{9,25},{17,1},{25,9},{2,18},{10... | collective-permute-start | bytes 6291464 | tf_op jit(solution)/shard_map/ppermute | solution.py:152
  662.7 69.3 %collective-permute-start.26 = (f32[1,4,256,256]{3,2,1,0:T(8,128)S(1)}, f32[1,4,256,256]{3,2,1,0:T(8,128)S(1)}, u32[]{:S(2)}, u32[]{:S(2)}) collective-permute-start(f32[1,4,256,256]{3,2,1,0:T(8,128)S(1)} %constant_dynamic-slice_fusion.4), channel_id=1, source_target_pairs={{0,16},{8,24},{16,0},{24,8},{1,17},{9,25},{17,1},{25,9},{2,18},{10... | collective-permute-start | bytes 3145736 | tf_op jit(solution)/shard_map/ppermute | solution.py:152
  665.3 88.7 %collective-permute-start.37 = (f32[1,4,256,256]{3,2,1,0:T(8,128)S(1)}, f32[1,4,256,256]{3,2,1,0:T(8,128)S(1)}, u32[]{:S(2)}, u32[]{:S(2)}) collective-permute-start(f32[1,4,256,256]{3,2,1,0:T(8,128)S(1)} %constant_dynamic-slice_fusion), channel_id=1, source_target_pairs={{0,16},{8,24},{16,0},{24,8},{1,17},{9,25},{17,1},{25,9},{2,18},{10... | collective-permute-start | bytes 3145736 | tf_op jit(solution)/shard_map/ppermute | solution.py:152
  690.6 68.9 %copy-start.14 = (f32[512,512]{1,0:T(8,128)}, f32[512,512]{1,0:T(8,128)S(1)}, u32[]{:S(2)}) copy-start(f32[512,512]{1,0:T(8,128)S(1)} %fusion.22) | copy-start | bytes 3145732
  (4 other events, 5.9 us)
Sparse Core Ops, SparseCore 0:
  46.3 130.8 all-reduce.1
  315.3 64.9 all-gather.1

commit v3 on v2

--- a/solution.py
+++ b/solution.py
@@ -92,47 +92,34 @@
     )(a)
 
 
-def split(x):
-    high = x.astype(jnp.bfloat16)
-    return high, (x - high.astype(F32)).astype(jnp.bfloat16)
-
-
-def spread_kernel(slot_ref, place_ref, part_ref, keep_ref, start_ref, high_ref, low_ref, factor_ref, piece_ref, *rest):
+def spread_kernel(slot_ref, place_ref, part_ref, keep_ref, left_ref, factor_ref, piece_ref, out_ref):
     t = pl.program_id(0)
-    high, low = split(factor_ref[0])
-    dims = (((1,), (0,)), ((), ()))
-    dot = lambda a, b: lax.dot_general(a, b, dims, preferred_element_type=F32)
-    value = dot(high_ref[...], high) + dot(high_ref[...], low) + dot(low_ref[...], high)
-    out_ref = rest[-1]
+    whole = factor_ref[0]
+    high = whole.astype(jnp.bfloat16)
+    low = (whole - high.astype(F32)).astype(jnp.bfloat16)
+    right = jnp.concatenate([high, low, high], axis=0)
+    value = lax.dot_general(left_ref[...], right, (((1,), (0,)), ((), ())), preferred_element_type=F32)
     out_ref[0] = jnp.where(keep_ref[t] > 0, piece_ref[0] - value, 0.0)
-    if len(rest) == 2:
-        extra = rest[0][0]
-        rows = pl.ds(pl.multiple_of(start_ref[0], 8), extra.shape[0])
-        out_ref[0, rows, :] += extra
-
-
-def spread_update(slots, places, parts, keeps, mine, factor, pieces, width, start, extra=None):
-    high, low = split(mine.T)
+
+
+def spread_update(slots, places, parts, keeps, mine, factor, pieces, width):
+    turned = mine.T
+    rounded = lax.reduce_precision(turned, 8, 7)
+    high = rounded.astype(jnp.bfloat16)
+    low = (turned - rounded).astype(jnp.bfloat16)
+    left = jnp.concatenate([high, high, low], axis=1)
     count = slots.shape[0]
-    q, depth = high.shape
-    whole = lambda t, *refs: (0, 0)
-    block = lambda t, s, p, h, *refs: (s[t], 0, h[t])
-    piece = lambda t, s, p, h, *refs: (p[t], 0, h[t])
-    more = []
-    if extra is not None:
-        per = extra.shape[2] // width
-        more = [pl.BlockSpec((1, extra.shape[1], width), lambda t, *refs: (t // per, 0, t % per))]
+    q, depth = turned.shape
     return pl.pallas_call(
         spread_kernel,
         grid_spec=pltpu.PrefetchScalarGridSpec(
-            num_scalar_prefetch=5,
+            num_scalar_prefetch=4,
             grid=(count,),
             in_specs=[
-                pl.BlockSpec((q, depth), whole),
-                pl.BlockSpec((q, depth), whole),
-                pl.BlockSpec((1, depth, width), block),
-                pl.BlockSpec((1, q, width), piece),
-            ] + more,
+                pl.BlockSpec((q, 3 * depth), lambda t, *refs: (0, 0)),
+                pl.BlockSpec((1, depth, width), lambda t, s, p, h, k: (s[t], 0, h[t])),
+                pl.BlockSpec((1, q, width), lambda t, s, p, h, k: (p[t], 0, h[t])),
+            ],
             out_specs=pl.BlockSpec((1, q, width), lambda t, *refs: (t, 0, 0)),
         ),
         out_shape=jax.ShapeDtypeStruct((count, q, width), F32),
@@ -140,10 +127,10 @@
         cost_estimate=pl.CostEstimate(
             flops=6 * count * q * depth * width,
             bytes_accessed=4 * count * width * (2 * q + depth), transcendentals=0),
-    )(slots, places, parts, keeps, start, high, low, factor, pieces, *([] if extra is None else [extra]))
-
-
-def product(a, b, ca, cb, precision=lax.Precision.HIGHEST):
+    )(slots, places, parts, keeps, left, factor, pieces)
+
+
+def product(a, b, ca, cb, precision=lax.Precision.HIGH):
     return lax.dot_general(a, b, (((ca,), (cb,)), ((), ())), precision=precision)
 
 
@@ -180,23 +167,25 @@
     return jnp.concatenate([jnp.where(low == 0, part, other), jnp.where(low == 0, other, part)], axis=0)
 
 
-def line_gather(x, axis, ny):
-    n = lax.axis_size(axis)
-    nz = n // ny
-    z = lax.axis_index(axis) // ny
-    slots = [x]
-    up, down = [x], [x]
-    for step in range(1, nz):
-        up.append(lax.ppermute(up[-1], axis, [(c, c + ny) for c in range(n) if step - 1 <= c // ny < nz - 1]))
-        down.append(lax.ppermute(down[-1], axis, [(c, c - ny) for c in range(n) if 0 < c // ny <= nz - step]))
-    for k in range(1, nz):
-        slots.append(jnp.where(z >= k, up[k], down[nz - k]))
-    beside = []
-    for k in range(nz):
-        for j in range(1, ny):
-            pairs = [(c, c // ny * ny + (c % ny - j) % ny) for c in range(n)]
-            beside.append(lax.ppermute(slots[k], axis, pairs))
-    return slots + beside
+def share_rows(x, ny):
+    branches = lax.axis_size("branch")
+    groups = lax.axis_size("col")
+    nz = groups // ny
+    col = lax.axis_index("col")
+    branch = lax.axis_index("branch")
+    if nz != branches:
+        return lax.dynamic_slice_in_dim(lax.all_gather(x, "col"), branch * groups // branches, groups // branches, 0)
+    place = lambda b, z, y: b * groups + z * ny + y
+    got = jnp.where(col // ny == branch, x, 0.0)
+    for off in range(1, nz):
+        pairs = [(place(b, b, y), place(b, (b + off) % nz, y)) for b in range(branches) for y in range(ny)]
+        got = got + lax.ppermute(x, ("branch", "col"), pairs)
+    shares = [got]
+    for j in range(1, ny):
+        pairs = [(c, c // ny * ny + (c % ny - j) % ny) for c in range(groups)]
+        shares.append(lax.ppermute(got, "col", pairs))
+    order = (jnp.arange(ny) - col % ny) % ny
+    return jnp.take(jnp.stack(shares), order, axis=0)
 
 
 def on_device(child_fronts, extend_map, parent_front):
@@ -241,65 +230,52 @@
 
     pivots = lax.psum(placed(front[:P_SIZE]), "col")
 
-    pivot_units = PP // width
-    lead = jnp.concatenate(
-        [front[:P_SIZE]] + [jnp.where(keeps[u] > 0, unit_rows(u), 0.0) for u in range(pivot_units)], axis=0)
-    gathered = line_gather(lead, "col", ny)
-    back = (col // ny - source // ny) % nz
-    aside = (source % ny - col % ny) % ny
-    slots = jnp.where(aside == 0, back, nz + back * (ny - 1) + aside - 1)
-
-    share = PP // branches
-    ours = jnp.where(branch == 0, parent_front[:PP], 0.0).reshape(branches, share, pcols)
-    ours = lax.all_gather(sum_scatter(ours, "branch"), "col")
-    start = jnp.reshape(branch * share, (1,)).astype(jnp.int32)
-
-    moved = []
-    for a in range(per):
-        received = [unit_rows(col * per + a)]
-        for shift in range(1, groups):
-            pairs = [(c, (c + shift) % groups) for c in range(groups) if c >= pivot_devices]
-            received.append(lax.ppermute(unit_rows((col + shift) % groups * per + a), "col", pairs))
-        moved.append(jnp.stack(received))
-    shifts = (col - source) % groups
-
+    def rows_for(target):
+        return jnp.concatenate([unit_rows(target * per + a) for a in range(per)], axis=0)
+
+    def moved(shift, rows):
+        pairs = [(c, (c + shift) % groups) for c in range(groups) if c >= pivot_devices]
+        return lax.ppermute(rows, "col", pairs)
+
+    far = sorted(range(1, groups), key=lambda shift: abs(2 * shift - groups))
+    received = {0: rows_for(col)}
+    for shift in far[:5]:
+        received[shift] = moved(shift, rows_for((col + shift) % groups))
+
+    top = lax.all_gather(front[:P_SIZE], "col")
     inverse = inverse_factor(pivots)
     child_mine = product(inverse, front[:P_SIZE], 1, 0)
-    factor = jnp.stack([product(inverse, x[:P_SIZE], 1, 0) for x in gathered])
+    for shift in far[5:]:
+        rows, _ = lax.optimization_barrier((rows_for((col + shift) % groups), inverse))
+        received[shift] = moved(shift, rows)
+    places = (col - source) % groups
+
+    factor = jnp.stack([product(inverse, top[c], 1, 0) for c in range(groups)])
 
     def factor_columns(u):
-        block = lax.dynamic_slice(factor, (slots[u], 0, parts[u] * width), (1, P_SIZE, width))
+        block = lax.dynamic_slice(factor, (source[u], 0, parts[u] * width), (1, P_SIZE, width))
         return jnp.where(keeps[u] > 0, block[0], 0.0)
 
-    head = jnp.concatenate([factor_columns(u) for u in range(pivot_units)], axis=1)
-    head_rows = jnp.stack([x[P_SIZE:] for x in gathered])
-    first = spread_update(slots, slots, parts, keeps, head, factor, head_rows, width, start, ours)
-
-    def first_columns(begin, count):
-        wide = lax.dynamic_slice_in_dim(first, begin, count, 0)
-        return jnp.transpose(wide, (1, 0, 2)).reshape(PP, count * width)
-
-    corner = sum_all(first_columns(0, pivot_units), "branch")
-    top_mine = sum_all(first_columns(col * per, per), "branch")
-    side = sum_scatter(first.reshape((branches, units_total // branches) + first.shape[1:]), "branch")
-    side = jnp.transpose(side, (1, 0, 2)).reshape(PP, nrows)
+    mine = jnp.concatenate([factor_columns(col * per + a) for a in range(per)], axis=1)
+    mine_keep = jnp.repeat(lax.dynamic_slice_in_dim(keeps, col * per, per), width)[:, None] > 0
+    pieces = jnp.stack([jnp.where(mine_keep, received[shift], 0.0) for shift in range(groups)])
+
+    spread = spread_update(source, places, parts, keeps, mine, factor, pieces, width)
+    pivot_units = PP // width
+    first = jnp.where(branch == 0, parent_front[:PP].T, 0.0)
+    first = first + jnp.concatenate([spread[u] for u in range(pivot_units)], axis=1)
+    first = sum_all(first, "branch")
+    corner = lax.psum(placed(first.T) if pivot_devices > 1 else placed(first), "col")
+    side = share_rows(first, ny).reshape(nrows, PP)
+
+    added = sum_scatter(spread.reshape((branches, units_total // branches) + spread.shape[1:]), "branch")
+    assembled = parent_front + jnp.transpose(added, (0, 2, 1)).reshape(nrows, pcols)
 
     parent_inverse = inverse_factor(corner)
-    parent_mine = product(parent_inverse, top_mine, 1, 0)
-    row_factor = product(parent_inverse, side, 1, 0)
-
-    results = []
-    for a in range(per):
-        unit = col * per + a
-        spread = spread_update(
-            slots, shifts, parts, keeps * keeps[unit], factor_columns(unit), factor, moved[a], width, start)
-        spread = spread.reshape((branches, units_total // branches) + spread.shape[1:])
-        added = jnp.transpose(sum_scatter(spread, "branch"), (0, 2, 1)).reshape(nrows, width)
-        columns = slice(a * width, (a + 1) * width)
-        results.append(
-            parent_front[:, columns] + added
-            - product(row_factor, parent_mine[:, columns], 0, 0, lax.Precision.HIGH))
-    return (child_mine[None], parent_mine, jnp.concatenate(results, axis=1))
+    parent_mine = product(parent_inverse, first, 1, 1)
+    row_factor = product(side, parent_inverse, 1, 1)
+    result = assembled - product(row_factor, parent_mine, 1, 0)
+    return (child_mine[None], parent_mine, result)
 
 
 def solution(mesh):

time: 778 us -> 628 us (0.81)
  local copies, waits for them, and re-layouts: 93 us -> 35.3 us
  waiting for transfers between devices: 428 us -> 387 us
  starting transfers between devices: 67.6 us -> 40.8 us
  Pallas kernels: 78.6 us -> 58.2 us
    ppermute x24 -> x11, waiting for transfers between devices: 352 us -> 137 us  [the longest x7 114 us: moved(): return lax.ppermute(rows, 'col', pairs)]
    psum x1, waiting for transfers between devices: 0.02 us -> 122 us  [on_device(): pivots = lax.psum(placed(front[:P_SIZE]), 'col')]
    psum x0 -> x1, waiting for transfers between devices: none -> 76.4 us  [on_device(): lax.psum(placed(first.T) if pivot_devices > 1 else placed(first), 'col')]
    ppermute x14 -> x5, waiting for transfers between devices: 75.6 us -> 19.7 us  [flip(): return lax.ppermute(x, axis, [(i, i ^ bit) for i in range(n)])]
    unnamed x78 -> x23, local copies, waits for them, and re-layouts: 54.2 us -> 14.6 us
    all_gather x1, waiting for transfers between devices: 0.01 us -> 32.1 us  [on_device(): top = lax.all_gather(front[:P_SIZE], 'col')]
    pallas_call x3 -> x1, Pallas kernels: 35.7 us -> 14.9 us  [spread_update(): pl.pallas_call(spread_kernel, grid_spec=pltpu.PrefetchScalarGridSpec(num_...]
    ppermute x24 -> x11, starting transfers between devices: 58.6 us -> 38.8 us  [the longest x3 17.6 us: share_rows(): got = got + lax.ppermute(x, ('branch', 'col'), pairs)]
  transfers between devices with their start and end apart: 40 -> 19, of which waited for: 12 -> 12; matrix products, arithmetic and copies ran while one was open for 14% -> 10% of each run, Pallas kernels for 10% -> 7%
where the time goes in v3:
time: 628 us; the launch traced here: 624 us
  waiting for transfers between devices  387 us (62%)
  Pallas kernels  58.2 us (9%)
  other arithmetic  44.8 us (7%)
  starting transfers between devices  40.8 us (6%)
  local copies, waits for them, and re-layouts  35.3 us (6%)
  between operations  31 us (5%)
  matrix products  26.8 us (4%)
    psum x1, waiting for transfers between devices, on_device(): pivots = lax.psum(placed(front[:P_SIZE]), 'col')  122 us
    ppermute x7, waiting for transfers between devices, moved(): return lax.ppermute(rows, 'col', pairs)  114 us
    psum x1, waiting for transfers between devices, on_device(): lax.psum(placed(first.T) if pivot_devices > 1 else placed(first), 'col')  76.4 us
    pallas_call x2, Pallas kernels, inverse_factor(): pl.pallas_call(inverse_factor_kernel, out_shape=jax.ShapeDtypeStruct((n,...  43.2 us
    all_gather x1, waiting for transfers between devices, on_device(): top = lax.all_gather(front[:P_SIZE], 'col')  32.1 us
    dot_general x12, matrix products, product(): lax.dot_general(a, b, (((ca,), (cb,)), ((), ())), precision=precision)  26.8 us
    ppermute x3, waiting for transfers between devices, share_rows(): got = got + lax.ppermute(x, ('branch', 'col'), pairs)  20.4 us
    ppermute x5, waiting for transfers between devices, flip(): return lax.ppermute(x, axis, [(i, i ^ bit) for i in range(n)])  19.7 us
  transfers between devices with their start and end apart: 19, of which 12 were waited for; matrix products, arithmetic and copies ran while one was open for 10% of the time, Pallas kernels for 7%

profile of v3, /device:TPU:0, one launch (start us, length us, event | category | flops | bytes accessed | tf_op | source)
XLA Modules:
  0.0 624.1 jit_solution(5647011554570790767)
XLA Ops:
  7.2 2.3 bitcast_select_fusion.1
  9.6 2.3 slice.41
  24.3 5.8 dynamic-slice_bitcast_fusion.2
  31.2 1.3 collective-permute-start.5
  33.6 1.3 collective-permute-start.3
  35.9 1.5 collective-permute-start.2
  38.4 122.2 %all-reduce.3.cloned.1.call-done.a_ref = f32[512,512]{1,0:T(8,128)} async-done(((f32[512,512]{1,0:T(8,128)}), f32[512,512]{1,0:T(8,128)}) %all-reduce.3.cloned.1.call-update) | async-done | bytes 1048592 | tf_op jit(solution)/shard_map/psum | solution.py:231
  160.7 1.2 copy-done.3
  161.9 21.7 %shard_map.58 = f32[512,512]{1,0:T(8,128)S(1)} custom-call(f32[512,512]{1,0:T(8,128)S(1)} %copy-done.3), custom_call_target="tpu_custom_call" | custom-call | flops 134217728 | bytes 2097152 | tf_op jit(solution)/shard_map/pallas_call | solution.py:85
  183.6 1.3 collective-permute-start
  184.9 2.2 pad_maximum_fusion.3
  187.2 1.3 collective-permute-start.1
  195.2 1.4 copy.67
  197.8 1.3 pad_maximum_fusion.8
  199.1 1.3 pad_maximum_fusion.6
  200.4 1.2 fusion.10
  201.5 36.0 %collective-permute-done = f32[512,512]{1,0:T(8,128)} collective-permute-done((f32[512,512]{1,0:T(8,128)}, f32[512,512]{1,0:T(8,128)}, u32[]{:S(2)}, u32[]{:S(2)}) %collective-permute-start) | collective-permute-done | bytes 1048608 | tf_op jit(solution)/shard_map/ppermute | solution.py:238
  237.5 1.3 collective-permute-start.4
  238.8 2.7 bitcast_dynamic-update-slice_fusion.6
  241.5 1.3 collective-permute-start.6
  242.8 2.3 bitcast_dynamic-update-slice_fusion.5
  245.1 2.4 bitcast_dynamic-update-slice_fusion.4
  247.5 2.3 bitcast_dynamic-update-slice_fusion.3
  249.8 77.2 %collective-permute-done.4 = f32[512,512]{1,0:T(8,128)S(1)} collective-permute-done((f32[512,512]{1,0:T(8,128)S(1)}, f32[512,512]{1,0:T(8,128)S(1)}, u32[]{:S(2)}, u32[]{:S(2)}) %collective-permute-start.4) | collective-permute-done | bytes 1048608 | tf_op jit(solution)/shard_map/ppermute | solution.py:238
  327.0 1.1 bitcast_dynamic-update-slice_fusion.2
  328.2 2.3 bitcast_dynamic-update-slice_fusion.1
  332.7 32.1 %all-gather.2.cloned.1.call-done = f32[8,512,512]{2,1,0:T(8,128)} async-done(((f32[1,512,512]{2,1,0:T(8,128)}), f32[8,512,512]{2,1,0:T(8,128)}) %all-gather.2.cloned.1.call-update) | async-done | bytes 8388624 | tf_op jit(solution)/shard_map/all_gather | solution.py:245
  364.7 2.4 fusion.8
  367.1 2.5 fusion.7
  369.7 2.2 fusion.6
  377.2 3.3 copy-done.1
  380.6 1.3 pad_maximum_fusion.1
  381.9 1.7 copy.55.left_ref
  383.6 3.4 copy-done.2
  387.0 14.9 %shard_map.59 = f32[16,512,256]{2,1,0:T(8,128)S(1)} custom-call(s32[16]{0:T(128)S(1)} %get-tuple-element.10.slot_ref, s32[16]{0:T(128)S(1)} %get-tuple-element.9.place_ref, s32[16]{0:T(128)S(1)} %get-tuple-element.7.part_ref, s32[16]{0:T(128)S(1)} %gather_fusion.1, bf16[512,1536]{1,0:T(8,128)(2,1)S(1)} %copy.55.left_ref, f32[8,512,512]{2,1,0:T(8,128)S(1)} %copy-done.2, ...), custom_call_target="tpu_custom_call" | custom-call | flops 6442450944 | bytes 25165824 | tf_op jit(solution)/shard_map/pallas_call | solution.py:113
  401.9 2.2 dynamic-slice_bitcast_fusion
  404.3 2.1 copy-done
  407.0 5.1 collective-permute-done.7
  412.2 1.4 collective-permute-start.8
  413.6 12.6 %collective-permute-done.8 = f32[256,512]{1,0:T(8,128)S(1)} collective-permute-done((f32[256,512]{1,0:T(8,128)S(1)}, f32[256,512]{1,0:T(8,128)S(1)}, u32[]{:S(2)}, u32[]{:S(2)}) %collective-permute-start.8) | collective-permute-done | bytes 524320 | tf_op jit(solution)/shard_map/ppermute | solution.py:139
  426.4 2.0 collective-permute-done.9
  428.4 1.1 broadcast_select_fusion.2
  430.6 2.3 collective-permute-start.12
  432.9 12.9 %collective-permute-start.13 = (f32[512,512]{1,0:T(8,128)}, f32[512,512]{1,0:T(8,128)}, u32[]{:S(2)}, u32[]{:S(2)}) collective-permute-start(f32[512,512]{1,0:T(8,128)} %pad_maximum_fusion.9), channel_id=1, source_target_pairs={{0,4},{1,5},{10,14},{11,15},{20,16},{21,17},{30,26},{31,27}} | collective-permute-start | bytes 3145736 | tf_op jit(solution)/shard_map/ppermute | solution.py:182
  445.8 2.4 collective-permute-start.14
  448.2 9.2 %collective-permute-done.13 = f32[512,512]{1,0:T(8,128)} collective-permute-done((f32[512,512]{1,0:T(8,128)}, f32[512,512]{1,0:T(8,128)}, u32[]{:S(2)}, u32[]{:S(2)}) %collective-permute-start.13) | collective-permute-done | bytes 1048608 | tf_op jit(solution)/shard_map/ppermute | solution.py:182
  457.4 11.2 %collective-permute-done.14 = f32[512,512]{1,0:T(8,128)} collective-permute-done((f32[512,512]{1,0:T(8,128)}, f32[512,512]{1,0:T(8,128)}, u32[]{:S(2)}, u32[]{:S(2)}) %collective-permute-start.14) | collective-permute-done | bytes 1048608 | tf_op jit(solution)/shard_map/ppermute | solution.py:182
  468.6 3.7 add_add_fusion
  472.3 12.1 %collective-permute-start.15 = (f32[512,512]{1,0:T(8,128)}, f32[512,512]{1,0:T(8,128)}, u32[]{:S(2)}, u32[]{:S(2)}) collective-permute-start(f32[512,512]{1,0:T(8,128)} %get-tuple-element.31), channel_id=1, source_target_pairs={{0,1},{1,0},{2,3},{3,2},{4,5},{5,4},{6,7},{7,6},{8,9},{9,8},{10,11... | collective-permute-start | bytes 3145736 | tf_op jit(solution)/shard_map/ppermute | solution.py:186
  484.4 4.2 bitcast_add_fusion
  488.6 2.0 copy-done.5
  490.6 1.5 constant_dynamic-slice_fusion
  492.2 3.2 convolution_bitcast_fusion.8
  495.4 2.1 collective-permute-done.15
  497.5 3.1 pad_maximum_fusion
  500.6 2.3 gather_fusion.2
  502.9 76.4 %all-reduce.5.cloned.1.call-done.a_ref = f32[512,512]{1,0:T(8,128)} async-done(((f32[512,512]{1,0:T(8,128)}), f32[512,512]{1,0:T(8,128)}) %all-reduce.5.cloned.1.call-update) | async-done | bytes 1048592 | tf_op jit(solution)/shard_map/psum | solution.py:268
  579.3 1.2 copy-done.4
  580.6 21.5 %shard_map.60 = f32[512,512]{1,0:T(8,128)S(1)} custom-call(f32[512,512]{1,0:T(8,128)S(1)} %copy-done.4), custom_call_target="tpu_custom_call" | custom-call | flops 134217728 | bytes 2097152 | tf_op jit(solution)/shard_map/pallas_call | solution.py:85
  602.1 2.0 fusion.18
  604.3 3.3 fusion.23
  607.6 1.9 add_bitcast_fusion
  609.4 1.9 copy.58
  611.3 6.1 fusion
  (73 shorter events, 18.0 us)
Async XLA Ops:
  7.2 153.5 %all-reduce.3.cloned.1.call-start = ((), (), s32[]{:S(2)}) async-start(), calls=%async_computation | async-start | bytes 2097152 | tf_op jit(solution)/shard_map/psum | solution.py:231
  9.5 355.2 %all-gather.2.cloned.1.call-start = ((), (), s32[]{:S(2)}) async-start(), calls=%async_computation.1 | async-start | bytes 9437184 | tf_op jit(solution)/shard_map/all_gather | solution.py:245
  11.9 567.5 %all-reduce.5.cloned.1.call-start = ((), (), s32[]{:S(2)}) async-start(), calls=%async_computation.2 | async-start | bytes 2097152 | tf_op jit(solution)/shard_map/psum | solution.py:268
  30.2 159.6 %copy-start.10 = (s32[1,14]{1,0:T(1,128)S(1)}, s32[1,14]{1,0:T(1,128)}, u32[]{:S(2)}) copy-start(s32[1,14]{1,0:T(1,128)} %param.4) | copy-start | bytes 172
  30.2 165.0 %slice-start = ((f32[1024,512]{1,0:T(8,128)}), f32[512,512]{1,0:T(8,128)S(1)}, s32[]{:S(2)}) async-start(f32[1024,512]{1,0:T(8,128)} %param.5), calls=%async_computation.3 | async-start | bytes 2097152 | tf_op jit(solution)/shard_map/slice | solution.py:265
  31.2 296.9 %collective-permute-start.5 = (f32[512,512]{1,0:T(8,128)}, f32[512,512]{1,0:T(8,128)}, u32[]{:S(2)}, u32[]{:S(2)}) collective-permute-start(f32[512,512]{1,0:T(8,128)} %pad_maximum_fusion.7), channel_id=1, source_target_pairs={{1,7},{2,0},{3,1},{4,2},{5,3},{6,4},{7,5},{9,15},{10,8},{11,9},{12... | collective-permute-start | bytes 3145736 | tf_op jit(solution)/shard_map/ppermute | solution.py:238
  33.6 213.9 %collective-permute-start.3 = (f32[512,512]{1,0:T(8,128)}, f32[512,512]{1,0:T(8,128)}, u32[]{:S(2)}, u32[]{:S(2)}) collective-permute-start(f32[512,512]{1,0:T(8,128)} %pad_maximum_fusion.5), channel_id=1, source_target_pairs={{1,5},{2,6},{3,7},{4,0},{5,1},{6,2},{7,3},{9,13},{10,14},{11,15},{... | collective-permute-start | bytes 3145736 | tf_op jit(solution)/shard_map/ppermute | solution.py:238
  35.9 209.2 %collective-permute-start.2 = (f32[512,512]{1,0:T(8,128)}, f32[512,512]{1,0:T(8,128)}, u32[]{:S(2)}, u32[]{:S(2)}) collective-permute-start(f32[512,512]{1,0:T(8,128)} %pad_maximum_fusion.4), channel_id=1, source_target_pairs={{1,4},{2,5},{3,6},{4,7},{5,0},{6,1},{7,2},{9,12},{10,13},{11,14},{... | collective-permute-start | bytes 3145736 | tf_op jit(solution)/shard_map/ppermute | solution.py:238
  160.7 1.2 copy-start.3
  183.6 53.9 %collective-permute-start = (f32[512,512]{1,0:T(8,128)}, f32[512,512]{1,0:T(8,128)}, u32[]{:S(2)}, u32[]{:S(2)}) collective-permute-start(f32[512,512]{1,0:T(8,128)} %pad_maximum_fusion.2), channel_id=1, source_target_pairs={{1,2},{2,3},{3,4},{4,5},{5,6},{6,7},{7,0},{9,10},{10,11},{11,12},{... | collective-permute-start | bytes 3145736 | tf_op jit(solution)/shard_map/ppermute | solution.py:238
  187.2 54.3 %collective-permute-start.1 = (f32[512,512]{1,0:T(8,128)}, f32[512,512]{1,0:T(8,128)}, u32[]{:S(2)}, u32[]{:S(2)}) collective-permute-start(f32[512,512]{1,0:T(8,128)} %pad_maximum_fusion.3), channel_id=1, source_target_pairs={{1,3},{2,4},{3,5},{4,6},{5,7},{6,0},{7,1},{9,11},{10,12},{11,13},{... | collective-permute-start | bytes 3145736 | tf_op jit(solution)/shard_map/ppermute | solution.py:238
  237.5 89.5 %collective-permute-start.4 = (f32[512,512]{1,0:T(8,128)S(1)}, f32[512,512]{1,0:T(8,128)S(1)}, u32[]{:S(2)}, u32[]{:S(2)}) collective-permute-start(f32[512,512]{1,0:T(8,128)S(1)} %pad_maximum_fusion.6), channel_id=1, source_target_pairs={{1,6},{2,7},{3,0},{4,1},{5,2},{6,3},{7,4},{9,14},{10,15},{11,8},{1... | collective-permute-start | bytes 3145736 | tf_op jit(solution)/shard_map/ppermute | solution.py:238
  241.5 90.1 %collective-permute-start.6 = (f32[512,512]{1,0:T(8,128)S(1)}, f32[512,512]{1,0:T(8,128)S(1)}, u32[]{:S(2)}, u32[]{:S(2)}) collective-permute-start(f32[512,512]{1,0:T(8,128)S(1)} %pad_maximum_fusion.8), channel_id=1, source_target_pairs={{1,0},{2,1},{3,2},{4,3},{5,4},{6,5},{7,6},{9,8},{10,9},{11,10},{12... | collective-permute-start | bytes 3145736 | tf_op jit(solution)/shard_map/ppermute | solution.py:238
  364.7 7.2 %copy-start.7 = (f32[8,512,512]{2,1,0:T(8,128)S(1)}, f32[8,512,512]{2,1,0:T(8,128)}, u32[]{:S(2)}) copy-start(f32[8,512,512]{2,1,0:T(8,128)} %all-gather.2.cloned.1.call-done) | copy-start | bytes 25165828
  377.2 3.3 copy-start.1
  383.6 3.4 copy-start.2
  401.9 4.5 copy-start
  401.9 4.6 copy-start.9
  404.2 80.2 %collective-permute-start.10 = (f32[2,4,512,256]{3,2,1,0:T(8,128)}, f32[2,4,512,256]{3,2,1,0:T(8,128)}, u32[]{:S(2)}, u32[]{:S(2)}) collective-permute-start(f32[2,4,512,256]{3,2,1,0:T(8,128)} %dynamic-slice_bitcast_fusion), channel_id=1, source_target_pairs={{0,8},{8,0},{16,24},{24,16},{1,9},{9,1},{17,25},{25,17},{2,10},{10... | collective-permute-start | bytes 12582920 | tf_op jit(solution)/shard_map/ppermute | solution.py:139
  406.8 5.3 collective-permute-start.7
  412.2 14.1 %collective-permute-start.8 = (f32[256,512]{1,0:T(8,128)S(1)}, f32[256,512]{1,0:T(8,128)S(1)}, u32[]{:S(2)}, u32[]{:S(2)}) collective-permute-start(f32[256,512]{1,0:T(8,128)S(1)} %dynamic-slice_add_fusion), channel_id=1, source_target_pairs={{0,16},{8,24},{16,0},{24,8},{1,17},{9,25},{17,1},{25,9},{2,18},{10... | collective-permute-start | bytes 1572872 | tf_op jit(solution)/shard_map/ppermute | solution.py:139
  426.3 2.1 collective-permute-start.9
  430.6 17.6 %collective-permute-start.12 = (f32[512,512]{1,0:T(8,128)}, f32[512,512]{1,0:T(8,128)}, u32[]{:S(2)}, u32[]{:S(2)}) collective-permute-start(f32[512,512]{1,0:T(8,128)} %pad_maximum_fusion.9), channel_id=1, source_target_pairs={{0,2},{1,3},{10,12},{11,13},{20,22},{21,23},{30,24},{31,25}} | collective-permute-start | bytes 3145736 | tf_op jit(solution)/shard_map/ppermute | solution.py:182
  432.9 24.5 %collective-permute-start.13 = (f32[512,512]{1,0:T(8,128)}, f32[512,512]{1,0:T(8,128)}, u32[]{:S(2)}, u32[]{:S(2)}) collective-permute-start(f32[512,512]{1,0:T(8,128)} %pad_maximum_fusion.9), channel_id=1, source_target_pairs={{0,4},{1,5},{10,14},{11,15},{20,16},{21,17},{30,26},{31,27}} | collective-permute-start | bytes 3145736 | tf_op jit(solution)/shard_map/ppermute | solution.py:182
  445.8 22.9 %collective-permute-start.14 = (f32[512,512]{1,0:T(8,128)}, f32[512,512]{1,0:T(8,128)}, u32[]{:S(2)}, u32[]{:S(2)}) collective-permute-start(f32[512,512]{1,0:T(8,128)} %pad_maximum_fusion.9), channel_id=1, source_target_pairs={{0,6},{1,7},{10,8},{11,9},{20,18},{21,19},{30,28},{31,29}} | collective-permute-start | bytes 3145736 | tf_op jit(solution)/shard_map/ppermute | solution.py:182
  472.3 25.2 %collective-permute-start.15 = (f32[512,512]{1,0:T(8,128)}, f32[512,512]{1,0:T(8,128)}, u32[]{:S(2)}, u32[]{:S(2)}) collective-permute-start(f32[512,512]{1,0:T(8,128)} %get-tuple-element.31), channel_id=1, source_target_pairs={{0,1},{1,0},{2,3},{3,2},{4,5},{5,4},{6,7},{7,6},{8,9},{9,8},{10,11... | collective-permute-start | bytes 3145736 | tf_op jit(solution)/shard_map/ppermute | solution.py:186
  488.6 2.0 copy-start.5
  492.0 115.5 %collective-permute-start.11 = (f32[1,4,512,256]{3,2,1,0:T(8,128)}, f32[1,4,512,256]{3,2,1,0:T(8,128)}, u32[]{:S(2)}, u32[]{:S(2)}) collective-permute-start(f32[1,4,512,256]{3,2,1,0:T(8,128)} %constant_dynamic-slice_fusion), channel_id=1, source_target_pairs={{0,16},{8,24},{16,0},{24,8},{1,17},{9,25},{17,1},{25,9},{2,18},{10... | collective-permute-start | bytes 6291464 | tf_op jit(solution)/shard_map/ppermute | solution.py:139
  579.3 1.2 copy-start.4
  580.6 27.0 %copy-start.6 = (f32[2,4,512,256]{3,2,1,0:T(8,128)S(1)}, f32[2,4,512,256]{3,2,1,0:T(8,128)}, u32[]{:S(2)}) copy-start(f32[2,4,512,256]{3,2,1,0:T(8,128)} %copy-done.5) | copy-start | bytes 12582916
  604.3 7.0 %copy-start.8 = (f32[512,512]{1,0:T(8,128)S(1)}, f32[512,512]{1,0:T(8,128)}, u32[]{:S(2)}) copy-start(f32[512,512]{1,0:T(8,128)} %fusion.18) | copy-start | bytes 3145732
Sparse Core Ops, SparseCore 0:
  12.1 148.5 all-reduce.2
  163.6 201.1 all-gather.1
  492.2 87.0 all-reduce.4

commit v4 on v3

--- a/solution.py
+++ b/solution.py
@@ -9,6 +9,8 @@
 P_SIZE = 512
 NP = 4096
 PP = 512
+EARLY = 4
+LATE = 5
 
 SUB = 8
 LANES = 128
@@ -102,14 +104,17 @@
     out_ref[0] = jnp.where(keep_ref[t] > 0, piece_ref[0] - value, 0.0)
 
 
-def spread_update(slots, places, parts, keeps, mine, factor, pieces, width):
-    turned = mine.T
+def three_part(x):
+    turned = x.T
     rounded = lax.reduce_precision(turned, 8, 7)
     high = rounded.astype(jnp.bfloat16)
     low = (turned - rounded).astype(jnp.bfloat16)
-    left = jnp.concatenate([high, high, low], axis=1)
+    return jnp.concatenate([high, high, low], axis=1)
+
+
+def spread_update(slots, places, parts, keeps, left, factor, pieces, width):
     count = slots.shape[0]
-    q, depth = turned.shape
+    q, depth = left.shape[0], left.shape[1] // 3
     return pl.pallas_call(
         spread_kernel,
         grid_spec=pltpu.PrefetchScalarGridSpec(
@@ -155,16 +160,20 @@
 
 def sum_all(x, axis):
     n = lax.axis_size(axis)
-    low = lax.axis_index(axis) % 2
-    half = x.shape[0] // 2
-    away = lax.dynamic_slice_in_dim(x, (1 - low) * half, half, 0)
-    part = lax.dynamic_slice_in_dim(x, low * half, half, 0) + flip(away, axis, 1)
-    bit = 2
-    while bit < n:
-        part = part + flip(part, axis, bit)
-        bit *= 2
-    other = flip(part, axis, 1)
-    return jnp.concatenate([jnp.where(low == 0, part, other), jnp.where(low == 0, other, part)], axis=0)
+    me = lax.axis_index(axis)
+    bits = []
+    while 1 << len(bits) < n:
+        bits.append(1 << len(bits))
+    for bit in bits:
+        high = (me // bit) % 2
+        half = x.shape[0] // 2
+        away = lax.dynamic_slice_in_dim(x, (1 - high) * half, half, 0)
+        x = lax.dynamic_slice_in_dim(x, high * half, half, 0) + flip(away, axis, bit)
+    for bit in reversed(bits):
+        high = (me // bit) % 2
+        other = flip(x, axis, bit)
+        x = jnp.concatenate([jnp.where(high == 0, x, other), jnp.where(high == 0, other, x)], axis=0)
+    return x
 
 
 def share_rows(x, ny):
@@ -228,7 +237,24 @@
         wide = lax.dynamic_update_slice_in_dim(wide, x, jnp.minimum(col, pivot_devices - 1) * ncols, 1)
         return jnp.where(col < pivot_devices, wide, 0.0)
 
-    pivots = lax.psum(placed(front[:P_SIZE]), "col")
+    top = lax.all_gather(front[:P_SIZE], "col")
+    pivots = jnp.concatenate([top[c] for c in range(pivot_devices)], axis=1) if pivot_devices > 1 else top[0]
+
+    pivot_units = PP // width
+
+    def pivot_column(b):
+        local = units[b] - col * per
+        ok = (local >= 0) & (local < per) & (keeps[b] > 0)
+        column = lax.dynamic_slice_in_dim(front, jnp.clip(local, 0, per - 1) * width, width, 1)
+        body = [
+            jnp.where(ok & (keeps[a] > 0), lax.dynamic_slice_in_dim(column, units[a] * width, width, 0), 0.0)
+            for a in range(pivot_units)
+        ]
+        return jnp.concatenate(body, axis=0)
+
+    corner = jnp.concatenate([pivot_column(b) for b in range(pivot_units)], axis=1)
+    corner = corner + jnp.where(branch == 0, placed(parent_front[:PP]), 0.0)
+    corner = sum_all(corner, "col")
 
     def rows_for(target):
         return jnp.concatenate([unit_rows(target * per + a) for a in range(per)], axis=0)
@@ -239,15 +265,18 @@
 
     far = sorted(range(1, groups), key=lambda shift: abs(2 * shift - groups))
     received = {0: rows_for(col)}
-    for shift in far[:5]:
+    for shift in far[:EARLY]:
         received[shift] = moved(shift, rows_for((col + shift) % groups))
-
-    top = lax.all_gather(front[:P_SIZE], "col")
+    for shift in far[EARLY:LATE]:
+        rows, _ = lax.optimization_barrier((rows_for((col + shift) % groups), corner))
+        received[shift] = moved(shift, rows)
+    pivots, received, corner = lax.optimization_barrier((pivots, received, corner))
+    for shift in far[LATE:]:
+        rows, _ = lax.optimization_barrier((rows_for((col + shift) % groups), pivots))
+        received[shift] = moved(shift, rows)
+
     inverse = inverse_factor(pivots)
     child_mine = product(inverse, front[:P_SIZE], 1, 0)
-    for shift in far[5:]:
-        rows, _ = lax.optimization_barrier((rows_for((col + shift) % groups), inverse))
-        received[shift] = moved(shift, rows)
     places = (col - source) % groups
 
     factor = jnp.stack([product(inverse, top[c], 1, 0) for c in range(groups)])
@@ -256,22 +285,25 @@
         block = lax.dynamic_slice(factor, (source[u], 0, parts[u] * width), (1, P_SIZE, width))
         return jnp.where(keeps[u] > 0, block[0], 0.0)
 
+    head = jnp.concatenate([factor_columns(u) for u in range(pivot_units)], axis=1)
+    corner = sum_all(corner - product(head, head, 0, 0), "branch")
+    parent_inverse = inverse_factor(corner)
+
     mine = jnp.concatenate([factor_columns(col * per + a) for a in range(per)], axis=1)
     mine_keep = jnp.repeat(lax.dynamic_slice_in_dim(keeps, col * per, per), width)[:, None] > 0
     pieces = jnp.stack([jnp.where(mine_keep, received[shift], 0.0) for shift in range(groups)])
-
-    spread = spread_update(source, places, parts, keeps, mine, factor, pieces, width)
-    pivot_units = PP // width
-    first = jnp.where(branch == 0, parent_front[:PP].T, 0.0)
-    first = first + jnp.concatenate([spread[u] for u in range(pivot_units)], axis=1)
-    first = sum_all(first, "branch")
-    corner = lax.psum(placed(first.T) if pivot_devices > 1 else placed(first), "col")
+    left = three_part(mine)
+    n = pivot_units
+    first = spread_update(source[:n], places[:n], parts[:n], keeps[:n], left, factor, pieces, width)
+    left, first = lax.optimization_barrier((left, first))
+    first = jnp.concatenate([first[u] for u in range(n)], axis=1)
+    first = sum_all(first + jnp.where(branch == 0, parent_front[:PP].T, 0.0), "branch")
     side = share_rows(first, ny).reshape(nrows, PP)
 
+    spread = spread_update(source, places, parts, keeps, left, factor, pieces, width)
     added = sum_scatter(spread.reshape((branches, units_total // branches) + spread.shape[1:]), "branch")
     assembled = parent_front + jnp.transpose(added, (0, 2, 1)).reshape(nrows, pcols)
 
-    parent_inverse = inverse_factor(corner)
     parent_mine = product(parent_inverse, first, 1, 1)
     row_factor = product(side, parent_inverse, 1, 1)
     result = assembled - product(row_factor, parent_mine, 1, 0)

time: 628 us -> 583 us (0.928)
  the two profiles are of different devices: /device:TPU:0 before, /device:TPU:25 now
where the time goes in v4:
time: 583 us; the launch traced here: 577 us
  waiting for transfers between devices  261 us (45%)
  starting transfers between devices  87.9 us (15%)
  Pallas kernels  60.1 us (10%)
  other arithmetic  53.9 us (9%)
  local copies, waits for them, and re-layouts  46.1 us (8%)
  between operations  40.6 us (7%)
  matrix products  28 us (5%)
    ppermute x16, waiting for transfers between devices, flip(): return lax.ppermute(x, axis, [(i, i ^ bit) for i in range(n)])  137 us
    ppermute x7, waiting for transfers between devices, moved(): return lax.ppermute(rows, 'col', pairs)  89.4 us
    ppermute x16, starting transfers between devices, flip(): return lax.ppermute(x, axis, [(i, i ^ bit) for i in range(n)])  44.2 us
    pallas_call x2, Pallas kernels, inverse_factor(): pl.pallas_call(inverse_factor_kernel, out_shape=jax.ShapeDtypeStruct((n,...  43.2 us
    ppermute x7, starting transfers between devices, moved(): return lax.ppermute(rows, 'col', pairs)  36.6 us
    ppermute x3, waiting for transfers between devices, share_rows(): got = got + lax.ppermute(x, ('branch', 'col'), pairs)  32.8 us
    dot_general x13, matrix products, product(): lax.dot_general(a, b, (((ca,), (cb,)), ((), ())), precision=precision)  28 us
    unnamed x43, local copies, waits for them, and re-layouts  18.1 us
  transfers between devices with their start and end apart: 28, of which 15 were waited for; matrix products, arithmetic and copies ran while one was open for 16% of the time, Pallas kernels for 4%

profile of v4, /device:TPU:25, one launch (start us, length us, event | category | flops | bytes accessed | tf_op | source)
XLA Modules:
  0.0 577.1 jit_solution(9265888309157564041)
XLA Ops:
  7.2 2.3 slice.88
  18.1 1.8 constant_dynamic-slice_fusion.12
  22.5 22.6 %collective-permute-done.4 = f32[256,512]{0,1:T(8,128)S(1)} collective-permute-done((f32[256,512]{0,1:T(8,128)S(1)}, f32[256,512]{0,1:T(8,128)S(1)}, u32[]{:S(2)}, u32[]{:S(2)}) %collective-permute-start.4) | collective-permute-done | bytes 524320 | tf_op jit(solution)/shard_map/ppermute | solution.py:144
  45.6 19.4 %collective-permute-done.5 = f32[128,512]{0,1:T(8,128)S(1)} collective-permute-done((f32[128,512]{0,1:T(8,128)S(1)}, f32[128,512]{0,1:T(8,128)S(1)}, u32[]{:S(2)}, u32[]{:S(2)}) %collective-permute-start.5) | collective-permute-done | bytes 262176 | tf_op jit(solution)/shard_map/ppermute | solution.py:144
  65.2 30.9 %collective-permute-done.6 = f32[64,512]{0,1:T(8,128)S(1)} collective-permute-done((f32[64,512]{0,1:T(8,128)S(1)}, f32[64,512]{0,1:T(8,128)S(1)}, u32[]{:S(2)}, u32[]{:S(2)}) %collective-permute-start.6) | collective-permute-done | bytes 131104 | tf_op jit(solution)/shard_map/ppermute | solution.py:144
  106.4 18.5 %collective-permute-done.7 = f32[64,512]{0,1:T(8,128)S(1)} collective-permute-done((f32[64,512]{0,1:T(8,128)S(1)}, f32[64,512]{0,1:T(8,128)S(1)}, u32[]{:S(2)}, u32[]{:S(2)}) %collective-permute-start.7) | collective-permute-done | bytes 131104 | tf_op jit(solution)/shard_map/ppermute | solution.py:144
  125.8 6.0 %dynamic-slice_bitcast_fusion.2 = (f32[256,512]{1,0:T(8,128)S(1)}, f32[256,512]{1,0:T(8,128)}, f32[256,512]{1,0:T(8,128)}, f32[256,512]{1,0:T(8,128)}, f32[256,5...) fusion(f32[1,4096,512]{2,1,0:T(8,128)} %param.3, ...), kind=kLoop, calls=%fused_computation.74 | loop fusion | bytes 16777280 | tf_op jit(solution)/shard_map/dynamic_slice | solution.py:231
  132.9 1.9 collective-permute-start.3
  134.8 20.8 %collective-permute-done.8 = f32[128,512]{0,1:T(8,128)S(1)} collective-permute-done((f32[128,512]{0,1:T(8,128)}, f32[128,512]{0,1:T(8,128)S(1)}, u32[]{:S(2)}, u32[]{:S(2)}) %collective-permute-start.8) | collective-permute-done | bytes 262176 | tf_op jit(solution)/shard_map/ppermute | solution.py:144
  156.5 14.4 %collective-permute-start.9 = (f32[256,512]{0,1:T(8,128)}, f32[256,512]{0,1:T(8,128)S(1)}, u32[]{:S(2)}, u32[]{:S(2)}) collective-permute-start(f32[256,512]{0,1:T(8,128)} %pad_maximum_fusion.13), channel_id=1, source_target_pairs={{0,1},{1,0},{2,3},{3,2},{4,5},{5,4},{6,7},{7,6},{8,9},{9,8},{10,11... | collective-permute-start | bytes 1572872 | tf_op jit(solution)/shard_map/ppermute | solution.py:144
  171.0 2.2 pad_maximum_fusion.5
  173.2 1.9 collective-permute-start.2
  175.1 2.3 pad_maximum_fusion.4
  177.4 1.9 collective-permute-start.1
  179.3 2.2 pad_maximum_fusion.3
  181.6 1.9 collective-permute-start
  183.5 3.0 pad_maximum_fusion.7
  186.5 4.5 collective-permute-done.9
  192.2 2.4 collective-permute-start.10
  208.9 1.5 all-gather.2.cloned.1.call-done
  211.9 80.8 %collective-permute-done.1 = f32[512,512]{1,0:T(8,128)} collective-permute-done((f32[512,512]{1,0:T(8,128)}, f32[512,512]{1,0:T(8,128)}, u32[]{:S(2)}, u32[]{:S(2)}) %collective-permute-start.1) | collective-permute-done | bytes 1048608 | tf_op jit(solution)/shard_map/ppermute | solution.py:264
  292.7 21.7 %shard_map.58 = f32[512,512]{1,0:T(8,128)S(1)} custom-call(f32[512,512]{1,0:T(8,128)S(1)} %slice_bitcast_fusion.14.a_ref), custom_call_target="tpu_custom_call" | custom-call | flops 134217728 | bytes 2097152 | tf_op jit(solution)/shard_map/pallas_call | solution.py:87
  314.4 1.9 collective-permute-start.15
  316.3 24.7 %collective-permute-start.16 = (f32[512,512]{1,0:T(8,128)}, f32[512,512]{1,0:T(8,128)}, u32[]{:S(2)}, u32[]{:S(2)}) collective-permute-start(f32[512,512]{1,0:T(8,128)} %pad_maximum_fusion.11), channel_id=1, source_target_pairs={{1,0},{2,1},{3,2},{4,3},{5,4},{6,5},{7,6},{9,8},{10,9},{11,10},{12... | collective-permute-start | bytes 3145736 | tf_op jit(solution)/shard_map/ppermute | solution.py:264
  340.9 2.2 fusion.8
  343.2 2.2 fusion.7
  353.0 3.3 copy-done
  357.8 1.7 copy.93.left_ref
  359.5 1.5 bitcast_dynamic-update-slice_fusion.7
  361.0 1.6 collective-permute-done.15
  366.7 1.5 bitcast_dynamic-update-slice_fusion.3
  371.0 7.0 %collective-permute-done.16 = f32[512,512]{1,0:T(8,128)} collective-permute-done((f32[512,512]{1,0:T(8,128)}, f32[512,512]{1,0:T(8,128)}, u32[]{:S(2)}, u32[]{:S(2)}) %collective-permute-start.16) | collective-permute-done | bytes 1048608 | tf_op jit(solution)/shard_map/ppermute | solution.py:264
  379.4 2.0 shard_map.60
  381.4 3.3 copy-done.2
  385.6 1.7 copy.95.left_ref
  387.4 3.4 copy-done.1
  390.7 15.0 %shard_map.61 = f32[16,512,256]{2,1,0:T(8,128)S(1)} custom-call(s32[16]{0:T(128)S(1)} %get-tuple-element.30.slot_ref, s32[16]{0:T(128)S(1)} %get-tuple-element.29.place_ref, s32[16]{0:T(128)S(1)} %and_select_fusion.3.part_ref, s32[16]{0:T(128)S(1)} %gather_fusion.1, bf16[512,1536]{1,0:T(8,128)(2,1)S(1)} %copy.95.left_ref, f32[8,512,512]{2,1,0:T(8,128)S(1)} %copy-done.1, ...), custom_call_target="tpu_custom_call" | custom-call | flops 6442450944 | bytes 25165824 | tf_op jit(solution)/shard_map/pallas_call | solution.py:118
  405.8 3.5 copy-done.3
  409.3 2.2 dynamic-slice_bitcast_fusion
  411.5 2.4 collective-permute-start.21
  415.0 6.8 %collective-permute-done.17 = f32[256,512]{1,0:T(8,128)} collective-permute-done((f32[256,512]{1,0:T(8,128)}, f32[256,512]{1,0:T(8,128)}, u32[]{:S(2)}, u32[]{:S(2)}) %collective-permute-start.17) | collective-permute-done | bytes 524320 | tf_op jit(solution)/shard_map/ppermute | solution.py:144
  425.2 2.6 fusion.10
  428.1 3.4 collective-permute-done.18
  434.0 1.5 collective-permute-start.11
  435.6 3.7 collective-permute-done.19
  441.2 2.1 collective-permute-start.20
  446.1 6.4 %collective-permute-done.12 = f32[128,512]{0,1:T(8,128)S(1)} collective-permute-done((f32[128,512]{0,1:T(8,128)S(1)}, f32[128,512]{0,1:T(8,128)S(1)}, u32[]{:S(2)}, u32[]{:S(2)}) %collective-permute-start.12) | collective-permute-done | bytes 262176 | tf_op jit(solution)/shard_map/ppermute | solution.py:144
  456.4 1.6 collective-permute-start.23
  459.4 1.8 collective-permute-start.25
  463.3 4.2 bitcast_add_fusion
  467.5 2.0 copy-done.6
  470.9 15.0 %collective-permute-start.22 = (f32[1,4,512,256]{3,2,1,0:T(8,128)}, f32[1,4,512,256]{3,2,1,0:T(8,128)}, u32[]{:S(2)}, u32[]{:S(2)}) collective-permute-start(f32[1,4,512,256]{3,2,1,0:T(8,128)} %constant_dynamic-slice_fusion), channel_id=1, source_target_pairs={{0,16},{8,24},{16,0},{24,8},{1,17},{9,25},{17,1},{25,9},{2,18},{10... | collective-permute-start | bytes 6291464 | tf_op jit(solution)/shard_map/ppermute | solution.py:144
  485.9 32.8 %collective-permute-done.24 = f32[512,512]{1,0:T(8,128)} collective-permute-done((f32[512,512]{1,0:T(8,128)}, f32[512,512]{1,0:T(8,128)}, u32[]{:S(2)}, u32[]{:S(2)}) %collective-permute-start.24) | collective-permute-done | bytes 1048608 | tf_op jit(solution)/shard_map/ppermute | solution.py:191
  518.7 2.4 add_add_fusion
  521.1 2.3 collective-permute-start.26
  523.4 3.2 convolution_bitcast_fusion.8
  528.0 21.5 %shard_map.59 = f32[512,512]{1,0:T(8,128)S(1)} custom-call(f32[512,512]{1,0:T(8,128)S(1)} %pad_maximum_fusion.9.a_ref), custom_call_target="tpu_custom_call" | custom-call | flops 134217728 | bytes 2097152 | tf_op jit(solution)/shard_map/pallas_call | solution.py:87
  549.5 2.0 fusion.22
  551.5 2.9 pad_maximum_fusion
  554.4 2.3 gather_fusion.2
  556.9 3.3 fusion.27
  560.2 1.9 add_bitcast_fusion
  562.1 1.8 copy.98
  564.0 6.1 %fusion = f32[1024,512]{1,0:T(8,128)} fusion(f32[1024,512]{1,0:T(8,128)} %param.5, f32[4,256,512]{2,1,0:T(8,128)} %copy.98, f32[1024,512]{1,0:T(8,128)} %fusion.27, f32[512,512]{1,0:T(8,128)S(1)} %copy-done.11), kind=kOutput, calls=%fused_computation.8 | convolution fusion | flops 1611661312 | bytes 9437184 | tf_op jit(solution)/shard_map/dot_general | solution.py:139
  (146 shorter events, 56.7 us)
Async XLA Ops:
  7.2 13.3 %slice-start.2 = ((f32[1024,512]{1,0:T(8,128)}), f32[512,512]{1,0:T(8,128)S(1)}, s32[]{:S(2)}) async-start(f32[1024,512]{1,0:T(8,128)} %param.5), calls=%async_computation.3 | async-start | bytes 2097152 | tf_op jit(solution)/shard_map/slice | solution.py:256
  7.2 203.2 %all-gather.2.cloned.1.call-start = ((), (), s32[]{:S(2)}) async-start(), calls=%async_computation | async-start | bytes 9437184 | tf_op jit(solution)/shard_map/all_gather | solution.py:240
  20.8 111.0 %copy-start.9 = (f32[512,512]{0,1:T(8,128)}, f32[512,512]{0,1:T(8,128)S(1)}, u32[]{:S(2)}) copy-start(f32[512,512]{0,1:T(8,128)S(1)} %copy.112) | copy-start | bytes 3145732
  21.2 23.9 %collective-permute-start.4 = (f32[256,512]{0,1:T(8,128)S(1)}, f32[256,512]{0,1:T(8,128)S(1)}, u32[]{:S(2)}, u32[]{:S(2)}) collective-permute-start(f32[256,512]{0,1:T(8,128)S(1)} %constant_dynamic-slice_fusion.8), channel_id=1, source_target_pairs={{0,1},{1,0},{2,3},{3,2},{4,5},{5,4},{6,7},{7,6},{8,9},{9,8},{10,11... | collective-permute-start | bytes 1572872 | tf_op jit(solution)/shard_map/ppermute | solution.py:144
  45.2 19.7 %collective-permute-start.5 = (f32[128,512]{0,1:T(8,128)S(1)}, f32[128,512]{0,1:T(8,128)S(1)}, u32[]{:S(2)}, u32[]{:S(2)}) collective-permute-start(f32[128,512]{0,1:T(8,128)S(1)} %constant_dynamic-slice_fusion.7), channel_id=1, source_target_pairs={{0,2},{1,3},{2,0},{3,1},{4,6},{5,7},{6,4},{7,5},{8,10},{9,11},{10,... | collective-permute-start | bytes 786440 | tf_op jit(solution)/shard_map/ppermute | solution.py:144
  65.1 31.0 %collective-permute-start.6 = (f32[64,512]{0,1:T(8,128)S(1)}, f32[64,512]{0,1:T(8,128)S(1)}, u32[]{:S(2)}, u32[]{:S(2)}) collective-permute-start(f32[64,512]{0,1:T(8,128)S(1)} %constant_dynamic-slice_fusion.6), channel_id=1, source_target_pairs={{0,4},{1,5},{2,6},{3,7},{4,0},{5,1},{6,2},{7,3},{8,12},{9,13},{10,... | collective-permute-start | bytes 393224 | tf_op jit(solution)/shard_map/ppermute | solution.py:144
  96.2 28.7 %collective-permute-start.7 = (f32[64,512]{0,1:T(8,128)S(1)}, f32[64,512]{0,1:T(8,128)S(1)}, u32[]{:S(2)}, u32[]{:S(2)}) collective-permute-start(f32[64,512]{0,1:T(8,128)S(1)} %dynamic-slice_add_fusion.4), channel_id=1, source_target_pairs={{0,4},{1,5},{2,6},{3,7},{4,0},{5,1},{6,2},{7,3},{8,12},{9,13},{10,... | collective-permute-start | bytes 393224 | tf_op jit(solution)/shard_map/ppermute | solution.py:144
  125.8 29.8 %collective-permute-start.8 = (f32[128,512]{0,1:T(8,128)}, f32[128,512]{0,1:T(8,128)S(1)}, u32[]{:S(2)}, u32[]{:S(2)}) collective-permute-start(f32[128,512]{0,1:T(8,128)} %pad_maximum_fusion.16), channel_id=1, source_target_pairs={{0,2},{1,3},{2,0},{3,1},{4,6},{5,7},{6,4},{7,5},{8,10},{9,11},{10,... | collective-permute-start | bytes 786440 | tf_op jit(solution)/shard_map/ppermute | solution.py:144
  132.9 79.0 %collective-permute-start.3 = (f32[512,512]{1,0:T(8,128)}, f32[512,512]{1,0:T(8,128)}, u32[]{:S(2)}, u32[]{:S(2)}) collective-permute-start(f32[512,512]{1,0:T(8,128)} %pad_maximum_fusion.6), channel_id=1, source_target_pairs={{1,6},{2,7},{3,0},{4,1},{5,2},{6,3},{7,4},{9,14},{10,15},{11,8},{1... | collective-permute-start | bytes 3145736 | tf_op jit(solution)/shard_map/ppermute | solution.py:264
  134.8 72.0 %copy-start.16 = (f32[256,512]{1,0:T(8,128)S(1)}, f32[256,512]{1,0:T(8,128)}, u32[]{:S(2)}) copy-start(f32[256,512]{1,0:T(8,128)} %get-tuple-element.46) | copy-start | bytes 1572868
  156.5 34.5 %collective-permute-start.9 = (f32[256,512]{0,1:T(8,128)}, f32[256,512]{0,1:T(8,128)S(1)}, u32[]{:S(2)}, u32[]{:S(2)}) collective-permute-start(f32[256,512]{0,1:T(8,128)} %pad_maximum_fusion.13), channel_id=1, source_target_pairs={{0,1},{1,0},{2,3},{3,2},{4,5},{5,4},{6,7},{7,6},{8,9},{9,8},{10,11... | collective-permute-start | bytes 1572872 | tf_op jit(solution)/shard_map/ppermute | solution.py:144
  173.2 38.6 %collective-permute-start.2 = (f32[512,512]{1,0:T(8,128)}, f32[512,512]{1,0:T(8,128)}, u32[]{:S(2)}, u32[]{:S(2)}) collective-permute-start(f32[512,512]{1,0:T(8,128)} %pad_maximum_fusion.5), channel_id=1, source_target_pairs={{1,5},{2,6},{3,7},{4,0},{5,1},{6,2},{7,3},{9,13},{10,14},{11,15},{... | collective-permute-start | bytes 3145736 | tf_op jit(solution)/shard_map/ppermute | solution.py:264
  177.4 115.2 %collective-permute-start.1 = (f32[512,512]{1,0:T(8,128)}, f32[512,512]{1,0:T(8,128)}, u32[]{:S(2)}, u32[]{:S(2)}) collective-permute-start(f32[512,512]{1,0:T(8,128)} %pad_maximum_fusion.4), channel_id=1, source_target_pairs={{1,4},{2,5},{3,6},{4,7},{5,0},{6,1},{7,2},{9,12},{10,13},{11,14},{... | collective-permute-start | bytes 3145736 | tf_op jit(solution)/shard_map/ppermute | solution.py:264
  181.6 111.1 %collective-permute-start = (f32[512,512]{1,0:T(8,128)}, f32[512,512]{1,0:T(8,128)}, u32[]{:S(2)}, u32[]{:S(2)}) collective-permute-start(f32[512,512]{1,0:T(8,128)} %pad_maximum_fusion.3), channel_id=1, source_target_pairs={{1,3},{2,4},{3,5},{4,6},{5,7},{6,0},{7,1},{9,11},{10,12},{11,13},{... | collective-permute-start | bytes 3145736 | tf_op jit(solution)/shard_map/ppermute | solution.py:264
  192.2 100.4 %collective-permute-start.10 = (f32[512,512]{1,0:T(8,128)}, f32[512,512]{1,0:T(8,128)}, u32[]{:S(2)}, u32[]{:S(2)}) collective-permute-start(f32[512,512]{1,0:T(8,128)} %get-tuple-element.16), channel_id=1, source_target_pairs={{1,7},{2,0},{3,1},{4,2},{5,3},{6,4},{7,5},{9,15},{10,8},{11,9},{12... | collective-permute-start | bytes 3145736 | tf_op jit(solution)/shard_map/ppermute | solution.py:264
  210.4 135.0 %copy-start.8 = (f32[8,512,512]{2,1,0:T(8,128)S(1)}, f32[8,512,512]{2,1,0:T(8,128)}, u32[]{:S(2)}) copy-start(f32[8,512,512]{2,1,0:T(8,128)} %all-gather.2.cloned.1.call-done) | copy-start | bytes 25165828
  314.4 48.2 %collective-permute-start.15 = (f32[512,512]{1,0:T(8,128)}, f32[512,512]{1,0:T(8,128)}, u32[]{:S(2)}, u32[]{:S(2)}) collective-permute-start(f32[512,512]{1,0:T(8,128)} %get-tuple-element.20), channel_id=1, source_target_pairs={{1,2},{2,3},{3,4},{4,5},{5,6},{6,7},{7,0},{9,10},{10,11},{11,12},{... | collective-permute-start | bytes 3145736 | tf_op jit(solution)/shard_map/ppermute | solution.py:264
  316.3 61.7 %collective-permute-start.16 = (f32[512,512]{1,0:T(8,128)}, f32[512,512]{1,0:T(8,128)}, u32[]{:S(2)}, u32[]{:S(2)}) collective-permute-start(f32[512,512]{1,0:T(8,128)} %pad_maximum_fusion.11), channel_id=1, source_target_pairs={{1,0},{2,1},{3,2},{4,3},{5,4},{6,5},{7,6},{9,8},{10,9},{11,10},{12... | collective-permute-start | bytes 3145736 | tf_op jit(solution)/shard_map/ppermute | solution.py:264
  353.0 3.3 copy-start
  359.5 19.9 %slice-start = ((s8[8388608]{0:T(1024)(128)(4,1)}), s8[4194304]{0:T(1024)(128)(4,1)S(1)}, s32[]{:S(2)}) async-start(s8[8388608]{0:T(1024)(128)(4,1)} %bitcast.209), calls=%async_computation.1 | async-start | bytes 8388608
  366.7 12.7 %slice-start.1 = ((s8[8388608]{0:T(1024)(128)(4,1)}), s8[4194304]{0:T(1024)(128)(4,1)S(1)}, s32[]{:S(2)}) async-start(s8[8388608]{0:T(1024)(128)(4,1)} %bitcast.209), calls=%async_computation.2 | async-start | bytes 8388608
  381.4 3.3 copy-start.2
  384.7 1.0 copy-start.4
  387.4 3.4 copy-start.1
  405.8 3.5 copy-start.3
  405.8 8.2 %copy-start.5 = (f32[2,512,256]{2,1,0:T(8,128)S(1)}, f32[2,512,256]{2,1,0:T(8,128)}, u32[]{:S(2)}) copy-start(f32[2,512,256]{2,1,0:T(8,128)} %copy-done.4) | copy-start | bytes 3145732
  405.8 8.2 %copy-start.10 = (f32[512,512]{0,1:T(8,128)S(1)}, f32[512,512]{0,1:T(8,128)}, u32[]{:S(2)}) copy-start(f32[512,512]{0,1:T(8,128)} %copy-done.9) | copy-start | bytes 3145732
  409.3 18.6 %copy-start.12 = (f32[512,512]{0,1:T(8,128)S(1)}, f32[512,512]{0,1:T(8,128)}, u32[]{:S(2)}) copy-start(f32[512,512]{0,1:T(8,128)} %pad_maximum_fusion.8) | copy-start | bytes 3145732
  411.5 51.7 %collective-permute-start.21 = (f32[2,4,512,256]{3,2,1,0:T(8,128)}, f32[2,4,512,256]{3,2,1,0:T(8,128)}, u32[]{:S(2)}, u32[]{:S(2)}) collective-permute-start(f32[2,4,512,256]{3,2,1,0:T(8,128)} %dynamic-slice_bitcast_fusion), channel_id=1, source_target_pairs={{0,8},{8,0},{16,24},{24,16},{1,9},{9,1},{17,25},{25,17},{2,10},{10... | collective-permute-start | bytes 12582920 | tf_op jit(solution)/shard_map/ppermute | solution.py:144
  415.0 6.8 %collective-permute-start.17 = (f32[256,512]{1,0:T(8,128)}, f32[256,512]{1,0:T(8,128)}, u32[]{:S(2)}, u32[]{:S(2)}) collective-permute-start(f32[256,512]{1,0:T(8,128)} %constant_dynamic-slice_fusion.2), channel_id=1, source_target_pairs={{0,8},{8,0},{16,24},{24,16},{1,9},{9,1},{17,25},{25,17},{2,10},{10... | collective-permute-start | bytes 1572872 | tf_op jit(solution)/shard_map/ppermute | solution.py:144
  423.0 0.8 copy-start.15
  423.8 7.7 %collective-permute-start.18 = (f32[128,512]{1,0:T(8,128)S(1)}, f32[128,512]{1,0:T(8,128)}, u32[]{:S(2)}, u32[]{:S(2)}) collective-permute-start(f32[128,512]{1,0:T(8,128)S(1)} %constant_dynamic-slice_fusion.1), channel_id=1, source_target_pairs={{0,16},{8,24},{16,0},{24,8},{1,17},{9,25},{17,1},{25,9},{2,18},{10... | collective-permute-start | bytes 786440 | tf_op jit(solution)/shard_map/ppermute | solution.py:144
  432.5 6.8 %collective-permute-start.19 = (f32[128,512]{1,0:T(8,128)S(1)}, f32[128,512]{1,0:T(8,128)}, u32[]{:S(2)}, u32[]{:S(2)}) collective-permute-start(f32[128,512]{1,0:T(8,128)S(1)} %dynamic-slice_add_fusion.3), channel_id=1, source_target_pairs={{0,16},{8,24},{16,0},{24,8},{1,17},{9,25},{17,1},{25,9},{2,18},{10... | collective-permute-start | bytes 786440 | tf_op jit(solution)/shard_map/ppermute | solution.py:144
  434.0 9.3 %collective-permute-start.11 = (f32[256,512]{0,1:T(8,128)S(1)}, f32[256,512]{0,1:T(8,128)}, u32[]{:S(2)}, u32[]{:S(2)}) collective-permute-start(f32[256,512]{0,1:T(8,128)S(1)} %constant_dynamic-slice_fusion.5), channel_id=1, source_target_pairs={{0,8},{8,0},{16,24},{24,16},{1,9},{9,1},{17,25},{25,17},{2,10},{10... | collective-permute-start | bytes 1572872 | tf_op jit(solution)/shard_map/ppermute | solution.py:144
  440.3 13.8 %copy-start.14 = (f32[128,512]{1,0:T(8,128)}, f32[128,512]{1,0:T(8,128)S(1)}, u32[]{:S(2)}) copy-start(f32[128,512]{1,0:T(8,128)S(1)} %get-tuple-element.67) | copy-start | bytes 786436
  441.2 13.0 %collective-permute-start.20 = (f32[256,512]{1,0:T(8,128)}, f32[256,512]{1,0:T(8,128)}, u32[]{:S(2)}, u32[]{:S(2)}) collective-permute-start(f32[256,512]{1,0:T(8,128)} %pad_maximum_fusion.15), channel_id=1, source_target_pairs={{0,8},{8,0},{16,24},{24,16},{1,9},{9,1},{17,25},{25,17},{2,10},{10... | collective-permute-start | bytes 1572872 | tf_op jit(solution)/shard_map/ppermute | solution.py:144
  444.5 8.0 %collective-permute-start.12 = (f32[128,512]{0,1:T(8,128)S(1)}, f32[128,512]{0,1:T(8,128)S(1)}, u32[]{:S(2)}, u32[]{:S(2)}) collective-permute-start(f32[128,512]{0,1:T(8,128)S(1)} %get-tuple-element.70), channel_id=1, source_target_pairs={{0,16},{8,24},{16,0},{24,8},{1,17},{9,25},{17,1},{25,9},{2,18},{10... | collective-permute-start | bytes 786440 | tf_op jit(solution)/shard_map/ppermute | solution.py:144
  452.7 8.5 %collective-permute-start.13 = (f32[128,512]{1,0:T(8,128)S(1)}, f32[128,512]{1,0:T(8,128)S(1)}, u32[]{:S(2)}, u32[]{:S(2)}) collective-permute-start(f32[128,512]{1,0:T(8,128)S(1)} %add.488), channel_id=1, source_target_pairs={{0,16},{8,24},{16,0},{24,8},{1,17},{9,25},{17,1},{25,9},{2,18},{10... | collective-permute-start | bytes 786440 | tf_op jit(solution)/shard_map/ppermute | solution.py:144
  456.4 29.5 %collective-permute-start.23 = (f32[512,512]{1,0:T(8,128)}, f32[512,512]{1,0:T(8,128)}, u32[]{:S(2)}, u32[]{:S(2)}) collective-permute-start(f32[512,512]{1,0:T(8,128)} %pad_maximum_fusion.12), channel_id=1, source_target_pairs={{0,2},{1,3},{10,12},{11,13},{20,22},{21,23},{30,24},{31,25}} | collective-permute-start | bytes 3145736 | tf_op jit(solution)/shard_map/ppermute | solution.py:191
  458.1 60.6 %collective-permute-start.24 = (f32[512,512]{1,0:T(8,128)}, f32[512,512]{1,0:T(8,128)}, u32[]{:S(2)}, u32[]{:S(2)}) collective-permute-start(f32[512,512]{1,0:T(8,128)} %pad_maximum_fusion.12), channel_id=1, source_target_pairs={{0,4},{1,5},{10,14},{11,15},{20,16},{21,17},{30,26},{31,27}} | collective-permute-start | bytes 3145736 | tf_op jit(solution)/shard_map/ppermute | solution.py:191
  459.4 59.3 %collective-permute-start.25 = (f32[512,512]{1,0:T(8,128)}, f32[512,512]{1,0:T(8,128)}, u32[]{:S(2)}, u32[]{:S(2)}) collective-permute-start(f32[512,512]{1,0:T(8,128)} %pad_maximum_fusion.12), channel_id=1, source_target_pairs={{0,6},{1,7},{10,8},{11,9},{20,18},{21,19},{30,28},{31,29}} | collective-permute-start | bytes 3145736 | tf_op jit(solution)/shard_map/ppermute | solution.py:191
  461.3 9.6 %copy-start.13 = (f32[128,512]{1,0:T(8,128)}, f32[128,512]{1,0:T(8,128)S(1)}, u32[]{:S(2)}) copy-start(f32[128,512]{1,0:T(8,128)S(1)} %get-tuple-element.69) | copy-start | bytes 786436
  462.2 64.5 %collective-permute-start.14 = (f32[256,512]{1,0:T(8,128)}, f32[256,512]{1,0:T(8,128)}, u32[]{:S(2)}, u32[]{:S(2)}) collective-permute-start(f32[256,512]{1,0:T(8,128)} %pad_maximum_fusion.14), channel_id=1, source_target_pairs={{0,8},{8,0},{16,24},{24,16},{1,9},{9,1},{17,25},{25,17},{2,10},{10... | collective-permute-start | bytes 1572872 | tf_op jit(solution)/shard_map/ppermute | solution.py:144
  467.4 2.0 copy-start.6
  470.9 89.3 %collective-permute-start.22 = (f32[1,4,512,256]{3,2,1,0:T(8,128)}, f32[1,4,512,256]{3,2,1,0:T(8,128)}, u32[]{:S(2)}, u32[]{:S(2)}) collective-permute-start(f32[1,4,512,256]{3,2,1,0:T(8,128)} %constant_dynamic-slice_fusion), channel_id=1, source_target_pairs={{0,16},{8,24},{16,0},{24,8},{1,17},{9,25},{17,1},{25,9},{2,18},{10... | collective-permute-start | bytes 6291464 | tf_op jit(solution)/shard_map/ppermute | solution.py:144
  521.1 30.4 %collective-permute-start.26 = (f32[512,512]{1,0:T(8,128)S(1)}, f32[512,512]{1,0:T(8,128)}, u32[]{:S(2)}, u32[]{:S(2)}) collective-permute-start(f32[512,512]{1,0:T(8,128)S(1)} %add_add_fusion), channel_id=1, source_target_pairs={{0,1},{1,0},{2,3},{3,2},{4,5},{5,4},{6,7},{7,6},{8,9},{9,8},{10,11... | collective-permute-start | bytes 3145736 | tf_op jit(solution)/shard_map/ppermute | solution.py:195
  556.7 3.5 copy-start.7
  556.9 7.1 %copy-start.11 = (f32[512,512]{1,0:T(8,128)S(1)}, f32[512,512]{1,0:T(8,128)}, u32[]{:S(2)}) copy-start(f32[512,512]{1,0:T(8,128)} %fusion.22) | copy-start | bytes 3145732
Sparse Core Ops, SparseCore 0:
  10.7 199.6 all-gather.1

commit v5 on v4

--- a/solution.py
+++ b/solution.py
@@ -10,7 +10,6 @@
 NP = 4096
 PP = 512
 EARLY = 4
-LATE = 5
 
 SUB = 8
 LANES = 128
@@ -158,13 +157,15 @@
     return x[0]
 
 
-def sum_all(x, axis):
+def sum_all(x, axis, gates=()):
     n = lax.axis_size(axis)
     me = lax.axis_index(axis)
     bits = []
     while 1 << len(bits) < n:
         bits.append(1 << len(bits))
-    for bit in bits:
+    for step, bit in enumerate(bits):
+        if step < len(gates):
+            x, _ = lax.optimization_barrier((x, gates[step]))
         high = (me // bit) % 2
         half = x.shape[0] // 2
         away = lax.dynamic_slice_in_dim(x, (1 - high) * half, half, 0)
@@ -174,6 +175,26 @@
         other = flip(x, axis, bit)
         x = jnp.concatenate([jnp.where(high == 0, x, other), jnp.where(high == 0, other, x)], axis=0)
     return x
+
+
+def line_gather(x, axis, ny):
+    n = lax.axis_size(axis)
+    nz = n // ny
+    up, down = [x], [x]
+    for step in range(1, nz):
+        up.append(lax.ppermute(up[-1], axis, [(c, c + ny) for c in range(n) if step - 1 <= c // ny < nz - 1]))
+        down.append(lax.ppermute(down[-1], axis, [(c, c - ny) for c in range(n) if 0 < c // ny <= nz - step]))
+
+    def beside(y, j, rows):
+        pairs = [(c, c // ny * ny + (c % ny - j) % ny) for c in range(n) if c // ny in rows]
+        return lax.ppermute(y, axis, pairs)
+
+    got = [[x] + [beside(x, j, range(nz)) for j in range(1, ny)]]
+    for k in range(1, nz):
+        above, below = range(k, nz), range(k)
+        got.append([up[k] + down[nz - k]] + [
+            beside(up[k], j, above) + beside(down[nz - k], j, below) for j in range(1, ny)])
+    return got, list(zip(up[1:], down[1:]))
 
 
 def share_rows(x, ny):
@@ -237,8 +258,20 @@
         wide = lax.dynamic_update_slice_in_dim(wide, x, jnp.minimum(col, pivot_devices - 1) * ncols, 1)
         return jnp.where(col < pivot_devices, wide, 0.0)
 
-    top = lax.all_gather(front[:P_SIZE], "col")
-    pivots = jnp.concatenate([top[c] for c in range(pivot_devices)], axis=1) if pivot_devices > 1 else top[0]
+    gathered, ends = line_gather(front[:P_SIZE], "col", ny)
+    nz = groups // ny
+    z, y = col // ny, col % ny
+    back = (z - source // ny) % nz
+    aside = (source % ny - y) % ny
+    slots = back * ny + aside
+
+    def top_of(c):
+        return sum(
+            jnp.where((z == (c // ny + k) % nz) & (y == (c % ny - j) % ny), gathered[k][j], 0.0)
+            for k in range(nz) for j in range(ny))
+
+    pivots = [top_of(c) for c in range(pivot_devices)]
+    pivots = jnp.concatenate(pivots, axis=1) if pivot_devices > 1 else pivots[0]
 
     pivot_units = PP // width
 
@@ -254,7 +287,7 @@
 
     corner = jnp.concatenate([pivot_column(b) for b in range(pivot_units)], axis=1)
     corner = corner + jnp.where(branch == 0, placed(parent_front[:PP]), 0.0)
-    corner = sum_all(corner, "col")
+    corner = sum_all(corner, "col", [front[:8], *ends])
 
     def rows_for(target):
         return jnp.concatenate([unit_rows(target * per + a) for a in range(per)], axis=0)
@@ -266,23 +299,23 @@
     far = sorted(range(1, groups), key=lambda shift: abs(2 * shift - groups))
     received = {0: rows_for(col)}
     for shift in far[:EARLY]:
-        received[shift] = moved(shift, rows_for((col + shift) % groups))
-    for shift in far[EARLY:LATE]:
-        rows, _ = lax.optimization_barrier((rows_for((col + shift) % groups), corner))
+        rows, _ = lax.optimization_barrier((rows_for((col + shift) % groups), ends[-1]))
         received[shift] = moved(shift, rows)
-    pivots, received, corner = lax.optimization_barrier((pivots, received, corner))
-    for shift in far[LATE:]:
-        rows, _ = lax.optimization_barrier((rows_for((col + shift) % groups), pivots))
+
+    inverse = inverse_factor(pivots)
+    for shift in far[EARLY:]:
+        rows, _ = lax.optimization_barrier((rows_for((col + shift) % groups), inverse))
         received[shift] = moved(shift, rows)
-
-    inverse = inverse_factor(pivots)
+    places = (col - source) % groups
     child_mine = product(inverse, front[:P_SIZE], 1, 0)
-    places = (col - source) % groups
-
-    factor = jnp.stack([product(inverse, top[c], 1, 0) for c in range(groups)])
+
+    early = [received[shift] for shift in far[:EARLY]]
+    inverse, early, corner = lax.optimization_barrier((inverse, early, corner))
+    received.update(zip(far[:EARLY], early))
+    factor = jnp.stack([product(inverse, x, 1, 0) for line in gathered for x in line])
 
     def factor_columns(u):
-        block = lax.dynamic_slice(factor, (source[u], 0, parts[u] * width), (1, P_SIZE, width))
+        block = lax.dynamic_slice(factor, (slots[u], 0, parts[u] * width), (1, P_SIZE, width))
         return jnp.where(keeps[u] > 0, block[0], 0.0)
 
     head = jnp.concatenate([factor_columns(u) for u in range(pivot_units)], axis=1)
@@ -294,13 +327,13 @@
     pieces = jnp.stack([jnp.where(mine_keep, received[shift], 0.0) for shift in range(groups)])
     left = three_part(mine)
     n = pivot_units
-    first = spread_update(source[:n], places[:n], parts[:n], keeps[:n], left, factor, pieces, width)
+    first = spread_update(slots[:n], places[:n], parts[:n], keeps[:n], left, factor, pieces, width)
     left, first = lax.optimization_barrier((left, first))
     first = jnp.concatenate([first[u] for u in range(n)], axis=1)
     first = sum_all(first + jnp.where(branch == 0, parent_front[:PP].T, 0.0), "branch")
     side = share_rows(first, ny).reshape(nrows, PP)
 
-    spread = spread_update(source, places, parts, keeps, left, factor, pieces, width)
+    spread = spread_update(slots, places, parts, keeps, left, factor, pieces, width)
     added = sum_scatter(spread.reshape((branches, units_total // branches) + spread.shape[1:]), "branch")
     assembled = parent_front + jnp.transpose(added, (0, 2, 1)).reshape(nrows, pcols)
 

time: 583 us -> 526 us (0.902)
  the two profiles are of different devices: /device:TPU:25 before, /device:TPU:29 now
where the time goes in v5:
time: 526 us; the launch traced here: 519 us
  waiting for transfers between devices  170 us (32%)
  starting transfers between devices  119 us (23%)
  other arithmetic  64.4 us (12%)
  Pallas kernels  60.1 us (11%)
  local copies, waits for them, and re-layouts  50.6 us (10%)
  between operations  27.5 us (5%)
  matrix products  26.6 us (5%)
    ppermute x16, waiting for transfers between devices, flip(): return lax.ppermute(x, axis, [(i, i ^ bit) for i in range(n)])  82.1 us
    ppermute x7, starting transfers between devices, moved(): return lax.ppermute(rows, 'col', pairs)  60.5 us
    pallas_call x2, Pallas kernels, inverse_factor(): pl.pallas_call(inverse_factor_kernel, out_shape=jax.ShapeDtypeStruct((n,...  43.2 us
    ppermute x7, waiting for transfers between devices, moved(): return lax.ppermute(rows, 'col', pairs)  40.1 us
    ppermute x3, waiting for transfers between devices, share_rows(): got = got + lax.ppermute(x, ('branch', 'col'), pairs)  31.5 us
    dot_general x13, matrix products, product(): lax.dot_general(a, b, (((ca,), (cb,)), ((), ())), precision=precision)  26.6 us
    ppermute x16, starting transfers between devices, flip(): return lax.ppermute(x, axis, [(i, i ^ bit) for i in range(n)])  24.6 us
    unnamed x59, local copies, waits for them, and re-layouts  22.4 us
  transfers between devices with their start and end apart: 40, of which 13 were waited for; matrix products, arithmetic and copies ran while one was open for 20% of the time, Pallas kernels for 8%

profile of v5, /device:TPU:29, one launch (start us, length us, event | category | flops | bytes accessed | tf_op | source)
XLA Modules:
  0.0 518.6 jit_solution(8335089558266556968)
XLA Ops:
  0.6 2.4 slice_bitcast_fusion
  4.3 5.0 collective-permute-start.2
  23.6 5.6 %collective-permute-done.1 = f32[512,512]{1,0:T(8,128)} collective-permute-done((f32[512,512]{1,0:T(8,128)}, f32[512,512]{1,0:T(8,128)}, u32[]{:S(2)}, u32[]{:S(2)}) %collective-permute-start.1) | collective-permute-done | bytes 1048608 | tf_op jit(solution)/shard_map/ppermute | solution.py:185
  43.9 4.6 collective-permute-start.18
  48.4 6.4 %dynamic-slice_bitcast_fusion.2 = (f32[256,512]{1,0:T(8,128)}, f32[256,512]{1,0:T(8,128)}, f32[1,256,512]{2,1,0:T(8,128)S(1)}, f32[1,256,512]{2,1,0:T(8,128)S(1)...) fusion(f32[1,4096,512]{2,1,0:T(8,128)} %param.3, ...), kind=kLoop, calls=%fused_computation.67 | loop fusion | bytes 16777280 | tf_op jit(solution)/shard_map/dynamic_slice | solution.py:252
  54.8 5.2 %collective-permute-done.18 = f32[128,512]{0,1:T(8,128)S(1)} collective-permute-done((f32[128,512]{0,1:T(8,128)S(1)}, f32[128,512]{0,1:T(8,128)S(1)}, u32[]{:S(2)}, u32[]{:S(2)}) %collective-permute-start.18) | collective-permute-done | bytes 262176 | tf_op jit(solution)/shard_map/ppermute | solution.py:143
  60.2 2.1 collective-permute-start.19
  65.3 8.2 %collective-permute-done.19 = f32[64,512]{0,1:T(8,128)S(1)} collective-permute-done((f32[64,512]{0,1:T(8,128)S(1)}, f32[64,512]{0,1:T(8,128)S(1)}, u32[]{:S(2)}, u32[]{:S(2)}) %collective-permute-start.19) | collective-permute-done | bytes 131104 | tf_op jit(solution)/shard_map/ppermute | solution.py:143
  82.4 2.1 collective-permute-start.5
  84.6 1.9 collective-permute-done.20
  90.6 2.8 collective-permute-start.21
  97.4 3.2 pad_maximum_fusion.8
  100.6 3.1 collective-permute-start.8
  105.9 4.2 collective-permute-start.11
  110.1 2.9 pad_maximum_fusion.4
  118.7 10.8 %collective-permute-done.8 = f32[512,512]{1,0:T(8,128)S(1)} collective-permute-done((f32[512,512]{1,0:T(8,128)}, f32[512,512]{1,0:T(8,128)S(1)}, u32[]{:S(2)}, u32[]{:S(2)}) %collective-permute-start.8) | collective-permute-done | bytes 1048608 | tf_op jit(solution)/shard_map/ppermute | solution.py:190
  129.5 7.5 %collective-permute-start.16 = (f32[512,512]{1,0:T(8,128)}, f32[512,512]{1,0:T(8,128)}, u32[]{:S(2)}, u32[]{:S(2)}) collective-permute-start(f32[512,512]{1,0:T(8,128)} %get-tuple-element.23), channel_id=1, source_target_pairs={{1,3},{2,4},{3,5},{4,6},{5,7},{6,0},{7,1},{9,11},{10,12},{11,13},{... | collective-permute-start | bytes 3145736 | tf_op jit(solution)/shard_map/ppermute | solution.py:297
  137.1 2.1 collective-permute-start.15
  139.2 44.5 %collective-permute-done.22 = f32[256,512]{0,1:T(8,128)S(1)} collective-permute-done((f32[256,512]{0,1:T(8,128)S(1)}, f32[256,512]{0,1:T(8,128)S(1)}, u32[]{:S(2)}, u32[]{:S(2)}) %collective-permute-start.22) | collective-permute-done | bytes 524320 | tf_op jit(solution)/shard_map/ppermute | solution.py:143
  183.7 1.9 collective-permute-start.14
  185.6 7.3 %collective-permute-start.13 = (f32[512,512]{1,0:T(8,128)}, f32[512,512]{1,0:T(8,128)}, u32[]{:S(2)}, u32[]{:S(2)}) collective-permute-start(f32[512,512]{1,0:T(8,128)} %get-tuple-element.20), channel_id=1, source_target_pairs={{1,5},{2,6},{3,7},{4,0},{5,1},{6,2},{7,3},{9,13},{10,14},{11,15},{... | collective-permute-start | bytes 3145736 | tf_op jit(solution)/shard_map/ppermute | solution.py:297
  194.2 6.5 %select_add_fusion = (f32[512,512]{1,0:T(8,128)S(1)}, f32[512,512]{1,0:T(8,128)S(1)}, f32[512,512]{1,0:T(8,128)S(1)}, f32[512,512]{1,0:T(8,128)S(1)}, f32[512,51...) fusion(f32[512,512]{1,0:T(8,128)S(1)} %collective-permute-done, pred[]{:T(512)S(6)} %and.220, ...), kind=kLoop, calls=%fused_computation.58 | loop fusion | flops 5505024 | bytes 22020104 | tf_op jit(solution)/shard_map/add | solution.py:269
  200.7 21.7 %shard_map.58 = f32[512,512]{1,0:T(8,128)S(1)} custom-call(f32[512,512]{1,0:T(8,128)S(1)} %get-tuple-element.40.a_ref), custom_call_target="tpu_custom_call" | custom-call | flops 134217728 | bytes 2097152 | tf_op jit(solution)/shard_map/pallas_call | solution.py:86
  222.4 15.3 %collective-permute-start.27 = (f32[512,512]{1,0:T(8,128)}, f32[512,512]{1,0:T(8,128)}, u32[]{:S(2)}, u32[]{:S(2)}) collective-permute-start(f32[512,512]{1,0:T(8,128)} %get-tuple-element.28), channel_id=1, source_target_pairs={{1,2},{2,3},{3,4},{4,5},{5,6},{6,7},{7,0},{9,10},{10,11},{11,12},{... | collective-permute-start | bytes 3145736 | tf_op jit(solution)/shard_map/ppermute | solution.py:297
  237.7 40.1 %collective-permute-done.13 = f32[512,512]{1,0:T(8,128)} collective-permute-done((f32[512,512]{1,0:T(8,128)}, f32[512,512]{1,0:T(8,128)}, u32[]{:S(2)}, u32[]{:S(2)}) %collective-permute-start.13) | collective-permute-done | bytes 1048608 | tf_op jit(solution)/shard_map/ppermute | solution.py:297
  277.7 24.0 %collective-permute-start.28 = (f32[512,512]{1,0:T(8,128)}, f32[512,512]{1,0:T(8,128)}, u32[]{:S(2)}, u32[]{:S(2)}) collective-permute-start(f32[512,512]{1,0:T(8,128)} %get-tuple-element.33), channel_id=1, source_target_pairs={{1,7},{2,0},{3,1},{4,2},{5,3},{6,4},{7,5},{9,15},{10,8},{11,9},{12... | collective-permute-start | bytes 3145736 | tf_op jit(solution)/shard_map/ppermute | solution.py:297
  301.8 2.4 collective-permute-start.29
  304.1 2.2 fusion.8
  314.9 3.3 copy-done
  321.4 2.4 bitcast_dynamic-update-slice_fusion.6
  323.9 2.3 bitcast_dynamic-update-slice_fusion.5
  326.2 2.4 bitcast_dynamic-update-slice_fusion.4
  328.6 2.4 bitcast_dynamic-update-slice_fusion.3
  332.0 2.4 bitcast_dynamic-update-slice_fusion.1
  334.5 2.4 bitcast_dynamic-update-slice_fusion.piece_ref
  336.9 3.4 copy-done.1
  340.3 3.4 copy-done.3
  343.7 2.0 shard_map.60
  348.4 3.4 copy-done.2
  351.8 14.9 %shard_map.61 = f32[16,512,256]{2,1,0:T(8,128)S(1)} custom-call(s32[16]{0:T(128)S(1)} %get-tuple-element.125.slot_ref, s32[16]{0:T(128)S(1)} %get-tuple-element.37.place_ref, s32[16]{0:T(128)S(1)} %get-tuple-element.124.part_ref, s32[16]{0:T(128)S(1)} %gather_fusion.1, bf16[512,1536]{1,0:T(8,128)(2,1)S(1)} %copy.71.left_ref, f32[8,512,512]{2,1,0:T(8,128)S(1)} %copy-done.2, ...), custom_call_target="tpu_custom_call" | custom-call | flops 6442450944 | bytes 25165824 | tf_op jit(solution)/shard_map/pallas_call | solution.py:117
  366.7 3.5 copy-done.4
  370.3 2.2 dynamic-slice_bitcast_fusion
  374.5 6.8 %collective-permute-done.30 = f32[256,512]{1,0:T(8,128)} collective-permute-done((f32[256,512]{1,0:T(8,128)}, f32[256,512]{1,0:T(8,128)}, u32[]{:S(2)}, u32[]{:S(2)}) %collective-permute-start.30) | collective-permute-done | bytes 524320 | tf_op jit(solution)/shard_map/ppermute | solution.py:143
  384.4 2.6 fusion.10
  387.2 3.6 collective-permute-done.31
  394.8 3.9 collective-permute-done.32
  400.6 2.1 collective-permute-start.33
  405.3 6.6 %collective-permute-done.24 = f32[128,512]{0,1:T(8,128)S(1)} collective-permute-done((f32[128,512]{0,1:T(8,128)S(1)}, f32[128,512]{0,1:T(8,128)S(1)}, u32[]{:S(2)}, u32[]{:S(2)}) %collective-permute-start.24) | collective-permute-done | bytes 262176 | tf_op jit(solution)/shard_map/ppermute | solution.py:143
  418.6 1.8 collective-permute-start.38
  422.4 4.2 bitcast_add_fusion
  426.6 2.0 copy-done.7
  430.1 4.2 collective-permute-start.35
  434.3 31.5 %collective-permute-done.37 = f32[512,512]{1,0:T(8,128)} collective-permute-done((f32[512,512]{1,0:T(8,128)}, f32[512,512]{1,0:T(8,128)}, u32[]{:S(2)}, u32[]{:S(2)}) %collective-permute-start.37) | collective-permute-done | bytes 1048608 | tf_op jit(solution)/shard_map/ppermute | solution.py:212
  465.8 2.2 add_add_fusion
  468.0 3.6 collective-permute-start.39
  471.7 3.2 convolution_bitcast_fusion.8
  476.2 21.5 %shard_map.59 = f32[512,512]{1,0:T(8,128)S(1)} custom-call(f32[512,512]{1,0:T(8,128)S(1)} %pad_maximum_fusion.7.a_ref), custom_call_target="tpu_custom_call" | custom-call | flops 134217728 | bytes 2097152 | tf_op jit(solution)/shard_map/pallas_call | solution.py:86
  497.7 2.0 fusion.26
  499.8 3.0 pad_maximum_fusion
  502.8 2.3 gather_fusion.2
  505.3 3.3 fusion.31
  508.6 1.9 add_bitcast_fusion
  510.5 1.8 copy.74
  512.3 6.1 %fusion = f32[1024,512]{1,0:T(8,128)} fusion(f32[1024,512]{1,0:T(8,128)} %param.5, f32[4,256,512]{2,1,0:T(8,128)} %copy.74, f32[1024,512]{1,0:T(8,128)} %fusion.31, f32[512,512]{1,0:T(8,128)S(1)} %copy-done.11), kind=kOutput, calls=%fused_computation.8 | convolution fusion | flops 1611661312 | bytes 9437184 | tf_op jit(solution)/shard_map/dot_general | solution.py:138
  (180 shorter events, 74.6 us)
Async XLA Ops:
  0.6 20.2 %slice-start = ((f32[1024,512]{1,0:T(8,128)}), f32[512,512]{1,0:T(8,128)S(1)}, s32[]{:S(2)}) async-start(f32[1024,512]{1,0:T(8,128)} %param.5), calls=%async_computation | async-start | bytes 2097152 | tf_op jit(solution)/shard_map/slice | solution.py:289
  3.0 26.2 %collective-permute-start.1 = (f32[512,512]{1,0:T(8,128)}, f32[512,512]{1,0:T(8,128)}, u32[]{:S(2)}, u32[]{:S(2)}) collective-permute-start(f32[512,512]{1,0:T(8,128)} %slice_bitcast_fusion), channel_id=1, source_target_pairs={{0,2},{1,3},{2,4},{3,5},{4,6},{5,7},{8,10},{9,11},{10,12},{11,13},... | collective-permute-start | bytes 3145736 | tf_op jit(solution)/shard_map/ppermute | solution.py:185
  4.3 26.2 %collective-permute-start.2 = (f32[512,512]{1,0:T(8,128)}, f32[512,512]{1,0:T(8,128)}, u32[]{:S(2)}, u32[]{:S(2)}) collective-permute-start(f32[512,512]{1,0:T(8,128)} %slice_bitcast_fusion), channel_id=1, source_target_pairs={{2,0},{3,1},{4,2},{5,3},{6,4},{7,5},{10,8},{11,9},{12,10},{13,11},... | collective-permute-start | bytes 3145736 | tf_op jit(solution)/shard_map/ppermute | solution.py:186
  21.2 33.6 %copy-start.9 = (f32[512,512]{0,1:T(8,128)}, f32[512,512]{0,1:T(8,128)S(1)}, u32[]{:S(2)}) copy-start(f32[512,512]{0,1:T(8,128)S(1)} %copy.88) | copy-start | bytes 3145732
  23.4 19.2 %collective-permute-start.17 = (f32[256,512]{0,1:T(8,128)}, f32[256,512]{0,1:T(8,128)}, u32[]{:S(2)}, u32[]{:S(2)}) collective-permute-start(f32[256,512]{0,1:T(8,128)} %constant_dynamic-slice_fusion.10), channel_id=1, source_target_pairs={{0,1},{1,0},{2,3},{3,2},{4,5},{5,4},{6,7},{7,6},{8,9},{9,8},{10,11... | collective-permute-start | bytes 1572872 | tf_op jit(solution)/shard_map/ppermute | solution.py:143
  29.2 30.9 %collective-permute-start.7 = (f32[512,512]{1,0:T(8,128)}, f32[512,512]{1,0:T(8,128)}, u32[]{:S(2)}, u32[]{:S(2)}) collective-permute-start(f32[512,512]{1,0:T(8,128)} %collective-permute-done.1), channel_id=1, source_target_pairs={{2,4},{3,5},{4,6},{5,7},{10,12},{11,13},{12,14},{13,15},{18,20},{1... | collective-permute-start | bytes 3145736 | tf_op jit(solution)/shard_map/ppermute | solution.py:185
  30.5 29.6 %collective-permute-start.3 = (f32[512,512]{1,0:T(8,128)}, f32[512,512]{1,0:T(8,128)}, u32[]{:S(2)}, u32[]{:S(2)}) collective-permute-start(f32[512,512]{1,0:T(8,128)} %collective-permute-done.2), channel_id=1, source_target_pairs={{2,0},{3,1},{4,2},{5,3},{10,8},{11,9},{12,10},{13,11},{18,16},{19,... | collective-permute-start | bytes 3145736 | tf_op jit(solution)/shard_map/ppermute | solution.py:186
  32.2 58.5 %collective-permute-start = (f32[512,512]{1,0:T(8,128)}, f32[512,512]{1,0:T(8,128)S(1)}, u32[]{:S(2)}, u32[]{:S(2)}) collective-permute-start(f32[512,512]{1,0:T(8,128)} %slice_bitcast_fusion), channel_id=1, source_target_pairs={{0,1},{1,0},{2,3},{3,2},{4,5},{5,4},{6,7},{7,6},{8,9},{9,8},{10,11... | collective-permute-start | bytes 3145736 | tf_op jit(solution)/shard_map/ppermute | solution.py:190
  43.9 16.2 %collective-permute-start.18 = (f32[128,512]{0,1:T(8,128)S(1)}, f32[128,512]{0,1:T(8,128)S(1)}, u32[]{:S(2)}, u32[]{:S(2)}) collective-permute-start(f32[128,512]{0,1:T(8,128)S(1)} %constant_dynamic-slice_fusion.9), channel_id=1, source_target_pairs={{0,2},{1,3},{2,0},{3,1},{4,6},{5,7},{6,4},{7,5},{8,10},{9,11},{10,... | collective-permute-start | bytes 786440 | tf_op jit(solution)/shard_map/ppermute | solution.py:143
  60.0 50.1 %copy-start.22 = (f32[256,512]{1,0:T(8,128)S(1)}, f32[256,512]{1,0:T(8,128)}, u32[]{:S(2)}) copy-start(f32[256,512]{1,0:T(8,128)} %get-tuple-element.54) | copy-start | bytes 1572868
  60.2 13.2 %collective-permute-start.19 = (f32[64,512]{0,1:T(8,128)S(1)}, f32[64,512]{0,1:T(8,128)S(1)}, u32[]{:S(2)}, u32[]{:S(2)}) collective-permute-start(f32[64,512]{0,1:T(8,128)S(1)} %constant_dynamic-slice_fusion.8), channel_id=1, source_target_pairs={{0,4},{1,5},{2,6},{3,7},{4,0},{5,1},{6,2},{7,3},{8,12},{9,13},{10,... | collective-permute-start | bytes 393224 | tf_op jit(solution)/shard_map/ppermute | solution.py:143
  62.3 38.3 %collective-permute-start.12 = (f32[512,512]{1,0:T(8,128)}, f32[512,512]{1,0:T(8,128)}, u32[]{:S(2)}, u32[]{:S(2)}) collective-permute-start(f32[512,512]{1,0:T(8,128)} %collective-permute-done.2), channel_id=1, source_target_pairs={{0,1},{1,0},{2,3},{3,2},{4,5},{5,4},{8,9},{9,8},{10,11},{11,10},{1... | collective-permute-start | bytes 3145736 | tf_op jit(solution)/shard_map/ppermute | solution.py:190
  64.0 41.9 %collective-permute-start.10 = (f32[512,512]{1,0:T(8,128)}, f32[512,512]{1,0:T(8,128)}, u32[]{:S(2)}, u32[]{:S(2)}) collective-permute-start(f32[512,512]{1,0:T(8,128)} %collective-permute-done.7), channel_id=1, source_target_pairs={{4,6},{5,7},{12,14},{13,15},{20,22},{21,23},{28,30},{29,31}} | collective-permute-start | bytes 3145736 | tf_op jit(solution)/shard_map/ppermute | solution.py:185
  73.6 12.9 %collective-permute-start.20 = (f32[64,512]{0,1:T(8,128)S(1)}, f32[64,512]{0,1:T(8,128)S(1)}, u32[]{:S(2)}, u32[]{:S(2)}) collective-permute-start(f32[64,512]{0,1:T(8,128)S(1)} %dynamic-slice_add_fusion.4), channel_id=1, source_target_pairs={{0,4},{1,5},{2,6},{3,7},{4,0},{5,1},{6,2},{7,3},{8,12},{9,13},{10,... | collective-permute-start | bytes 393224 | tf_op jit(solution)/shard_map/ppermute | solution.py:143
  82.4 32.5 %collective-permute-start.5 = (f32[512,512]{1,0:T(8,128)}, f32[512,512]{1,0:T(8,128)}, u32[]{:S(2)}, u32[]{:S(2)}) collective-permute-start(f32[512,512]{1,0:T(8,128)} %collective-permute-done.1), channel_id=1, source_target_pairs={{2,3},{3,2},{4,5},{5,4},{6,7},{7,6},{10,11},{11,10},{12,13},{13,12... | collective-permute-start | bytes 3145736 | tf_op jit(solution)/shard_map/ppermute | solution.py:190
  87.2 26.0 %collective-permute-start.4 = (f32[512,512]{1,0:T(8,128)}, f32[512,512]{1,0:T(8,128)}, u32[]{:S(2)}, u32[]{:S(2)}) collective-permute-start(f32[512,512]{1,0:T(8,128)} %collective-permute-done.3), channel_id=1, source_target_pairs={{2,0},{3,1},{10,8},{11,9},{18,16},{19,17},{26,24},{27,25}} | collective-permute-start | bytes 3145736 | tf_op jit(solution)/shard_map/ppermute | solution.py:186
  90.6 14.6 %collective-permute-start.21 = (f32[128,512]{0,1:T(8,128)}, f32[128,512]{0,1:T(8,128)S(1)}, u32[]{:S(2)}, u32[]{:S(2)}) collective-permute-start(f32[128,512]{0,1:T(8,128)} %pad_maximum_fusion.15), channel_id=1, source_target_pairs={{0,2},{1,3},{2,0},{3,1},{4,6},{5,7},{6,4},{7,5},{8,10},{9,11},{10,... | collective-permute-start | bytes 786440 | tf_op jit(solution)/shard_map/ppermute | solution.py:143
  97.4 17.6 %copy-start.16 = (f32[256,512]{1,0:T(8,128)S(1)}, f32[256,512]{1,0:T(8,128)}, u32[]{:S(2)}) copy-start(f32[256,512]{1,0:T(8,128)} %get-tuple-element.47) | copy-start | bytes 1572868
  97.4 17.6 %copy-start.17 = (f32[256,512]{1,0:T(8,128)S(1)}, f32[256,512]{1,0:T(8,128)}, u32[]{:S(2)}) copy-start(f32[256,512]{1,0:T(8,128)} %get-tuple-element.62) | copy-start | bytes 1572868
  97.4 18.7 %copy-start.18 = (f32[256,512]{1,0:T(8,128)S(1)}, f32[256,512]{1,0:T(8,128)}, u32[]{:S(2)}) copy-start(f32[256,512]{1,0:T(8,128)} %get-tuple-element.58) | copy-start | bytes 1572868
  97.4 18.7 %copy-start.19 = (f32[256,512]{1,0:T(8,128)S(1)}, f32[256,512]{1,0:T(8,128)}, u32[]{:S(2)}) copy-start(f32[256,512]{1,0:T(8,128)} %get-tuple-element.59) | copy-start | bytes 1572868
  97.4 18.7 %copy-start.20 = (f32[256,512]{1,0:T(8,128)S(1)}, f32[256,512]{1,0:T(8,128)}, u32[]{:S(2)}) copy-start(f32[256,512]{1,0:T(8,128)} %get-tuple-element.60) | copy-start | bytes 1572868
  97.4 18.7 %copy-start.21 = (f32[256,512]{1,0:T(8,128)S(1)}, f32[256,512]{1,0:T(8,128)}, u32[]{:S(2)}) copy-start(f32[256,512]{1,0:T(8,128)} %get-tuple-element.61) | copy-start | bytes 1572868
  100.6 28.9 %collective-permute-start.8 = (f32[512,512]{1,0:T(8,128)}, f32[512,512]{1,0:T(8,128)S(1)}, u32[]{:S(2)}, u32[]{:S(2)}) collective-permute-start(f32[512,512]{1,0:T(8,128)} %collective-permute-done.7), channel_id=1, source_target_pairs={{4,5},{5,4},{6,7},{7,6},{12,13},{13,12},{14,15},{15,14},{20,21},{2... | collective-permute-start | bytes 3145736 | tf_op jit(solution)/shard_map/ppermute | solution.py:190
  105.2 31.8 %collective-permute-start.9 = (f32[512,512]{1,0:T(8,128)}, f32[512,512]{1,0:T(8,128)S(1)}, u32[]{:S(2)}, u32[]{:S(2)}) collective-permute-start(f32[512,512]{1,0:T(8,128)} %collective-permute-done.3), channel_id=1, source_target_pairs={{0,1},{1,0},{2,3},{3,2},{8,9},{9,8},{10,11},{11,10},{16,17},{17,16... | collective-permute-start | bytes 3145736 | tf_op jit(solution)/shard_map/ppermute | solution.py:190
  105.9 79.7 %collective-permute-start.11 = (f32[512,512]{1,0:T(8,128)}, f32[512,512]{1,0:T(8,128)S(1)}, u32[]{:S(2)}, u32[]{:S(2)}) collective-permute-start(f32[512,512]{1,0:T(8,128)} %collective-permute-done.10), channel_id=1, source_target_pairs={{6,7},{7,6},{14,15},{15,14},{22,23},{23,22},{30,31},{31,30}} | collective-permute-start | bytes 3145736 | tf_op jit(solution)/shard_map/ppermute | solution.py:190
  113.2 80.9 %collective-permute-start.6 = (f32[512,512]{1,0:T(8,128)}, f32[512,512]{1,0:T(8,128)}, u32[]{:S(2)}, u32[]{:S(2)}) collective-permute-start(f32[512,512]{1,0:T(8,128)} %collective-permute-done.4), channel_id=1, source_target_pairs={{0,1},{1,0},{8,9},{9,8},{16,17},{17,16},{24,25},{25,24}} | collective-permute-start | bytes 3145736 | tf_op jit(solution)/shard_map/ppermute | solution.py:190
  114.9 68.8 %collective-permute-start.22 = (f32[256,512]{0,1:T(8,128)S(1)}, f32[256,512]{0,1:T(8,128)S(1)}, u32[]{:S(2)}, u32[]{:S(2)}) collective-permute-start(f32[256,512]{0,1:T(8,128)S(1)} %pad_maximum_fusion.12), channel_id=1, source_target_pairs={{0,1},{1,0},{2,3},{3,2},{4,5},{5,4},{6,7},{7,6},{8,9},{9,8},{10,11... | collective-permute-start | bytes 1572872 | tf_op jit(solution)/shard_map/ppermute | solution.py:143
  129.5 108.1 %collective-permute-start.16 = (f32[512,512]{1,0:T(8,128)}, f32[512,512]{1,0:T(8,128)}, u32[]{:S(2)}, u32[]{:S(2)}) collective-permute-start(f32[512,512]{1,0:T(8,128)} %get-tuple-element.23), channel_id=1, source_target_pairs={{1,3},{2,4},{3,5},{4,6},{5,7},{6,0},{7,1},{9,11},{10,12},{11,13},{... | collective-permute-start | bytes 3145736 | tf_op jit(solution)/shard_map/ppermute | solution.py:297
  137.1 100.6 %collective-permute-start.15 = (f32[512,512]{1,0:T(8,128)}, f32[512,512]{1,0:T(8,128)S(1)}, u32[]{:S(2)}, u32[]{:S(2)}) collective-permute-start(f32[512,512]{1,0:T(8,128)} %get-tuple-element.22), channel_id=1, source_target_pairs={{1,6},{2,7},{3,0},{4,1},{5,2},{6,3},{7,4},{9,14},{10,15},{11,8},{1... | collective-permute-start | bytes 3145736 | tf_op jit(solution)/shard_map/ppermute | solution.py:297
  183.7 54.0 %collective-permute-start.14 = (f32[512,512]{1,0:T(8,128)}, f32[512,512]{1,0:T(8,128)}, u32[]{:S(2)}, u32[]{:S(2)}) collective-permute-start(f32[512,512]{1,0:T(8,128)} %get-tuple-element.21), channel_id=1, source_target_pairs={{1,4},{2,5},{3,6},{4,7},{5,0},{6,1},{7,2},{9,12},{10,13},{11,14},{... | collective-permute-start | bytes 3145736 | tf_op jit(solution)/shard_map/ppermute | solution.py:297
  185.6 8.5 %copy-start.23 = (f32[512,512]{1,0:T(8,128)}, f32[512,512]{1,0:T(8,128)S(1)}, u32[]{:S(2)}) copy-start(f32[512,512]{1,0:T(8,128)S(1)} %collective-permute-done.11) | copy-start | bytes 3145732
  185.6 92.1 %collective-permute-start.13 = (f32[512,512]{1,0:T(8,128)}, f32[512,512]{1,0:T(8,128)}, u32[]{:S(2)}, u32[]{:S(2)}) collective-permute-start(f32[512,512]{1,0:T(8,128)} %get-tuple-element.20), channel_id=1, source_target_pairs={{1,5},{2,6},{3,7},{4,0},{5,1},{6,2},{7,3},{9,13},{10,14},{11,15},{... | collective-permute-start | bytes 3145736 | tf_op jit(solution)/shard_map/ppermute | solution.py:297
  222.4 99.1 %collective-permute-start.27 = (f32[512,512]{1,0:T(8,128)}, f32[512,512]{1,0:T(8,128)}, u32[]{:S(2)}, u32[]{:S(2)}) collective-permute-start(f32[512,512]{1,0:T(8,128)} %get-tuple-element.28), channel_id=1, source_target_pairs={{1,2},{2,3},{3,4},{4,5},{5,6},{6,7},{7,0},{9,10},{10,11},{11,12},{... | collective-permute-start | bytes 3145736 | tf_op jit(solution)/shard_map/ppermute | solution.py:297
  237.6 73.9 %copy-start.24 = (f32[512,512]{1,0:T(8,128)}, f32[512,512]{1,0:T(8,128)S(1)}, u32[]{:S(2)}) copy-start(f32[512,512]{1,0:T(8,128)S(1)} %collective-permute-done.15) | copy-start | bytes 3145732
  277.7 54.3 %collective-permute-start.28 = (f32[512,512]{1,0:T(8,128)}, f32[512,512]{1,0:T(8,128)}, u32[]{:S(2)}, u32[]{:S(2)}) collective-permute-start(f32[512,512]{1,0:T(8,128)} %get-tuple-element.33), channel_id=1, source_target_pairs={{1,7},{2,0},{3,1},{4,2},{5,3},{6,4},{7,5},{9,15},{10,8},{11,9},{12... | collective-permute-start | bytes 3145736 | tf_op jit(solution)/shard_map/ppermute | solution.py:297
  301.8 32.7 %collective-permute-start.29 = (f32[512,512]{1,0:T(8,128)}, f32[512,512]{1,0:T(8,128)}, u32[]{:S(2)}, u32[]{:S(2)}) collective-permute-start(f32[512,512]{1,0:T(8,128)} %pad_maximum_fusion.10), channel_id=1, source_target_pairs={{1,0},{2,1},{3,2},{4,3},{5,4},{6,5},{7,6},{9,8},{10,9},{11,10},{12... | collective-permute-start | bytes 3145736 | tf_op jit(solution)/shard_map/ppermute | solution.py:297
  314.9 3.3 copy-start
  321.4 9.5 %copy-start.25 = (f32[512,512]{1,0:T(8,128)S(1)}, f32[512,512]{1,0:T(8,128)}, u32[]{:S(2)}) copy-start(f32[512,512]{1,0:T(8,128)} %copy-done.24) | copy-start | bytes 3145732
  336.9 3.4 copy-start.1
  340.3 3.4 copy-start.3
  348.4 3.4 copy-start.2
  366.7 3.5 copy-start.4
  366.7 6.6 %copy-start.6 = (f32[2,512,256]{2,1,0:T(8,128)S(1)}, f32[2,512,256]{2,1,0:T(8,128)}, u32[]{:S(2)}) copy-start(f32[2,512,256]{2,1,0:T(8,128)} %copy-done.5) | copy-start | bytes 3145732
  366.7 6.7 %copy-start.10 = (f32[512,512]{0,1:T(8,128)S(1)}, f32[512,512]{0,1:T(8,128)}, u32[]{:S(2)}) copy-start(f32[512,512]{0,1:T(8,128)} %copy-done.9) | copy-start | bytes 3145732
  370.3 16.7 %copy-start.12 = (f32[512,512]{0,1:T(8,128)S(1)}, f32[512,512]{0,1:T(8,128)}, u32[]{:S(2)}) copy-start(f32[512,512]{0,1:T(8,128)} %pad_maximum_fusion.6) | copy-start | bytes 3145732
  372.5 49.9 %collective-permute-start.34 = (f32[2,4,512,256]{3,2,1,0:T(8,128)}, f32[2,4,512,256]{3,2,1,0:T(8,128)}, u32[]{:S(2)}, u32[]{:S(2)}) collective-permute-start(f32[2,4,512,256]{3,2,1,0:T(8,128)} %dynamic-slice_bitcast_fusion), channel_id=1, source_target_pairs={{0,8},{8,0},{16,24},{24,16},{1,9},{9,1},{17,25},{25,17},{2,10},{10... | collective-permute-start | bytes 12582920 | tf_op jit(solution)/shard_map/ppermute | solution.py:143
  374.5 6.8 %collective-permute-start.30 = (f32[256,512]{1,0:T(8,128)}, f32[256,512]{1,0:T(8,128)}, u32[]{:S(2)}, u32[]{:S(2)}) collective-permute-start(f32[256,512]{1,0:T(8,128)} %constant_dynamic-slice_fusion.2), channel_id=1, source_target_pairs={{0,8},{8,0},{16,24},{24,16},{1,9},{9,1},{17,25},{25,17},{2,10},{10... | collective-permute-start | bytes 1572872 | tf_op jit(solution)/shard_map/ppermute | solution.py:143
  383.2 7.7 %collective-permute-start.31 = (f32[128,512]{1,0:T(8,128)S(1)}, f32[128,512]{1,0:T(8,128)}, u32[]{:S(2)}, u32[]{:S(2)}) collective-permute-start(f32[128,512]{1,0:T(8,128)S(1)} %constant_dynamic-slice_fusion.1), channel_id=1, source_target_pairs={{0,16},{8,24},{16,0},{24,8},{1,17},{9,25},{17,1},{25,9},{2,18},{10... | collective-permute-start | bytes 786440 | tf_op jit(solution)/shard_map/ppermute | solution.py:143
  391.9 6.8 %collective-permute-start.32 = (f32[128,512]{1,0:T(8,128)S(1)}, f32[128,512]{1,0:T(8,128)}, u32[]{:S(2)}, u32[]{:S(2)}) collective-permute-start(f32[128,512]{1,0:T(8,128)S(1)} %dynamic-slice_add_fusion.3), channel_id=1, source_target_pairs={{0,16},{8,24},{16,0},{24,8},{1,17},{9,25},{17,1},{25,9},{2,18},{10... | collective-permute-start | bytes 786440 | tf_op jit(solution)/shard_map/ppermute | solution.py:143
  393.2 9.5 %collective-permute-start.23 = (f32[256,512]{0,1:T(8,128)S(1)}, f32[256,512]{0,1:T(8,128)}, u32[]{:S(2)}, u32[]{:S(2)}) collective-permute-start(f32[256,512]{0,1:T(8,128)S(1)} %constant_dynamic-slice_fusion.7), channel_id=1, source_target_pairs={{0,8},{8,0},{16,24},{24,16},{1,9},{9,1},{17,25},{25,17},{2,10},{10... | collective-permute-start | bytes 1572872 | tf_op jit(solution)/shard_map/ppermute | solution.py:143
  399.7 13.7 %copy-start.14 = (f32[128,512]{1,0:T(8,128)}, f32[128,512]{1,0:T(8,128)S(1)}, u32[]{:S(2)}) copy-start(f32[128,512]{1,0:T(8,128)S(1)} %get-tuple-element.82) | copy-start | bytes 786436
  400.6 12.8 %collective-permute-start.33 = (f32[256,512]{1,0:T(8,128)}, f32[256,512]{1,0:T(8,128)}, u32[]{:S(2)}, u32[]{:S(2)}) collective-permute-start(f32[256,512]{1,0:T(8,128)} %pad_maximum_fusion.14), channel_id=1, source_target_pairs={{0,8},{8,0},{16,24},{24,16},{1,9},{9,1},{17,25},{25,17},{2,10},{10... | collective-permute-start | bytes 1572872 | tf_op jit(solution)/shard_map/ppermute | solution.py:143
  403.9 8.0 %collective-permute-start.24 = (f32[128,512]{0,1:T(8,128)S(1)}, f32[128,512]{0,1:T(8,128)S(1)}, u32[]{:S(2)}, u32[]{:S(2)}) collective-permute-start(f32[128,512]{0,1:T(8,128)S(1)} %get-tuple-element.85), channel_id=1, source_target_pairs={{0,16},{8,24},{16,0},{24,8},{1,17},{9,25},{17,1},{25,9},{2,18},{10... | collective-permute-start | bytes 786440 | tf_op jit(solution)/shard_map/ppermute | solution.py:143
  412.1 8.3 %collective-permute-start.25 = (f32[128,512]{1,0:T(8,128)S(1)}, f32[128,512]{1,0:T(8,128)S(1)}, u32[]{:S(2)}, u32[]{:S(2)}) collective-permute-start(f32[128,512]{1,0:T(8,128)S(1)} %add.549), channel_id=1, source_target_pairs={{0,16},{8,24},{16,0},{24,8},{1,17},{9,25},{17,1},{25,9},{2,18},{10... | collective-permute-start | bytes 786440 | tf_op jit(solution)/shard_map/ppermute | solution.py:143
  415.7 18.6 %collective-permute-start.36 = (f32[512,512]{1,0:T(8,128)}, f32[512,512]{1,0:T(8,128)}, u32[]{:S(2)}, u32[]{:S(2)}) collective-permute-start(f32[512,512]{1,0:T(8,128)} %pad_maximum_fusion.11), channel_id=1, source_target_pairs={{0,2},{1,3},{10,12},{11,13},{20,22},{21,23},{30,24},{31,25}} | collective-permute-start | bytes 3145736 | tf_op jit(solution)/shard_map/ppermute | solution.py:212
  417.3 48.5 %collective-permute-start.37 = (f32[512,512]{1,0:T(8,128)}, f32[512,512]{1,0:T(8,128)}, u32[]{:S(2)}, u32[]{:S(2)}) collective-permute-start(f32[512,512]{1,0:T(8,128)} %pad_maximum_fusion.11), channel_id=1, source_target_pairs={{0,4},{1,5},{10,14},{11,15},{20,16},{21,17},{30,26},{31,27}} | collective-permute-start | bytes 3145736 | tf_op jit(solution)/shard_map/ppermute | solution.py:212
  418.6 47.2 %collective-permute-start.38 = (f32[512,512]{1,0:T(8,128)}, f32[512,512]{1,0:T(8,128)}, u32[]{:S(2)}, u32[]{:S(2)}) collective-permute-start(f32[512,512]{1,0:T(8,128)} %pad_maximum_fusion.11), channel_id=1, source_target_pairs={{0,6},{1,7},{10,8},{11,9},{20,18},{21,19},{30,28},{31,29}} | collective-permute-start | bytes 3145736 | tf_op jit(solution)/shard_map/ppermute | solution.py:212
  420.5 9.6 %copy-start.13 = (f32[128,512]{1,0:T(8,128)}, f32[128,512]{1,0:T(8,128)S(1)}, u32[]{:S(2)}) copy-start(f32[128,512]{1,0:T(8,128)S(1)} %get-tuple-element.84) | copy-start | bytes 786436
  421.4 53.6 %collective-permute-start.26 = (f32[256,512]{1,0:T(8,128)}, f32[256,512]{1,0:T(8,128)}, u32[]{:S(2)}, u32[]{:S(2)}) collective-permute-start(f32[256,512]{1,0:T(8,128)} %pad_maximum_fusion.13), channel_id=1, source_target_pairs={{0,8},{8,0},{16,24},{24,16},{1,9},{9,1},{17,25},{25,17},{2,10},{10... | collective-permute-start | bytes 1572872 | tf_op jit(solution)/shard_map/ppermute | solution.py:143
  430.1 78.5 %collective-permute-start.35 = (f32[1,4,512,256]{3,2,1,0:T(8,128)}, f32[1,4,512,256]{3,2,1,0:T(8,128)}, u32[]{:S(2)}, u32[]{:S(2)}) collective-permute-start(f32[1,4,512,256]{3,2,1,0:T(8,128)} %constant_dynamic-slice_fusion), channel_id=1, source_target_pairs={{0,16},{8,24},{16,0},{24,8},{1,17},{9,25},{17,1},{25,9},{2,18},{10... | collective-permute-start | bytes 6291464 | tf_op jit(solution)/shard_map/ppermute | solution.py:143
  468.0 31.7 %collective-permute-start.39 = (f32[512,512]{1,0:T(8,128)S(1)}, f32[512,512]{1,0:T(8,128)}, u32[]{:S(2)}, u32[]{:S(2)}) collective-permute-start(f32[512,512]{1,0:T(8,128)S(1)} %add_add_fusion), channel_id=1, source_target_pairs={{0,1},{1,0},{2,3},{3,2},{4,5},{5,4},{6,7},{7,6},{8,9},{9,8},{10,11... | collective-permute-start | bytes 3145736 | tf_op jit(solution)/shard_map/ppermute | solution.py:216
  505.1 3.6 copy-start.8
  505.3 7.0 %copy-start.11 = (f32[512,512]{1,0:T(8,128)S(1)}, f32[512,512]{1,0:T(8,128)}, u32[]{:S(2)}) copy-start(f32[512,512]{1,0:T(8,128)} %fusion.26) | copy-start | bytes 3145732
  (4 other events, 4.5 us)

commit v6 on v5

--- a/solution.py
+++ b/solution.py
@@ -9,7 +9,7 @@
 P_SIZE = 512
 NP = 4096
 PP = 512
-EARLY = 4
+EARLY = 5
 
 SUB = 8
 LANES = 128
@@ -143,38 +143,40 @@
     return lax.ppermute(x, axis, [(i, i ^ bit) for i in range(n)])
 
 
-def sum_scatter(x, axis):
-    n = lax.axis_size(axis)
+def axis_bits(axis):
+    return [1 << i for i in range(lax.axis_size(axis).bit_length() - 1)]
+
+
+def halve(x, axis, steps=None):
     me = lax.axis_index(axis)
-    bit = 1
-    while bit < n:
-        pairs = x.reshape((x.shape[0] // 2, 2) + x.shape[1:])
-        mine = (me // bit) % 2
-        away = lax.dynamic_index_in_dim(pairs, 1 - mine, 1, keepdims=False)
-        home = lax.dynamic_index_in_dim(pairs, mine, 1, keepdims=False)
-        x = home + flip(away, axis, bit)
-        bit *= 2
-    return x[0]
-
-
-def sum_all(x, axis, gates=()):
-    n = lax.axis_size(axis)
-    me = lax.axis_index(axis)
-    bits = []
-    while 1 << len(bits) < n:
-        bits.append(1 << len(bits))
-    for step, bit in enumerate(bits):
-        if step < len(gates):
-            x, _ = lax.optimization_barrier((x, gates[step]))
+    for bit in axis_bits(axis):
         high = (me // bit) % 2
         half = x.shape[0] // 2
         away = lax.dynamic_slice_in_dim(x, (1 - high) * half, half, 0)
         x = lax.dynamic_slice_in_dim(x, high * half, half, 0) + flip(away, axis, bit)
-    for bit in reversed(bits):
+        if steps is not None:
+            steps.append(x)
+    return x
+
+
+def join(x, axis, steps=None):
+    me = lax.axis_index(axis)
+    for bit in reversed(axis_bits(axis)):
         high = (me // bit) % 2
         other = flip(x, axis, bit)
         x = jnp.concatenate([jnp.where(high == 0, x, other), jnp.where(high == 0, other, x)], axis=0)
+        if steps is not None:
+            steps.append(x)
     return x
+
+
+def scatter_sum(parts, axis):
+    parts = list(parts)
+    for bit in axis_bits(axis):
+        for m in reversed(range(len(parts))):
+            if m & bit and not m & (bit - 1):
+                parts[m ^ bit] = parts[m ^ bit] + flip(parts[m], axis, bit)
+    return parts[0]
 
 
 def line_gather(x, axis, ny):
@@ -197,25 +199,26 @@
     return got, list(zip(up[1:], down[1:]))
 
 
-def share_rows(x, ny):
+def share_line(x, ny):
     branches = lax.axis_size("branch")
     groups = lax.axis_size("col")
     nz = groups // ny
-    col = lax.axis_index("col")
-    branch = lax.axis_index("branch")
-    if nz != branches:
-        return lax.dynamic_slice_in_dim(lax.all_gather(x, "col"), branch * groups // branches, groups // branches, 0)
     place = lambda b, z, y: b * groups + z * ny + y
-    got = jnp.where(col // ny == branch, x, 0.0)
+    got = jnp.where(lax.axis_index("col") // ny == lax.axis_index("branch"), x, 0.0)
     for off in range(1, nz):
         pairs = [(place(b, b, y), place(b, (b + off) % nz, y)) for b in range(branches) for y in range(ny)]
         got = got + lax.ppermute(x, ("branch", "col"), pairs)
+    return got
+
+
+def share_beside(got, ny):
+    groups = lax.axis_size("col")
+    y = lax.axis_index("col") % ny
     shares = [got]
     for j in range(1, ny):
         pairs = [(c, c // ny * ny + (c % ny - j) % ny) for c in range(groups)]
         shares.append(lax.ppermute(got, "col", pairs))
-    order = (jnp.arange(ny) - col % ny) % ny
-    return jnp.take(jnp.stack(shares), order, axis=0)
+    return [sum(jnp.where(y == (i - j) % ny, shares[j], 0.0) for j in range(ny)) for i in range(ny)]
 
 
 def on_device(child_fronts, extend_map, parent_front):
@@ -287,7 +290,7 @@
 
     corner = jnp.concatenate([pivot_column(b) for b in range(pivot_units)], axis=1)
     corner = corner + jnp.where(branch == 0, placed(parent_front[:PP]), 0.0)
-    corner = sum_all(corner, "col", [front[:8], *ends])
+    corner = lax.psum(halve(corner, "branch"), "col")
 
     def rows_for(target):
         return jnp.concatenate([unit_rows(target * per + a) for a in range(per)], axis=0)
@@ -318,29 +321,46 @@
         block = lax.dynamic_slice(factor, (slots[u], 0, parts[u] * width), (1, P_SIZE, width))
         return jnp.where(keeps[u] > 0, block[0], 0.0)
 
-    head = jnp.concatenate([factor_columns(u) for u in range(pivot_units)], axis=1)
-    corner = sum_all(corner - product(head, head, 0, 0), "branch")
-    parent_inverse = inverse_factor(corner)
-
     mine = jnp.concatenate([factor_columns(col * per + a) for a in range(per)], axis=1)
     mine_keep = jnp.repeat(lax.dynamic_slice_in_dim(keeps, col * per, per), width)[:, None] > 0
     pieces = jnp.stack([jnp.where(mine_keep, received[shift], 0.0) for shift in range(groups)])
     left = three_part(mine)
     n = pivot_units
     first = spread_update(slots[:n], places[:n], parts[:n], keeps[:n], left, factor, pieces, width)
-    left, first = lax.optimization_barrier((left, first))
     first = jnp.concatenate([first[u] for u in range(n)], axis=1)
-    first = sum_all(first + jnp.where(branch == 0, parent_front[:PP].T, 0.0), "branch")
-    side = share_rows(first, ny).reshape(nrows, PP)
-
-    spread = spread_update(slots, places, parts, keeps, left, factor, pieces, width)
-    added = sum_scatter(spread.reshape((branches, units_total // branches) + spread.shape[1:]), "branch")
+    steps = []
+    first = first + jnp.where(branch == 0, parent_front[:PP].T, 0.0)
+    first = join(halve(first, "branch", steps), "branch", steps)
+
+    head = jnp.concatenate([factor_columns(u) for u in range(pivot_units)], axis=1)
+    head, _ = lax.optimization_barrier((head, received[far[EARLY]]))
+    corner = corner - halve(product(head, head, 0, 0), "branch")
+    corner, _ = lax.optimization_barrier((corner, received[far[-1]]))
+    parent_inverse = inverse_factor(join(corner, "branch"))
+
+    owned = units_total // branches
+    order = list(reversed(range(branches)))
+    spread = [None] * branches
+    for i, m in enumerate(order):
+        gated, _ = lax.optimization_barrier((left, steps[min(i, len(steps) - 1)]))
+        at = lambda table: lax.dynamic_slice_in_dim(table, (branch ^ m) * owned, owned)
+        spread[m] = spread_update(at(slots), at(places), at(parts), at(keeps), gated, factor, pieces, width)
+    added = scatter_sum(spread, "branch")
     assembled = parent_front + jnp.transpose(added, (0, 2, 1)).reshape(nrows, pcols)
 
     parent_mine = product(parent_inverse, first, 1, 1)
-    row_factor = product(side, parent_inverse, 1, 1)
-    result = assembled - product(row_factor, parent_mine, 1, 0)
-    return (child_mine[None], parent_mine, result)
+    if nz == branches:
+        line, parent_inverse = lax.optimization_barrier((share_line(first, ny), parent_inverse))
+        sides = share_beside(line, ny)
+    else:
+        sides = lax.dynamic_slice_in_dim(
+            lax.all_gather(first, "col"), branch * groups // branches, groups // branches, 0)
+        sides = [sides[i] for i in range(groups // branches)]
+    results = []
+    for i, side in enumerate(sides):
+        rows = assembled[i * pcols:(i + 1) * pcols]
+        results.append(rows - product(product(side, parent_inverse, 1, 1), parent_mine, 1, 0))
+    return (child_mine[None], parent_mine, jnp.concatenate(results, axis=0))
 
 
 def solution(mesh):

time: 526 us -> 554 us (1.053)
  the two profiles are of different devices: /device:TPU:29 before, /device:TPU:0 now
where the time goes in v6:
time: 554 us; the launch traced here: 547 us
  waiting for transfers between devices  234 us (42%)
  local copies, waits for them, and re-layouts  64.9 us (12%)
  other arithmetic  64.1 us (12%)
  Pallas kernels  60.6 us (11%)
  starting transfers between devices  57 us (10%)
  between operations  41.1 us (7%)
  matrix products  24.9 us (4%)
    psum x1, waiting for transfers between devices, on_device(): corner = lax.psum(halve(corner, 'branch'), 'col')  139 us
    pallas_call x2, Pallas kernels, inverse_factor(): pl.pallas_call(inverse_factor_kernel, out_shape=jax.ShapeDtypeStruct((n,...  43.2 us
    unnamed x69, local copies, waits for them, and re-layouts  38 us
    ppermute x7, waiting for transfers between devices, beside(): return lax.ppermute(y, axis, pairs)  31.1 us
    ppermute x13, waiting for transfers between devices, flip(): return lax.ppermute(x, axis, [(i, i ^ bit) for i in range(n)])  29.2 us
    dot_general x15, matrix products, product(): lax.dot_general(a, b, (((ca,), (cb,)), ((), ())), precision=precision)  24.9 us
    ppermute x3, waiting for transfers between devices, line_gather(): lax.ppermute(down[-1], axis, [(c, c - ny) for c in range(n) if 0 < c // n...  19.1 us
    pallas_call x5, Pallas kernels, spread_update(): pl.pallas_call(spread_kernel, grid_spec=pltpu.PrefetchScalarGridSpec(num_...  17.5 us
  transfers between devices with their start and end apart: 38, of which 12 were waited for; matrix products, arithmetic and copies ran while one was open for 18% of the time, Pallas kernels for 11%

profile of v6, /device:TPU:0, one launch (start us, length us, event | category | flops | bytes accessed | tf_op | source)
XLA Modules:
  0.0 546.7 jit_solution(10137362385040294982)
XLA Ops:
  8.6 5.9 %collective-permute-start.1 = (f32[512,512]{1,0:T(8,128)S(1)}, f32[512,512]{1,0:T(8,128)}, u32[]{:S(2)}, u32[]{:S(2)}) collective-permute-start(f32[512,512]{1,0:T(8,128)S(1)} %slice_bitcast_fusion), channel_id=1, source_target_pairs={{0,2},{1,3},{2,4},{3,5},{4,6},{5,7},{8,10},{9,11},{10,12},{11,13},... | collective-permute-start | bytes 3145736 | tf_op jit(solution)/shard_map/ppermute | solution.py:187
  26.0 10.0 %collective-permute-done.1 = f32[512,512]{1,0:T(8,128)} collective-permute-done((f32[512,512]{1,0:T(8,128)S(1)}, f32[512,512]{1,0:T(8,128)}, u32[]{:S(2)}, u32[]{:S(2)}) %collective-permute-start.1) | collective-permute-done | bytes 1048608 | tf_op jit(solution)/shard_map/ppermute | solution.py:187
  37.6 3.6 collective-permute-done.2
  47.6 2.4 collective-permute-start.12
  51.7 15.5 %collective-permute-done.3 = f32[512,512]{1,0:T(8,128)} collective-permute-done((f32[512,512]{1,0:T(8,128)}, f32[512,512]{1,0:T(8,128)}, u32[]{:S(2)}, u32[]{:S(2)}) %collective-permute-start.3) | collective-permute-done | bytes 1048608 | tf_op jit(solution)/shard_map/ppermute | solution.py:188
  72.7 3.5 collective-permute-done.19
  76.9 1.7 collective-permute-start.8
  78.6 15.8 %collective-permute-done.12 = f32[512,512]{1,0:T(8,128)} collective-permute-done((f32[512,512]{1,0:T(8,128)}, f32[512,512]{1,0:T(8,128)}, u32[]{:S(2)}, u32[]{:S(2)}) %collective-permute-start.12) | collective-permute-done | bytes 1048608 | tf_op jit(solution)/shard_map/ppermute | solution.py:192
  94.4 3.4 collective-permute-start.9
  97.9 1.7 collective-permute-start.11
  99.5 2.4 collective-permute-start.6
  112.2 4.5 constant_dynamic-slice_fusion.3
  128.6 15.3 %collective-permute-done.6 = f32[512,512]{1,0:T(8,128)} collective-permute-done((f32[512,512]{1,0:T(8,128)}, f32[512,512]{1,0:T(8,128)}, u32[]{:S(2)}, u32[]{:S(2)}) %collective-permute-start.6) | collective-permute-done | bytes 1048608 | tf_op jit(solution)/shard_map/ppermute | solution.py:192
  157.7 8.6 %select_add_fusion = (f32[512,512]{1,0:T(8,128)S(1)}, f32[512,512]{1,0:T(8,128)}, f32[512,512]{1,0:T(8,128)}, f32[512,512]{1,0:T(8,128)}, f32[512,512]{1,0:T(8,1...) fusion(f32[512,512]{1,0:T(8,128)S(1)} %collective-permute-done, pred[]{:T(512)S(6)} %and.167, pred[]{:T(512)S(6)} %and.166, ...), kind=kLoop, calls=%fused_computation.59 | loop fusion | flops 5505024 | bytes 22020104 | tf_op jit(solution)/shard_map/add | solution.py:272
  166.3 21.7 %shard_map.58 = f32[512,512]{1,0:T(8,128)S(1)} custom-call(f32[512,512]{1,0:T(8,128)S(1)} %get-tuple-element.50.a_ref), custom_call_target="tpu_custom_call" | custom-call | flops 134217728 | bytes 2097152 | tf_op jit(solution)/shard_map/pallas_call | solution.py:86
  189.3 139.1 %all-reduce.2.cloned.1.call-done = f32[128,512]{0,1:T(8,128)} async-done(((f32[128,512]{0,1:T(8,128)}), f32[128,512]{0,1:T(8,128)}) %all-reduce.2.cloned.1.call-update) | async-done | bytes 262160 | tf_op jit(solution)/shard_map/psum | solution.py:293
  330.0 2.2 fusion.7
  333.3 2.2 fusion.5
  341.8 3.2 copy-done
  346.4 1.9 copy.67.left_ref
  349.7 2.4 bitcast_dynamic-update-slice_fusion.6
  352.1 2.3 bitcast_dynamic-update-slice_fusion.5
  354.4 2.4 bitcast_dynamic-update-slice_fusion.4
  356.8 2.6 bitcast_dynamic-update-slice_fusion.3
  359.4 2.4 bitcast_dynamic-update-slice_fusion.2
  361.8 2.3 bitcast_dynamic-update-slice_fusion.1
  364.1 2.4 bitcast_dynamic-update-slice_fusion.piece_ref
  366.5 3.4 copy-done.5
  369.9 2.0 shard_map.60
  378.7 4.9 collective-permute-done.27
  383.6 1.7 dynamic-slice_add_fusion.3
  388.1 1.7 copy.72.left_ref
  389.8 3.4 copy-done.1
  393.2 3.4 copy-done.6
  396.5 4.4 shard_map.64
  405.9 6.8 %collective-permute-done.24 = f32[128,512]{1,0:T(8,128)S(1)} collective-permute-done((f32[128,512]{1,0:T(8,128)S(1)}, f32[128,512]{1,0:T(8,128)S(1)}, u32[]{:S(2)}, u32[]{:S(2)}) %collective-permute-start.24) | collective-permute-done | bytes 262176 | tf_op jit(solution)/shard_map/ppermute | solution.py:143
  414.6 5.7 %collective-permute-start.33 = (f32[512,512]{1,0:T(8,128)}, f32[512,512]{1,0:T(8,128)}, u32[]{:S(2)}, u32[]{:S(2)}) collective-permute-start(f32[512,512]{1,0:T(8,128)} %pad_maximum_fusion.11), channel_id=1, source_target_pairs={{0,2},{1,3},{10,12},{11,13},{20,22},{21,23},{30,24},{31,25}} | collective-permute-start | bytes 3145736 | tf_op jit(solution)/shard_map/ppermute | solution.py:210
  420.3 2.8 collective-permute-start.34
  423.1 2.4 collective-permute-start.35
  426.4 1.7 copy.71.left_ref
  428.1 3.4 copy-done.2
  431.5 3.4 copy-done.7
  434.8 3.4 shard_map.63
  439.5 1.7 copy.70.left_ref
  441.3 3.4 copy-done.3
  444.6 3.4 copy-done.8
  448.0 4.5 shard_map.62
  454.3 21.5 %shard_map.59 = f32[512,512]{1,0:T(8,128)S(1)} custom-call(f32[512,512]{1,0:T(8,128)S(1)} %pad_maximum_fusion.10.a_ref), custom_call_target="tpu_custom_call" | custom-call | flops 134217728 | bytes 2097152 | tf_op jit(solution)/shard_map/pallas_call | solution.py:86
  475.9 3.4 add.538
  479.4 2.4 add_add_fusion
  483.1 3.2 convolution_bitcast_fusion.8
  486.3 2.7 copy.69.left_ref
  489.0 3.4 copy-done.4
  492.4 3.4 copy-done.9
  497.2 3.3 shard_map.61
  501.6 5.5 collective-permute-done.36
  507.0 2.3 fusion.10
  509.3 2.0 fusion.43
  511.3 2.0 fusion.14
  513.3 13.9 %collective-permute-done.32 = f32[4,512,256]{2,1,0:T(8,128)} collective-permute-done((f32[4,512,256]{2,1,0:T(8,128)}, f32[4,512,256]{2,1,0:T(8,128)}, u32[]{:S(2)}, u32[]{:S(2)}) %collective-permute-start.32) | collective-permute-done | bytes 2097184 | tf_op jit(solution)/shard_map/ppermute | solution.py:143
  527.3 4.2 add_bitcast_fusion
  531.5 1.9 copy.73
  533.4 1.9 bitcast_add_fusion
  535.3 2.7 slice_subtract_fusion.1
  (183 shorter events, 77.5 us)
Async XLA Ops:
  7.2 36.3 %slice-start.2 = ((f32[1024,512]{1,0:T(8,128)}), f32[512,512]{1,0:T(8,128)S(1)}, s32[]{:S(2)}) async-start(f32[1024,512]{1,0:T(8,128)} %param.5), calls=%async_computation.3 | async-start | bytes 2097152 | tf_op jit(solution)/shard_map/slice | solution.py:292
  7.2 321.2 %all-reduce.2.cloned.1.call-start = ((), (), s32[]{:S(2)}) async-start(), calls=%async_computation | async-start | bytes 524288 | tf_op jit(solution)/shard_map/psum | solution.py:293
  8.6 32.5 %copy-start.29 = (f32[512,512]{1,0:T(8,128)}, f32[512,512]{1,0:T(8,128)S(1)}, u32[]{:S(2)}) copy-start(f32[512,512]{1,0:T(8,128)S(1)} %slice_bitcast_fusion) | copy-start | bytes 3145732
  8.6 27.3 %collective-permute-start.1 = (f32[512,512]{1,0:T(8,128)S(1)}, f32[512,512]{1,0:T(8,128)}, u32[]{:S(2)}, u32[]{:S(2)}) collective-permute-start(f32[512,512]{1,0:T(8,128)S(1)} %slice_bitcast_fusion), channel_id=1, source_target_pairs={{0,2},{1,3},{2,4},{3,5},{4,6},{5,7},{8,10},{9,11},{10,12},{11,13},... | collective-permute-start | bytes 3145736 | tf_op jit(solution)/shard_map/ppermute | solution.py:187
  14.5 26.6 %collective-permute-start.2 = (f32[512,512]{1,0:T(8,128)S(1)}, f32[512,512]{1,0:T(8,128)}, u32[]{:S(2)}, u32[]{:S(2)}) collective-permute-start(f32[512,512]{1,0:T(8,128)S(1)} %slice_bitcast_fusion), channel_id=1, source_target_pairs={{2,0},{3,1},{4,2},{5,3},{6,4},{7,5},{10,8},{11,9},{12,10},{13,11},... | collective-permute-start | bytes 3145736 | tf_op jit(solution)/shard_map/ppermute | solution.py:188
  35.9 14.0 %collective-permute-start.7 = (f32[512,512]{1,0:T(8,128)}, f32[512,512]{1,0:T(8,128)}, u32[]{:S(2)}, u32[]{:S(2)}) collective-permute-start(f32[512,512]{1,0:T(8,128)} %collective-permute-done.1), channel_id=1, source_target_pairs={{2,4},{3,5},{4,6},{5,7},{10,12},{11,13},{12,14},{13,15},{18,20},{1... | collective-permute-start | bytes 3145736 | tf_op jit(solution)/shard_map/ppermute | solution.py:187
  41.1 26.1 %collective-permute-start.3 = (f32[512,512]{1,0:T(8,128)}, f32[512,512]{1,0:T(8,128)}, u32[]{:S(2)}, u32[]{:S(2)}) collective-permute-start(f32[512,512]{1,0:T(8,128)} %collective-permute-done.2), channel_id=1, source_target_pairs={{2,0},{3,1},{4,2},{5,3},{10,8},{11,9},{12,10},{13,11},{18,16},{19,... | collective-permute-start | bytes 3145736 | tf_op jit(solution)/shard_map/ppermute | solution.py:188
  43.8 72.9 %copy-start.14 = (f32[512,512]{0,1:T(8,128)}, f32[512,512]{0,1:T(8,128)S(1)}, u32[]{:S(2)}) copy-start(f32[512,512]{0,1:T(8,128)S(1)} %copy.86) | copy-start | bytes 3145732
  46.1 22.5 %collective-permute-start.18 = (f32[256,512]{0,1:T(8,128)}, f32[256,512]{0,1:T(8,128)}, u32[]{:S(2)}, u32[]{:S(2)}) collective-permute-start(f32[256,512]{0,1:T(8,128)} %constant_dynamic-slice_fusion.7), channel_id=1, source_target_pairs={{0,8},{8,0},{16,24},{24,16},{1,9},{9,1},{17,25},{25,17},{2,10},{10... | collective-permute-start | bytes 1572872 | tf_op jit(solution)/shard_map/ppermute | solution.py:143
  46.1 30.9 %collective-permute-start = (f32[512,512]{1,0:T(8,128)}, f32[512,512]{1,0:T(8,128)S(1)}, u32[]{:S(2)}, u32[]{:S(2)}) collective-permute-start(f32[512,512]{1,0:T(8,128)} %copy-done.29), channel_id=1, source_target_pairs={{0,1},{1,0},{2,3},{3,2},{4,5},{5,4},{6,7},{7,6},{8,9},{9,8},{10,11... | collective-permute-start | bytes 3145736 | tf_op jit(solution)/shard_map/ppermute | solution.py:192
  47.6 46.8 %collective-permute-start.12 = (f32[512,512]{1,0:T(8,128)}, f32[512,512]{1,0:T(8,128)}, u32[]{:S(2)}, u32[]{:S(2)}) collective-permute-start(f32[512,512]{1,0:T(8,128)} %collective-permute-done.2), channel_id=1, source_target_pairs={{0,1},{1,0},{2,3},{3,2},{4,5},{5,4},{8,9},{9,8},{10,11},{11,10},{1... | collective-permute-start | bytes 3145736 | tf_op jit(solution)/shard_map/ppermute | solution.py:192
  50.0 47.8 %collective-permute-start.10 = (f32[512,512]{1,0:T(8,128)}, f32[512,512]{1,0:T(8,128)}, u32[]{:S(2)}, u32[]{:S(2)}) collective-permute-start(f32[512,512]{1,0:T(8,128)} %collective-permute-done.7), channel_id=1, source_target_pairs={{4,6},{5,7},{12,14},{13,15},{20,22},{21,23},{28,30},{29,31}} | collective-permute-start | bytes 3145736 | tf_op jit(solution)/shard_map/ppermute | solution.py:187
  67.2 32.3 %collective-permute-start.4 = (f32[512,512]{1,0:T(8,128)}, f32[512,512]{1,0:T(8,128)}, u32[]{:S(2)}, u32[]{:S(2)}) collective-permute-start(f32[512,512]{1,0:T(8,128)} %collective-permute-done.3), channel_id=1, source_target_pairs={{2,0},{3,1},{10,8},{11,9},{18,16},{19,17},{26,24},{27,25}} | collective-permute-start | bytes 3145736 | tf_op jit(solution)/shard_map/ppermute | solution.py:188
  69.7 7.2 %copy-start.26 = (f32[256,512]{0,1:T(8,128)}, f32[256,512]{0,1:T(8,128)S(1)}, u32[]{:S(2)}) copy-start(f32[256,512]{0,1:T(8,128)S(1)} %dynamic-slice_add_fusion.2) | copy-start | bytes 1572868
  69.8 6.4 %collective-permute-start.19 = (f32[128,512]{0,1:T(8,128)S(1)}, f32[128,512]{0,1:T(8,128)S(1)}, u32[]{:S(2)}, u32[]{:S(2)}) collective-permute-start(f32[128,512]{0,1:T(8,128)S(1)} %constant_dynamic-slice_fusion.6), channel_id=1, source_target_pairs={{0,16},{8,24},{16,0},{24,8},{1,17},{9,25},{17,1},{25,9},{2,18},{10... | collective-permute-start | bytes 786440 | tf_op jit(solution)/shard_map/ppermute | solution.py:143
  76.2 47.2 %collective-permute-start.5 = (f32[512,512]{1,0:T(8,128)}, f32[512,512]{1,0:T(8,128)S(1)}, u32[]{:S(2)}, u32[]{:S(2)}) collective-permute-start(f32[512,512]{1,0:T(8,128)} %collective-permute-done.1), channel_id=1, source_target_pairs={{2,3},{3,2},{4,5},{5,4},{6,7},{7,6},{10,11},{11,10},{12,13},{13,12... | collective-permute-start | bytes 3145736 | tf_op jit(solution)/shard_map/ppermute | solution.py:192
  76.9 47.7 %collective-permute-start.8 = (f32[512,512]{1,0:T(8,128)}, f32[512,512]{1,0:T(8,128)}, u32[]{:S(2)}, u32[]{:S(2)}) collective-permute-start(f32[512,512]{1,0:T(8,128)} %collective-permute-done.7), channel_id=1, source_target_pairs={{4,5},{5,4},{6,7},{7,6},{12,13},{13,12},{14,15},{15,14},{20,21},{2... | collective-permute-start | bytes 3145736 | tf_op jit(solution)/shard_map/ppermute | solution.py:192
  94.4 31.6 %collective-permute-start.9 = (f32[512,512]{1,0:T(8,128)}, f32[512,512]{1,0:T(8,128)}, u32[]{:S(2)}, u32[]{:S(2)}) collective-permute-start(f32[512,512]{1,0:T(8,128)} %collective-permute-done.3), channel_id=1, source_target_pairs={{0,1},{1,0},{2,3},{3,2},{8,9},{9,8},{10,11},{11,10},{16,17},{17,16... | collective-permute-start | bytes 3145736 | tf_op jit(solution)/shard_map/ppermute | solution.py:192
  97.9 29.4 %collective-permute-start.11 = (f32[512,512]{1,0:T(8,128)}, f32[512,512]{1,0:T(8,128)}, u32[]{:S(2)}, u32[]{:S(2)}) collective-permute-start(f32[512,512]{1,0:T(8,128)} %collective-permute-done.10), channel_id=1, source_target_pairs={{6,7},{7,6},{14,15},{15,14},{22,23},{23,22},{30,31},{31,30}} | collective-permute-start | bytes 3145736 | tf_op jit(solution)/shard_map/ppermute | solution.py:192
  99.5 44.3 %collective-permute-start.6 = (f32[512,512]{1,0:T(8,128)}, f32[512,512]{1,0:T(8,128)}, u32[]{:S(2)}, u32[]{:S(2)}) collective-permute-start(f32[512,512]{1,0:T(8,128)} %collective-permute-done.4), channel_id=1, source_target_pairs={{0,1},{1,0},{8,9},{9,8},{16,17},{17,16},{24,25},{25,24}} | collective-permute-start | bytes 3145736 | tf_op jit(solution)/shard_map/ppermute | solution.py:192
  116.7 40.2 %copy-start.27 = (f32[256,512]{0,1:T(8,128)S(1)}, f32[256,512]{0,1:T(8,128)}, u32[]{:S(2)}) copy-start(f32[256,512]{0,1:T(8,128)} %copy-done.26) | copy-start | bytes 1572868
  123.4 34.3 %copy-start.28 = (f32[512,512]{1,0:T(8,128)}, f32[512,512]{1,0:T(8,128)S(1)}, u32[]{:S(2)}) copy-start(f32[512,512]{1,0:T(8,128)S(1)} %collective-permute-done.5) | copy-start | bytes 3145732
  123.4 64.6 %collective-permute-start.17 = (f32[512,512]{1,0:T(8,128)}, f32[512,512]{1,0:T(8,128)}, u32[]{:S(2)}, u32[]{:S(2)}) collective-permute-start(f32[512,512]{1,0:T(8,128)} %pad_maximum_fusion.6), channel_id=1, source_target_pairs={{1,7},{2,0},{3,1},{4,2},{5,3},{6,4},{7,5},{9,15},{10,8},{11,9},{12... | collective-permute-start | bytes 3145736 | tf_op jit(solution)/shard_map/ppermute | solution.py:300
  124.7 203.7 %collective-permute-start.16 = (f32[512,512]{1,0:T(8,128)}, f32[512,512]{1,0:T(8,128)}, u32[]{:S(2)}, u32[]{:S(2)}) collective-permute-start(f32[512,512]{1,0:T(8,128)} %get-tuple-element.28), channel_id=1, source_target_pairs={{1,3},{2,4},{3,5},{4,6},{5,7},{6,0},{7,1},{9,11},{10,12},{11,13},{... | collective-permute-start | bytes 3145736 | tf_op jit(solution)/shard_map/ppermute | solution.py:300
  126.0 202.4 %collective-permute-start.15 = (f32[512,512]{1,0:T(8,128)}, f32[512,512]{1,0:T(8,128)}, u32[]{:S(2)}, u32[]{:S(2)}) collective-permute-start(f32[512,512]{1,0:T(8,128)} %get-tuple-element.27), channel_id=1, source_target_pairs={{1,6},{2,7},{3,0},{4,1},{5,2},{6,3},{7,4},{9,14},{10,15},{11,8},{1... | collective-permute-start | bytes 3145736 | tf_op jit(solution)/shard_map/ppermute | solution.py:300
  127.3 201.1 %collective-permute-start.14 = (f32[512,512]{1,0:T(8,128)}, f32[512,512]{1,0:T(8,128)}, u32[]{:S(2)}, u32[]{:S(2)}) collective-permute-start(f32[512,512]{1,0:T(8,128)} %get-tuple-element.26), channel_id=1, source_target_pairs={{1,4},{2,5},{3,6},{4,7},{5,0},{6,1},{7,2},{9,12},{10,13},{11,14},{... | collective-permute-start | bytes 3145736 | tf_op jit(solution)/shard_map/ppermute | solution.py:300
  143.9 184.6 %collective-permute-start.13 = (f32[512,512]{1,0:T(8,128)}, f32[512,512]{1,0:T(8,128)}, u32[]{:S(2)}, u32[]{:S(2)}) collective-permute-start(f32[512,512]{1,0:T(8,128)} %get-tuple-element.25), channel_id=1, source_target_pairs={{1,5},{2,6},{3,7},{4,0},{5,1},{6,2},{7,3},{9,13},{10,14},{11,15},{... | collective-permute-start | bytes 3145736 | tf_op jit(solution)/shard_map/ppermute | solution.py:300
  188.0 161.6 %collective-permute-start.20 = (f32[512,512]{1,0:T(8,128)}, f32[512,512]{1,0:T(8,128)}, u32[]{:S(2)}, u32[]{:S(2)}) collective-permute-start(f32[512,512]{1,0:T(8,128)} %get-tuple-element.32), channel_id=1, source_target_pairs={{1,2},{2,3},{3,4},{4,5},{5,6},{6,7},{7,0},{9,10},{10,11},{11,12},{... | collective-permute-start | bytes 3145736 | tf_op jit(solution)/shard_map/ppermute | solution.py:300
  328.4 7.1 %copy-start.25 = (f32[512,512]{1,0:T(8,128)S(1)}, f32[512,512]{1,0:T(8,128)}, u32[]{:S(2)}) copy-start(f32[512,512]{1,0:T(8,128)} %get-tuple-element.52) | copy-start | bytes 3145732
  328.4 8.2 %copy-start.24 = (f32[512,512]{1,0:T(8,128)S(1)}, f32[512,512]{1,0:T(8,128)}, u32[]{:S(2)}) copy-start(f32[512,512]{1,0:T(8,128)} %get-tuple-element.53) | copy-start | bytes 3145732
  328.4 9.2 %copy-start.23 = (f32[512,512]{1,0:T(8,128)S(1)}, f32[512,512]{1,0:T(8,128)}, u32[]{:S(2)}) copy-start(f32[512,512]{1,0:T(8,128)} %get-tuple-element.54) | copy-start | bytes 3145732
  328.4 35.7 %collective-permute-start.23 = (f32[512,512]{1,0:T(8,128)}, f32[512,512]{1,0:T(8,128)}, u32[]{:S(2)}, u32[]{:S(2)}) collective-permute-start(f32[512,512]{1,0:T(8,128)} %get-tuple-element.34), channel_id=1, source_target_pairs={{1,0},{2,1},{3,2},{4,3},{5,4},{6,5},{7,6},{9,8},{10,9},{11,10},{12... | collective-permute-start | bytes 3145736 | tf_op jit(solution)/shard_map/ppermute | solution.py:300
  332.2 6.4 %copy-start.22 = (f32[512,512]{1,0:T(8,128)S(1)}, f32[512,512]{1,0:T(8,128)}, u32[]{:S(2)}) copy-start(f32[512,512]{1,0:T(8,128)} %get-tuple-element.55) | copy-start | bytes 3145732
  348.3 18.2 %slice-start = ((s8[8388608]{0:T(1024)(128)(4,1)}), s8[4194304]{0:T(1024)(128)(4,1)S(1)}, s32[]{:S(2)}) async-start(s8[8388608]{0:T(1024)(128)(4,1)} %bitcast.174), calls=%async_computation.1 | async-start | bytes 8388608
  356.8 9.7 %slice-start.1 = ((s8[8388608]{0:T(1024)(128)(4,1)}), s8[4194304]{0:T(1024)(128)(4,1)S(1)}, s32[]{:S(2)}) async-start(s8[8388608]{0:T(1024)(128)(4,1)} %bitcast.174), calls=%async_computation.2 | async-start | bytes 8388608
  366.5 3.4 copy-start.5
  372.2 2.0 collective-permute-start.26
  373.4 4.2 collective-permute-start.21
  375.0 8.7 %collective-permute-start.27 = (f32[128,512]{1,0:T(8,128)}, f32[128,512]{1,0:T(8,128)}, u32[]{:S(2)}, u32[]{:S(2)}) collective-permute-start(f32[128,512]{1,0:T(8,128)} %constant_dynamic-slice_fusion), channel_id=1, source_target_pairs={{0,16},{8,24},{16,0},{24,8},{1,17},{9,25},{17,1},{25,9},{2,18},{10... | collective-permute-start | bytes 786440 | tf_op jit(solution)/shard_map/ppermute | solution.py:143
  385.3 15.6 %collective-permute-start.28 = (f32[128,512]{1,0:T(8,128)}, f32[128,512]{1,0:T(8,128)}, u32[]{:S(2)}, u32[]{:S(2)}) collective-permute-start(f32[128,512]{1,0:T(8,128)} %dynamic-slice_add_fusion.3), channel_id=1, source_target_pairs={{0,16},{8,24},{16,0},{24,8},{1,17},{9,25},{17,1},{25,9},{2,18},{10... | collective-permute-start | bytes 786440 | tf_op jit(solution)/shard_map/ppermute | solution.py:143
  387.5 15.8 %collective-permute-start.22 = (f32[128,512]{1,0:T(8,128)}, f32[128,512]{1,0:T(8,128)}, u32[]{:S(2)}, u32[]{:S(2)}) collective-permute-start(f32[128,512]{1,0:T(8,128)} %constant_dynamic-slice_fusion.4), channel_id=1, source_target_pairs={{0,16},{8,24},{16,0},{24,8},{1,17},{9,25},{17,1},{25,9},{2,18},{10... | collective-permute-start | bytes 786440 | tf_op jit(solution)/shard_map/ppermute | solution.py:143
  389.8 3.4 copy-start.1
  393.2 3.4 copy-start.6
  400.9 75.0 %collective-permute-start.31 = (f32[4,512,256]{2,1,0:T(8,128)}, f32[4,512,256]{2,1,0:T(8,128)}, u32[]{:S(2)}, u32[]{:S(2)}) collective-permute-start(f32[4,512,256]{2,1,0:T(8,128)} %shard_map.64), channel_id=1, source_target_pairs={{0,8},{8,0},{16,24},{24,16},{1,9},{9,1},{17,25},{25,17},{2,10},{10... | collective-permute-start | bytes 6291464 | tf_op jit(solution)/shard_map/ppermute | solution.py:143
  402.8 9.8 %collective-permute-start.29 = (f32[256,512]{1,0:T(8,128)}, f32[256,512]{1,0:T(8,128)S(1)}, u32[]{:S(2)}, u32[]{:S(2)}) collective-permute-start(f32[256,512]{1,0:T(8,128)} %pad_maximum_fusion.13), channel_id=1, source_target_pairs={{0,8},{8,0},{16,24},{24,16},{1,9},{9,1},{17,25},{25,17},{2,10},{10... | collective-permute-start | bytes 1572872 | tf_op jit(solution)/shard_map/ppermute | solution.py:143
  404.3 8.3 %collective-permute-start.24 = (f32[128,512]{1,0:T(8,128)S(1)}, f32[128,512]{1,0:T(8,128)S(1)}, u32[]{:S(2)}, u32[]{:S(2)}) collective-permute-start(f32[128,512]{1,0:T(8,128)S(1)} %add_subtract_fusion), channel_id=1, source_target_pairs={{0,16},{8,24},{16,0},{24,8},{1,17},{9,25},{17,1},{25,9},{2,18},{10... | collective-permute-start | bytes 786440 | tf_op jit(solution)/shard_map/ppermute | solution.py:143
  414.6 64.7 %collective-permute-start.33 = (f32[512,512]{1,0:T(8,128)}, f32[512,512]{1,0:T(8,128)}, u32[]{:S(2)}, u32[]{:S(2)}) collective-permute-start(f32[512,512]{1,0:T(8,128)} %pad_maximum_fusion.11), channel_id=1, source_target_pairs={{0,2},{1,3},{10,12},{11,13},{20,22},{21,23},{30,24},{31,25}} | collective-permute-start | bytes 3145736 | tf_op jit(solution)/shard_map/ppermute | solution.py:210
  420.3 59.0 %collective-permute-start.34 = (f32[512,512]{1,0:T(8,128)}, f32[512,512]{1,0:T(8,128)}, u32[]{:S(2)}, u32[]{:S(2)}) collective-permute-start(f32[512,512]{1,0:T(8,128)} %pad_maximum_fusion.11), channel_id=1, source_target_pairs={{0,4},{1,5},{10,14},{11,15},{20,16},{21,17},{30,26},{31,27}} | collective-permute-start | bytes 3145736 | tf_op jit(solution)/shard_map/ppermute | solution.py:210
  423.1 56.2 %collective-permute-start.35 = (f32[512,512]{1,0:T(8,128)}, f32[512,512]{1,0:T(8,128)}, u32[]{:S(2)}, u32[]{:S(2)}) collective-permute-start(f32[512,512]{1,0:T(8,128)} %pad_maximum_fusion.11), channel_id=1, source_target_pairs={{0,6},{1,7},{10,8},{11,9},{20,18},{21,19},{30,28},{31,29}} | collective-permute-start | bytes 3145736 | tf_op jit(solution)/shard_map/ppermute | solution.py:210
  426.4 26.2 %collective-permute-start.25 = (f32[256,512]{1,0:T(8,128)}, f32[256,512]{1,0:T(8,128)}, u32[]{:S(2)}, u32[]{:S(2)}) collective-permute-start(f32[256,512]{1,0:T(8,128)} %pad_maximum_fusion.12), channel_id=1, source_target_pairs={{0,8},{8,0},{16,24},{24,16},{1,9},{9,1},{17,25},{25,17},{2,10},{10... | collective-permute-start | bytes 1572872 | tf_op jit(solution)/shard_map/ppermute | solution.py:143
  428.1 3.4 copy-start.2
  431.5 3.4 copy-start.7
  441.2 3.4 copy-start.3
  444.6 3.4 copy-start.8
  448.0 27.9 %copy-start.11 = (f32[4,512,256]{2,1,0:T(8,128)S(1)}, f32[4,512,256]{2,1,0:T(8,128)}, u32[]{:S(2)}) copy-start(f32[4,512,256]{2,1,0:T(8,128)} %copy-done.10) | copy-start | bytes 6291460
  452.5 26.9 %copy-start.17 = (f32[256,512]{1,0:T(8,128)S(1)}, f32[256,512]{1,0:T(8,128)}, u32[]{:S(2)}) copy-start(f32[256,512]{1,0:T(8,128)} %copy-done.16) | copy-start | bytes 1572868
  452.5 26.9 %copy-start.20 = (f32[256,512]{1,0:T(8,128)S(1)}, f32[256,512]{1,0:T(8,128)}, u32[]{:S(2)}) copy-start(f32[256,512]{1,0:T(8,128)} %copy-done.19) | copy-start | bytes 1572868
  452.5 60.8 %collective-permute-start.30 = (f32[4,512,256]{2,1,0:T(8,128)}, f32[4,512,256]{2,1,0:T(8,128)}, u32[]{:S(2)}, u32[]{:S(2)}) collective-permute-start(f32[4,512,256]{2,1,0:T(8,128)} %shard_map.62), channel_id=1, source_target_pairs={{0,8},{8,0},{16,24},{24,16},{1,9},{9,1},{17,25},{25,17},{2,10},{10... | collective-permute-start | bytes 6291464 | tf_op jit(solution)/shard_map/ppermute | solution.py:143
  479.3 47.9 %collective-permute-start.32 = (f32[4,512,256]{2,1,0:T(8,128)}, f32[4,512,256]{2,1,0:T(8,128)}, u32[]{:S(2)}, u32[]{:S(2)}) collective-permute-start(f32[4,512,256]{2,1,0:T(8,128)} %add.538), channel_id=1, source_target_pairs={{0,16},{8,24},{16,0},{24,8},{1,17},{9,25},{17,1},{25,9},{2,18},{10... | collective-permute-start | bytes 6291464 | tf_op jit(solution)/shard_map/ppermute | solution.py:143
  481.7 25.3 %collective-permute-start.36 = (f32[512,512]{1,0:T(8,128)S(1)}, f32[512,512]{1,0:T(8,128)}, u32[]{:S(2)}, u32[]{:S(2)}) collective-permute-start(f32[512,512]{1,0:T(8,128)S(1)} %add_add_fusion), channel_id=1, source_target_pairs={{0,1},{1,0},{2,3},{3,2},{4,5},{5,4},{6,7},{7,6},{8,9},{9,8},{10,11... | collective-permute-start | bytes 3145736 | tf_op jit(solution)/shard_map/ppermute | solution.py:220
  489.0 3.4 copy-start.4
  492.4 3.4 copy-start.9
  497.1 3.3 copy-start.21
  501.6 33.7 %copy-start.13 = (f32[512,512]{1,0:T(8,128)}, f32[512,512]{1,0:T(8,128)S(1)}, u32[]{:S(2)}) copy-start(f32[512,512]{1,0:T(8,128)S(1)} %fusion.33) | copy-start | bytes 3145732
  (7 other events, 13.9 us)
Sparse Core Ops, SparseCore 0:
  157.9 170.4 all-reduce.1

commit v7 on v6

--- a/solution.py
+++ b/solution.py
@@ -127,7 +127,7 @@
             out_specs=pl.BlockSpec((1, q, width), lambda t, *refs: (t, 0, 0)),
         ),
         out_shape=jax.ShapeDtypeStruct((count, q, width), F32),
-        compiler_params=pltpu.CompilerParams(vmem_limit_bytes=32 * 1024 * 1024),
+        compiler_params=pltpu.CompilerParams(vmem_limit_bytes=56 * 1024 * 1024),
         cost_estimate=pl.CostEstimate(
             flops=6 * count * q * depth * width,
             bytes_accessed=4 * count * width * (2 * q + depth), transcendentals=0),
@@ -172,31 +172,84 @@
 
 def scatter_sum(parts, axis):
     parts = list(parts)
+    terms = [parts[0]]
     for bit in axis_bits(axis):
         for m in reversed(range(len(parts))):
             if m & bit and not m & (bit - 1):
-                parts[m ^ bit] = parts[m ^ bit] + flip(parts[m], axis, bit)
-    return parts[0]
-
-
-def line_gather(x, axis, ny):
+                sent = parts[m]
+                other = flip(sent, axis, bit)
+                if m == bit:
+                    terms.append(other)
+                else:
+                    parts[m ^ bit] = parts[m ^ bit] + other
+    return terms, sent
+
+
+def three_rows(x):
+    high = x.astype(jnp.bfloat16)
+    return high, (x - high.astype(F32)).astype(jnp.bfloat16)
+
+
+def finish_kernel(parent_ref, side_ref, inverse_ref, mine_ref, *rest):
+    terms, out_ref = rest[:-1], rest[-1]
+    total = terms[0][0]
+    for term in terms[1:]:
+        total = total + term[0]
+    dot = lambda a, b, cb: lax.dot_general(a, b, (((1,), (cb,)), ((), ())), preferred_element_type=F32)
+    high, low = three_rows(side_ref[0])
+    ihigh, ilow = three_rows(inverse_ref[...])
+    factor = dot(jnp.concatenate([high, high, low], axis=1), jnp.concatenate([ihigh, ilow, ihigh], axis=1), 1)
+    high, low = three_rows(factor)
+    mhigh, mlow = three_rows(mine_ref[...])
+    outer = dot(jnp.concatenate([high, high, low], axis=1), jnp.concatenate([mhigh, mlow, mhigh], axis=0), 0)
+    out_ref[...] = parent_ref[...] + total.T - outer
+
+
+def finish(parent, terms, sides, inverse, mine):
+    count, q, width = terms[0].shape
+    depth = inverse.shape[0]
+    sides = sides.reshape(count, width, depth)
+    whole = lambda t: (0, 0)
+    block = lambda t: (t, 0, 0)
+    return pl.pallas_call(
+        finish_kernel,
+        grid=(count,),
+        in_specs=[
+            pl.BlockSpec((width, q), lambda t: (t, 0)),
+            pl.BlockSpec((1, width, depth), block),
+            pl.BlockSpec((depth, depth), whole),
+            pl.BlockSpec((depth, q), whole),
+        ] + [pl.BlockSpec((1, q, width), block)] * len(terms),
+        out_specs=pl.BlockSpec((width, q), lambda t: (t, 0)),
+        out_shape=jax.ShapeDtypeStruct(parent.shape, F32),
+        compiler_params=pltpu.CompilerParams(vmem_limit_bytes=48 * 1024 * 1024),
+        cost_estimate=pl.CostEstimate(
+            flops=6 * count * width * depth * (q + depth), bytes_accessed=8 * parent.size * 4, transcendentals=0),
+    )(parent, sides, inverse, mine, *terms)
+
+
+def line_gather(x, axis, ny, gates):
     n = lax.axis_size(axis)
     nz = n // ny
-    up, down = [x], [x]
-    for step in range(1, nz):
-        up.append(lax.ppermute(up[-1], axis, [(c, c + ny) for c in range(n) if step - 1 <= c // ny < nz - 1]))
-        down.append(lax.ppermute(down[-1], axis, [(c, c - ny) for c in range(n) if 0 < c // ny <= nz - step]))
 
     def beside(y, j, rows):
         pairs = [(c, c // ny * ny + (c % ny - j) % ny) for c in range(n) if c // ny in rows]
         return lax.ppermute(y, axis, pairs)
 
-    got = [[x] + [beside(x, j, range(nz)) for j in range(1, ny)]]
+    own = [beside(x, j, range(nz)) for j in range(1, ny)]
+    up, down = [x], [x]
+    for step in range(1, nz):
+        ends = (up[-1], down[-1])
+        if 1 < step < len(gates) + 2:
+            ends, _ = lax.optimization_barrier((ends, gates[step - 2](own)))
+        up.append(lax.ppermute(ends[0], axis, [(c, c + ny) for c in range(n) if step - 1 <= c // ny < nz - 1]))
+        down.append(lax.ppermute(ends[1], axis, [(c, c - ny) for c in range(n) if 0 < c // ny <= nz - step]))
+    got = [[x] + own]
     for k in range(1, nz):
         above, below = range(k, nz), range(k)
         got.append([up[k] + down[nz - k]] + [
             beside(up[k], j, above) + beside(down[nz - k], j, below) for j in range(1, ny)])
-    return got, list(zip(up[1:], down[1:]))
+    return got, (up[-1], down[-1])
 
 
 def share_line(x, ny):
@@ -261,21 +314,6 @@
         wide = lax.dynamic_update_slice_in_dim(wide, x, jnp.minimum(col, pivot_devices - 1) * ncols, 1)
         return jnp.where(col < pivot_devices, wide, 0.0)
 
-    gathered, ends = line_gather(front[:P_SIZE], "col", ny)
-    nz = groups // ny
-    z, y = col // ny, col % ny
-    back = (z - source // ny) % nz
-    aside = (source % ny - y) % ny
-    slots = back * ny + aside
-
-    def top_of(c):
-        return sum(
-            jnp.where((z == (c // ny + k) % nz) & (y == (c % ny - j) % ny), gathered[k][j], 0.0)
-            for k in range(nz) for j in range(ny))
-
-    pivots = [top_of(c) for c in range(pivot_devices)]
-    pivots = jnp.concatenate(pivots, axis=1) if pivot_devices > 1 else pivots[0]
-
     pivot_units = PP // width
 
     def pivot_column(b):
@@ -290,7 +328,10 @@
 
     corner = jnp.concatenate([pivot_column(b) for b in range(pivot_units)], axis=1)
     corner = corner + jnp.where(branch == 0, placed(parent_front[:PP]), 0.0)
-    corner = lax.psum(halve(corner, "branch"), "col")
+    corner_steps = []
+    corner = halve(corner, "branch", corner_steps)
+    corner = halve(corner, "col", corner_steps)
+    corner = join(corner, "col", corner_steps)
 
     def rows_for(target):
         return jnp.concatenate([unit_rows(target * per + a) for a in range(per)], axis=0)
@@ -300,20 +341,39 @@
         return lax.ppermute(rows, "col", pairs)
 
     far = sorted(range(1, groups), key=lambda shift: abs(2 * shift - groups))
+    rows = [rows_for((col + shift) % groups) for shift in far]
+
+    in_branch, in_col = len(axis_bits("branch")), len(axis_bits("col"))
+    gathered, ends = line_gather(front[:P_SIZE], "col", ny, [
+        lambda own: (own, rows, corner_steps[in_branch - 1]), lambda own: corner_steps[in_branch + in_col - 1]])
+    nz = groups // ny
+    z, y = col // ny, col % ny
+    back = (z - source // ny) % nz
+    aside = (source % ny - y) % ny
+    slots = back * ny + aside
+
+    def top_of(c):
+        return sum(
+            jnp.where((z == (c // ny + k) % nz) & (y == (c % ny - j) % ny), gathered[k][j], 0.0)
+            for k in range(nz) for j in range(ny))
+
+    pivots = [top_of(c) for c in range(pivot_devices)]
+    pivots = jnp.concatenate(pivots, axis=1) if pivot_devices > 1 else pivots[0]
+
     received = {0: rows_for(col)}
-    for shift in far[:EARLY]:
-        rows, _ = lax.optimization_barrier((rows_for((col + shift) % groups), ends[-1]))
-        received[shift] = moved(shift, rows)
+    for shift, row in zip(far[:EARLY], rows):
+        row, _ = lax.optimization_barrier((row, (ends, corner)))
+        received[shift] = moved(shift, row)
 
     inverse = inverse_factor(pivots)
-    for shift in far[EARLY:]:
-        rows, _ = lax.optimization_barrier((rows_for((col + shift) % groups), inverse))
-        received[shift] = moved(shift, rows)
+    for shift, row in zip(far[EARLY:], rows[EARLY:]):
+        row, _ = lax.optimization_barrier((row, inverse))
+        received[shift] = moved(shift, row)
     places = (col - source) % groups
     child_mine = product(inverse, front[:P_SIZE], 1, 0)
 
     early = [received[shift] for shift in far[:EARLY]]
-    inverse, early, corner = lax.optimization_barrier((inverse, early, corner))
+    inverse, early = lax.optimization_barrier((inverse, early))
     received.update(zip(far[:EARLY], early))
     factor = jnp.stack([product(inverse, x, 1, 0) for line in gathered for x in line])
 
@@ -336,31 +396,27 @@
     head, _ = lax.optimization_barrier((head, received[far[EARLY]]))
     corner = corner - halve(product(head, head, 0, 0), "branch")
     corner, _ = lax.optimization_barrier((corner, received[far[-1]]))
-    parent_inverse = inverse_factor(join(corner, "branch"))
+    corner = join(corner, "branch")
 
     owned = units_total // branches
-    order = list(reversed(range(branches)))
     spread = [None] * branches
-    for i, m in enumerate(order):
-        gated, _ = lax.optimization_barrier((left, steps[min(i, len(steps) - 1)]))
+    for i, m in enumerate(reversed(range(branches))):
+        table, _ = lax.optimization_barrier((slots, steps[min(i, len(steps) - 1)]))
         at = lambda table: lax.dynamic_slice_in_dim(table, (branch ^ m) * owned, owned)
-        spread[m] = spread_update(at(slots), at(places), at(parts), at(keeps), gated, factor, pieces, width)
-    added = scatter_sum(spread, "branch")
-    assembled = parent_front + jnp.transpose(added, (0, 2, 1)).reshape(nrows, pcols)
+        spread[m] = spread_update(at(table), at(places), at(parts), at(keeps), left, factor, pieces, width)
+    terms, sent = scatter_sum(spread, "branch")
+    corner, _ = lax.optimization_barrier((corner, sent))
+    parent_inverse = inverse_factor(corner)
 
     parent_mine = product(parent_inverse, first, 1, 1)
     if nz == branches:
         line, parent_inverse = lax.optimization_barrier((share_line(first, ny), parent_inverse))
-        sides = share_beside(line, ny)
+        sides = jnp.concatenate(share_beside(line, ny), axis=0)
     else:
         sides = lax.dynamic_slice_in_dim(
-            lax.all_gather(first, "col"), branch * groups // branches, groups // branches, 0)
-        sides = [sides[i] for i in range(groups // branches)]
-    results = []
-    for i, side in enumerate(sides):
-        rows = assembled[i * pcols:(i + 1) * pcols]
-        results.append(rows - product(product(side, parent_inverse, 1, 1), parent_mine, 1, 0))
-    return (child_mine[None], parent_mine, jnp.concatenate(results, axis=0))
+            lax.all_gather(first, "col"), branch * groups // branches, groups // branches, 0).reshape(nrows, PP)
+    result = finish(parent_front, terms, sides, parent_inverse, parent_mine)
+    return (child_mine[None], parent_mine, result)
 
 
 def solution(mesh):

time: 554 us -> 524 us (0.946)
  local copies, waits for them, and re-layouts: 64.9 us -> 28.2 us
  Pallas kernels: 60.6 us -> 93 us
  starting transfers between devices: 57 us -> 72.5 us
  between operations: 41.1 us -> 27.6 us
  other arithmetic: 64.1 us -> 51.5 us
  matrix products: 24.9 us -> 14.5 us
    psum x1 -> x0, waiting for transfers between devices: 139 us -> none  [on_device(): corner = lax.psum(halve(corner, 'branch'), 'col')]
    ppermute x7, waiting for transfers between devices: 0.02 us -> 74 us  [moved(): return lax.ppermute(rows, 'col', pairs)]
    ppermute x13 -> x19, waiting for transfers between devices: 29.2 us -> 89.3 us  [flip(): return lax.ppermute(x, axis, [(i, i ^ bit) for i in range(n)])]
    unnamed x69 -> x33, local copies, waits for them, and re-layouts: 38 us -> 5.58 us
    ppermute x6, waiting for transfers between devices: 29.1 us -> 0.02 us  [the longest x3 0.01 us: line_gather(): lax.ppermute(ends[0], axis, [(c, c + ny) for c in range(n) if step - 1 <=...]
    ppermute x7, waiting for transfers between devices: 31.1 us -> 52.3 us  [beside(): return lax.ppermute(y, axis, pairs)]
    pallas_call x5, Pallas kernels: 17.5 us -> 31 us  [spread_update(): pl.pallas_call(spread_kernel, grid_spec=pltpu.PrefetchScalarGridSpec(num_...]
    pallas_call x2, Pallas kernels: 43.2 us -> 54.5 us  [inverse_factor(): pl.pallas_call(inverse_factor_kernel, out_shape=jax.ShapeDtypeStruct((n,...]
  transfers between devices with their start and end apart: 38 -> 43, of which waited for: 12 -> 17; matrix products, arithmetic and copies ran while one was open for 18% -> 15% of each run, Pallas kernels for 11% -> 16%
where the time goes in v7:
time: 524 us; the launch traced here: 517 us
  waiting for transfers between devices  229 us (44%)
  Pallas kernels  93 us (18%)
  starting transfers between devices  72.5 us (14%)
  other arithmetic  51.5 us (10%)
  local copies, waits for them, and re-layouts  28.2 us (5%)
  between operations  27.6 us (5%)
  matrix products  14.5 us (3%)
    ppermute x19, waiting for transfers between devices, flip(): return lax.ppermute(x, axis, [(i, i ^ bit) for i in range(n)])  89.3 us
    ppermute x7, waiting for transfers between devices, moved(): return lax.ppermute(rows, 'col', pairs)  74 us
    pallas_call x2, Pallas kernels, inverse_factor(): pl.pallas_call(inverse_factor_kernel, out_shape=jax.ShapeDtypeStruct((n,...  54.5 us
    ppermute x7, waiting for transfers between devices, beside(): return lax.ppermute(y, axis, pairs)  52.3 us
    pallas_call x5, Pallas kernels, spread_update(): pl.pallas_call(spread_kernel, grid_spec=pltpu.PrefetchScalarGridSpec(num_...  31 us
    ppermute x19, starting transfers between devices, flip(): return lax.ppermute(x, axis, [(i, i ^ bit) for i in range(n)])  18.3 us
    ppermute x3, starting transfers between devices, share_line(): got = got + lax.ppermute(x, ('branch', 'col'), pairs)  17.4 us
    unnamed x7, other arithmetic  16.3 us
  transfers between devices with their start and end apart: 43, of which 17 were waited for; matrix products, arithmetic and copies ran while one was open for 15% of the time, Pallas kernels for 16%

profile of v7, /device:TPU:0, one launch (start us, length us, event | category | flops | bytes accessed | tf_op | source)
XLA Modules:
  0.0 516.8 jit_solution(16105397808126181257)
XLA Ops:
  9.2 1.6 constant_dynamic-slice_fusion.14
  13.4 2.3 slice_bitcast_fusion
  15.6 2.5 collective-permute-start
  18.1 4.5 collective-permute-start.1
  34.0 5.5 %constant_dynamic-slice_fusion.3 = (f32[1,256,512]{2,1,0:T(8,128)}, f32[256,512]{1,0:T(8,128)S(1)}, f32[256,512]{1,0:T(8,128)S(1)}, f32[256,512]{1,0:T(8,128)S(1...) fusion(f32[1,4096,512]{2,1,0:T(8,128)} %param.3, ...), kind=kLoop, calls=%fused_computation.106 | loop fusion | bytes 16777280 | tf_op jit(solution)/shard_map/dynamic_slice | solution.py:308
  42.1 1.6 collective-permute-start.4
  43.8 1.5 pad_maximum_fusion.4
  45.3 1.5 pad_maximum_fusion.2
  46.8 3.6 collective-permute-done.4
  52.2 1.7 collective-permute-start.5
  55.2 2.9 collective-permute-done.7
  58.3 2.1 collective-permute-start.8
  60.5 27.0 %collective-permute-done.8 = f32[32,512]{0,1:T(8,128)S(1)} collective-permute-done((f32[32,512]{0,1:T(8,128)S(1)}, f32[32,512]{0,1:T(8,128)S(1)}, u32[]{:S(2)}, u32[]{:S(2)}) %collective-permute-start.8) | collective-permute-done | bytes 65568 | tf_op jit(solution)/shard_map/ppermute | solution.py:143
  87.8 11.4 %collective-permute-done.9 = f32[16,512]{0,1:T(8,128)} collective-permute-done((f32[16,512]{0,1:T(8,128)S(1)}, f32[16,512]{0,1:T(8,128)}, u32[]{:S(2)}, u32[]{:S(2)}) %collective-permute-start.9) | collective-permute-done | bytes 32800 | tf_op jit(solution)/shard_map/ppermute | solution.py:143
  100.3 1.7 collective-permute-start.11
  103.3 1.7 collective-permute-start.15
  104.9 5.6 %collective-permute-start.18 = (f32[16,512]{0,1:T(8,128)S(1)}, f32[16,512]{0,1:T(8,128)}, u32[]{:S(2)}, u32[]{:S(2)}) collective-permute-start(f32[16,512]{0,1:T(8,128)S(1)} %dynamic-slice_add_fusion.4), channel_id=1, source_target_pairs={{0,4},{1,5},{2,6},{3,7},{4,0},{5,1},{6,2},{7,3},{8,12},{9,13},{10,... | collective-permute-start | bytes 98312 | tf_op jit(solution)/shard_map/ppermute | solution.py:143
  110.5 10.9 %collective-permute-done.18 = f32[16,512]{0,1:T(8,128)} collective-permute-done((f32[16,512]{0,1:T(8,128)S(1)}, f32[16,512]{0,1:T(8,128)}, u32[]{:S(2)}, u32[]{:S(2)}) %collective-permute-start.18) | collective-permute-done | bytes 32800 | tf_op jit(solution)/shard_map/ppermute | solution.py:143
  122.7 12.8 %collective-permute-done.19 = f32[32,512]{1,0:T(8,128)S(1)} collective-permute-done((f32[32,512]{1,0:T(8,128)S(1)}, f32[32,512]{1,0:T(8,128)S(1)}, u32[]{:S(2)}, u32[]{:S(2)}) %collective-permute-start.19) | collective-permute-done | bytes 65568 | tf_op jit(solution)/shard_map/ppermute | solution.py:143
  135.6 2.0 collective-permute-start.20
  137.5 2.0 collective-permute-start.17
  139.6 1.9 collective-permute-done.20
  141.4 1.6 collective-permute-start.13
  143.1 4.4 collective-permute-start.14
  147.5 1.9 collective-permute-start.12
  149.4 1.7 collective-permute-start.16
  153.3 12.6 %collective-permute-done.17 = f32[512,512]{1,0:T(8,128)} collective-permute-done((f32[512,512]{1,0:T(8,128)}, f32[512,512]{1,0:T(8,128)}, u32[]{:S(2)}, u32[]{:S(2)}) %collective-permute-start.17) | collective-permute-done | bytes 1048608 | tf_op jit(solution)/shard_map/ppermute | solution.py:237
  168.4 19.9 %collective-permute-done.14 = f32[512,512]{1,0:T(8,128)} collective-permute-done((f32[512,512]{1,0:T(8,128)}, f32[512,512]{1,0:T(8,128)}, u32[]{:S(2)}, u32[]{:S(2)}) %collective-permute-start.14) | collective-permute-done | bytes 1048608 | tf_op jit(solution)/shard_map/ppermute | solution.py:237
  189.6 19.9 %collective-permute-done.12 = f32[512,512]{1,0:T(8,128)} collective-permute-done((f32[512,512]{1,0:T(8,128)}, f32[512,512]{1,0:T(8,128)}, u32[]{:S(2)}, u32[]{:S(2)}) %collective-permute-start.12) | collective-permute-done | bytes 1048608 | tf_op jit(solution)/shard_map/ppermute | solution.py:237
  210.8 1.5 collective-permute-start.21
  223.8 2.2 fusion.9
  225.9 7.1 %select_add_fusion.2 = (f32[512,512]{1,0:T(8,128)S(1)}, f32[512,512]{1,0:T(8,128)S(1)}, f32[512,512]{1,0:T(8,128)S(1)}, f32[512,512]{1,0:T(8,128)S(1)}, f32[512,...) fusion(f32[512,512]{1,0:T(8,128)S(1)} %collective-permute-done, pred[]{:T(512)S(6)} %and.211, ...), kind=kLoop, calls=%fused_computation.49 | loop fusion | flops 5505024 | bytes 22020104 | tf_op jit(solution)/shard_map/add | solution.py:356
  233.0 33.0 %shard_map.58 = f32[512,512]{1,0:T(8,128)S(1)} custom-call(f32[512,512]{1,0:T(8,128)S(1)} %get-tuple-element.58.a_ref), custom_call_target="tpu_custom_call" | custom-call | flops 134217728 | bytes 2097152 | tf_op jit(solution)/shard_map/pallas_call | solution.py:86
  267.3 59.1 %collective-permute-done.22 = f32[512,512]{1,0:T(8,128)} collective-permute-done((f32[512,512]{1,0:T(8,128)}, f32[512,512]{1,0:T(8,128)}, u32[]{:S(2)}, u32[]{:S(2)}) %collective-permute-start.22) | collective-permute-done | bytes 1048608 | tf_op jit(solution)/shard_map/ppermute | solution.py:341
  327.7 2.2 fusion.7
  337.0 3.3 copy-done.2
  343.0 2.7 copy.90.left_ref
  345.7 2.3 bitcast_dynamic-update-slice_fusion.6
  348.0 2.4 bitcast_dynamic-update-slice_fusion.5
  350.4 2.4 bitcast_dynamic-update-slice_fusion.4
  352.8 2.3 bitcast_dynamic-update-slice_fusion.3
  355.1 2.3 bitcast_dynamic-update-slice_fusion.2
  357.5 2.4 bitcast_dynamic-update-slice_fusion.1
  359.9 15.0 %collective-permute-done.29 = f32[512,512]{1,0:T(8,128)} collective-permute-done((f32[512,512]{1,0:T(8,128)}, f32[512,512]{1,0:T(8,128)}, u32[]{:S(2)}, u32[]{:S(2)}) %collective-permute-start.29) | collective-permute-done | bytes 1048608 | tf_op jit(solution)/shard_map/ppermute | solution.py:341
  374.8 2.3 bitcast_dynamic-update-slice_fusion.piece_ref
  377.2 4.6 shard_map.59
  385.4 2.0 collective-permute-start.33
  388.6 6.5 %shard_map.61 = f32[4,512,256]{2,1,0:T(8,128)} custom-call(s32[4]{0:T(128)} %dynamic_slice.356.slot_ref, s32[4]{0:T(128)} %get-tuple-element.165.place_ref, s32[4]{0:T(128)} %get-tuple-element.115.part_ref, s32[4]{0:T(128)} %get-tuple-element.111.keep_ref, bf16[512,1536]{1,0:T(8,128)(2,1)} %copy.90.left_ref, f32[8,512,512]{2,1,0:T(8,128)} %copy-done.2, ...), custom_call_target="tpu_custom_call" | custom-call | flops 1610612736 | bytes 6291456 | tf_op jit(solution)/shard_map/pallas_call | solution.py:117
  396.0 1.5 collective-permute-start.28
  397.5 6.9 %collective-permute-done.35 = f32[128,512]{1,0:T(8,128)S(1)} collective-permute-done((f32[128,512]{1,0:T(8,128)S(1)}, f32[128,512]{1,0:T(8,128)S(1)}, u32[]{:S(2)}, u32[]{:S(2)}) %collective-permute-start.35) | collective-permute-done | bytes 262176 | tf_op jit(solution)/shard_map/ppermute | solution.py:143
  405.3 4.3 collective-permute-done.28
  410.0 7.6 %collective-permute-done.30 = f32[128,512]{1,0:T(8,128)S(1)} collective-permute-done((f32[128,512]{1,0:T(8,128)S(1)}, f32[128,512]{1,0:T(8,128)S(1)}, u32[]{:S(2)}, u32[]{:S(2)}) %collective-permute-start.30) | collective-permute-done | bytes 262176 | tf_op jit(solution)/shard_map/ppermute | solution.py:143
  419.9 12.9 %collective-permute-start.37 = (f32[512,512]{1,0:T(8,128)}, f32[512,512]{1,0:T(8,128)}, u32[]{:S(2)}, u32[]{:S(2)}) collective-permute-start(f32[512,512]{1,0:T(8,128)} %pad_maximum_fusion.11), channel_id=1, source_target_pairs={{0,2},{1,3},{10,12},{11,13},{20,22},{21,23},{30,24},{31,25}} | collective-permute-start | bytes 3145736 | tf_op jit(solution)/shard_map/ppermute | solution.py:263
  432.8 2.3 collective-permute-start.38
  435.0 2.3 collective-permute-start.39
  438.7 6.5 %shard_map.60 = f32[4,512,256]{2,1,0:T(8,128)} custom-call(s32[4]{0:T(128)} %dynamic_slice.352.slot_ref, s32[4]{0:T(128)} %get-tuple-element.164.place_ref, s32[4]{0:T(128)} %get-tuple-element.116.part_ref, s32[4]{0:T(128)} %get-tuple-element.112.keep_ref, bf16[512,1536]{1,0:T(8,128)(2,1)} %copy.90.left_ref, f32[8,512,512]{2,1,0:T(8,128)} %copy-done.2, ...), custom_call_target="tpu_custom_call" | custom-call | flops 1610612736 | bytes 6291456 | tf_op jit(solution)/shard_map/pallas_call | solution.py:117
  445.8 6.8 %shard_map.64 = f32[4,512,256]{2,1,0:T(8,128)} custom-call(s32[4]{0:T(128)} %dynamic_slice.364.slot_ref, s32[4]{0:T(128)} %get-tuple-element.167.place_ref, s32[4]{0:T(128)} %get-tuple-element.113.part_ref, s32[4]{0:T(128)} %get-tuple-element.109.keep_ref, bf16[512,1536]{1,0:T(8,128)(2,1)} %copy.90.left_ref, f32[8,512,512]{2,1,0:T(8,128)} %copy-done.2, ...), custom_call_target="tpu_custom_call" | custom-call | flops 1610612736 | bytes 6291456 | tf_op jit(solution)/shard_map/pallas_call | solution.py:117
  453.2 3.2 add.574
  456.6 21.5 %shard_map.62.inverse_ref = f32[512,512]{1,0:T(8,128)S(1)} custom-call(f32[512,512]{1,0:T(8,128)S(1)} %pad_maximum_fusion.10.a_ref), custom_call_target="tpu_custom_call" | custom-call | flops 134217728 | bytes 2097152 | tf_op jit(solution)/shard_map/pallas_call | solution.py:86
  478.1 2.4 add_add_fusion
  480.6 3.2 convolution_bitcast_fusion.8
  484.4 6.5 %shard_map.63.rest_0_ = f32[4,512,256]{2,1,0:T(8,128)} custom-call(s32[4]{0:T(128)} %dynamic_slice.360.slot_ref, s32[4]{0:T(128)} %get-tuple-element.166.place_ref, s32[4]{0:T(128)} %get-tuple-element.114.part_ref, s32[4]{0:T(128)} %get-tuple-element.110.keep_ref, bf16[512,1536]{1,0:T(8,128)(2,1)} %copy.90.left_ref, f32[8,512,512]{2,1,0:T(8,128)} %copy-done.2, ...), custom_call_target="tpu_custom_call" | custom-call | flops 1610612736 | bytes 6291456 | tf_op jit(solution)/shard_map/pallas_call | solution.py:117
  491.9 13.7 %collective-permute-done.40 = f32[512,512]{1,0:T(8,128)S(1)} collective-permute-done((f32[512,512]{1,0:T(8,128)S(1)}, f32[512,512]{1,0:T(8,128)S(1)}, u32[]{:S(2)}, u32[]{:S(2)}) %collective-permute-start.40) | collective-permute-done | bytes 1048608 | tf_op jit(solution)/shard_map/ppermute | solution.py:273
  508.8 7.5 %shard_map.65 = f32[1024,512]{1,0:T(8,128)} custom-call(f32[1024,512]{1,0:T(8,128)S(1)} %copy-done, f32[4,256,512]{2,1,0:T(8,128)} %bitcast.165, f32[512,512]{1,0:T(8,128)S(1)} %shard_map.62.inverse_ref, f32[512,512]{1,0:T(8,128)S(1)} %fusion.17.mine_ref, f32[4,512,256]{2,1,0:T(8,128)} %shard_map.63.rest_0_, f32[4,512,256]{2,1,0:T(8,128)} %copy-done.4, ...), custom_call_target="tpu_custom_call" | custom-call | flops 3221225472 | bytes 16777216 | tf_op jit(solution)/shard_map/pallas_call | solution.py:214
  (161 shorter events, 54.3 us)
Async XLA Ops:
  0.6 10.7 %slice-start = ((f32[1024,512]{1,0:T(8,128)}), f32[512,512]{1,0:T(8,128)S(1)}, s32[]{:S(2)}) async-start(f32[1024,512]{1,0:T(8,128)} %parent_ref.1), calls=%async_computation | async-start | bytes 2097152 | tf_op jit(solution)/shard_map/slice | solution.py:330
  2.3 148.8 %copy-start.11 = (s32[16]{0:T(128)}, s32[16]{0:T(128)S(1)}, u32[]{:S(2)}) copy-start(s32[16]{0:T(128)S(1)} %get-tuple-element.55) | copy-start | bytes 196
  7.2 143.9 %copy-start.10 = (s32[16]{0:T(128)}, s32[16]{0:T(128)S(1)}, u32[]{:S(2)}) copy-start(s32[16]{0:T(128)S(1)} %gather_fusion.1) | copy-start | bytes 196
  12.9 28.1 %collective-permute-start.3 = (f32[256,512]{0,1:T(8,128)}, f32[256,512]{0,1:T(8,128)}, u32[]{:S(2)}, u32[]{:S(2)}) collective-permute-start(f32[256,512]{0,1:T(8,128)} %constant_dynamic-slice_fusion.10), channel_id=1, source_target_pairs={{0,8},{8,0},{16,24},{24,16},{1,9},{9,1},{17,25},{25,17},{2,10},{10... | collective-permute-start | bytes 1572872 | tf_op jit(solution)/shard_map/ppermute | solution.py:143
  15.6 36.5 %collective-permute-start = (f32[512,512]{1,0:T(8,128)}, f32[512,512]{1,0:T(8,128)S(1)}, u32[]{:S(2)}, u32[]{:S(2)}) collective-permute-start(f32[512,512]{1,0:T(8,128)} %slice_bitcast_fusion), channel_id=1, source_target_pairs={{0,1},{1,0},{2,3},{3,2},{4,5},{5,4},{6,7},{7,6},{8,9},{9,8},{10,11... | collective-permute-start | bytes 3145736 | tf_op jit(solution)/shard_map/ppermute | solution.py:237
  18.1 34.1 %collective-permute-start.1 = (f32[512,512]{1,0:T(8,128)}, f32[512,512]{1,0:T(8,128)}, u32[]{:S(2)}, u32[]{:S(2)}) collective-permute-start(f32[512,512]{1,0:T(8,128)} %slice_bitcast_fusion), channel_id=1, source_target_pairs={{0,2},{1,3},{2,4},{3,5},{4,6},{5,7},{8,10},{9,11},{10,12},{11,13},... | collective-permute-start | bytes 3145736 | tf_op jit(solution)/shard_map/ppermute | solution.py:245
  22.6 29.6 %collective-permute-start.2 = (f32[512,512]{1,0:T(8,128)}, f32[512,512]{1,0:T(8,128)}, u32[]{:S(2)}, u32[]{:S(2)}) collective-permute-start(f32[512,512]{1,0:T(8,128)} %slice_bitcast_fusion), channel_id=1, source_target_pairs={{2,0},{3,1},{4,2},{5,3},{6,4},{7,5},{10,8},{11,9},{12,10},{13,11},... | collective-permute-start | bytes 3145736 | tf_op jit(solution)/shard_map/ppermute | solution.py:246
  42.1 8.3 %collective-permute-start.4 = (f32[128,512]{0,1:T(8,128)S(1)}, f32[128,512]{0,1:T(8,128)S(1)}, u32[]{:S(2)}, u32[]{:S(2)}) collective-permute-start(f32[128,512]{0,1:T(8,128)S(1)} %constant_dynamic-slice_fusion.9), channel_id=1, source_target_pairs={{0,16},{8,24},{16,0},{24,8},{1,17},{9,25},{17,1},{25,9},{2,18},{10... | collective-permute-start | bytes 786440 | tf_op jit(solution)/shard_map/ppermute | solution.py:143
  43.8 180.0 %copy-start.7 = (f32[1,256,512]{2,1,0:T(8,128)S(1)}, f32[1,256,512]{2,1,0:T(8,128)}, u32[]{:S(2)}) copy-start(f32[1,256,512]{2,1,0:T(8,128)} %get-tuple-element.65) | copy-start | bytes 1572868
  50.5 7.5 %collective-permute-start.7 = (f32[64,512]{0,1:T(8,128)S(1)}, f32[64,512]{0,1:T(8,128)S(1)}, u32[]{:S(2)}, u32[]{:S(2)}) collective-permute-start(f32[64,512]{0,1:T(8,128)S(1)} %constant_dynamic-slice_fusion.8), channel_id=1, source_target_pairs={{0,1},{1,0},{2,3},{3,2},{4,5},{5,4},{6,7},{7,6},{8,9},{9,8},{10,11... | collective-permute-start | bytes 393224 | tf_op jit(solution)/shard_map/ppermute | solution.py:143
  52.2 49.8 %collective-permute-start.5 = (f32[512,512]{1,0:T(8,128)}, f32[512,512]{1,0:T(8,128)}, u32[]{:S(2)}, u32[]{:S(2)}) collective-permute-start(f32[512,512]{1,0:T(8,128)} %collective-permute-done.1), channel_id=1, source_target_pairs={{2,4},{3,5},{4,6},{5,7},{10,12},{11,13},{12,14},{13,15},{18,20},{1... | collective-permute-start | bytes 3145736 | tf_op jit(solution)/shard_map/ppermute | solution.py:245
  53.9 48.1 %collective-permute-start.6 = (f32[512,512]{1,0:T(8,128)}, f32[512,512]{1,0:T(8,128)}, u32[]{:S(2)}, u32[]{:S(2)}) collective-permute-start(f32[512,512]{1,0:T(8,128)} %collective-permute-done.2), channel_id=1, source_target_pairs={{2,0},{3,1},{4,2},{5,3},{10,8},{11,9},{12,10},{13,11},{18,16},{19,... | collective-permute-start | bytes 3145736 | tf_op jit(solution)/shard_map/ppermute | solution.py:246
  58.3 29.1 %collective-permute-start.8 = (f32[32,512]{0,1:T(8,128)S(1)}, f32[32,512]{0,1:T(8,128)S(1)}, u32[]{:S(2)}, u32[]{:S(2)}) collective-permute-start(f32[32,512]{0,1:T(8,128)S(1)} %constant_dynamic-slice_fusion.7), channel_id=1, source_target_pairs={{0,2},{1,3},{2,0},{3,1},{4,6},{5,7},{6,4},{7,5},{8,10},{9,11},{10,... | collective-permute-start | bytes 196616 | tf_op jit(solution)/shard_map/ppermute | solution.py:143
  87.7 11.5 %collective-permute-start.9 = (f32[16,512]{0,1:T(8,128)S(1)}, f32[16,512]{0,1:T(8,128)}, u32[]{:S(2)}, u32[]{:S(2)}) collective-permute-start(f32[16,512]{0,1:T(8,128)S(1)} %constant_dynamic-slice_fusion.6), channel_id=1, source_target_pairs={{0,4},{1,5},{2,6},{3,7},{4,0},{5,1},{6,2},{7,3},{8,12},{9,13},{10,... | collective-permute-start | bytes 98312 | tf_op jit(solution)/shard_map/ppermute | solution.py:143
  100.3 42.8 %collective-permute-start.11 = (f32[512,512]{1,0:T(8,128)}, f32[512,512]{1,0:T(8,128)}, u32[]{:S(2)}, u32[]{:S(2)}) collective-permute-start(f32[512,512]{1,0:T(8,128)} %collective-permute-done.1), channel_id=1, source_target_pairs={{2,3},{3,2},{4,5},{5,4},{6,7},{7,6},{10,11},{11,10},{12,13},{13,12... | collective-permute-start | bytes 3145736 | tf_op jit(solution)/shard_map/ppermute | solution.py:237
  102.0 45.5 %collective-permute-start.10 = (f32[512,512]{1,0:T(8,128)}, f32[512,512]{1,0:T(8,128)}, u32[]{:S(2)}, u32[]{:S(2)}) collective-permute-start(f32[512,512]{1,0:T(8,128)} %collective-permute-done.6), channel_id=1, source_target_pairs={{2,0},{3,1},{10,8},{11,9},{18,16},{19,17},{26,24},{27,25}} | collective-permute-start | bytes 3145736 | tf_op jit(solution)/shard_map/ppermute | solution.py:246
  103.3 46.1 %collective-permute-start.15 = (f32[512,512]{1,0:T(8,128)}, f32[512,512]{1,0:T(8,128)}, u32[]{:S(2)}, u32[]{:S(2)}) collective-permute-start(f32[512,512]{1,0:T(8,128)} %collective-permute-done.5), channel_id=1, source_target_pairs={{4,6},{5,7},{12,14},{13,15},{20,22},{21,23},{28,30},{29,31}} | collective-permute-start | bytes 3145736 | tf_op jit(solution)/shard_map/ppermute | solution.py:245
  104.9 16.5 %collective-permute-start.18 = (f32[16,512]{0,1:T(8,128)S(1)}, f32[16,512]{0,1:T(8,128)}, u32[]{:S(2)}, u32[]{:S(2)}) collective-permute-start(f32[16,512]{0,1:T(8,128)S(1)} %dynamic-slice_add_fusion.4), channel_id=1, source_target_pairs={{0,4},{1,5},{2,6},{3,7},{4,0},{5,1},{6,2},{7,3},{8,12},{9,13},{10,... | collective-permute-start | bytes 98312 | tf_op jit(solution)/shard_map/ppermute | solution.py:143
  122.6 12.9 %collective-permute-start.19 = (f32[32,512]{1,0:T(8,128)S(1)}, f32[32,512]{1,0:T(8,128)S(1)}, u32[]{:S(2)}, u32[]{:S(2)}) collective-permute-start(f32[32,512]{1,0:T(8,128)S(1)} %pad_maximum_fusion.16), channel_id=1, source_target_pairs={{0,2},{1,3},{2,0},{3,1},{4,6},{5,7},{6,4},{7,5},{8,10},{9,11},{10,... | collective-permute-start | bytes 196616 | tf_op jit(solution)/shard_map/ppermute | solution.py:143
  135.6 5.9 %collective-permute-start.20 = (f32[64,512]{1,0:T(8,128)S(1)}, f32[64,512]{1,0:T(8,128)S(1)}, u32[]{:S(2)}, u32[]{:S(2)}) collective-permute-start(f32[64,512]{1,0:T(8,128)S(1)} %pad_maximum_fusion.15), channel_id=1, source_target_pairs={{0,1},{1,0},{2,3},{3,2},{4,5},{5,4},{6,7},{7,6},{8,9},{9,8},{10,11... | collective-permute-start | bytes 393224 | tf_op jit(solution)/shard_map/ppermute | solution.py:143
  137.5 28.3 %collective-permute-start.17 = (f32[512,512]{1,0:T(8,128)}, f32[512,512]{1,0:T(8,128)}, u32[]{:S(2)}, u32[]{:S(2)}) collective-permute-start(f32[512,512]{1,0:T(8,128)} %collective-permute-done.2), channel_id=1, source_target_pairs={{0,1},{1,0},{2,3},{3,2},{4,5},{5,4},{8,9},{9,8},{10,11},{11,10},{1... | collective-permute-start | bytes 3145736 | tf_op jit(solution)/shard_map/ppermute | solution.py:237
  141.4 25.7 %collective-permute-start.13 = (f32[512,512]{1,0:T(8,128)}, f32[512,512]{1,0:T(8,128)}, u32[]{:S(2)}, u32[]{:S(2)}) collective-permute-start(f32[512,512]{1,0:T(8,128)} %collective-permute-done.5), channel_id=1, source_target_pairs={{4,5},{5,4},{6,7},{7,6},{12,13},{13,12},{14,15},{15,14},{20,21},{2... | collective-permute-start | bytes 3145736 | tf_op jit(solution)/shard_map/ppermute | solution.py:237
  143.1 45.2 %collective-permute-start.14 = (f32[512,512]{1,0:T(8,128)}, f32[512,512]{1,0:T(8,128)}, u32[]{:S(2)}, u32[]{:S(2)}) collective-permute-start(f32[512,512]{1,0:T(8,128)} %collective-permute-done.6), channel_id=1, source_target_pairs={{0,1},{1,0},{2,3},{3,2},{8,9},{9,8},{10,11},{11,10},{16,17},{17,16... | collective-permute-start | bytes 3145736 | tf_op jit(solution)/shard_map/ppermute | solution.py:237
  147.5 62.0 %collective-permute-start.12 = (f32[512,512]{1,0:T(8,128)}, f32[512,512]{1,0:T(8,128)}, u32[]{:S(2)}, u32[]{:S(2)}) collective-permute-start(f32[512,512]{1,0:T(8,128)} %collective-permute-done.10), channel_id=1, source_target_pairs={{0,1},{1,0},{8,9},{9,8},{16,17},{17,16},{24,25},{25,24}} | collective-permute-start | bytes 3145736 | tf_op jit(solution)/shard_map/ppermute | solution.py:237
  149.4 61.4 %collective-permute-start.16 = (f32[512,512]{1,0:T(8,128)}, f32[512,512]{1,0:T(8,128)}, u32[]{:S(2)}, u32[]{:S(2)}) collective-permute-start(f32[512,512]{1,0:T(8,128)} %collective-permute-done.15), channel_id=1, source_target_pairs={{6,7},{7,6},{14,15},{15,14},{22,23},{23,22},{30,31},{31,30}} | collective-permute-start | bytes 3145736 | tf_op jit(solution)/shard_map/ppermute | solution.py:237
  151.9 81.1 %copy-start.8 = (s32[16]{0:T(128)}, s32[16]{0:T(128)S(1)}, u32[]{:S(2)}) copy-start(s32[16]{0:T(128)S(1)} %get-tuple-element.152) | copy-start | bytes 196
  151.9 81.1 %copy-start.12 = (s32[16]{0:T(128)}, s32[16]{0:T(128)S(1)}, u32[]{:S(2)}) copy-start(s32[16]{0:T(128)S(1)} %get-tuple-element.54) | copy-start | bytes 196
  165.8 100.2 %collective-permute-start.25 = (f32[512,512]{1,0:T(8,128)}, f32[512,512]{1,0:T(8,128)}, u32[]{:S(2)}, u32[]{:S(2)}) collective-permute-start(f32[512,512]{1,0:T(8,128)} %get-tuple-element.37), channel_id=1, source_target_pairs={{1,7},{2,0},{3,1},{4,2},{5,3},{6,4},{7,5},{9,15},{10,8},{11,9},{12... | collective-permute-start | bytes 3145736 | tf_op jit(solution)/shard_map/ppermute | solution.py:341
  167.1 100.2 %collective-permute-start.24 = (f32[512,512]{1,0:T(8,128)}, f32[512,512]{1,0:T(8,128)}, u32[]{:S(2)}, u32[]{:S(2)}) collective-permute-start(f32[512,512]{1,0:T(8,128)} %get-tuple-element.36), channel_id=1, source_target_pairs={{1,3},{2,4},{3,5},{4,6},{5,7},{6,0},{7,1},{9,11},{10,12},{11,13},{... | collective-permute-start | bytes 3145736 | tf_op jit(solution)/shard_map/ppermute | solution.py:341
  188.3 79.0 %collective-permute-start.23 = (f32[512,512]{1,0:T(8,128)}, f32[512,512]{1,0:T(8,128)}, u32[]{:S(2)}, u32[]{:S(2)}) collective-permute-start(f32[512,512]{1,0:T(8,128)} %get-tuple-element.35), channel_id=1, source_target_pairs={{1,6},{2,7},{3,0},{4,1},{5,2},{6,3},{7,4},{9,14},{10,15},{11,8},{1... | collective-permute-start | bytes 3145736 | tf_op jit(solution)/shard_map/ppermute | solution.py:341
  209.5 116.9 %collective-permute-start.22 = (f32[512,512]{1,0:T(8,128)}, f32[512,512]{1,0:T(8,128)}, u32[]{:S(2)}, u32[]{:S(2)}) collective-permute-start(f32[512,512]{1,0:T(8,128)} %get-tuple-element.34), channel_id=1, source_target_pairs={{1,4},{2,5},{3,6},{4,7},{5,0},{6,1},{7,2},{9,12},{10,13},{11,14},{... | collective-permute-start | bytes 3145736 | tf_op jit(solution)/shard_map/ppermute | solution.py:341
  210.8 115.6 %collective-permute-start.21 = (f32[512,512]{1,0:T(8,128)}, f32[512,512]{1,0:T(8,128)}, u32[]{:S(2)}, u32[]{:S(2)}) collective-permute-start(f32[512,512]{1,0:T(8,128)} %get-tuple-element.33), channel_id=1, source_target_pairs={{1,5},{2,6},{3,7},{4,0},{5,1},{6,2},{7,3},{9,13},{10,14},{11,15},{... | collective-permute-start | bytes 3145736 | tf_op jit(solution)/shard_map/ppermute | solution.py:341
  266.0 79.7 %collective-permute-start.26 = (f32[512,512]{1,0:T(8,128)}, f32[512,512]{1,0:T(8,128)}, u32[]{:S(2)}, u32[]{:S(2)}) collective-permute-start(f32[512,512]{1,0:T(8,128)} %get-tuple-element.39), channel_id=1, source_target_pairs={{1,2},{2,3},{3,4},{4,5},{5,6},{6,7},{7,0},{9,10},{10,11},{11,12},{... | collective-permute-start | bytes 3145736 | tf_op jit(solution)/shard_map/ppermute | solution.py:341
  326.4 48.4 %collective-permute-start.29 = (f32[512,512]{1,0:T(8,128)}, f32[512,512]{1,0:T(8,128)}, u32[]{:S(2)}, u32[]{:S(2)}) collective-permute-start(f32[512,512]{1,0:T(8,128)} %pad_maximum_fusion.8), channel_id=1, source_target_pairs={{1,0},{2,1},{3,2},{4,3},{5,4},{6,5},{7,6},{9,8},{10,9},{11,10},{12... | collective-permute-start | bytes 3145736 | tf_op jit(solution)/shard_map/ppermute | solution.py:341
  337.0 3.3 copy-start.2
  377.2 6.2 %copy-start.5 = (f32[512,256]{1,0:T(8,128)S(1)}, f32[512,256]{1,0:T(8,128)}, u32[]{:S(2)}) copy-start(f32[512,256]{1,0:T(8,128)} %get-tuple-element.83) | copy-start | bytes 1572868
  377.2 6.2 %copy-start.6 = (f32[512,256]{1,0:T(8,128)S(1)}, f32[512,256]{1,0:T(8,128)}, u32[]{:S(2)}) copy-start(f32[512,256]{1,0:T(8,128)} %get-tuple-element.84) | copy-start | bytes 1572868
  381.8 5.6 %copy-start.9 = (s32[16]{0:T(128)S(1)}, s32[16]{0:T(128)}, u32[]{:S(2)}) copy-start(s32[16]{0:T(128)} %copy-done.8) | copy-start | bytes 196
  381.8 6.3 %copy-start.13 = (s32[16]{0:T(128)S(1)}, s32[16]{0:T(128)}, u32[]{:S(2)}) copy-start(s32[16]{0:T(128)} %copy-done.12) | copy-start | bytes 196
  383.3 2.0 collective-permute-start.32
  384.6 11.2 %collective-permute-start.27 = (f32[256,512]{1,0:T(8,128)S(1)}, f32[256,512]{1,0:T(8,128)S(1)}, u32[]{:S(2)}, u32[]{:S(2)}) collective-permute-start(f32[256,512]{1,0:T(8,128)S(1)} %constant_dynamic-slice_fusion.5), channel_id=1, source_target_pairs={{0,8},{8,0},{16,24},{24,16},{1,9},{9,1},{17,25},{25,17},{2,10},{10... | collective-permute-start | bytes 1572872 | tf_op jit(solution)/shard_map/ppermute | solution.py:143
  385.4 9.8 %collective-permute-start.33 = (f32[128,512]{1,0:T(8,128)S(1)}, f32[128,512]{1,0:T(8,128)S(1)}, u32[]{:S(2)}, u32[]{:S(2)}) collective-permute-start(f32[128,512]{1,0:T(8,128)S(1)} %constant_dynamic-slice_fusion), channel_id=1, source_target_pairs={{0,16},{8,24},{16,0},{24,8},{1,17},{9,25},{17,1},{25,9},{2,18},{10... | collective-permute-start | bytes 786440 | tf_op jit(solution)/shard_map/ppermute | solution.py:143
  395.2 57.5 %collective-permute-start.34 = (f32[4,512,256]{2,1,0:T(8,128)}, f32[4,512,256]{2,1,0:T(8,128)}, u32[]{:S(2)}, u32[]{:S(2)}) collective-permute-start(f32[4,512,256]{2,1,0:T(8,128)} %shard_map.61), channel_id=1, source_target_pairs={{0,8},{8,0},{16,24},{24,16},{1,9},{9,1},{17,25},{25,17},{2,10},{10... | collective-permute-start | bytes 6291464 | tf_op jit(solution)/shard_map/ppermute | solution.py:143
  395.2 9.2 %collective-permute-start.35 = (f32[128,512]{1,0:T(8,128)S(1)}, f32[128,512]{1,0:T(8,128)S(1)}, u32[]{:S(2)}, u32[]{:S(2)}) collective-permute-start(f32[128,512]{1,0:T(8,128)S(1)} %dynamic-slice_add_fusion.3), channel_id=1, source_target_pairs={{0,16},{8,24},{16,0},{24,8},{1,17},{9,25},{17,1},{25,9},{2,18},{10... | collective-permute-start | bytes 786440 | tf_op jit(solution)/shard_map/ppermute | solution.py:143
  396.0 13.6 %collective-permute-start.28 = (f32[128,512]{1,0:T(8,128)S(1)}, f32[128,512]{1,0:T(8,128)S(1)}, u32[]{:S(2)}, u32[]{:S(2)}) collective-permute-start(f32[128,512]{1,0:T(8,128)S(1)} %constant_dynamic-slice_fusion.4), channel_id=1, source_target_pairs={{0,16},{8,24},{16,0},{24,8},{1,17},{9,25},{17,1},{25,9},{2,18},{10... | collective-permute-start | bytes 786440 | tf_op jit(solution)/shard_map/ppermute | solution.py:143
  405.3 12.4 %collective-permute-start.36 = (f32[256,512]{1,0:T(8,128)}, f32[256,512]{1,0:T(8,128)}, u32[]{:S(2)}, u32[]{:S(2)}) collective-permute-start(f32[256,512]{1,0:T(8,128)} %pad_maximum_fusion.13), channel_id=1, source_target_pairs={{0,8},{8,0},{16,24},{24,16},{1,9},{9,1},{17,25},{25,17},{2,10},{10... | collective-permute-start | bytes 1572872 | tf_op jit(solution)/shard_map/ppermute | solution.py:143
  409.7 8.0 %collective-permute-start.30 = (f32[128,512]{1,0:T(8,128)S(1)}, f32[128,512]{1,0:T(8,128)S(1)}, u32[]{:S(2)}, u32[]{:S(2)}) collective-permute-start(f32[128,512]{1,0:T(8,128)S(1)} %add_subtract_fusion), channel_id=1, source_target_pairs={{0,16},{8,24},{16,0},{24,8},{1,17},{9,25},{17,1},{25,9},{2,18},{10... | collective-permute-start | bytes 786440 | tf_op jit(solution)/shard_map/ppermute | solution.py:143
  419.9 58.2 %collective-permute-start.37 = (f32[512,512]{1,0:T(8,128)}, f32[512,512]{1,0:T(8,128)}, u32[]{:S(2)}, u32[]{:S(2)}) collective-permute-start(f32[512,512]{1,0:T(8,128)} %pad_maximum_fusion.11), channel_id=1, source_target_pairs={{0,2},{1,3},{10,12},{11,13},{20,22},{21,23},{30,24},{31,25}} | collective-permute-start | bytes 3145736 | tf_op jit(solution)/shard_map/ppermute | solution.py:263
  432.8 45.3 %collective-permute-start.38 = (f32[512,512]{1,0:T(8,128)}, f32[512,512]{1,0:T(8,128)}, u32[]{:S(2)}, u32[]{:S(2)}) collective-permute-start(f32[512,512]{1,0:T(8,128)} %pad_maximum_fusion.11), channel_id=1, source_target_pairs={{0,4},{1,5},{10,14},{11,15},{20,16},{21,17},{30,26},{31,27}} | collective-permute-start | bytes 3145736 | tf_op jit(solution)/shard_map/ppermute | solution.py:263
  435.0 43.1 %collective-permute-start.39 = (f32[512,512]{1,0:T(8,128)}, f32[512,512]{1,0:T(8,128)}, u32[]{:S(2)}, u32[]{:S(2)}) collective-permute-start(f32[512,512]{1,0:T(8,128)} %pad_maximum_fusion.11), channel_id=1, source_target_pairs={{0,6},{1,7},{10,8},{11,9},{20,18},{21,19},{30,28},{31,29}} | collective-permute-start | bytes 3145736 | tf_op jit(solution)/shard_map/ppermute | solution.py:263
  438.1 18.3 %collective-permute-start.31 = (f32[256,512]{1,0:T(8,128)}, f32[256,512]{1,0:T(8,128)S(1)}, u32[]{:S(2)}, u32[]{:S(2)}) collective-permute-start(f32[256,512]{1,0:T(8,128)} %pad_maximum_fusion.12), channel_id=1, source_target_pairs={{0,8},{8,0},{16,24},{24,16},{1,9},{9,1},{17,25},{25,17},{2,10},{10... | collective-permute-start | bytes 1572872 | tf_op jit(solution)/shard_map/ppermute | solution.py:143
  445.8 7.4 %copy-start.3 = (f32[4,512,256]{2,1,0:T(8,128)S(1)}, f32[4,512,256]{2,1,0:T(8,128)}, u32[]{:S(2)}) copy-start(f32[4,512,256]{2,1,0:T(8,128)} %shard_map.60) | copy-start | bytes 6291460
  452.6 54.8 %collective-permute-start.41 = (f32[4,512,256]{2,1,0:T(8,128)}, f32[4,512,256]{2,1,0:T(8,128)S(1)}, u32[]{:S(2)}, u32[]{:S(2)}) collective-permute-start(f32[4,512,256]{2,1,0:T(8,128)} %shard_map.64), channel_id=1, source_target_pairs={{0,8},{8,0},{16,24},{24,16},{1,9},{9,1},{17,25},{25,17},{2,10},{10... | collective-permute-start | bytes 6291464 | tf_op jit(solution)/shard_map/ppermute | solution.py:143
  456.4 51.1 %collective-permute-start.42 = (f32[4,512,256]{2,1,0:T(8,128)}, f32[4,512,256]{2,1,0:T(8,128)}, u32[]{:S(2)}, u32[]{:S(2)}) collective-permute-start(f32[4,512,256]{2,1,0:T(8,128)} %add.574), channel_id=1, source_target_pairs={{0,16},{8,24},{16,0},{24,8},{1,17},{9,25},{17,1},{25,9},{2,18},{10... | collective-permute-start | bytes 6291464 | tf_op jit(solution)/shard_map/ppermute | solution.py:143
  480.5 25.2 %collective-permute-start.40 = (f32[512,512]{1,0:T(8,128)S(1)}, f32[512,512]{1,0:T(8,128)S(1)}, u32[]{:S(2)}, u32[]{:S(2)}) collective-permute-start(f32[512,512]{1,0:T(8,128)S(1)} %add_add_fusion), channel_id=1, source_target_pairs={{0,1},{1,0},{2,3},{3,2},{4,5},{5,4},{6,7},{7,6},{8,9},{9,8},{10,11... | collective-permute-start | bytes 3145736 | tf_op jit(solution)/shard_map/ppermute | solution.py:273
  490.9 18.0 %copy-start = (f32[1024,512]{1,0:T(8,128)S(1)}, f32[1024,512]{1,0:T(8,128)}, u32[]{:S(2)}) copy-start(f32[1024,512]{1,0:T(8,128)} %parent_ref.1) | copy-start | bytes 6291460
  491.9 24.5 %copy-start.1 = (f32[512,512]{1,0:T(8,128)}, f32[512,512]{1,0:T(8,128)S(1)}, u32[]{:S(2)}) copy-start(f32[512,512]{1,0:T(8,128)S(1)} %fusion.17.mine_ref) | copy-start | bytes 3145732
  507.5 1.4 copy-start.4

commit v8 on v7

--- a/solution.py
+++ b/solution.py
@@ -228,30 +228,6 @@
     )(parent, sides, inverse, mine, *terms)
 
 
-def line_gather(x, axis, ny, gates):
-    n = lax.axis_size(axis)
-    nz = n // ny
-
-    def beside(y, j, rows):
-        pairs = [(c, c // ny * ny + (c % ny - j) % ny) for c in range(n) if c // ny in rows]
-        return lax.ppermute(y, axis, pairs)
-
-    own = [beside(x, j, range(nz)) for j in range(1, ny)]
-    up, down = [x], [x]
-    for step in range(1, nz):
-        ends = (up[-1], down[-1])
-        if 1 < step < len(gates) + 2:
-            ends, _ = lax.optimization_barrier((ends, gates[step - 2](own)))
-        up.append(lax.ppermute(ends[0], axis, [(c, c + ny) for c in range(n) if step - 1 <= c // ny < nz - 1]))
-        down.append(lax.ppermute(ends[1], axis, [(c, c - ny) for c in range(n) if 0 < c // ny <= nz - step]))
-    got = [[x] + own]
-    for k in range(1, nz):
-        above, below = range(k, nz), range(k)
-        got.append([up[k] + down[nz - k]] + [
-            beside(up[k], j, above) + beside(down[nz - k], j, below) for j in range(1, ny)])
-    return got, (up[-1], down[-1])
-
-
 def share_line(x, ny):
     branches = lax.axis_size("branch")
     groups = lax.axis_size("col")
@@ -328,10 +304,7 @@
 
     corner = jnp.concatenate([pivot_column(b) for b in range(pivot_units)], axis=1)
     corner = corner + jnp.where(branch == 0, placed(parent_front[:PP]), 0.0)
-    corner_steps = []
-    corner = halve(corner, "branch", corner_steps)
-    corner = halve(corner, "col", corner_steps)
-    corner = join(corner, "col", corner_steps)
+    corner = join(halve(halve(corner, "branch"), "col"), "col")
 
     def rows_for(target):
         return jnp.concatenate([unit_rows(target * per + a) for a in range(per)], axis=0)
@@ -343,26 +316,12 @@
     far = sorted(range(1, groups), key=lambda shift: abs(2 * shift - groups))
     rows = [rows_for((col + shift) % groups) for shift in far]
 
-    in_branch, in_col = len(axis_bits("branch")), len(axis_bits("col"))
-    gathered, ends = line_gather(front[:P_SIZE], "col", ny, [
-        lambda own: (own, rows, corner_steps[in_branch - 1]), lambda own: corner_steps[in_branch + in_col - 1]])
-    nz = groups // ny
-    z, y = col // ny, col % ny
-    back = (z - source // ny) % nz
-    aside = (source % ny - y) % ny
-    slots = back * ny + aside
-
-    def top_of(c):
-        return sum(
-            jnp.where((z == (c // ny + k) % nz) & (y == (c % ny - j) % ny), gathered[k][j], 0.0)
-            for k in range(nz) for j in range(ny))
-
-    pivots = [top_of(c) for c in range(pivot_devices)]
-    pivots = jnp.concatenate(pivots, axis=1) if pivot_devices > 1 else pivots[0]
+    top = lax.all_gather(front[:P_SIZE], "col")
+    pivots = jnp.concatenate([top[c] for c in range(pivot_devices)], axis=1) if pivot_devices > 1 else top[0]
 
     received = {0: rows_for(col)}
     for shift, row in zip(far[:EARLY], rows):
-        row, _ = lax.optimization_barrier((row, (ends, corner)))
+        row, _ = lax.optimization_barrier((row, (pivots, corner)))
         received[shift] = moved(shift, row)
 
     inverse = inverse_factor(pivots)
@@ -375,10 +334,10 @@
     early = [received[shift] for shift in far[:EARLY]]
     inverse, early = lax.optimization_barrier((inverse, early))
     received.update(zip(far[:EARLY], early))
-    factor = jnp.stack([product(inverse, x, 1, 0) for line in gathered for x in line])
+    factor = jnp.stack([product(inverse, top[c], 1, 0) for c in range(groups)])
 
     def factor_columns(u):
-        block = lax.dynamic_slice(factor, (slots[u], 0, parts[u] * width), (1, P_SIZE, width))
+        block = lax.dynamic_slice(factor, (source[u], 0, parts[u] * width), (1, P_SIZE, width))
         return jnp.where(keeps[u] > 0, block[0], 0.0)
 
     mine = jnp.concatenate([factor_columns(col * per + a) for a in range(per)], axis=1)
@@ -386,7 +345,7 @@
     pieces = jnp.stack([jnp.where(mine_keep, received[shift], 0.0) for shift in range(groups)])
     left = three_part(mine)
     n = pivot_units
-    first = spread_update(slots[:n], places[:n], parts[:n], keeps[:n], left, factor, pieces, width)
+    first = spread_update(source[:n], places[:n], parts[:n], keeps[:n], left, factor, pieces, width)
     first = jnp.concatenate([first[u] for u in range(n)], axis=1)
     steps = []
     first = first + jnp.where(branch == 0, parent_front[:PP].T, 0.0)
@@ -401,7 +360,7 @@
     owned = units_total // branches
     spread = [None] * branches
     for i, m in enumerate(reversed(range(branches))):
-        table, _ = lax.optimization_barrier((slots, steps[min(i, len(steps) - 1)]))
+        table, _ = lax.optimization_barrier((source, steps[min(i, len(steps) - 1)]))
         at = lambda table: lax.dynamic_slice_in_dim(table, (branch ^ m) * owned, owned)
         spread[m] = spread_update(at(table), at(places), at(parts), at(keeps), left, factor, pieces, width)
     terms, sent = scatter_sum(spread, "branch")
@@ -409,7 +368,7 @@
     parent_inverse = inverse_factor(corner)
 
     parent_mine = product(parent_inverse, first, 1, 1)
-    if nz == branches:
+    if groups // ny == branches:
         line, parent_inverse = lax.optimization_barrier((share_line(first, ny), parent_inverse))
         sides = jnp.concatenate(share_beside(line, ny), axis=0)
     else:

time: 524 us -> 523 us (level)
  waiting for transfers between devices: 229 us -> 215 us
  between operations: 27.6 us -> 40.8 us
  Pallas kernels: 93 us -> 81.6 us
  starting transfers between devices: 72.5 us -> 83.6 us
    ppermute x13 -> x0, waiting for transfers between devices: 52.4 us -> none  [the longest x7 52.3 us: beside(): return lax.ppermute(y, axis, pairs)]
    ppermute x13 -> x0, starting transfers between devices: 27.5 us -> none  [the longest x7 15.8 us: beside(): return lax.ppermute(y, axis, pairs)]
    ppermute x3, starting transfers between devices: 17.4 us -> 43.6 us  [share_line(): got = got + lax.ppermute(x, ('branch', 'col'), pairs)]
    ppermute x7, waiting for transfers between devices: 74 us -> 91.4 us  [moved(): return lax.ppermute(rows, 'col', pairs)]
    ppermute x1, starting transfers between devices: 0.07 us -> 15.5 us  [share_beside(): shares.append(lax.ppermute(got, 'col', pairs))]
    all_gather x0 -> x1, waiting for transfers between devices: none -> 15.3 us  [on_device(): top = lax.all_gather(front[:P_SIZE], 'col')]
    pallas_call x2, Pallas kernels: 54.5 us -> 43.1 us  [inverse_factor(): pl.pallas_call(inverse_factor_kernel, out_shape=jax.ShapeDtypeStruct((n,...]
    add x1 -> x0, other arithmetic: 7.08 us -> none  [top_of(): sum((jnp.where((z == (c // ny + k) % nz) & (y == (c % ny - j) % ny), gath...]
  transfers between devices with their start and end apart: 43 -> 31, of which waited for: 17 -> 16; matrix products, arithmetic and copies ran while one was open for 15% -> 16% of each run, Pallas kernels for 16% -> 13%
where the time goes in v8:
time: 523 us; the launch traced here: 516 us
  waiting for transfers between devices  215 us (41%)
  starting transfers between devices  83.6 us (16%)
  Pallas kernels  81.6 us (16%)
  other arithmetic  50.5 us (10%)
  between operations  40.8 us (8%)
  local copies, waits for them, and re-layouts  30.8 us (6%)
  matrix products  14.5 us (3%)
    ppermute x19, waiting for transfers between devices, flip(): return lax.ppermute(x, axis, [(i, i ^ bit) for i in range(n)])  95.5 us
    ppermute x7, waiting for transfers between devices, moved(): return lax.ppermute(rows, 'col', pairs)  91.4 us
    ppermute x3, starting transfers between devices, share_line(): got = got + lax.ppermute(x, ('branch', 'col'), pairs)  43.6 us
    pallas_call x2, Pallas kernels, inverse_factor(): pl.pallas_call(inverse_factor_kernel, out_shape=jax.ShapeDtypeStruct((n,...  43.1 us
    pallas_call x5, Pallas kernels, spread_update(): pl.pallas_call(spread_kernel, grid_spec=pltpu.PrefetchScalarGridSpec(num_...  31 us
    ppermute x1, starting transfers between devices, share_beside(): shares.append(lax.ppermute(got, 'col', pairs))  15.5 us
    unnamed x7, other arithmetic  15.3 us
    all_gather x1, waiting for transfers between devices, on_device(): top = lax.all_gather(front[:P_SIZE], 'col')  15.3 us
  transfers between devices with their start and end apart: 31, of which 16 were waited for; matrix products, arithmetic and copies ran while one was open for 16% of the time, Pallas kernels for 13%

profile of v8, /device:TPU:0, one launch (start us, length us, event | category | flops | bytes accessed | tf_op | source)
XLA Modules:
  0.0 516.3 jit_solution(15336622708596816444)
XLA Ops:
  7.2 2.3 slice.88
  18.6 1.6 constant_dynamic-slice_fusion.14
  22.2 1.5 collective-permute-done
  23.9 2.8 collective-permute-start.1
  26.7 6.6 %collective-permute-done.1 = f32[128,512]{0,1:T(8,128)S(1)} collective-permute-done((f32[128,512]{0,1:T(8,128)S(1)}, f32[128,512]{0,1:T(8,128)S(1)}, u32[]{:S(2)}, u32[]{:S(2)}) %collective-permute-start.1) | collective-permute-done | bytes 262176 | tf_op jit(solution)/shard_map/ppermute | solution.py:143
  33.5 1.8 collective-permute-start.2
  35.3 6.2 %collective-permute-done.2 = f32[64,512]{0,1:T(8,128)S(1)} collective-permute-done((f32[64,512]{0,1:T(8,128)S(1)}, f32[64,512]{0,1:T(8,128)S(1)}, u32[]{:S(2)}, u32[]{:S(2)}) %collective-permute-start.2) | collective-permute-done | bytes 131104 | tf_op jit(solution)/shard_map/ppermute | solution.py:143
  41.8 1.6 collective-permute-start.3
  53.4 10.4 %collective-permute-done.3 = f32[32,512]{0,1:T(8,128)S(1)} collective-permute-done((f32[32,512]{0,1:T(8,128)S(1)}, f32[32,512]{0,1:T(8,128)S(1)}, u32[]{:S(2)}, u32[]{:S(2)}) %collective-permute-start.3) | collective-permute-done | bytes 65568 | tf_op jit(solution)/shard_map/ppermute | solution.py:143
  64.4 6.3 %constant_dynamic-slice_fusion.3 = (f32[1,256,512]{2,1,0:T(8,128)S(1)}, f32[256,512]{1,0:T(8,128)S(1)}, f32[256,512]{1,0:T(8,128)}, f32[256,512]{1,0:T(8,128)}, ...) fusion(f32[1,4096,512]{2,1,0:T(8,128)} %param.3, ...), kind=kLoop, calls=%fused_computation.113 | loop fusion | bytes 16777280 | tf_op jit(solution)/shard_map/dynamic_slice | solution.py:284
  70.7 20.3 %collective-permute-done.4 = f32[16,512]{0,1:T(8,128)} collective-permute-done((f32[16,512]{0,1:T(8,128)S(1)}, f32[16,512]{0,1:T(8,128)}, u32[]{:S(2)}, u32[]{:S(2)}) %collective-permute-start.4) | collective-permute-done | bytes 32800 | tf_op jit(solution)/shard_map/ppermute | solution.py:143
  92.3 3.2 pad_maximum_fusion.2
  95.5 29.1 %collective-permute-done.5 = f32[16,512]{0,1:T(8,128)} collective-permute-done((f32[16,512]{0,1:T(8,128)S(1)}, f32[16,512]{0,1:T(8,128)}, u32[]{:S(2)}, u32[]{:S(2)}) %collective-permute-start.5) | collective-permute-done | bytes 32800 | tf_op jit(solution)/shard_map/ppermute | solution.py:143
  124.5 1.8 broadcast_select_fusion.5
  127.5 3.0 pad_maximum_fusion.4
  130.5 6.4 %collective-permute-done.6 = f32[32,512]{1,0:T(8,128)S(1)} collective-permute-done((f32[32,512]{1,0:T(8,128)S(1)}, f32[32,512]{1,0:T(8,128)S(1)}, u32[]{:S(2)}, u32[]{:S(2)}) %collective-permute-start.6) | collective-permute-done | bytes 65568 | tf_op jit(solution)/shard_map/ppermute | solution.py:143
  136.9 1.7 collective-permute-start.7
  138.6 2.7 pad_maximum_fusion.6
  142.0 15.3 %all-gather.2.cloned.1.call-done = f32[8,512,512]{2,1,0:T(8,128)} async-done(((f32[1,512,512]{2,1,0:T(8,128)}), f32[8,512,512]{2,1,0:T(8,128)}) %all-gather.2.cloned.1.call-update) | async-done | bytes 8388624 | tf_op jit(solution)/shard_map/all_gather | solution.py:319
  157.3 1.3 slice_bitcast_fusion.14.a_ref
  158.6 1.3 collective-permute-start.8
  159.9 1.3 collective-permute-start.9
  161.2 1.3 collective-permute-start.10
  162.5 1.3 collective-permute-start.11
  163.8 1.5 collective-permute-start.12
  179.8 21.7 %shard_map.58 = f32[512,512]{1,0:T(8,128)S(1)} custom-call(f32[512,512]{1,0:T(8,128)S(1)} %slice_bitcast_fusion.14.a_ref), custom_call_target="tpu_custom_call" | custom-call | flops 134217728 | bytes 2097152 | tf_op jit(solution)/shard_map/pallas_call | solution.py:86
  201.4 75.2 %collective-permute-done.8 = f32[512,512]{1,0:T(8,128)} collective-permute-done((f32[512,512]{1,0:T(8,128)}, f32[512,512]{1,0:T(8,128)}, u32[]{:S(2)}, u32[]{:S(2)}) %collective-permute-start.8) | collective-permute-done | bytes 1048608 | tf_op jit(solution)/shard_map/ppermute | solution.py:314
  276.7 1.3 collective-permute-start.13
  278.0 1.3 collective-permute-start.16
  279.3 2.2 fusion.7
  288.7 3.3 copy-done.2
  292.3 14.2 %collective-permute-done.13 = f32[512,512]{1,0:T(8,128)S(1)} collective-permute-done((f32[512,512]{1,0:T(8,128)}, f32[512,512]{1,0:T(8,128)S(1)}, u32[]{:S(2)}, u32[]{:S(2)}) %collective-permute-start.13) | collective-permute-done | bytes 1048608 | tf_op jit(solution)/shard_map/ppermute | solution.py:314
  307.5 1.3 pad_maximum_fusion.1
  308.8 2.6 copy.90.left_ref
  311.4 2.4 bitcast_dynamic-update-slice_fusion.6
  313.8 2.4 bitcast_dynamic-update-slice_fusion.5
  316.1 2.4 bitcast_dynamic-update-slice_fusion.4
  318.5 2.4 bitcast_dynamic-update-slice_fusion.3
  320.9 2.4 bitcast_dynamic-update-slice_fusion.2
  323.3 2.3 bitcast_dynamic-update-slice_fusion.1
  325.6 1.9 collective-permute-done.16
  328.6 4.6 shard_map.59
  333.2 1.3 slice_bitcast_fusion.16
  340.8 5.7 %collective-permute-done.20 = f32[128,512]{1,0:T(8,128)} collective-permute-done((f32[128,512]{1,0:T(8,128)}, f32[128,512]{1,0:T(8,128)}, u32[]{:S(2)}, u32[]{:S(2)}) %collective-permute-start.20) | collective-permute-done | bytes 262176 | tf_op jit(solution)/shard_map/ppermute | solution.py:143
  350.3 6.5 %shard_map.61 = f32[4,512,256]{2,1,0:T(8,128)} custom-call(s32[4]{0:T(128)} %dynamic_slice.356.slot_ref, s32[4]{0:T(128)} %get-tuple-element.148.place_ref, s32[4]{0:T(128)} %get-tuple-element.100.part_ref, s32[4]{0:T(128)} %get-tuple-element.96.keep_ref, bf16[512,1536]{1,0:T(8,128)(2,1)} %copy.90.left_ref, f32[8,512,512]{2,1,0:T(8,128)} %copy-done.2, ...), custom_call_target="tpu_custom_call" | custom-call | flops 1610612736 | bytes 6291456 | tf_op jit(solution)/shard_map/pallas_call | solution.py:117
  357.5 3.1 collective-permute-done.15
  361.8 5.4 %collective-permute-done.17 = f32[128,512]{1,0:T(8,128)S(1)} collective-permute-done((f32[128,512]{1,0:T(8,128)S(1)}, f32[128,512]{1,0:T(8,128)S(1)}, u32[]{:S(2)}, u32[]{:S(2)}) %collective-permute-start.17) | collective-permute-done | bytes 262176 | tf_op jit(solution)/shard_map/ppermute | solution.py:143
  367.2 1.1 broadcast_select_fusion.1
  369.4 21.5 %collective-permute-start.26 = (f32[512,512]{1,0:T(8,128)}, f32[512,512]{1,0:T(8,128)}, u32[]{:S(2)}, u32[]{:S(2)}) collective-permute-start(f32[512,512]{1,0:T(8,128)} %pad_maximum_fusion.11), channel_id=1, source_target_pairs={{0,6},{1,7},{10,8},{11,9},{20,18},{21,19},{30,28},{31,29}} | collective-permute-start | bytes 3145736 | tf_op jit(solution)/shard_map/ppermute | solution.py:239
  390.9 19.9 %collective-permute-start.25 = (f32[512,512]{1,0:T(8,128)}, f32[512,512]{1,0:T(8,128)}, u32[]{:S(2)}, u32[]{:S(2)}) collective-permute-start(f32[512,512]{1,0:T(8,128)} %pad_maximum_fusion.11), channel_id=1, source_target_pairs={{0,4},{1,5},{10,14},{11,15},{20,16},{21,17},{30,26},{31,27}} | collective-permute-start | bytes 3145736 | tf_op jit(solution)/shard_map/ppermute | solution.py:239
  410.8 2.2 collective-permute-start.24
  414.5 6.5 %shard_map.60 = f32[4,512,256]{2,1,0:T(8,128)} custom-call(s32[4]{0:T(128)} %dynamic_slice.352.slot_ref, s32[4]{0:T(128)} %get-tuple-element.147.place_ref, s32[4]{0:T(128)} %get-tuple-element.101.part_ref, s32[4]{0:T(128)} %get-tuple-element.97.keep_ref, bf16[512,1536]{1,0:T(8,128)(2,1)} %copy.90.left_ref, f32[8,512,512]{2,1,0:T(8,128)} %copy-done.2, ...), custom_call_target="tpu_custom_call" | custom-call | flops 1610612736 | bytes 6291456 | tf_op jit(solution)/shard_map/pallas_call | solution.py:117
  421.7 6.8 %shard_map.64 = f32[4,512,256]{2,1,0:T(8,128)} custom-call(s32[4]{0:T(128)} %dynamic_slice.364.slot_ref, s32[4]{0:T(128)} %get-tuple-element.150.place_ref, s32[4]{0:T(128)} %get-tuple-element.98.part_ref, s32[4]{0:T(128)} %get-tuple-element.94.keep_ref, bf16[512,1536]{1,0:T(8,128)(2,1)} %copy.90.left_ref, f32[8,512,512]{2,1,0:T(8,128)} %copy-done.2, ...), custom_call_target="tpu_custom_call" | custom-call | flops 1610612736 | bytes 6291456 | tf_op jit(solution)/shard_map/pallas_call | solution.py:117
  429.1 3.2 add.501
  433.1 1.1 broadcast_select_fusion.3
  434.3 21.5 %shard_map.62.inverse_ref = f32[512,512]{1,0:T(8,128)S(1)} custom-call(f32[512,512]{1,0:T(8,128)S(1)} %pad_maximum_fusion.10.a_ref), custom_call_target="tpu_custom_call" | custom-call | flops 134217728 | bytes 2097152 | tf_op jit(solution)/shard_map/pallas_call | solution.py:86
  455.8 3.4 add_add_fusion
  459.2 15.5 %collective-permute-start.27 = (f32[512,512]{1,0:T(8,128)}, f32[512,512]{1,0:T(8,128)}, u32[]{:S(2)}, u32[]{:S(2)}) collective-permute-start(f32[512,512]{1,0:T(8,128)} %add_add_fusion), channel_id=1, source_target_pairs={{0,1},{1,0},{2,3},{3,2},{4,5},{5,4},{6,7},{7,6},{8,9},{9,8},{10,11... | collective-permute-start | bytes 3145736 | tf_op jit(solution)/shard_map/ppermute | solution.py:249
  474.6 3.2 convolution_bitcast_fusion.8
  478.4 6.5 %shard_map.63.rest_0_ = f32[4,512,256]{2,1,0:T(8,128)} custom-call(s32[4]{0:T(128)} %dynamic_slice.360.slot_ref, s32[4]{0:T(128)} %get-tuple-element.149.place_ref, s32[4]{0:T(128)} %get-tuple-element.99.part_ref, s32[4]{0:T(128)} %get-tuple-element.95.keep_ref, bf16[512,1536]{1,0:T(8,128)(2,1)} %copy.90.left_ref, f32[8,512,512]{2,1,0:T(8,128)} %copy-done.2, ...), custom_call_target="tpu_custom_call" | custom-call | flops 1610612736 | bytes 6291456 | tf_op jit(solution)/shard_map/pallas_call | solution.py:117
  486.0 12.3 %collective-permute-done.27 = f32[512,512]{1,0:T(8,128)} collective-permute-done((f32[512,512]{1,0:T(8,128)}, f32[512,512]{1,0:T(8,128)}, u32[]{:S(2)}, u32[]{:S(2)}) %collective-permute-start.27) | collective-permute-done | bytes 1048608 | tf_op jit(solution)/shard_map/ppermute | solution.py:249
  498.3 1.8 select_add_fusion.1
  500.1 1.5 pad_maximum_fusion
  501.6 7.5 %shard_map.65 = f32[1024,512]{1,0:T(8,128)} custom-call(f32[1024,512]{1,0:T(8,128)S(1)} %copy-done, f32[4,256,512]{2,1,0:T(8,128)} %bitcast.179, f32[512,512]{1,0:T(8,128)S(1)} %shard_map.62.inverse_ref, f32[512,512]{1,0:T(8,128)S(1)} %fusion.14.mine_ref, f32[4,512,256]{2,1,0:T(8,128)} %shard_map.63.rest_0_, f32[4,512,256]{2,1,0:T(8,128)} %collective-permute-done.28.rest_1_, ...), custom_call_target="tpu_custom_call" | custom-call | flops 3221225472 | bytes 16777216 | tf_op jit(solution)/shard_map/pallas_call | solution.py:214
  (151 shorter events, 41.6 us)
Async XLA Ops:
  7.2 13.6 %slice-start = ((f32[1024,512]{1,0:T(8,128)}), f32[512,512]{1,0:T(8,128)S(1)}, s32[]{:S(2)}) async-start(f32[1024,512]{1,0:T(8,128)} %parent_ref.1), calls=%async_computation.1 | async-start | bytes 2097152 | tf_op jit(solution)/shard_map/slice | solution.py:306
  7.2 150.1 %all-gather.2.cloned.1.call-start = ((), (), s32[]{:S(2)}) async-start(), calls=%async_computation | async-start | bytes 9437184 | tf_op jit(solution)/shard_map/all_gather | solution.py:319
  11.8 12.0 %copy-start.18 = (s32[16]{0:T(128)}, s32[16]{0:T(128)S(1)}, u32[]{:S(2)}) copy-start(s32[16]{0:T(128)S(1)} %get-tuple-element.46) | copy-start | bytes 196
  16.5 158.3 %copy-start.13 = (s32[16]{0:T(128)}, s32[16]{0:T(128)S(1)}, u32[]{:S(2)}) copy-start(s32[16]{0:T(128)S(1)} %gather_fusion.1) | copy-start | bytes 196
  21.1 49.6 %copy-start.4 = (f32[512,512]{0,1:T(8,128)}, f32[512,512]{0,1:T(8,128)S(1)}, u32[]{:S(2)}) copy-start(f32[512,512]{0,1:T(8,128)S(1)} %copy.108) | copy-start | bytes 3145732
  21.5 2.3 collective-permute-start
  23.9 9.4 %collective-permute-start.1 = (f32[128,512]{0,1:T(8,128)S(1)}, f32[128,512]{0,1:T(8,128)S(1)}, u32[]{:S(2)}, u32[]{:S(2)}) collective-permute-start(f32[128,512]{0,1:T(8,128)S(1)} %constant_dynamic-slice_fusion.9), channel_id=1, source_target_pairs={{0,16},{8,24},{16,0},{24,8},{1,17},{9,25},{17,1},{25,9},{2,18},{10... | collective-permute-start | bytes 786440 | tf_op jit(solution)/shard_map/ppermute | solution.py:143
  33.5 8.0 %collective-permute-start.2 = (f32[64,512]{0,1:T(8,128)S(1)}, f32[64,512]{0,1:T(8,128)S(1)}, u32[]{:S(2)}, u32[]{:S(2)}) collective-permute-start(f32[64,512]{0,1:T(8,128)S(1)} %constant_dynamic-slice_fusion.8), channel_id=1, source_target_pairs={{0,1},{1,0},{2,3},{3,2},{4,5},{5,4},{6,7},{7,6},{8,9},{9,8},{10,11... | collective-permute-start | bytes 393224 | tf_op jit(solution)/shard_map/ppermute | solution.py:143
  41.8 22.0 %collective-permute-start.3 = (f32[32,512]{0,1:T(8,128)S(1)}, f32[32,512]{0,1:T(8,128)S(1)}, u32[]{:S(2)}, u32[]{:S(2)}) collective-permute-start(f32[32,512]{0,1:T(8,128)S(1)} %constant_dynamic-slice_fusion.7), channel_id=1, source_target_pairs={{0,2},{1,3},{2,0},{3,1},{4,6},{5,7},{6,4},{7,5},{8,10},{9,11},{10,... | collective-permute-start | bytes 196616 | tf_op jit(solution)/shard_map/ppermute | solution.py:143
  64.1 27.0 %collective-permute-start.4 = (f32[16,512]{0,1:T(8,128)S(1)}, f32[16,512]{0,1:T(8,128)}, u32[]{:S(2)}, u32[]{:S(2)}) collective-permute-start(f32[16,512]{0,1:T(8,128)S(1)} %constant_dynamic-slice_fusion.6), channel_id=1, source_target_pairs={{0,4},{1,5},{2,6},{3,7},{4,0},{5,1},{6,2},{7,3},{8,12},{9,13},{10,... | collective-permute-start | bytes 98312 | tf_op jit(solution)/shard_map/ppermute | solution.py:143
  92.2 3.3 copy-start.11
  92.2 46.4 %copy-start.9 = (f32[256,512]{1,0:T(8,128)S(1)}, f32[256,512]{1,0:T(8,128)}, u32[]{:S(2)}) copy-start(f32[256,512]{1,0:T(8,128)} %get-tuple-element.52) | copy-start | bytes 1572868
  92.2 32.4 %collective-permute-start.5 = (f32[16,512]{0,1:T(8,128)S(1)}, f32[16,512]{0,1:T(8,128)}, u32[]{:S(2)}, u32[]{:S(2)}) collective-permute-start(f32[16,512]{0,1:T(8,128)S(1)} %dynamic-slice_add_fusion.4), channel_id=1, source_target_pairs={{0,4},{1,5},{2,6},{3,7},{4,0},{5,1},{6,2},{7,3},{8,12},{9,13},{10,... | collective-permute-start | bytes 98312 | tf_op jit(solution)/shard_map/ppermute | solution.py:143
  92.3 85.3 %copy-start.7 = (f32[256,512]{1,0:T(8,128)S(1)}, f32[256,512]{1,0:T(8,128)}, u32[]{:S(2)}) copy-start(f32[256,512]{1,0:T(8,128)} %get-tuple-element.63) | copy-start | bytes 1572868
  92.3 85.3 %copy-start.8 = (f32[256,512]{1,0:T(8,128)S(1)}, f32[256,512]{1,0:T(8,128)}, u32[]{:S(2)}) copy-start(f32[256,512]{1,0:T(8,128)} %get-tuple-element.64) | copy-start | bytes 1572868
  127.5 9.4 %collective-permute-start.6 = (f32[32,512]{1,0:T(8,128)S(1)}, f32[32,512]{1,0:T(8,128)S(1)}, u32[]{:S(2)}, u32[]{:S(2)}) collective-permute-start(f32[32,512]{1,0:T(8,128)S(1)} %pad_maximum_fusion.16), channel_id=1, source_target_pairs={{0,2},{1,3},{2,0},{3,1},{4,6},{5,7},{6,4},{7,5},{8,10},{9,11},{10,... | collective-permute-start | bytes 196616 | tf_op jit(solution)/shard_map/ppermute | solution.py:143
  136.9 5.0 collective-permute-start.7
  158.6 118.1 %collective-permute-start.8 = (f32[512,512]{1,0:T(8,128)}, f32[512,512]{1,0:T(8,128)}, u32[]{:S(2)}, u32[]{:S(2)}) collective-permute-start(f32[512,512]{1,0:T(8,128)} %get-tuple-element.25), channel_id=1, source_target_pairs={{1,5},{2,6},{3,7},{4,0},{5,1},{6,2},{7,3},{9,13},{10,14},{11,15},{... | collective-permute-start | bytes 3145736 | tf_op jit(solution)/shard_map/ppermute | solution.py:314
  159.9 118.1 %collective-permute-start.9 = (f32[512,512]{1,0:T(8,128)}, f32[512,512]{1,0:T(8,128)}, u32[]{:S(2)}, u32[]{:S(2)}) collective-permute-start(f32[512,512]{1,0:T(8,128)} %get-tuple-element.26), channel_id=1, source_target_pairs={{1,4},{2,5},{3,6},{4,7},{5,0},{6,1},{7,2},{9,12},{10,13},{11,14},{... | collective-permute-start | bytes 3145736 | tf_op jit(solution)/shard_map/ppermute | solution.py:314
  161.2 118.1 %collective-permute-start.10 = (f32[512,512]{1,0:T(8,128)}, f32[512,512]{1,0:T(8,128)}, u32[]{:S(2)}, u32[]{:S(2)}) collective-permute-start(f32[512,512]{1,0:T(8,128)} %get-tuple-element.27), channel_id=1, source_target_pairs={{1,6},{2,7},{3,0},{4,1},{5,2},{6,3},{7,4},{9,14},{10,15},{11,8},{1... | collective-permute-start | bytes 3145736 | tf_op jit(solution)/shard_map/ppermute | solution.py:314
  162.5 116.8 %collective-permute-start.11 = (f32[512,512]{1,0:T(8,128)}, f32[512,512]{1,0:T(8,128)}, u32[]{:S(2)}, u32[]{:S(2)}) collective-permute-start(f32[512,512]{1,0:T(8,128)} %get-tuple-element.28), channel_id=1, source_target_pairs={{1,3},{2,4},{3,5},{4,6},{5,7},{6,0},{7,1},{9,11},{10,12},{11,13},{... | collective-permute-start | bytes 3145736 | tf_op jit(solution)/shard_map/ppermute | solution.py:314
  163.8 115.5 %collective-permute-start.12 = (f32[512,512]{1,0:T(8,128)}, f32[512,512]{1,0:T(8,128)}, u32[]{:S(2)}, u32[]{:S(2)}) collective-permute-start(f32[512,512]{1,0:T(8,128)} %get-tuple-element.29), channel_id=1, source_target_pairs={{1,7},{2,0},{3,1},{4,2},{5,3},{6,4},{7,5},{9,15},{10,8},{11,9},{12... | collective-permute-start | bytes 3145736 | tf_op jit(solution)/shard_map/ppermute | solution.py:314
  166.5 118.1 %copy-start.15 = (s32[16]{0:T(128)}, s32[16]{0:T(128)S(1)}, u32[]{:S(2)}) copy-start(s32[16]{0:T(128)S(1)} %and_select_fusion.1) | copy-start | bytes 196
  177.6 104.0 %copy-start.3 = (f32[8,512,512]{2,1,0:T(8,128)S(1)}, f32[8,512,512]{2,1,0:T(8,128)}, u32[]{:S(2)}) copy-start(f32[8,512,512]{2,1,0:T(8,128)} %all-gather.2.cloned.1.call-done) | copy-start | bytes 25165828
  276.7 29.9 %collective-permute-start.13 = (f32[512,512]{1,0:T(8,128)}, f32[512,512]{1,0:T(8,128)S(1)}, u32[]{:S(2)}, u32[]{:S(2)}) collective-permute-start(f32[512,512]{1,0:T(8,128)} %get-tuple-element.31), channel_id=1, source_target_pairs={{1,2},{2,3},{3,4},{4,5},{5,6},{6,7},{7,0},{9,10},{10,11},{11,12},{... | collective-permute-start | bytes 3145736 | tf_op jit(solution)/shard_map/ppermute | solution.py:314
  278.0 49.5 %collective-permute-start.16 = (f32[512,512]{1,0:T(8,128)}, f32[512,512]{1,0:T(8,128)S(1)}, u32[]{:S(2)}, u32[]{:S(2)}) collective-permute-start(f32[512,512]{1,0:T(8,128)} %pad_maximum_fusion.9), channel_id=1, source_target_pairs={{1,0},{2,1},{3,2},{4,3},{5,4},{6,5},{7,6},{9,8},{10,9},{11,10},{12... | collective-permute-start | bytes 3145736 | tf_op jit(solution)/shard_map/ppermute | solution.py:314
  288.7 3.3 copy-start.2
  306.6 1.0 copy-start.10
  328.6 5.9 %copy-start.5 = (f32[512,512]{0,1:T(8,128)S(1)}, f32[512,512]{0,1:T(8,128)}, u32[]{:S(2)}) copy-start(f32[512,512]{0,1:T(8,128)} %copy-done.4) | copy-start | bytes 3145732
  333.2 3.3 copy-start.14
  333.2 3.3 copy-start.17
  333.2 5.8 %copy-start.16 = (s32[16]{0:T(128)S(1)}, s32[16]{0:T(128)}, u32[]{:S(2)}) copy-start(s32[16]{0:T(128)} %copy-done.15) | copy-start | bytes 196
  333.2 16.4 %copy-start.19 = (s32[16]{0:T(128)S(1)}, s32[16]{0:T(128)}, u32[]{:S(2)}) copy-start(s32[16]{0:T(128)} %copy-done.18) | copy-start | bytes 196
  334.7 2.4 collective-permute-start.19
  335.9 3.7 collective-permute-start.14
  337.9 8.6 %collective-permute-start.20 = (f32[128,512]{1,0:T(8,128)}, f32[128,512]{1,0:T(8,128)}, u32[]{:S(2)}, u32[]{:S(2)}) collective-permute-start(f32[128,512]{1,0:T(8,128)} %constant_dynamic-slice_fusion), channel_id=1, source_target_pairs={{0,16},{8,24},{16,0},{24,8},{1,17},{9,25},{17,1},{25,9},{2,18},{10... | collective-permute-start | bytes 786440 | tf_op jit(solution)/shard_map/ppermute | solution.py:143
  347.5 9.3 %collective-permute-start.22 = (f32[128,512]{1,0:T(8,128)S(1)}, f32[128,512]{1,0:T(8,128)S(1)}, u32[]{:S(2)}, u32[]{:S(2)}) collective-permute-start(f32[128,512]{1,0:T(8,128)S(1)} %dynamic-slice_add_fusion.3), channel_id=1, source_target_pairs={{0,16},{8,24},{16,0},{24,8},{1,17},{9,25},{17,1},{25,9},{2,18},{10... | collective-permute-start | bytes 786440 | tf_op jit(solution)/shard_map/ppermute | solution.py:143
  348.6 11.9 %collective-permute-start.15 = (f32[128,512]{1,0:T(8,128)S(1)}, f32[128,512]{1,0:T(8,128)S(1)}, u32[]{:S(2)}, u32[]{:S(2)}) collective-permute-start(f32[128,512]{1,0:T(8,128)S(1)} %constant_dynamic-slice_fusion.4), channel_id=1, source_target_pairs={{0,16},{8,24},{16,0},{24,8},{1,17},{9,25},{17,1},{25,9},{2,18},{10... | collective-permute-start | bytes 786440 | tf_op jit(solution)/shard_map/ppermute | solution.py:143
  356.8 71.7 %collective-permute-start.21 = (f32[4,512,256]{2,1,0:T(8,128)}, f32[4,512,256]{2,1,0:T(8,128)}, u32[]{:S(2)}, u32[]{:S(2)}) collective-permute-start(f32[4,512,256]{2,1,0:T(8,128)} %shard_map.61), channel_id=1, source_target_pairs={{0,8},{8,0},{16,24},{24,16},{1,9},{9,1},{17,25},{25,17},{2,10},{10... | collective-permute-start | bytes 6291464 | tf_op jit(solution)/shard_map/ppermute | solution.py:143
  356.9 10.3 %collective-permute-start.23 = (f32[256,512]{1,0:T(8,128)S(1)}, f32[256,512]{1,0:T(8,128)}, u32[]{:S(2)}, u32[]{:S(2)}) collective-permute-start(f32[256,512]{1,0:T(8,128)S(1)} %pad_maximum_fusion.13), channel_id=1, source_target_pairs={{0,8},{8,0},{16,24},{24,16},{1,9},{9,1},{17,25},{25,17},{2,10},{10... | collective-permute-start | bytes 1572872 | tf_op jit(solution)/shard_map/ppermute | solution.py:143
  360.6 6.5 %collective-permute-start.17 = (f32[128,512]{1,0:T(8,128)S(1)}, f32[128,512]{1,0:T(8,128)S(1)}, u32[]{:S(2)}, u32[]{:S(2)}) collective-permute-start(f32[128,512]{1,0:T(8,128)S(1)} %add_subtract_fusion), channel_id=1, source_target_pairs={{0,16},{8,24},{16,0},{24,8},{1,17},{9,25},{17,1},{25,9},{2,18},{10... | collective-permute-start | bytes 786440 | tf_op jit(solution)/shard_map/ppermute | solution.py:143
  369.4 86.3 %collective-permute-start.26 = (f32[512,512]{1,0:T(8,128)}, f32[512,512]{1,0:T(8,128)}, u32[]{:S(2)}, u32[]{:S(2)}) collective-permute-start(f32[512,512]{1,0:T(8,128)} %pad_maximum_fusion.11), channel_id=1, source_target_pairs={{0,6},{1,7},{10,8},{11,9},{20,18},{21,19},{30,28},{31,29}} | collective-permute-start | bytes 3145736 | tf_op jit(solution)/shard_map/ppermute | solution.py:239
  390.9 64.8 %collective-permute-start.25 = (f32[512,512]{1,0:T(8,128)}, f32[512,512]{1,0:T(8,128)}, u32[]{:S(2)}, u32[]{:S(2)}) collective-permute-start(f32[512,512]{1,0:T(8,128)} %pad_maximum_fusion.11), channel_id=1, source_target_pairs={{0,4},{1,5},{10,14},{11,15},{20,16},{21,17},{30,26},{31,27}} | collective-permute-start | bytes 3145736 | tf_op jit(solution)/shard_map/ppermute | solution.py:239
  410.8 45.0 %collective-permute-start.24 = (f32[512,512]{1,0:T(8,128)}, f32[512,512]{1,0:T(8,128)}, u32[]{:S(2)}, u32[]{:S(2)}) collective-permute-start(f32[512,512]{1,0:T(8,128)} %pad_maximum_fusion.11), channel_id=1, source_target_pairs={{0,2},{1,3},{10,12},{11,13},{20,22},{21,23},{30,24},{31,25}} | collective-permute-start | bytes 3145736 | tf_op jit(solution)/shard_map/ppermute | solution.py:239
  413.9 18.4 %collective-permute-start.18 = (f32[256,512]{1,0:T(8,128)}, f32[256,512]{1,0:T(8,128)S(1)}, u32[]{:S(2)}, u32[]{:S(2)}) collective-permute-start(f32[256,512]{1,0:T(8,128)} %pad_maximum_fusion.12), channel_id=1, source_target_pairs={{0,8},{8,0},{16,24},{24,16},{1,9},{9,1},{17,25},{25,17},{2,10},{10... | collective-permute-start | bytes 1572872 | tf_op jit(solution)/shard_map/ppermute | solution.py:143
  421.7 7.4 %copy-start.6 = (f32[4,512,256]{2,1,0:T(8,128)S(1)}, f32[4,512,256]{2,1,0:T(8,128)}, u32[]{:S(2)}) copy-start(f32[4,512,256]{2,1,0:T(8,128)} %shard_map.60) | copy-start | bytes 6291460
  428.5 73.2 %collective-permute-start.28 = (f32[4,512,256]{2,1,0:T(8,128)}, f32[4,512,256]{2,1,0:T(8,128)}, u32[]{:S(2)}, u32[]{:S(2)}) collective-permute-start(f32[4,512,256]{2,1,0:T(8,128)} %shard_map.64), channel_id=1, source_target_pairs={{0,8},{8,0},{16,24},{24,16},{1,9},{9,1},{17,25},{25,17},{2,10},{10... | collective-permute-start | bytes 6291464 | tf_op jit(solution)/shard_map/ppermute | solution.py:143
  432.3 0.8 copy-start.12
  433.1 68.6 %collective-permute-start.29 = (f32[4,512,256]{2,1,0:T(8,128)}, f32[4,512,256]{2,1,0:T(8,128)}, u32[]{:S(2)}, u32[]{:S(2)}) collective-permute-start(f32[4,512,256]{2,1,0:T(8,128)} %add.501), channel_id=1, source_target_pairs={{0,16},{8,24},{16,0},{24,8},{1,17},{9,25},{17,1},{25,9},{2,18},{10... | collective-permute-start | bytes 6291464 | tf_op jit(solution)/shard_map/ppermute | solution.py:143
  459.2 39.1 %collective-permute-start.27 = (f32[512,512]{1,0:T(8,128)}, f32[512,512]{1,0:T(8,128)}, u32[]{:S(2)}, u32[]{:S(2)}) collective-permute-start(f32[512,512]{1,0:T(8,128)} %add_add_fusion), channel_id=1, source_target_pairs={{0,1},{1,0},{2,3},{3,2},{4,5},{5,4},{6,7},{7,6},{8,9},{9,8},{10,11... | collective-permute-start | bytes 3145736 | tf_op jit(solution)/shard_map/ppermute | solution.py:249
  484.9 16.7 %copy-start = (f32[1024,512]{1,0:T(8,128)S(1)}, f32[1024,512]{1,0:T(8,128)}, u32[]{:S(2)}) copy-start(f32[1024,512]{1,0:T(8,128)} %parent_ref.1) | copy-start | bytes 6291460
  486.0 23.2 %copy-start.1 = (f32[512,512]{1,0:T(8,128)}, f32[512,512]{1,0:T(8,128)S(1)}, u32[]{:S(2)}) copy-start(f32[512,512]{1,0:T(8,128)S(1)} %fusion.14.mine_ref) | copy-start | bytes 3145732
Sparse Core Ops, SparseCore 0:
  10.7 146.5 all-gather.1

commit v9 on v8

--- a/solution.py
+++ b/solution.py
@@ -9,7 +9,7 @@
 P_SIZE = 512
 NP = 4096
 PP = 512
-EARLY = 5
+EARLY = 3
 
 SUB = 8
 LANES = 128
@@ -147,9 +147,11 @@
     return [1 << i for i in range(lax.axis_size(axis).bit_length() - 1)]
 
 
-def halve(x, axis, steps=None):
+def halve(x, axis, steps=None, gates=()):
     me = lax.axis_index(axis)
-    for bit in axis_bits(axis):
+    for step, bit in enumerate(axis_bits(axis)):
+        if step < len(gates):
+            x, _ = lax.optimization_barrier((x, gates[step]))
         high = (me // bit) % 2
         half = x.shape[0] // 2
         away = lax.dynamic_slice_in_dim(x, (1 - high) * half, half, 0)
@@ -228,6 +230,24 @@
     )(parent, sides, inverse, mine, *terms)
 
 
+def line_gather(x, axis, ny, gates):
+    n = lax.axis_size(axis)
+    nz = n // ny
+    up, down = [x], [x]
+    for step in range(1, nz):
+        ends = (up[-1], down[-1])
+        if 1 < step < len(gates) + 2:
+            ends, _ = lax.optimization_barrier((ends, gates[step - 2]))
+        up.append(lax.ppermute(ends[0], axis, [(c, c + ny) for c in range(n) if step - 1 <= c // ny < nz - 1]))
+        down.append(lax.ppermute(ends[1], axis, [(c, c - ny) for c in range(n) if 0 < c // ny <= nz - step]))
+    return [x] + [up[k] + down[nz - k] for k in range(1, nz)], list(zip(up, down))
+
+
+def from_beside(x, axis, ny, j):
+    n = lax.axis_size(axis)
+    return lax.ppermute(x, axis, [(c, c // ny * ny + (c % ny - j) % ny) for c in range(n)])
+
+
 def share_line(x, ny):
     branches = lax.axis_size("branch")
     groups = lax.axis_size("col")
@@ -304,55 +324,74 @@
 
     corner = jnp.concatenate([pivot_column(b) for b in range(pivot_units)], axis=1)
     corner = corner + jnp.where(branch == 0, placed(parent_front[:PP]), 0.0)
-    corner = join(halve(halve(corner, "branch"), "col"), "col")
+    corner = halve(corner, "branch")
 
     def rows_for(target):
         return jnp.concatenate([unit_rows(target * per + a) for a in range(per)], axis=0)
 
-    def moved(shift, rows):
-        pairs = [(c, (c + shift) % groups) for c in range(groups) if c >= pivot_devices]
+    def moved(k, rows):
+        pairs = [(c, c ^ k) for c in range(groups) if c >= pivot_devices]
         return lax.ppermute(rows, "col", pairs)
 
-    far = sorted(range(1, groups), key=lambda shift: abs(2 * shift - groups))
-    rows = [rows_for((col + shift) % groups) for shift in far]
-
-    top = lax.all_gather(front[:P_SIZE], "col")
-    pivots = jnp.concatenate([top[c] for c in range(pivot_devices)], axis=1) if pivot_devices > 1 else top[0]
-
-    received = {0: rows_for(col)}
-    for shift, row in zip(far[:EARLY], rows):
-        row, _ = lax.optimization_barrier((row, (pivots, corner)))
-        received[shift] = moved(shift, row)
+    near, far = list(range(1, ny)), list(reversed(range(ny, groups)))
+    rows = {k: rows_for(col ^ k) for k in range(groups)}
+    received = {0: rows[0]}
+    for k in near:
+        received[k] = moved(k, rows[k])
+
+    z, y = col // ny, col % ny
+    head = front[:P_SIZE]
+    beside = [from_beside(head, "col", ny, j) for j in near]
+    line, steps = line_gather(head, "col", ny, [(corner, [rows[k] for k in far])])
+    corner = halve(corner, "col", gates=[head[:8]] + steps[2:])
+    corner = join(corner, "col")
+
+    def in_line(c, parts):
+        return sum(jnp.where(z == (c // ny + k) % len(line), parts[k], 0.0) for k in range(len(line)))
+
+    pivot_line = in_line(0, line)
+    pivot_parts = [pivot_line] + [from_beside(pivot_line, "col", ny, j) for j in near]
+    pivots = [
+        sum(jnp.where(y == (c - j) % ny, pivot_parts[j], 0.0) for j in range(ny)) for c in range(pivot_devices)]
+    pivots = jnp.concatenate(pivots, axis=1) if pivot_devices > 1 else pivots[0]
+
+    for k in far[:EARLY]:
+        row, _ = lax.optimization_barrier((rows[k], (steps[-1], corner)))
+        received[k] = moved(k, row)
+    others = lax.optimization_barrier((jnp.stack(line[1:]), corner))[0]
+    others = [from_beside(others, "col", ny, j) for j in near]
+    gathered = line + [x for j in range(ny - 1) for x in [beside[j]] + [others[j][k] for k in range(len(line) - 1)]]
+    slots = (source % ny - y) % ny * len(line) + (z - source // ny) % len(line)
 
     inverse = inverse_factor(pivots)
-    for shift, row in zip(far[EARLY:], rows[EARLY:]):
-        row, _ = lax.optimization_barrier((row, inverse))
-        received[shift] = moved(shift, row)
-    places = (col - source) % groups
+    for k in far[EARLY:]:
+        row, _ = lax.optimization_barrier((rows[k], inverse))
+        received[k] = moved(k, row)
+    places = col ^ source
     child_mine = product(inverse, front[:P_SIZE], 1, 0)
 
-    early = [received[shift] for shift in far[:EARLY]]
+    early = [received[k] for k in far[:EARLY]]
     inverse, early = lax.optimization_barrier((inverse, early))
     received.update(zip(far[:EARLY], early))
-    factor = jnp.stack([product(inverse, top[c], 1, 0) for c in range(groups)])
+    factor = jnp.stack([product(inverse, x, 1, 0) for x in gathered])
 
     def factor_columns(u):
-        block = lax.dynamic_slice(factor, (source[u], 0, parts[u] * width), (1, P_SIZE, width))
+        block = lax.dynamic_slice(factor, (slots[u], 0, parts[u] * width), (1, P_SIZE, width))
         return jnp.where(keeps[u] > 0, block[0], 0.0)
 
     mine = jnp.concatenate([factor_columns(col * per + a) for a in range(per)], axis=1)
     mine_keep = jnp.repeat(lax.dynamic_slice_in_dim(keeps, col * per, per), width)[:, None] > 0
-    pieces = jnp.stack([jnp.where(mine_keep, received[shift], 0.0) for shift in range(groups)])
+    pieces = jnp.stack([jnp.where(mine_keep, received[k], 0.0) for k in range(groups)])
     left = three_part(mine)
     n = pivot_units
-    first = spread_update(source[:n], places[:n], parts[:n], keeps[:n], left, factor, pieces, width)
+    first = spread_update(slots[:n], places[:n], parts[:n], keeps[:n], left, factor, pieces, width)
     first = jnp.concatenate([first[u] for u in range(n)], axis=1)
     steps = []
     first = first + jnp.where(branch == 0, parent_front[:PP].T, 0.0)
     first = join(halve(first, "branch", steps), "branch", steps)
 
     head = jnp.concatenate([factor_columns(u) for u in range(pivot_units)], axis=1)
-    head, _ = lax.optimization_barrier((head, received[far[EARLY]]))
+    head, _ = lax.optimization_barrier((head, received[far[-2]]))
     corner = corner - halve(product(head, head, 0, 0), "branch")
     corner, _ = lax.optimization_barrier((corner, received[far[-1]]))
     corner = join(corner, "branch")
@@ -360,7 +399,7 @@
     owned = units_total // branches
     spread = [None] * branches
     for i, m in enumerate(reversed(range(branches))):
-        table, _ = lax.optimization_barrier((source, steps[min(i, len(steps) - 1)]))
+        table, _ = lax.optimization_barrier((slots, steps[min(i, len(steps) - 1)]))
         at = lambda table: lax.dynamic_slice_in_dim(table, (branch ^ m) * owned, owned)
         spread[m] = spread_update(at(table), at(places), at(parts), at(keeps), left, factor, pieces, width)
     terms, sent = scatter_sum(spread, "branch")

time: 523 us -> 498 us (0.952)
  waiting for transfers between devices: 215 us -> 234 us
  starting transfers between devices: 83.6 us -> 67.3 us
  other arithmetic: 50.5 us -> 36.9 us
  between operations: 40.8 us -> 28.3 us
    ppermute x7, waiting for transfers between devices: 91.4 us -> 136 us  [moved(): return lax.ppermute(rows, 'col', pairs)]
    ppermute x3, starting transfers between devices: 43.6 us -> 6.76 us  [share_line(): got = got + lax.ppermute(x, ('branch', 'col'), pairs)]
    ppermute x19, waiting for transfers between devices: 95.5 us -> 62 us  [flip(): return lax.ppermute(x, axis, [(i, i ^ bit) for i in range(n)])]
    ppermute x0 -> x9, waiting for transfers between devices: none -> 23.7 us  [the longest x3 23.7 us: line_gather(): lax.ppermute(ends[1], axis, [(c, c - ny) for c in range(n) if 0 < c // ny...]
    ppermute x0 -> x9, starting transfers between devices: none -> 22.3 us  [the longest x3 9.65 us: from_beside(): lax.ppermute(x, axis, [(c, c // ny * ny + (c % ny - j) % ny) for c in ran...]
    all_gather x1 -> x0, waiting for transfers between devices: 15.3 us -> none  [on_device(): top = lax.all_gather(front[:P_SIZE], 'col')]
    ppermute x1, starting transfers between devices: 15.5 us -> 5.89 us  [share_beside(): shares.append(lax.ppermute(got, 'col', pairs))]
    unnamed x7, other arithmetic: 15.3 us -> 5.99 us
  transfers between devices with their start and end apart: 31 -> 39, of which waited for: 16 -> 16; matrix products, arithmetic and copies ran while one was open for 16% -> 12% of each run, Pallas kernels for 13% -> 14%
where the time goes in v9:
time: 498 us; the launch traced here: 491 us
  waiting for transfers between devices  234 us (47%)
  Pallas kernels  81.6 us (16%)
  starting transfers between devices  67.3 us (14%)
  other arithmetic  36.9 us (7%)
  between operations  28.3 us (6%)
  local copies, waits for them, and re-layouts  27.4 us (6%)
  matrix products  15.8 us (3%)
    ppermute x7, waiting for transfers between devices, moved(): return lax.ppermute(rows, 'col', pairs)  136 us
    ppermute x19, waiting for transfers between devices, flip(): return lax.ppermute(x, axis, [(i, i ^ bit) for i in range(n)])  62 us
    pallas_call x2, Pallas kernels, inverse_factor(): pl.pallas_call(inverse_factor_kernel, out_shape=jax.ShapeDtypeStruct((n,...  43.1 us
    pallas_call x5, Pallas kernels, spread_update(): pl.pallas_call(spread_kernel, grid_spec=pltpu.PrefetchScalarGridSpec(num_...  30.9 us
    ppermute x3, waiting for transfers between devices, line_gather(): lax.ppermute(ends[1], axis, [(c, c - ny) for c in range(n) if 0 < c // ny...  23.7 us
    ppermute x19, starting transfers between devices, flip(): return lax.ppermute(x, axis, [(i, i ^ bit) for i in range(n)])  23.1 us
    dot_general x11, matrix products, product(): lax.dot_general(a, b, (((ca,), (cb,)), ((), ())), precision=precision)  15.8 us
    ppermute x1, waiting for transfers between devices, share_beside(): shares.append(lax.ppermute(got, 'col', pairs))  12 us
  transfers between devices with their start and end apart: 39, of which 16 were waited for; matrix products, arithmetic and copies ran while one was open for 12% of the time, Pallas kernels for 14%

profile of v9, /device:TPU:0, one launch (start us, length us, event | category | flops | bytes accessed | tf_op | source)
XLA Modules:
  0.0 490.8 jit_solution(350759801789141541)
XLA Ops:
  9.2 1.6 constant_dynamic-slice_fusion.14
  13.5 2.3 slice_bitcast_fusion.6
  15.8 5.4 %collective-permute-start = (f32[512,512]{1,0:T(8,128)}, f32[512,512]{1,0:T(8,128)}, u32[]{:S(2)}, u32[]{:S(2)}) collective-permute-start(f32[512,512]{1,0:T(8,128)} %slice_bitcast_fusion.6), channel_id=1, source_target_pairs={{0,2},{1,3},{2,4},{3,5},{4,6},{5,7},{8,10},{9,11},{10,12},{11,13},... | collective-permute-start | bytes 3145736 | tf_op jit(solution)/shard_map/ppermute | solution.py:241
  32.8 5.6 %dynamic-slice_bitcast_fusion.1 = (f32[256,512]{1,0:T(8,128)S(1)}, f32[256,512]{1,0:T(8,128)S(1)}, f32[256,512]{1,0:T(8,128)S(1)}, f32[256,512]{1,0:T(8,128)S(1)...) fusion(f32[1,4096,512]{2,1,0:T(8,128)} %param.3, ...), kind=kLoop, calls=%fused_computation.62 | loop fusion | bytes 16777280 | tf_op jit(solution)/shard_map/dynamic_slice | solution.py:304
  38.4 1.5 pad_maximum_fusion.7
  41.1 1.4 collective-permute-start.3
  42.5 1.6 pad_maximum_fusion.5
  44.0 1.6 pad_maximum_fusion.3
  45.6 3.8 collective-permute-done.3
  50.8 1.7 collective-permute-start.6
  52.5 23.7 %collective-permute-done.4 = f32[512,512]{1,0:T(8,128)S(1)} collective-permute-done((f32[512,512]{1,0:T(8,128)}, f32[512,512]{1,0:T(8,128)S(1)}, u32[]{:S(2)}, u32[]{:S(2)}) %collective-permute-start.4) | collective-permute-done | bytes 1048608 | tf_op jit(solution)/shard_map/ppermute | solution.py:242
  77.5 1.6 collective-permute-start.7
  79.3 1.6 collective-permute-start.9
  83.3 3.7 collective-permute-done.9
  87.2 4.0 collective-permute-start.10
  91.4 15.7 %collective-permute-done.10 = f32[32,512]{0,1:T(8,128)S(1)} collective-permute-done((f32[32,512]{0,1:T(8,128)S(1)}, f32[32,512]{0,1:T(8,128)S(1)}, u32[]{:S(2)}, u32[]{:S(2)}) %collective-permute-start.10) | collective-permute-done | bytes 65568 | tf_op jit(solution)/shard_map/ppermute | solution.py:143
  107.4 2.8 collective-permute-start.11
  110.8 8.8 %collective-permute-done.11 = f32[16,512]{0,1:T(8,128)S(1)} collective-permute-done((f32[16,512]{0,1:T(8,128)S(1)}, f32[16,512]{0,1:T(8,128)S(1)}, u32[]{:S(2)}, u32[]{:S(2)}) %collective-permute-start.11) | collective-permute-done | bytes 32800 | tf_op jit(solution)/shard_map/ppermute | solution.py:143
  120.5 9.4 %collective-permute-done.12 = f32[16,512]{0,1:T(8,128)S(1)} collective-permute-done((f32[16,512]{0,1:T(8,128)S(1)}, f32[16,512]{0,1:T(8,128)S(1)}, u32[]{:S(2)}, u32[]{:S(2)}) %collective-permute-start.12) | collective-permute-done | bytes 32800 | tf_op jit(solution)/shard_map/ppermute | solution.py:143
  130.2 4.4 collective-permute-start.13
  135.3 1.6 collective-permute-done.13
  136.9 2.6 collective-permute-start.14
  139.6 5.1 %select_add_fusion.3 = (f32[512,512]{1,0:T(8,128)}, f32[512,512]{1,0:T(8,128)S(1)}, f32[512,512]{1,0:T(8,128)S(1)}, f32[512,512]{1,0:T(8,128)S(1)}) fusion(pred[]{:T(512)S(6)} %eq.104, pred[]{:T(512)S(6)} %eq.103, pred[]{:T(512)S(6)} %eq.96, pred[]{:T(512)S(6)} %eq.95, f32[1,4096,512]{2,1,0:T(8,128)} %param.3, f32[512,512]{1,0:T(8,128)} %collective-permute-done, ...), kind=kLoop, calls=%fused_computation.54 | loop fusion | flops 2621440 | bytes 11534340 | tf_op jit(solution)/shard_map/add | solution.py:350
  144.7 1.3 collective-permute-start.17
  146.0 1.3 collective-permute-start.16
  147.3 1.5 collective-permute-start.15
  161.0 1.5 fusion.9
  162.5 9.5 %collective-permute-start.18 = (f32[512,512]{1,0:T(8,128)}, f32[512,512]{1,0:T(8,128)S(1)}, u32[]{:S(2)}, u32[]{:S(2)}) collective-permute-start(f32[512,512]{1,0:T(8,128)} %slice_bitcast_fusion.6), channel_id=1, source_target_pairs={{0,1},{1,0},{2,3},{3,2},{4,5},{5,4},{6,7},{7,6},{8,9},{9,8},{10,11... | collective-permute-start | bytes 3145736 | tf_op jit(solution)/shard_map/ppermute | solution.py:248
  172.0 1.4 bitcast_dynamic-update-slice_fusion.6
  173.8 1.5 select_add_fusion.2.a_ref
  175.3 21.7 %shard_map.58 = f32[512,512]{1,0:T(8,128)S(1)} custom-call(f32[512,512]{1,0:T(8,128)S(1)} %select_add_fusion.2.a_ref), custom_call_target="tpu_custom_call" | custom-call | flops 134217728 | bytes 2097152 | tf_op jit(solution)/shard_map/pallas_call | solution.py:86
  197.0 41.4 %collective-permute-done.17 = f32[512,512]{1,0:T(8,128)} collective-permute-done((f32[512,512]{1,0:T(8,128)}, f32[512,512]{1,0:T(8,128)}, u32[]{:S(2)}, u32[]{:S(2)}) %collective-permute-start.17) | collective-permute-done | bytes 1048608 | tf_op jit(solution)/shard_map/ppermute | solution.py:334
  242.3 2.2 fusion.7
  244.5 2.2 fusion.6
  249.8 11.8 %collective-permute-done.23 = f32[512,512]{1,0:T(8,128)S(1)} collective-permute-done((f32[512,512]{1,0:T(8,128)S(1)}, f32[512,512]{1,0:T(8,128)S(1)}, u32[]{:S(2)}, u32[]{:S(2)}) %collective-permute-start.23) | collective-permute-done | bytes 1048608 | tf_op jit(solution)/shard_map/ppermute | solution.py:334
  261.7 23.2 %collective-permute-done.20 = f32[512,512]{1,0:T(8,128)S(1)} collective-permute-done((f32[512,512]{1,0:T(8,128)S(1)}, f32[512,512]{1,0:T(8,128)S(1)}, u32[]{:S(2)}, u32[]{:S(2)}) %collective-permute-start.20) | collective-permute-done | bytes 1048608 | tf_op jit(solution)/shard_map/ppermute | solution.py:334
  285.0 59.6 %collective-permute-done.27 = f32[512,512]{1,0:T(8,128)S(1)} collective-permute-done((f32[512,512]{1,0:T(8,128)S(1)}, f32[512,512]{1,0:T(8,128)S(1)}, u32[]{:S(2)}, u32[]{:S(2)}) %collective-permute-start.27) | collective-permute-done | bytes 1048608 | tf_op jit(solution)/shard_map/ppermute | solution.py:334
  344.8 1.4 bitcast_dynamic-update-slice_fusion.2
  346.2 1.4 bitcast_dynamic-update-slice_fusion.1
  347.6 1.4 bitcast_dynamic-update-slice_fusion.piece_ref
  352.0 3.3 copy-done.2
  356.7 1.6 copy.90.left_ref
  358.3 4.6 shard_map.59
  366.5 1.7 collective-permute-start.29
  369.5 6.5 %shard_map.61 = f32[4,512,256]{2,1,0:T(8,128)} custom-call(s32[4]{0:T(128)} %dynamic_slice.356.slot_ref, s32[4]{0:T(128)} %get-tuple-element.158.place_ref, s32[4]{0:T(128)} %get-tuple-element.108.part_ref, s32[4]{0:T(128)} %get-tuple-element.104.keep_ref, bf16[512,1536]{1,0:T(8,128)(2,1)} %copy.90.left_ref, f32[8,512,512]{2,1,0:T(8,128)} %copy-done.2, ...), custom_call_target="tpu_custom_call" | custom-call | flops 1610612736 | bytes 6291456 | tf_op jit(solution)/shard_map/pallas_call | solution.py:117
  376.8 1.4 collective-permute-start.22
  378.3 6.9 %collective-permute-done.31 = f32[128,512]{1,0:T(8,128)S(1)} collective-permute-done((f32[128,512]{1,0:T(8,128)S(1)}, f32[128,512]{1,0:T(8,128)S(1)}, u32[]{:S(2)}, u32[]{:S(2)}) %collective-permute-start.31) | collective-permute-done | bytes 262176 | tf_op jit(solution)/shard_map/ppermute | solution.py:143
  386.0 4.3 collective-permute-done.22
  390.8 7.6 %collective-permute-done.24 = f32[128,512]{1,0:T(8,128)S(1)} collective-permute-done((f32[128,512]{1,0:T(8,128)S(1)}, f32[128,512]{1,0:T(8,128)S(1)}, u32[]{:S(2)}, u32[]{:S(2)}) %collective-permute-start.24) | collective-permute-done | bytes 262176 | tf_op jit(solution)/shard_map/ppermute | solution.py:143
  400.7 2.3 collective-permute-start.33
  402.9 2.3 collective-permute-start.34
  405.2 2.3 collective-permute-start.35
  408.9 6.5 %shard_map.60 = f32[4,512,256]{2,1,0:T(8,128)} custom-call(s32[4]{0:T(128)} %dynamic_slice.352.slot_ref, s32[4]{0:T(128)} %get-tuple-element.157.place_ref, s32[4]{0:T(128)} %get-tuple-element.109.part_ref, s32[4]{0:T(128)} %get-tuple-element.105.keep_ref, bf16[512,1536]{1,0:T(8,128)(2,1)} %copy.90.left_ref, f32[8,512,512]{2,1,0:T(8,128)} %copy-done.2, ...), custom_call_target="tpu_custom_call" | custom-call | flops 1610612736 | bytes 6291456 | tf_op jit(solution)/shard_map/pallas_call | solution.py:117
  416.0 6.8 %shard_map.64 = f32[4,512,256]{2,1,0:T(8,128)} custom-call(s32[4]{0:T(128)} %dynamic_slice.364.slot_ref, s32[4]{0:T(128)} %get-tuple-element.160.place_ref, s32[4]{0:T(128)} %get-tuple-element.106.part_ref, s32[4]{0:T(128)} %get-tuple-element.102.keep_ref, bf16[512,1536]{1,0:T(8,128)(2,1)} %copy.90.left_ref, f32[8,512,512]{2,1,0:T(8,128)} %copy-done.2, ...), custom_call_target="tpu_custom_call" | custom-call | flops 1610612736 | bytes 6291456 | tf_op jit(solution)/shard_map/pallas_call | solution.py:117
  423.4 3.2 add.489
  426.7 21.5 %shard_map.62.inverse_ref = f32[512,512]{1,0:T(8,128)S(1)} custom-call(f32[512,512]{1,0:T(8,128)S(1)} %pad_maximum_fusion.10.a_ref), custom_call_target="tpu_custom_call" | custom-call | flops 134217728 | bytes 2097152 | tf_op jit(solution)/shard_map/pallas_call | solution.py:86
  448.3 2.4 add_add_fusion
  450.6 5.9 %collective-permute-start.36 = (f32[512,512]{1,0:T(8,128)S(1)}, f32[512,512]{1,0:T(8,128)S(1)}, u32[]{:S(2)}, u32[]{:S(2)}) collective-permute-start(f32[512,512]{1,0:T(8,128)S(1)} %add_add_fusion), channel_id=1, source_target_pairs={{0,1},{1,0},{2,3},{3,2},{4,5},{5,4},{6,7},{7,6},{8,9},{9,8},{10,11... | collective-permute-start | bytes 3145736 | tf_op jit(solution)/shard_map/ppermute | solution.py:269
  456.5 3.2 convolution_bitcast_fusion.8
  460.3 6.5 %shard_map.63.rest_0_ = f32[4,512,256]{2,1,0:T(8,128)} custom-call(s32[4]{0:T(128)} %dynamic_slice.360.slot_ref, s32[4]{0:T(128)} %get-tuple-element.159.place_ref, s32[4]{0:T(128)} %get-tuple-element.107.part_ref, s32[4]{0:T(128)} %get-tuple-element.103.keep_ref, bf16[512,1536]{1,0:T(8,128)(2,1)} %copy.90.left_ref, f32[8,512,512]{2,1,0:T(8,128)} %copy-done.2, ...), custom_call_target="tpu_custom_call" | custom-call | flops 1610612736 | bytes 6291456 | tf_op jit(solution)/shard_map/pallas_call | solution.py:117
  467.8 12.0 %collective-permute-done.36 = f32[512,512]{1,0:T(8,128)S(1)} collective-permute-done((f32[512,512]{1,0:T(8,128)S(1)}, f32[512,512]{1,0:T(8,128)S(1)}, u32[]{:S(2)}, u32[]{:S(2)}) %collective-permute-start.36) | collective-permute-done | bytes 1048608 | tf_op jit(solution)/shard_map/ppermute | solution.py:269
  480.2 1.5 pad_maximum_fusion.1
  481.7 1.4 copy-done.8
  483.0 7.5 %shard_map.65 = f32[1024,512]{1,0:T(8,128)} custom-call(f32[1024,512]{1,0:T(8,128)S(1)} %copy-done, f32[4,256,512]{2,1,0:T(8,128)} %bitcast.177, f32[512,512]{1,0:T(8,128)S(1)} %shard_map.62.inverse_ref, f32[512,512]{1,0:T(8,128)S(1)} %fusion.16.mine_ref, f32[4,512,256]{2,1,0:T(8,128)} %shard_map.63.rest_0_, f32[4,512,256]{2,1,0:T(8,128)} %copy-done.8, ...), custom_call_target="tpu_custom_call" | custom-call | flops 3221225472 | bytes 16777216 | tf_op jit(solution)/shard_map/pallas_call | solution.py:216
  (167 shorter events, 43.8 us)
Async XLA Ops:
  0.6 10.7 %slice-start = ((f32[1024,512]{1,0:T(8,128)}), f32[512,512]{1,0:T(8,128)S(1)}, s32[]{:S(2)}) async-start(f32[1024,512]{1,0:T(8,128)} %parent_ref.1), calls=%async_computation | async-start | bytes 2097152 | tf_op jit(solution)/shard_map/slice | solution.py:326
  3.0 131.6 %copy-start.17 = (s32[16]{0:T(128)}, s32[16]{0:T(128)S(1)}, u32[]{:S(2)}) copy-start(s32[16]{0:T(128)S(1)} %get-tuple-element.51) | copy-start | bytes 196
  7.2 141.7 %copy-start.16 = (s32[16]{0:T(128)}, s32[16]{0:T(128)S(1)}, u32[]{:S(2)}) copy-start(s32[16]{0:T(128)S(1)} %gather_fusion.1) | copy-start | bytes 196
  11.7 26.7 %copy-start.5 = (f32[512,512]{0,1:T(8,128)}, f32[512,512]{0,1:T(8,128)S(1)}, u32[]{:S(2)}) copy-start(f32[512,512]{0,1:T(8,128)S(1)} %copy.108) | copy-start | bytes 3145732
  12.9 27.1 %collective-permute-start.2 = (f32[256,512]{0,1:T(8,128)}, f32[256,512]{0,1:T(8,128)}, u32[]{:S(2)}, u32[]{:S(2)}) collective-permute-start(f32[256,512]{0,1:T(8,128)} %constant_dynamic-slice_fusion.10), channel_id=1, source_target_pairs={{0,8},{8,0},{16,24},{24,16},{1,9},{9,1},{17,25},{25,17},{2,10},{10... | collective-permute-start | bytes 1572872 | tf_op jit(solution)/shard_map/ppermute | solution.py:143
  15.8 33.7 %collective-permute-start = (f32[512,512]{1,0:T(8,128)}, f32[512,512]{1,0:T(8,128)}, u32[]{:S(2)}, u32[]{:S(2)}) collective-permute-start(f32[512,512]{1,0:T(8,128)} %slice_bitcast_fusion.6), channel_id=1, source_target_pairs={{0,2},{1,3},{2,4},{3,5},{4,6},{5,7},{8,10},{9,11},{10,12},{11,13},... | collective-permute-start | bytes 3145736 | tf_op jit(solution)/shard_map/ppermute | solution.py:241
  21.2 28.3 %collective-permute-start.1 = (f32[512,512]{1,0:T(8,128)}, f32[512,512]{1,0:T(8,128)}, u32[]{:S(2)}, u32[]{:S(2)}) collective-permute-start(f32[512,512]{1,0:T(8,128)} %slice_bitcast_fusion.6), channel_id=1, source_target_pairs={{2,0},{3,1},{4,2},{5,3},{6,4},{7,5},{10,8},{11,9},{12,10},{13,11},... | collective-permute-start | bytes 3145736 | tf_op jit(solution)/shard_map/ppermute | solution.py:242
  41.1 8.4 %collective-permute-start.3 = (f32[128,512]{0,1:T(8,128)S(1)}, f32[128,512]{0,1:T(8,128)S(1)}, u32[]{:S(2)}, u32[]{:S(2)}) collective-permute-start(f32[128,512]{0,1:T(8,128)S(1)} %constant_dynamic-slice_fusion.9), channel_id=1, source_target_pairs={{0,16},{8,24},{16,0},{24,8},{1,17},{9,25},{17,1},{25,9},{2,18},{10... | collective-permute-start | bytes 786440 | tf_op jit(solution)/shard_map/ppermute | solution.py:143
  49.5 26.7 %collective-permute-start.4 = (f32[512,512]{1,0:T(8,128)}, f32[512,512]{1,0:T(8,128)S(1)}, u32[]{:S(2)}, u32[]{:S(2)}) collective-permute-start(f32[512,512]{1,0:T(8,128)} %collective-permute-done.1), channel_id=1, source_target_pairs={{2,0},{3,1},{4,2},{5,3},{10,8},{11,9},{12,10},{13,11},{18,16},{19,... | collective-permute-start | bytes 3145736 | tf_op jit(solution)/shard_map/ppermute | solution.py:242
  50.8 26.7 %collective-permute-start.6 = (f32[512,512]{1,0:T(8,128)}, f32[512,512]{1,0:T(8,128)}, u32[]{:S(2)}, u32[]{:S(2)}) collective-permute-start(f32[512,512]{1,0:T(8,128)} %collective-permute-done), channel_id=1, source_target_pairs={{2,4},{3,5},{4,6},{5,7},{10,12},{11,13},{12,14},{13,15},{18,20},{1... | collective-permute-start | bytes 3145736 | tf_op jit(solution)/shard_map/ppermute | solution.py:241
  76.2 60.7 %copy-start.10 = (f32[512,512]{1,0:T(8,128)}, f32[512,512]{1,0:T(8,128)S(1)}, u32[]{:S(2)}) copy-start(f32[512,512]{1,0:T(8,128)S(1)} %collective-permute-done.4) | copy-start | bytes 3145732
  76.2 31.0 %collective-permute-start.5 = (f32[512,512]{1,0:T(8,128)S(1)}, f32[512,512]{1,0:T(8,128)}, u32[]{:S(2)}, u32[]{:S(2)}) collective-permute-start(f32[512,512]{1,0:T(8,128)S(1)} %collective-permute-done.4), channel_id=1, source_target_pairs={{2,0},{3,1},{10,8},{11,9},{18,16},{19,17},{26,24},{27,25}} | collective-permute-start | bytes 3145736 | tf_op jit(solution)/shard_map/ppermute | solution.py:242
  77.5 29.7 %collective-permute-start.7 = (f32[512,512]{1,0:T(8,128)}, f32[512,512]{1,0:T(8,128)}, u32[]{:S(2)}, u32[]{:S(2)}) collective-permute-start(f32[512,512]{1,0:T(8,128)} %collective-permute-done.6), channel_id=1, source_target_pairs={{4,6},{5,7},{12,14},{13,15},{20,22},{21,23},{28,30},{29,31}} | collective-permute-start | bytes 3145736 | tf_op jit(solution)/shard_map/ppermute | solution.py:241
  79.3 7.7 %collective-permute-start.9 = (f32[64,512]{0,1:T(8,128)S(1)}, f32[64,512]{0,1:T(8,128)S(1)}, u32[]{:S(2)}, u32[]{:S(2)}) collective-permute-start(f32[64,512]{0,1:T(8,128)S(1)} %constant_dynamic-slice_fusion.8), channel_id=1, source_target_pairs={{0,1},{1,0},{2,3},{3,2},{4,5},{5,4},{6,7},{7,6},{8,9},{9,8},{10,11... | collective-permute-start | bytes 393224 | tf_op jit(solution)/shard_map/ppermute | solution.py:143
  82.0 80.5 %collective-permute-start.26 = (f32[512,512]{1,0:T(8,128)}, f32[512,512]{1,0:T(8,128)}, u32[]{:S(2)}, u32[]{:S(2)}) collective-permute-start(f32[512,512]{1,0:T(8,128)} %pad_maximum_fusion.11), channel_id=1, source_target_pairs={{1,0},{2,3},{3,2},{4,5},{5,4},{6,7},{7,6},{9,8},{10,11},{11,10},{1... | collective-permute-start | bytes 3145736 | tf_op jit(solution)/shard_map/ppermute | solution.py:334
  87.2 19.8 %collective-permute-start.10 = (f32[32,512]{0,1:T(8,128)S(1)}, f32[32,512]{0,1:T(8,128)S(1)}, u32[]{:S(2)}, u32[]{:S(2)}) collective-permute-start(f32[32,512]{0,1:T(8,128)S(1)} %constant_dynamic-slice_fusion.7), channel_id=1, source_target_pairs={{0,2},{1,3},{2,0},{3,1},{4,6},{5,7},{6,4},{7,5},{8,10},{9,11},{10,... | collective-permute-start | bytes 196616 | tf_op jit(solution)/shard_map/ppermute | solution.py:143
  91.3 71.1 %copy-start.14 = (s32[16]{0:T(128)}, s32[16]{0:T(128)S(1)}, u32[]{:S(2)}) copy-start(s32[16]{0:T(128)S(1)} %get-tuple-element.145) | copy-start | bytes 196
  91.3 71.1 %copy-start.18 = (s32[16]{0:T(128)}, s32[16]{0:T(128)S(1)}, u32[]{:S(2)}) copy-start(s32[16]{0:T(128)S(1)} %get-tuple-element.50) | copy-start | bytes 196
  107.4 12.3 %collective-permute-start.11 = (f32[16,512]{0,1:T(8,128)S(1)}, f32[16,512]{0,1:T(8,128)S(1)}, u32[]{:S(2)}, u32[]{:S(2)}) collective-permute-start(f32[16,512]{0,1:T(8,128)S(1)} %constant_dynamic-slice_fusion.6), channel_id=1, source_target_pairs={{0,4},{1,5},{2,6},{3,7},{4,0},{5,1},{6,2},{7,3},{8,12},{9,13},{10,... | collective-permute-start | bytes 98312 | tf_op jit(solution)/shard_map/ppermute | solution.py:143
  119.8 10.2 %collective-permute-start.12 = (f32[16,512]{0,1:T(8,128)S(1)}, f32[16,512]{0,1:T(8,128)S(1)}, u32[]{:S(2)}, u32[]{:S(2)}) collective-permute-start(f32[16,512]{0,1:T(8,128)S(1)} %dynamic-slice_add_fusion.4), channel_id=1, source_target_pairs={{0,4},{1,5},{2,6},{3,7},{4,0},{5,1},{6,2},{7,3},{8,12},{9,13},{10,... | collective-permute-start | bytes 98312 | tf_op jit(solution)/shard_map/ppermute | solution.py:143
  130.2 6.7 %collective-permute-start.13 = (f32[32,512]{1,0:T(8,128)S(1)}, f32[32,512]{1,0:T(8,128)S(1)}, u32[]{:S(2)}, u32[]{:S(2)}) collective-permute-start(f32[32,512]{1,0:T(8,128)S(1)} %pad_maximum_fusion.17), channel_id=1, source_target_pairs={{0,2},{1,3},{2,0},{3,1},{4,6},{5,7},{6,4},{7,5},{8,10},{9,11},{10,... | collective-permute-start | bytes 196616 | tf_op jit(solution)/shard_map/ppermute | solution.py:143
  136.9 7.8 %collective-permute-start.14 = (f32[64,512]{1,0:T(8,128)S(1)}, f32[64,512]{1,0:T(8,128)S(1)}, u32[]{:S(2)}, u32[]{:S(2)}) collective-permute-start(f32[64,512]{1,0:T(8,128)S(1)} %pad_maximum_fusion.16), channel_id=1, source_target_pairs={{0,1},{1,0},{2,3},{3,2},{4,5},{5,4},{6,7},{7,6},{8,9},{9,8},{10,11... | collective-permute-start | bytes 393224 | tf_op jit(solution)/shard_map/ppermute | solution.py:143
  144.7 29.1 %copy-start.4 = (f32[512,512]{1,0:T(8,128)}, f32[512,512]{1,0:T(8,128)S(1)}, u32[]{:S(2)}) copy-start(f32[512,512]{1,0:T(8,128)S(1)} %get-tuple-element.55) | copy-start | bytes 3145732
  144.7 29.0 %collective-permute-start.8 = (f32[512,512]{1,0:T(8,128)}, f32[512,512]{1,0:T(8,128)}, u32[]{:S(2)}, u32[]{:S(2)}) collective-permute-start(f32[512,512]{1,0:T(8,128)} %get-tuple-element.54), channel_id=1, source_target_pairs={{0,1},{1,0},{2,3},{3,2},{4,5},{5,4},{6,7},{7,6},{8,9},{9,8},{10,11... | collective-permute-start | bytes 3145736 | tf_op jit(solution)/shard_map/ppermute | solution.py:248
  144.7 93.6 %collective-permute-start.17 = (f32[512,512]{1,0:T(8,128)}, f32[512,512]{1,0:T(8,128)}, u32[]{:S(2)}, u32[]{:S(2)}) collective-permute-start(f32[512,512]{1,0:T(8,128)} %get-tuple-element.33), channel_id=1, source_target_pairs={{1,4},{2,7},{3,6},{4,1},{5,0},{6,3},{7,2},{9,12},{10,15},{11,14},{... | collective-permute-start | bytes 3145736 | tf_op jit(solution)/shard_map/ppermute | solution.py:334
  146.0 93.6 %collective-permute-start.16 = (f32[512,512]{1,0:T(8,128)}, f32[512,512]{1,0:T(8,128)}, u32[]{:S(2)}, u32[]{:S(2)}) collective-permute-start(f32[512,512]{1,0:T(8,128)} %get-tuple-element.32), channel_id=1, source_target_pairs={{1,7},{2,4},{3,5},{4,2},{5,3},{6,0},{7,1},{9,15},{10,12},{11,13},{... | collective-permute-start | bytes 3145736 | tf_op jit(solution)/shard_map/ppermute | solution.py:334
  147.3 93.6 %collective-permute-start.15 = (f32[512,512]{1,0:T(8,128)}, f32[512,512]{1,0:T(8,128)}, u32[]{:S(2)}, u32[]{:S(2)}) collective-permute-start(f32[512,512]{1,0:T(8,128)} %get-tuple-element.31), channel_id=1, source_target_pairs={{1,6},{2,5},{3,4},{4,3},{5,2},{6,1},{7,0},{9,14},{10,13},{11,12},{... | collective-permute-start | bytes 3145736 | tf_op jit(solution)/shard_map/ppermute | solution.py:334
  160.9 77.4 %copy-start.12 = (f32[512,512]{1,0:T(8,128)S(1)}, f32[512,512]{1,0:T(8,128)}, u32[]{:S(2)}) copy-start(f32[512,512]{1,0:T(8,128)} %get-tuple-element.38) | copy-start | bytes 3145732
  160.9 78.7 %copy-start.11 = (f32[512,512]{1,0:T(8,128)S(1)}, f32[512,512]{1,0:T(8,128)}, u32[]{:S(2)}) copy-start(f32[512,512]{1,0:T(8,128)} %get-tuple-element.36) | copy-start | bytes 3145732
  160.9 80.0 %copy-start.13 = (f32[512,512]{1,0:T(8,128)S(1)}, f32[512,512]{1,0:T(8,128)}, u32[]{:S(2)}) copy-start(f32[512,512]{1,0:T(8,128)} %get-tuple-element.40) | copy-start | bytes 3145732
  162.5 86.3 %collective-permute-start.18 = (f32[512,512]{1,0:T(8,128)}, f32[512,512]{1,0:T(8,128)S(1)}, u32[]{:S(2)}, u32[]{:S(2)}) collective-permute-start(f32[512,512]{1,0:T(8,128)} %slice_bitcast_fusion.6), channel_id=1, source_target_pairs={{0,1},{1,0},{2,3},{3,2},{4,5},{5,4},{6,7},{7,6},{8,9},{9,8},{10,11... | collective-permute-start | bytes 3145736 | tf_op jit(solution)/shard_map/ppermute | solution.py:248
  173.7 175.2 %collective-permute-start.19 = (f32[3,512,512]{2,1,0:T(8,128)S(1)}, f32[3,512,512]{2,1,0:T(8,128)S(1)}, u32[]{:S(2)}, u32[]{:S(2)}) collective-permute-start(f32[3,512,512]{2,1,0:T(8,128)S(1)} %pad_maximum_fusion), channel_id=1, source_target_pairs={{0,1},{1,0},{2,3},{3,2},{4,5},{5,4},{6,7},{7,6},{8,9},{9,8},{10,11... | collective-permute-start | bytes 9437192 | tf_op jit(solution)/shard_map/ppermute | solution.py:248
  238.3 23.2 %collective-permute-start.23 = (f32[512,512]{1,0:T(8,128)S(1)}, f32[512,512]{1,0:T(8,128)S(1)}, u32[]{:S(2)}, u32[]{:S(2)}) collective-permute-start(f32[512,512]{1,0:T(8,128)S(1)} %copy-done.12), channel_id=1, source_target_pairs={{1,3},{2,0},{3,1},{4,6},{5,7},{6,4},{7,5},{9,11},{10,8},{11,9},{12... | collective-permute-start | bytes 3145736 | tf_op jit(solution)/shard_map/ppermute | solution.py:334
  239.6 45.3 %collective-permute-start.20 = (f32[512,512]{1,0:T(8,128)S(1)}, f32[512,512]{1,0:T(8,128)S(1)}, u32[]{:S(2)}, u32[]{:S(2)}) collective-permute-start(f32[512,512]{1,0:T(8,128)S(1)} %copy-done.11), channel_id=1, source_target_pairs={{1,2},{2,1},{3,0},{4,7},{5,6},{6,5},{7,4},{9,10},{10,9},{11,8},{12... | collective-permute-start | bytes 3145736 | tf_op jit(solution)/shard_map/ppermute | solution.py:334
  241.0 103.7 %collective-permute-start.27 = (f32[512,512]{1,0:T(8,128)S(1)}, f32[512,512]{1,0:T(8,128)S(1)}, u32[]{:S(2)}, u32[]{:S(2)}) collective-permute-start(f32[512,512]{1,0:T(8,128)S(1)} %copy-done.13), channel_id=1, source_target_pairs={{1,5},{2,6},{3,7},{4,0},{5,1},{6,2},{7,3},{9,13},{10,14},{11,15},{... | collective-permute-start | bytes 3145736 | tf_op jit(solution)/shard_map/ppermute | solution.py:334
  348.9 7.5 %copy-start.3 = (f32[8,512,512]{2,1,0:T(8,128)}, f32[8,512,512]{2,1,0:T(8,128)S(1)}, u32[]{:S(2)}) copy-start(f32[8,512,512]{2,1,0:T(8,128)S(1)} %bitcast_dynamic-update-slice_fusion.piece_ref) | copy-start | bytes 25165828
  352.0 3.3 copy-start.2
  358.3 5.9 %copy-start.6 = (f32[512,512]{0,1:T(8,128)S(1)}, f32[512,512]{0,1:T(8,128)}, u32[]{:S(2)}) copy-start(f32[512,512]{0,1:T(8,128)} %copy-done.5) | copy-start | bytes 3145732
  358.3 6.2 %copy-start.9 = (f32[512,256]{1,0:T(8,128)S(1)}, f32[512,256]{1,0:T(8,128)}, u32[]{:S(2)}) copy-start(f32[512,256]{1,0:T(8,128)} %get-tuple-element.77) | copy-start | bytes 1572868
  362.9 5.4 %copy-start.15 = (s32[16]{0:T(128)S(1)}, s32[16]{0:T(128)}, u32[]{:S(2)}) copy-start(s32[16]{0:T(128)} %copy-done.14) | copy-start | bytes 196
  362.9 6.0 %copy-start.19 = (s32[16]{0:T(128)S(1)}, s32[16]{0:T(128)}, u32[]{:S(2)}) copy-start(s32[16]{0:T(128)} %copy-done.18) | copy-start | bytes 196
  364.4 2.0 collective-permute-start.28
  365.8 11.0 %collective-permute-start.21 = (f32[256,512]{1,0:T(8,128)S(1)}, f32[256,512]{1,0:T(8,128)S(1)}, u32[]{:S(2)}, u32[]{:S(2)}) collective-permute-start(f32[256,512]{1,0:T(8,128)S(1)} %constant_dynamic-slice_fusion.5), channel_id=1, source_target_pairs={{0,8},{8,0},{16,24},{24,16},{1,9},{9,1},{17,25},{25,17},{2,10},{10... | collective-permute-start | bytes 1572872 | tf_op jit(solution)/shard_map/ppermute | solution.py:143
  366.5 9.4 %collective-permute-start.29 = (f32[128,512]{1,0:T(8,128)S(1)}, f32[128,512]{1,0:T(8,128)S(1)}, u32[]{:S(2)}, u32[]{:S(2)}) collective-permute-start(f32[128,512]{1,0:T(8,128)S(1)} %constant_dynamic-slice_fusion), channel_id=1, source_target_pairs={{0,16},{8,24},{16,0},{24,8},{1,17},{9,25},{17,1},{25,9},{2,18},{10... | collective-permute-start | bytes 786440 | tf_op jit(solution)/shard_map/ppermute | solution.py:143
  375.9 46.9 %collective-permute-start.30 = (f32[4,512,256]{2,1,0:T(8,128)}, f32[4,512,256]{2,1,0:T(8,128)}, u32[]{:S(2)}, u32[]{:S(2)}) collective-permute-start(f32[4,512,256]{2,1,0:T(8,128)} %shard_map.61), channel_id=1, source_target_pairs={{0,8},{8,0},{16,24},{24,16},{1,9},{9,1},{17,25},{25,17},{2,10},{10... | collective-permute-start | bytes 6291464 | tf_op jit(solution)/shard_map/ppermute | solution.py:143
  376.0 9.2 %collective-permute-start.31 = (f32[128,512]{1,0:T(8,128)S(1)}, f32[128,512]{1,0:T(8,128)S(1)}, u32[]{:S(2)}, u32[]{:S(2)}) collective-permute-start(f32[128,512]{1,0:T(8,128)S(1)} %dynamic-slice_add_fusion.3), channel_id=1, source_target_pairs={{0,16},{8,24},{16,0},{24,8},{1,17},{9,25},{17,1},{25,9},{2,18},{10... | collective-permute-start | bytes 786440 | tf_op jit(solution)/shard_map/ppermute | solution.py:143
  376.8 13.5 %collective-permute-start.22 = (f32[128,512]{1,0:T(8,128)S(1)}, f32[128,512]{1,0:T(8,128)S(1)}, u32[]{:S(2)}, u32[]{:S(2)}) collective-permute-start(f32[128,512]{1,0:T(8,128)S(1)} %constant_dynamic-slice_fusion.4), channel_id=1, source_target_pairs={{0,16},{8,24},{16,0},{24,8},{1,17},{9,25},{17,1},{25,9},{2,18},{10... | collective-permute-start | bytes 786440 | tf_op jit(solution)/shard_map/ppermute | solution.py:143
  386.0 12.4 %collective-permute-start.32 = (f32[256,512]{1,0:T(8,128)}, f32[256,512]{1,0:T(8,128)}, u32[]{:S(2)}, u32[]{:S(2)}) collective-permute-start(f32[256,512]{1,0:T(8,128)} %pad_maximum_fusion.14), channel_id=1, source_target_pairs={{0,8},{8,0},{16,24},{24,16},{1,9},{9,1},{17,25},{25,17},{2,10},{10... | collective-permute-start | bytes 1572872 | tf_op jit(solution)/shard_map/ppermute | solution.py:143
  390.4 8.0 %collective-permute-start.24 = (f32[128,512]{1,0:T(8,128)S(1)}, f32[128,512]{1,0:T(8,128)S(1)}, u32[]{:S(2)}, u32[]{:S(2)}) collective-permute-start(f32[128,512]{1,0:T(8,128)S(1)} %add_subtract_fusion), channel_id=1, source_target_pairs={{0,16},{8,24},{16,0},{24,8},{1,17},{9,25},{17,1},{25,9},{2,18},{10... | collective-permute-start | bytes 786440 | tf_op jit(solution)/shard_map/ppermute | solution.py:143
  400.7 47.5 %collective-permute-start.33 = (f32[512,512]{1,0:T(8,128)}, f32[512,512]{1,0:T(8,128)}, u32[]{:S(2)}, u32[]{:S(2)}) collective-permute-start(f32[512,512]{1,0:T(8,128)} %pad_maximum_fusion.12), channel_id=1, source_target_pairs={{0,2},{1,3},{10,12},{11,13},{20,22},{21,23},{30,24},{31,25}} | collective-permute-start | bytes 3145736 | tf_op jit(solution)/shard_map/ppermute | solution.py:259
  402.9 45.3 %collective-permute-start.34 = (f32[512,512]{1,0:T(8,128)}, f32[512,512]{1,0:T(8,128)}, u32[]{:S(2)}, u32[]{:S(2)}) collective-permute-start(f32[512,512]{1,0:T(8,128)} %pad_maximum_fusion.12), channel_id=1, source_target_pairs={{0,4},{1,5},{10,14},{11,15},{20,16},{21,17},{30,26},{31,27}} | collective-permute-start | bytes 3145736 | tf_op jit(solution)/shard_map/ppermute | solution.py:259
  405.2 43.1 %collective-permute-start.35 = (f32[512,512]{1,0:T(8,128)}, f32[512,512]{1,0:T(8,128)}, u32[]{:S(2)}, u32[]{:S(2)}) collective-permute-start(f32[512,512]{1,0:T(8,128)} %pad_maximum_fusion.12), channel_id=1, source_target_pairs={{0,6},{1,7},{10,8},{11,9},{20,18},{21,19},{30,28},{31,29}} | collective-permute-start | bytes 3145736 | tf_op jit(solution)/shard_map/ppermute | solution.py:259
  408.3 18.3 %collective-permute-start.25 = (f32[256,512]{1,0:T(8,128)}, f32[256,512]{1,0:T(8,128)S(1)}, u32[]{:S(2)}, u32[]{:S(2)}) collective-permute-start(f32[256,512]{1,0:T(8,128)} %pad_maximum_fusion.13), channel_id=1, source_target_pairs={{0,8},{8,0},{16,24},{24,16},{1,9},{9,1},{17,25},{25,17},{2,10},{10... | collective-permute-start | bytes 1572872 | tf_op jit(solution)/shard_map/ppermute | solution.py:143
  416.0 7.4 %copy-start.7 = (f32[4,512,256]{2,1,0:T(8,128)S(1)}, f32[4,512,256]{2,1,0:T(8,128)}, u32[]{:S(2)}) copy-start(f32[4,512,256]{2,1,0:T(8,128)} %shard_map.60) | copy-start | bytes 6291460
  422.8 58.9 %collective-permute-start.37 = (f32[4,512,256]{2,1,0:T(8,128)}, f32[4,512,256]{2,1,0:T(8,128)S(1)}, u32[]{:S(2)}, u32[]{:S(2)}) collective-permute-start(f32[4,512,256]{2,1,0:T(8,128)} %shard_map.64), channel_id=1, source_target_pairs={{0,8},{8,0},{16,24},{24,16},{1,9},{9,1},{17,25},{25,17},{2,10},{10... | collective-permute-start | bytes 6291464 | tf_op jit(solution)/shard_map/ppermute | solution.py:143
  426.6 55.1 %collective-permute-start.38 = (f32[4,512,256]{2,1,0:T(8,128)}, f32[4,512,256]{2,1,0:T(8,128)}, u32[]{:S(2)}, u32[]{:S(2)}) collective-permute-start(f32[4,512,256]{2,1,0:T(8,128)} %add.489), channel_id=1, source_target_pairs={{0,16},{8,24},{16,0},{24,8},{1,17},{9,25},{17,1},{25,9},{2,18},{10... | collective-permute-start | bytes 6291464 | tf_op jit(solution)/shard_map/ppermute | solution.py:143
  450.6 29.2 %collective-permute-start.36 = (f32[512,512]{1,0:T(8,128)S(1)}, f32[512,512]{1,0:T(8,128)S(1)}, u32[]{:S(2)}, u32[]{:S(2)}) collective-permute-start(f32[512,512]{1,0:T(8,128)S(1)} %add_add_fusion), channel_id=1, source_target_pairs={{0,1},{1,0},{2,3},{3,2},{4,5},{5,4},{6,7},{7,6},{8,9},{9,8},{10,11... | collective-permute-start | bytes 3145736 | tf_op jit(solution)/shard_map/ppermute | solution.py:269
  466.8 16.2 %copy-start = (f32[1024,512]{1,0:T(8,128)S(1)}, f32[1024,512]{1,0:T(8,128)}, u32[]{:S(2)}) copy-start(f32[1024,512]{1,0:T(8,128)} %parent_ref.1) | copy-start | bytes 6291460
  467.8 22.7 %copy-start.1 = (f32[512,512]{1,0:T(8,128)}, f32[512,512]{1,0:T(8,128)S(1)}, u32[]{:S(2)}) copy-start(f32[512,512]{1,0:T(8,128)S(1)} %fusion.16.mine_ref) | copy-start | bytes 3145732
  481.7 1.4 copy-start.8

commit v10 on v9

--- a/solution.py
+++ b/solution.py
@@ -343,8 +343,8 @@
     head = front[:P_SIZE]
     beside = [from_beside(head, "col", ny, j) for j in near]
     line, steps = line_gather(head, "col", ny, [(corner, [rows[k] for k in far])])
-    corner = halve(corner, "col", gates=[head[:8]] + steps[2:])
-    corner = join(corner, "col")
+    halved = halve(corner, "col", gates=[head[:8]] + steps[2:])
+    corner = join(halved, "col")
 
     def in_line(c, parts):
         return sum(jnp.where(z == (c // ny + k) % len(line), parts[k], 0.0) for k in range(len(line)))
@@ -356,22 +356,22 @@
     pivots = jnp.concatenate(pivots, axis=1) if pivot_devices > 1 else pivots[0]
 
     for k in far[:EARLY]:
-        row, _ = lax.optimization_barrier((rows[k], (steps[-1], corner)))
+        row, _ = lax.optimization_barrier((rows[k], (steps[-1], halved, beside)))
         received[k] = moved(k, row)
-    others = lax.optimization_barrier((jnp.stack(line[1:]), corner))[0]
+    others = lax.optimization_barrier((jnp.stack(line[1:]), pivots))[0]
     others = [from_beside(others, "col", ny, j) for j in near]
     gathered = line + [x for j in range(ny - 1) for x in [beside[j]] + [others[j][k] for k in range(len(line) - 1)]]
     slots = (source % ny - y) % ny * len(line) + (z - source // ny) % len(line)
 
     inverse = inverse_factor(pivots)
     for k in far[EARLY:]:
-        row, _ = lax.optimization_barrier((rows[k], inverse))
+        row, _ = lax.optimization_barrier((rows[k], pivots if k == far[EARLY] else others))
         received[k] = moved(k, row)
     places = col ^ source
     child_mine = product(inverse, front[:P_SIZE], 1, 0)
 
     early = [received[k] for k in far[:EARLY]]
-    inverse, early = lax.optimization_barrier((inverse, early))
+    inverse, early, corner = lax.optimization_barrier((inverse, early, corner))
     received.update(zip(far[:EARLY], early))
     factor = jnp.stack([product(inverse, x, 1, 0) for x in gathered])
 
@@ -391,9 +391,8 @@
     first = join(halve(first, "branch", steps), "branch", steps)
 
     head = jnp.concatenate([factor_columns(u) for u in range(pivot_units)], axis=1)
-    head, _ = lax.optimization_barrier((head, received[far[-2]]))
     corner = corner - halve(product(head, head, 0, 0), "branch")
-    corner, _ = lax.optimization_barrier((corner, received[far[-1]]))
+    corner, _ = lax.optimization_barrier((corner, received[far[-2]]))
     corner = join(corner, "branch")
 
     owned = units_total // branches

time: 498 us -> 552 us (1.11)
  waiting for transfers between devices: 234 us -> 258 us
  other arithmetic: 36.9 us -> 56.8 us
    ppermute x19, waiting for transfers between devices: 62 us -> 116 us  [flip(): return lax.ppermute(x, axis, [(i, i ^ bit) for i in range(n)])]
    ppermute x7, waiting for transfers between devices: 136 us -> 97.5 us  [moved(): return lax.ppermute(rows, 'col', pairs)]
    unnamed x7, other arithmetic: 5.99 us -> 16.5 us
    ppermute x3, waiting for transfers between devices: 0.01 us -> 8.48 us  [from_beside(): lax.ppermute(x, axis, [(c, c // ny * ny + (c % ny - j) % ny) for c in ran...]
    ppermute x19, starting transfers between devices: 23.1 us -> 31.2 us  [flip(): return lax.ppermute(x, axis, [(i, i ^ bit) for i in range(n)])]
    ppermute x3, starting transfers between devices: 9.65 us -> 1.89 us  [from_beside(): lax.ppermute(x, axis, [(c, c // ny * ny + (c % ny - j) % ny) for c in ran...]
  transfers between devices with their start and end apart: 39 -> 39, of which waited for: 16 -> 13; matrix products, arithmetic and copies ran while one was open for 12% -> 16% of each run, Pallas kernels for 14% -> 13%
where the time goes in v10:
time: 552 us; the launch traced here: 543 us
  waiting for transfers between devices  258 us (47%)
  Pallas kernels  81.6 us (15%)
  starting transfers between devices  66.5 us (12%)
  other arithmetic  56.8 us (10%)
  local copies, waits for them, and re-layouts  31.5 us (6%)
  between operations  27.3 us (5%)
  matrix products  21 us (4%)
    ppermute x19, waiting for transfers between devices, flip(): return lax.ppermute(x, axis, [(i, i ^ bit) for i in range(n)])  116 us
    ppermute x7, waiting for transfers between devices, moved(): return lax.ppermute(rows, 'col', pairs)  97.5 us
    pallas_call x2, Pallas kernels, inverse_factor(): pl.pallas_call(inverse_factor_kernel, out_shape=jax.ShapeDtypeStruct((n,...  43.1 us
    ppermute x19, starting transfers between devices, flip(): return lax.ppermute(x, axis, [(i, i ^ bit) for i in range(n)])  31.2 us
    pallas_call x5, Pallas kernels, spread_update(): pl.pallas_call(spread_kernel, grid_spec=pltpu.PrefetchScalarGridSpec(num_...  31 us
    ppermute x3, waiting for transfers between devices, line_gather(): lax.ppermute(ends[1], axis, [(c, c - ny) for c in range(n) if 0 < c // ny...  23.9 us
    dot_general x11, matrix products, product(): lax.dot_general(a, b, (((ca,), (cb,)), ((), ())), precision=precision)  21 us
    unnamed x7, other arithmetic  16.5 us
  transfers between devices with their start and end apart: 39, of which 13 were waited for; matrix products, arithmetic and copies ran while one was open for 16% of the time, Pallas kernels for 13%

profile of v10, /device:TPU:0, one launch (start us, length us, event | category | flops | bytes accessed | tf_op | source)
XLA Modules:
  0.0 542.6 jit_solution(1852481657446760908)
XLA Ops:
  0.6 2.4 slice_bitcast_fusion.6
  4.3 6.6 %collective-permute-start = (f32[512,512]{1,0:T(8,128)}, f32[512,512]{1,0:T(8,128)}, u32[]{:S(2)}, u32[]{:S(2)}) collective-permute-start(f32[512,512]{1,0:T(8,128)} %slice_bitcast_fusion.6), channel_id=1, source_target_pairs={{0,2},{1,3},{2,4},{3,5},{4,6},{5,7},{8,10},{9,11},{10,12},{11,13},... | collective-permute-start | bytes 3145736 | tf_op jit(solution)/shard_map/ppermute | solution.py:241
  19.8 1.6 constant_dynamic-slice_fusion.14
  33.7 5.6 %dynamic-slice_bitcast_fusion.1 = (f32[256,512]{1,0:T(8,128)S(1)}, f32[256,512]{1,0:T(8,128)S(1)}, f32[256,512]{1,0:T(8,128)S(1)}, f32[256,512]{1,0:T(8,128)S(1)...) fusion(f32[1,4096,512]{2,1,0:T(8,128)} %param.3, ...), kind=kLoop, calls=%fused_computation.65 | loop fusion | bytes 16777280 | tf_op jit(solution)/shard_map/dynamic_slice | solution.py:304
  43.0 1.9 collective-permute-start.3
  46.0 1.6 pad_maximum_fusion.3
  47.6 4.3 collective-permute-done.3
  53.3 1.7 collective-permute-start.6
  55.0 23.9 %collective-permute-done.4 = f32[512,512]{1,0:T(8,128)S(1)} collective-permute-done((f32[512,512]{1,0:T(8,128)}, f32[512,512]{1,0:T(8,128)S(1)}, u32[]{:S(2)}, u32[]{:S(2)}) %collective-permute-start.4) | collective-permute-done | bytes 1048608 | tf_op jit(solution)/shard_map/ppermute | solution.py:242
  80.2 1.7 collective-permute-start.7
  81.9 1.8 collective-permute-start.12
  86.7 27.1 %collective-permute-done.9 = f32[64,512]{0,1:T(8,128)S(1)} collective-permute-done((f32[64,512]{0,1:T(8,128)S(1)}, f32[64,512]{0,1:T(8,128)S(1)}, u32[]{:S(2)}, u32[]{:S(2)}) %collective-permute-start.9) | collective-permute-done | bytes 131104 | tf_op jit(solution)/shard_map/ppermute | solution.py:143
  114.0 5.1 select_add_fusion.3
  120.1 5.3 collective-permute-start.10
  125.4 2.3 fusion.13
  127.7 3.7 collective-permute-done.10
  132.7 3.2 collective-permute-start.11
  135.9 1.9 pad_maximum_fusion
  137.9 10.2 %collective-permute-done.11 = f32[16,512]{0,1:T(8,128)S(1)} collective-permute-done((f32[16,512]{0,1:T(8,128)S(1)}, f32[16,512]{0,1:T(8,128)S(1)}, u32[]{:S(2)}, u32[]{:S(2)}) %collective-permute-start.11) | collective-permute-done | bytes 32800 | tf_op jit(solution)/shard_map/ppermute | solution.py:143
  148.3 8.5 %collective-permute-done.8 = f32[512,512]{1,0:T(8,128)} collective-permute-done((f32[512,512]{1,0:T(8,128)}, f32[512,512]{1,0:T(8,128)}, u32[]{:S(2)}, u32[]{:S(2)}) %collective-permute-start.8) | collective-permute-done | bytes 1048608 | tf_op jit(solution)/shard_map/ppermute | solution.py:248
  158.4 1.8 broadcast_select_fusion.5
  161.3 5.2 collective-permute-start.17
  182.9 8.2 %collective-permute-start.18 = (f32[64,512]{1,0:T(8,128)S(1)}, f32[64,512]{1,0:T(8,128)S(1)}, u32[]{:S(2)}, u32[]{:S(2)}) collective-permute-start(f32[64,512]{1,0:T(8,128)S(1)} %pad_maximum_fusion.15), channel_id=1, source_target_pairs={{0,1},{1,0},{2,3},{3,2},{4,5},{5,4},{6,7},{7,6},{8,9},{9,8},{10,11... | collective-permute-start | bytes 393224 | tf_op jit(solution)/shard_map/ppermute | solution.py:143
  191.1 2.3 bitcast_dynamic-update-slice_fusion.6
  193.4 58.4 %collective-permute-done.18 = f32[64,512]{1,0:T(8,128)S(1)} collective-permute-done((f32[64,512]{1,0:T(8,128)S(1)}, f32[64,512]{1,0:T(8,128)S(1)}, u32[]{:S(2)}, u32[]{:S(2)}) %collective-permute-start.18) | collective-permute-done | bytes 131104 | tf_op jit(solution)/shard_map/ppermute | solution.py:143
  251.9 1.6 collective-permute-start.27
  253.5 21.7 %shard_map.58 = f32[512,512]{1,0:T(8,128)S(1)} custom-call(f32[512,512]{1,0:T(8,128)S(1)} %select_add_fusion.2.a_ref), custom_call_target="tpu_custom_call" | custom-call | flops 134217728 | bytes 2097152 | tf_op jit(solution)/shard_map/pallas_call | solution.py:86
  275.2 56.5 %collective-permute-done.15 = f32[512,512]{1,0:T(8,128)} collective-permute-done((f32[512,512]{1,0:T(8,128)}, f32[512,512]{1,0:T(8,128)}, u32[]{:S(2)}, u32[]{:S(2)}) %collective-permute-start.15) | collective-permute-done | bytes 1048608 | tf_op jit(solution)/shard_map/ppermute | solution.py:334
  331.7 2.2 fusion.7
  337.0 2.2 fusion.3
  341.9 2.2 fusion.2
  344.1 2.2 fusion.1
  346.3 2.2 fusion.factor_ref
  348.6 3.3 copy-done.2
  353.4 1.6 copy.90.left_ref
  355.0 41.0 %collective-permute-done.26 = f32[512,512]{1,0:T(8,128)} collective-permute-done((f32[512,512]{1,0:T(8,128)}, f32[512,512]{1,0:T(8,128)}, u32[]{:S(2)}, u32[]{:S(2)}) %collective-permute-start.26) | collective-permute-done | bytes 1048608 | tf_op jit(solution)/shard_map/ppermute | solution.py:334
  396.0 2.4 bitcast_dynamic-update-slice_fusion.5
  398.4 2.4 bitcast_dynamic-update-slice_fusion.4
  400.8 2.3 bitcast_dynamic-update-slice_fusion.3
  403.1 2.4 bitcast_dynamic-update-slice_fusion.2
  405.5 2.3 bitcast_dynamic-update-slice_fusion.1
  407.8 2.3 bitcast_dynamic-update-slice_fusion.piece_ref
  410.2 4.6 shard_map.59
  417.1 2.7 fusion.9
  423.7 1.7 collective-permute-start.29
  427.1 4.9 collective-permute-done.29
  433.0 1.7 collective-permute-start.31
  435.8 6.5 %shard_map.61 = f32[4,512,256]{2,1,0:T(8,128)} custom-call(s32[4]{0:T(128)} %dynamic_slice.356.slot_ref, s32[4]{0:T(128)} %get-tuple-element.156.place_ref, s32[4]{0:T(128)} %get-tuple-element.108.part_ref, s32[4]{0:T(128)} %get-tuple-element.104.keep_ref, bf16[512,1536]{1,0:T(8,128)(2,1)} %copy.90.left_ref, f32[8,512,512]{2,1,0:T(8,128)} %copy-done.2, ...), custom_call_target="tpu_custom_call" | custom-call | flops 1610612736 | bytes 6291456 | tf_op jit(solution)/shard_map/pallas_call | solution.py:117
  443.7 2.4 collective-permute-done.21
  446.1 1.7 collective-permute-start.23
  447.8 4.9 collective-permute-done.23
  454.9 2.3 collective-permute-start.34
  457.1 2.3 collective-permute-start.33
  459.4 2.3 collective-permute-start.35
  463.1 6.5 %shard_map.60 = f32[4,512,256]{2,1,0:T(8,128)} custom-call(s32[4]{0:T(128)} %dynamic_slice.352.slot_ref, s32[4]{0:T(128)} %get-tuple-element.155.place_ref, s32[4]{0:T(128)} %get-tuple-element.109.part_ref, s32[4]{0:T(128)} %get-tuple-element.105.keep_ref, bf16[512,1536]{1,0:T(8,128)(2,1)} %copy.90.left_ref, f32[8,512,512]{2,1,0:T(8,128)} %copy-done.2, ...), custom_call_target="tpu_custom_call" | custom-call | flops 1610612736 | bytes 6291456 | tf_op jit(solution)/shard_map/pallas_call | solution.py:117
  470.2 6.8 %shard_map.64 = f32[4,512,256]{2,1,0:T(8,128)} custom-call(s32[4]{0:T(128)} %dynamic_slice.364.slot_ref, s32[4]{0:T(128)} %get-tuple-element.158.place_ref, s32[4]{0:T(128)} %get-tuple-element.106.part_ref, s32[4]{0:T(128)} %get-tuple-element.102.keep_ref, bf16[512,1536]{1,0:T(8,128)(2,1)} %copy.90.left_ref, f32[8,512,512]{2,1,0:T(8,128)} %copy-done.2, ...), custom_call_target="tpu_custom_call" | custom-call | flops 1610612736 | bytes 6291456 | tf_op jit(solution)/shard_map/pallas_call | solution.py:117
  477.6 3.2 add.489
  480.9 21.5 %shard_map.62.inverse_ref = f32[512,512]{1,0:T(8,128)S(1)} custom-call(f32[512,512]{1,0:T(8,128)S(1)} %pad_maximum_fusion.9.a_ref), custom_call_target="tpu_custom_call" | custom-call | flops 134217728 | bytes 2097152 | tf_op jit(solution)/shard_map/pallas_call | solution.py:86
  502.4 2.4 add_add_fusion
  504.8 3.5 collective-permute-start.36
  508.3 3.2 convolution_bitcast_fusion.8
  512.1 6.5 %shard_map.63.rest_0_ = f32[4,512,256]{2,1,0:T(8,128)} custom-call(s32[4]{0:T(128)} %dynamic_slice.360.slot_ref, s32[4]{0:T(128)} %get-tuple-element.157.place_ref, s32[4]{0:T(128)} %get-tuple-element.107.part_ref, s32[4]{0:T(128)} %get-tuple-element.103.keep_ref, bf16[512,1536]{1,0:T(8,128)(2,1)} %copy.90.left_ref, f32[8,512,512]{2,1,0:T(8,128)} %copy-done.2, ...), custom_call_target="tpu_custom_call" | custom-call | flops 1610612736 | bytes 6291456 | tf_op jit(solution)/shard_map/pallas_call | solution.py:117
  519.7 12.0 %collective-permute-done.36 = f32[512,512]{1,0:T(8,128)S(1)} collective-permute-done((f32[512,512]{1,0:T(8,128)S(1)}, f32[512,512]{1,0:T(8,128)S(1)}, u32[]{:S(2)}, u32[]{:S(2)}) %collective-permute-start.36) | collective-permute-done | bytes 1048608 | tf_op jit(solution)/shard_map/ppermute | solution.py:269
  534.9 7.5 %shard_map.65 = f32[1024,512]{1,0:T(8,128)} custom-call(f32[1024,512]{1,0:T(8,128)S(1)} %copy-done, f32[4,256,512]{2,1,0:T(8,128)} %bitcast.175, f32[512,512]{1,0:T(8,128)S(1)} %shard_map.62.inverse_ref, f32[512,512]{1,0:T(8,128)S(1)} %fusion.21.mine_ref, f32[4,512,256]{2,1,0:T(8,128)} %shard_map.63.rest_0_, f32[4,512,256]{2,1,0:T(8,128)} %copy-done.10, ...), custom_call_target="tpu_custom_call" | custom-call | flops 3221225472 | bytes 16777216 | tf_op jit(solution)/shard_map/pallas_call | solution.py:216
  (170 shorter events, 57.2 us)
Async XLA Ops:
  0.6 21.3 %slice-start = ((f32[1024,512]{1,0:T(8,128)}), f32[512,512]{1,0:T(8,128)S(1)}, s32[]{:S(2)}) async-start(f32[1024,512]{1,0:T(8,128)} %parent_ref.1), calls=%async_computation | async-start | bytes 2097152 | tf_op jit(solution)/shard_map/slice | solution.py:326
  3.0 48.9 %collective-permute-start.1 = (f32[512,512]{1,0:T(8,128)}, f32[512,512]{1,0:T(8,128)}, u32[]{:S(2)}, u32[]{:S(2)}) collective-permute-start(f32[512,512]{1,0:T(8,128)} %slice_bitcast_fusion.6), channel_id=1, source_target_pairs={{2,0},{3,1},{4,2},{5,3},{6,4},{7,5},{10,8},{11,9},{12,10},{13,11},... | collective-permute-start | bytes 3145736 | tf_op jit(solution)/shard_map/ppermute | solution.py:242
  4.3 47.7 %collective-permute-start = (f32[512,512]{1,0:T(8,128)}, f32[512,512]{1,0:T(8,128)}, u32[]{:S(2)}, u32[]{:S(2)}) collective-permute-start(f32[512,512]{1,0:T(8,128)} %slice_bitcast_fusion.6), channel_id=1, source_target_pairs={{0,2},{1,3},{2,4},{3,5},{4,6},{5,7},{8,10},{9,11},{10,12},{11,13},... | collective-permute-start | bytes 3145736 | tf_op jit(solution)/shard_map/ppermute | solution.py:241
  17.7 68.8 %copy-start.16 = (s32[16]{0:T(128)}, s32[16]{0:T(128)S(1)}, u32[]{:S(2)}) copy-start(s32[16]{0:T(128)S(1)} %gather_fusion.1) | copy-start | bytes 196
  22.3 16.9 %copy-start.7 = (f32[512,512]{0,1:T(8,128)}, f32[512,512]{0,1:T(8,128)S(1)}, u32[]{:S(2)}) copy-start(f32[512,512]{0,1:T(8,128)S(1)} %copy.108) | copy-start | bytes 3145732
  23.5 18.3 %collective-permute-start.2 = (f32[256,512]{0,1:T(8,128)}, f32[256,512]{0,1:T(8,128)}, u32[]{:S(2)}, u32[]{:S(2)}) collective-permute-start(f32[256,512]{0,1:T(8,128)} %constant_dynamic-slice_fusion.10), channel_id=1, source_target_pairs={{0,8},{8,0},{16,24},{24,16},{1,9},{9,1},{17,25},{25,17},{2,10},{10... | collective-permute-start | bytes 1572872 | tf_op jit(solution)/shard_map/ppermute | solution.py:143
  43.0 8.9 %collective-permute-start.3 = (f32[128,512]{0,1:T(8,128)S(1)}, f32[128,512]{0,1:T(8,128)S(1)}, u32[]{:S(2)}, u32[]{:S(2)}) collective-permute-start(f32[128,512]{0,1:T(8,128)S(1)} %constant_dynamic-slice_fusion.9), channel_id=1, source_target_pairs={{0,16},{8,24},{16,0},{24,8},{1,17},{9,25},{17,1},{25,9},{2,18},{10... | collective-permute-start | bytes 786440 | tf_op jit(solution)/shard_map/ppermute | solution.py:143
  52.0 27.0 %collective-permute-start.4 = (f32[512,512]{1,0:T(8,128)}, f32[512,512]{1,0:T(8,128)S(1)}, u32[]{:S(2)}, u32[]{:S(2)}) collective-permute-start(f32[512,512]{1,0:T(8,128)} %collective-permute-done.1), channel_id=1, source_target_pairs={{2,0},{3,1},{4,2},{5,3},{10,8},{11,9},{12,10},{13,11},{18,16},{19,... | collective-permute-start | bytes 3145736 | tf_op jit(solution)/shard_map/ppermute | solution.py:242
  53.3 27.0 %collective-permute-start.6 = (f32[512,512]{1,0:T(8,128)}, f32[512,512]{1,0:T(8,128)}, u32[]{:S(2)}, u32[]{:S(2)}) collective-permute-start(f32[512,512]{1,0:T(8,128)} %collective-permute-done), channel_id=1, source_target_pairs={{2,4},{3,5},{4,6},{5,7},{10,12},{11,13},{12,14},{13,15},{18,20},{1... | collective-permute-start | bytes 3145736 | tf_op jit(solution)/shard_map/ppermute | solution.py:241
  78.9 35.0 %copy-start.12 = (f32[512,512]{1,0:T(8,128)}, f32[512,512]{1,0:T(8,128)S(1)}, u32[]{:S(2)}) copy-start(f32[512,512]{1,0:T(8,128)S(1)} %collective-permute-done.4) | copy-start | bytes 3145732
  78.9 35.0 %collective-permute-start.5 = (f32[512,512]{1,0:T(8,128)S(1)}, f32[512,512]{1,0:T(8,128)}, u32[]{:S(2)}, u32[]{:S(2)}) collective-permute-start(f32[512,512]{1,0:T(8,128)S(1)} %collective-permute-done.4), channel_id=1, source_target_pairs={{2,0},{3,1},{10,8},{11,9},{18,16},{19,17},{26,24},{27,25}} | collective-permute-start | bytes 3145736 | tf_op jit(solution)/shard_map/ppermute | solution.py:242
  80.2 33.8 %collective-permute-start.7 = (f32[512,512]{1,0:T(8,128)}, f32[512,512]{1,0:T(8,128)}, u32[]{:S(2)}, u32[]{:S(2)}) collective-permute-start(f32[512,512]{1,0:T(8,128)} %collective-permute-done.6), channel_id=1, source_target_pairs={{4,6},{5,7},{12,14},{13,15},{20,22},{21,23},{28,30},{29,31}} | collective-permute-start | bytes 3145736 | tf_op jit(solution)/shard_map/ppermute | solution.py:241
  81.9 87.7 %collective-permute-start.12 = (f32[512,512]{1,0:T(8,128)}, f32[512,512]{1,0:T(8,128)}, u32[]{:S(2)}, u32[]{:S(2)}) collective-permute-start(f32[512,512]{1,0:T(8,128)} %slice_bitcast_fusion.6), channel_id=1, source_target_pairs={{0,1},{1,0},{2,3},{3,2},{4,5},{5,4},{6,7},{7,6},{8,9},{9,8},{10,11... | collective-permute-start | bytes 3145736 | tf_op jit(solution)/shard_map/ppermute | solution.py:248
  83.8 30.0 %collective-permute-start.9 = (f32[64,512]{0,1:T(8,128)S(1)}, f32[64,512]{0,1:T(8,128)S(1)}, u32[]{:S(2)}, u32[]{:S(2)}) collective-permute-start(f32[64,512]{0,1:T(8,128)S(1)} %constant_dynamic-slice_fusion.8), channel_id=1, source_target_pairs={{0,1},{1,0},{2,3},{3,2},{4,5},{5,4},{6,7},{7,6},{8,9},{9,8},{10,11... | collective-permute-start | bytes 393224 | tf_op jit(solution)/shard_map/ppermute | solution.py:143
  85.2 97.8 %collective-permute-start.25 = (f32[512,512]{1,0:T(8,128)}, f32[512,512]{1,0:T(8,128)}, u32[]{:S(2)}, u32[]{:S(2)}) collective-permute-start(f32[512,512]{1,0:T(8,128)} %pad_maximum_fusion.10), channel_id=1, source_target_pairs={{1,0},{2,3},{3,2},{4,5},{5,4},{6,7},{7,6},{9,8},{10,11},{11,10},{1... | collective-permute-start | bytes 3145736 | tf_op jit(solution)/shard_map/ppermute | solution.py:334
  119.1 29.2 %copy-start.5 = (f32[512,512]{1,0:T(8,128)}, f32[512,512]{1,0:T(8,128)S(1)}, u32[]{:S(2)}) copy-start(f32[512,512]{1,0:T(8,128)S(1)} %get-tuple-element.55) | copy-start | bytes 3145732
  119.1 74.3 %copy-start.3 = (f32[512,512]{1,0:T(8,128)}, f32[512,512]{1,0:T(8,128)S(1)}, u32[]{:S(2)}) copy-start(f32[512,512]{1,0:T(8,128)S(1)} %get-tuple-element.56) | copy-start | bytes 3145732
  119.1 37.7 %collective-permute-start.8 = (f32[512,512]{1,0:T(8,128)}, f32[512,512]{1,0:T(8,128)}, u32[]{:S(2)}, u32[]{:S(2)}) collective-permute-start(f32[512,512]{1,0:T(8,128)} %get-tuple-element.54), channel_id=1, source_target_pairs={{0,1},{1,0},{2,3},{3,2},{4,5},{5,4},{6,7},{7,6},{8,9},{9,8},{10,11... | collective-permute-start | bytes 3145736 | tf_op jit(solution)/shard_map/ppermute | solution.py:248
  120.1 11.4 %collective-permute-start.10 = (f32[32,512]{0,1:T(8,128)}, f32[32,512]{0,1:T(8,128)}, u32[]{:S(2)}, u32[]{:S(2)}) collective-permute-start(f32[32,512]{0,1:T(8,128)} %constant_dynamic-slice_fusion.7), channel_id=1, source_target_pairs={{0,2},{1,3},{2,0},{3,1},{4,6},{5,7},{6,4},{7,5},{8,10},{9,11},{10,... | collective-permute-start | bytes 196616 | tf_op jit(solution)/shard_map/ppermute | solution.py:143
  132.7 15.4 %collective-permute-start.11 = (f32[16,512]{0,1:T(8,128)S(1)}, f32[16,512]{0,1:T(8,128)S(1)}, u32[]{:S(2)}, u32[]{:S(2)}) collective-permute-start(f32[16,512]{0,1:T(8,128)S(1)} %constant_dynamic-slice_fusion.6), channel_id=1, source_target_pairs={{0,4},{1,5},{2,6},{3,7},{4,0},{5,1},{6,2},{7,3},{8,12},{9,13},{10,... | collective-permute-start | bytes 98312 | tf_op jit(solution)/shard_map/ppermute | solution.py:143
  148.2 10.2 %copy-start.13 = (f32[16,512]{0,1:T(8,128)}, f32[16,512]{0,1:T(8,128)S(1)}, u32[]{:S(2)}) copy-start(f32[16,512]{0,1:T(8,128)S(1)} %dynamic-slice_add_fusion.4) | copy-start | bytes 98308
  148.2 10.2 %collective-permute-start.16 = (f32[16,512]{0,1:T(8,128)S(1)}, f32[16,512]{0,1:T(8,128)}, u32[]{:S(2)}, u32[]{:S(2)}) collective-permute-start(f32[16,512]{0,1:T(8,128)S(1)} %dynamic-slice_add_fusion.4), channel_id=1, source_target_pairs={{0,4},{1,5},{2,6},{3,7},{4,0},{5,1},{6,2},{7,3},{8,12},{9,13},{10,... | collective-permute-start | bytes 98312 | tf_op jit(solution)/shard_map/ppermute | solution.py:143
  158.2 181.0 %collective-permute-start.19 = (f32[3,512,512]{2,1,0:T(8,128)}, f32[3,512,512]{2,1,0:T(8,128)}, u32[]{:S(2)}, u32[]{:S(2)}) collective-permute-start(f32[3,512,512]{2,1,0:T(8,128)} %pad_maximum_fusion), channel_id=1, source_target_pairs={{0,1},{1,0},{2,3},{3,2},{4,5},{5,4},{6,7},{7,6},{8,9},{9,8},{10,11... | collective-permute-start | bytes 9437192 | tf_op jit(solution)/shard_map/ppermute | solution.py:248
  158.4 177.6 %copy-start.14 = (s32[16]{0:T(128)}, s32[16]{0:T(128)S(1)}, u32[]{:S(2)}) copy-start(s32[16]{0:T(128)S(1)} %get-tuple-element.145) | copy-start | bytes 196
  158.4 177.6 %copy-start.19 = (s32[16]{0:T(128)}, s32[16]{0:T(128)S(1)}, u32[]{:S(2)}) copy-start(s32[16]{0:T(128)S(1)} %get-tuple-element.50) | copy-start | bytes 196
  161.3 10.9 %collective-permute-start.17 = (f32[32,512]{1,0:T(8,128)S(1)}, f32[32,512]{1,0:T(8,128)S(1)}, u32[]{:S(2)}, u32[]{:S(2)}) collective-permute-start(f32[32,512]{1,0:T(8,128)S(1)} %pad_maximum_fusion.16), channel_id=1, source_target_pairs={{0,2},{1,3},{2,0},{3,1},{4,6},{5,7},{6,4},{7,5},{8,10},{9,11},{10,... | collective-permute-start | bytes 196616 | tf_op jit(solution)/shard_map/ppermute | solution.py:143
  169.6 105.6 %collective-permute-start.13 = (f32[512,512]{1,0:T(8,128)}, f32[512,512]{1,0:T(8,128)}, u32[]{:S(2)}, u32[]{:S(2)}) collective-permute-start(f32[512,512]{1,0:T(8,128)} %get-tuple-element.31), channel_id=1, source_target_pairs={{1,6},{2,5},{3,4},{4,3},{5,2},{6,1},{7,0},{9,14},{10,13},{11,12},{... | collective-permute-start | bytes 3145736 | tf_op jit(solution)/shard_map/ppermute | solution.py:334
  170.9 104.3 %collective-permute-start.14 = (f32[512,512]{1,0:T(8,128)}, f32[512,512]{1,0:T(8,128)}, u32[]{:S(2)}, u32[]{:S(2)}) collective-permute-start(f32[512,512]{1,0:T(8,128)} %get-tuple-element.32), channel_id=1, source_target_pairs={{1,7},{2,4},{3,5},{4,2},{5,3},{6,0},{7,1},{9,15},{10,12},{11,13},{... | collective-permute-start | bytes 3145736 | tf_op jit(solution)/shard_map/ppermute | solution.py:334
  172.2 159.5 %collective-permute-start.15 = (f32[512,512]{1,0:T(8,128)}, f32[512,512]{1,0:T(8,128)}, u32[]{:S(2)}, u32[]{:S(2)}) collective-permute-start(f32[512,512]{1,0:T(8,128)} %pad_maximum_fusion.5), channel_id=1, source_target_pairs={{1,4},{2,7},{3,6},{4,1},{5,0},{6,3},{7,2},{9,12},{10,15},{11,14},{... | collective-permute-start | bytes 3145736 | tf_op jit(solution)/shard_map/ppermute | solution.py:334
  182.9 151.1 %copy-start.6 = (f32[512,512]{1,0:T(8,128)S(1)}, f32[512,512]{1,0:T(8,128)}, u32[]{:S(2)}) copy-start(f32[512,512]{1,0:T(8,128)} %copy-done.5) | copy-start | bytes 3145732
  182.9 68.9 %collective-permute-start.18 = (f32[64,512]{1,0:T(8,128)S(1)}, f32[64,512]{1,0:T(8,128)S(1)}, u32[]{:S(2)}, u32[]{:S(2)}) collective-permute-start(f32[64,512]{1,0:T(8,128)S(1)} %pad_maximum_fusion.15), channel_id=1, source_target_pairs={{0,1},{1,0},{2,3},{3,2},{4,5},{5,4},{6,7},{7,6},{8,9},{9,8},{10,11... | collective-permute-start | bytes 393224 | tf_op jit(solution)/shard_map/ppermute | solution.py:143
  251.8 83.1 %copy-start.4 = (f32[512,512]{1,0:T(8,128)S(1)}, f32[512,512]{1,0:T(8,128)}, u32[]{:S(2)}) copy-start(f32[512,512]{1,0:T(8,128)} %copy-done.3) | copy-start | bytes 3145732
  251.9 148.9 %collective-permute-start.27 = (f32[512,512]{1,0:T(8,128)}, f32[512,512]{1,0:T(8,128)}, u32[]{:S(2)}, u32[]{:S(2)}) collective-permute-start(f32[512,512]{1,0:T(8,128)} %get-tuple-element.40), channel_id=1, source_target_pairs={{1,5},{2,6},{3,7},{4,0},{5,1},{6,2},{7,3},{9,13},{10,14},{11,15},{... | collective-permute-start | bytes 3145736 | tf_op jit(solution)/shard_map/ppermute | solution.py:334
  339.3 59.1 %collective-permute-start.22 = (f32[512,512]{1,0:T(8,128)}, f32[512,512]{1,0:T(8,128)}, u32[]{:S(2)}, u32[]{:S(2)}) collective-permute-start(f32[512,512]{1,0:T(8,128)} %get-tuple-element.37), channel_id=1, source_target_pairs={{1,2},{2,1},{3,0},{4,7},{5,6},{6,5},{7,4},{9,10},{10,9},{11,8},{12... | collective-permute-start | bytes 3145736 | tf_op jit(solution)/shard_map/ppermute | solution.py:334
  340.6 55.5 %collective-permute-start.26 = (f32[512,512]{1,0:T(8,128)}, f32[512,512]{1,0:T(8,128)}, u32[]{:S(2)}, u32[]{:S(2)}) collective-permute-start(f32[512,512]{1,0:T(8,128)} %pad_maximum_fusion.8), channel_id=1, source_target_pairs={{1,3},{2,0},{3,1},{4,6},{5,7},{6,4},{7,5},{9,11},{10,8},{11,9},{12... | collective-permute-start | bytes 3145736 | tf_op jit(solution)/shard_map/ppermute | solution.py:334
  348.6 3.3 copy-start.2
  410.2 5.9 %copy-start.8 = (f32[512,512]{0,1:T(8,128)S(1)}, f32[512,512]{0,1:T(8,128)}, u32[]{:S(2)}) copy-start(f32[512,512]{0,1:T(8,128)} %copy-done.7) | copy-start | bytes 3145732
  414.8 6.4 %copy-start.17 = (s32[16]{0:T(128)S(1)}, s32[16]{0:T(128)}, u32[]{:S(2)}) copy-start(s32[16]{0:T(128)} %copy-done.16) | copy-start | bytes 196
  414.8 6.4 %copy-start.18 = (s32[16]{0:T(128)S(1)}, s32[16]{0:T(128)}, u32[]{:S(2)}) copy-start(s32[16]{0:T(128)} %get-tuple-element.51) | copy-start | bytes 196
  414.8 10.6 %copy-start.15 = (s32[16]{0:T(128)S(1)}, s32[16]{0:T(128)}, u32[]{:S(2)}) copy-start(s32[16]{0:T(128)} %copy-done.14) | copy-start | bytes 196
  414.8 20.4 %copy-start.20 = (s32[16]{0:T(128)S(1)}, s32[16]{0:T(128)}, u32[]{:S(2)}) copy-start(s32[16]{0:T(128)} %copy-done.19) | copy-start | bytes 196
  417.1 4.7 collective-permute-start.28
  420.6 5.4 collective-permute-start.20
  422.9 0.8 copy-start.11
  423.7 8.3 %collective-permute-start.29 = (f32[128,512]{1,0:T(8,128)S(1)}, f32[128,512]{1,0:T(8,128)S(1)}, u32[]{:S(2)}, u32[]{:S(2)}) collective-permute-start(f32[128,512]{1,0:T(8,128)S(1)} %constant_dynamic-slice_fusion), channel_id=1, source_target_pairs={{0,16},{8,24},{16,0},{24,8},{1,17},{9,25},{17,1},{25,9},{2,18},{10... | collective-permute-start | bytes 786440 | tf_op jit(solution)/shard_map/ppermute | solution.py:143
  433.0 9.3 %collective-permute-start.31 = (f32[128,512]{1,0:T(8,128)S(1)}, f32[128,512]{1,0:T(8,128)S(1)}, u32[]{:S(2)}, u32[]{:S(2)}) collective-permute-start(f32[128,512]{1,0:T(8,128)S(1)} %dynamic-slice_add_fusion.3), channel_id=1, source_target_pairs={{0,16},{8,24},{16,0},{24,8},{1,17},{9,25},{17,1},{25,9},{2,18},{10... | collective-permute-start | bytes 786440 | tf_op jit(solution)/shard_map/ppermute | solution.py:143
  434.7 11.4 %collective-permute-start.21 = (f32[128,512]{1,0:T(8,128)S(1)}, f32[128,512]{1,0:T(8,128)S(1)}, u32[]{:S(2)}, u32[]{:S(2)}) collective-permute-start(f32[128,512]{1,0:T(8,128)S(1)} %constant_dynamic-slice_fusion.4), channel_id=1, source_target_pairs={{0,16},{8,24},{16,0},{24,8},{1,17},{9,25},{17,1},{25,9},{2,18},{10... | collective-permute-start | bytes 786440 | tf_op jit(solution)/shard_map/ppermute | solution.py:143
  442.3 34.7 %collective-permute-start.30 = (f32[4,512,256]{2,1,0:T(8,128)}, f32[4,512,256]{2,1,0:T(8,128)}, u32[]{:S(2)}, u32[]{:S(2)}) collective-permute-start(f32[4,512,256]{2,1,0:T(8,128)} %shard_map.61), channel_id=1, source_target_pairs={{0,8},{8,0},{16,24},{24,16},{1,9},{9,1},{17,25},{25,17},{2,10},{10... | collective-permute-start | bytes 6291464 | tf_op jit(solution)/shard_map/ppermute | solution.py:143
  443.2 9.5 %collective-permute-start.32 = (f32[256,512]{1,0:T(8,128)}, f32[256,512]{1,0:T(8,128)}, u32[]{:S(2)}, u32[]{:S(2)}) collective-permute-start(f32[256,512]{1,0:T(8,128)} %pad_maximum_fusion.13), channel_id=1, source_target_pairs={{0,8},{8,0},{16,24},{24,16},{1,9},{9,1},{17,25},{25,17},{2,10},{10... | collective-permute-start | bytes 1572872 | tf_op jit(solution)/shard_map/ppermute | solution.py:143
  446.1 6.5 %collective-permute-start.23 = (f32[128,512]{1,0:T(8,128)S(1)}, f32[128,512]{1,0:T(8,128)S(1)}, u32[]{:S(2)}, u32[]{:S(2)}) collective-permute-start(f32[128,512]{1,0:T(8,128)S(1)} %add_subtract_fusion), channel_id=1, source_target_pairs={{0,16},{8,24},{16,0},{24,8},{1,17},{9,25},{17,1},{25,9},{2,18},{10... | collective-permute-start | bytes 786440 | tf_op jit(solution)/shard_map/ppermute | solution.py:143
  454.9 47.5 %collective-permute-start.34 = (f32[512,512]{1,0:T(8,128)}, f32[512,512]{1,0:T(8,128)}, u32[]{:S(2)}, u32[]{:S(2)}) collective-permute-start(f32[512,512]{1,0:T(8,128)} %pad_maximum_fusion.11), channel_id=1, source_target_pairs={{0,4},{1,5},{10,14},{11,15},{20,16},{21,17},{30,26},{31,27}} | collective-permute-start | bytes 3145736 | tf_op jit(solution)/shard_map/ppermute | solution.py:259
  457.1 45.3 %collective-permute-start.33 = (f32[512,512]{1,0:T(8,128)}, f32[512,512]{1,0:T(8,128)}, u32[]{:S(2)}, u32[]{:S(2)}) collective-permute-start(f32[512,512]{1,0:T(8,128)} %pad_maximum_fusion.11), channel_id=1, source_target_pairs={{0,2},{1,3},{10,12},{11,13},{20,22},{21,23},{30,24},{31,25}} | collective-permute-start | bytes 3145736 | tf_op jit(solution)/shard_map/ppermute | solution.py:259
  459.4 43.0 %collective-permute-start.35 = (f32[512,512]{1,0:T(8,128)}, f32[512,512]{1,0:T(8,128)}, u32[]{:S(2)}, u32[]{:S(2)}) collective-permute-start(f32[512,512]{1,0:T(8,128)} %pad_maximum_fusion.11), channel_id=1, source_target_pairs={{0,6},{1,7},{10,8},{11,9},{20,18},{21,19},{30,28},{31,29}} | collective-permute-start | bytes 3145736 | tf_op jit(solution)/shard_map/ppermute | solution.py:259
  462.5 18.3 %collective-permute-start.24 = (f32[256,512]{1,0:T(8,128)}, f32[256,512]{1,0:T(8,128)S(1)}, u32[]{:S(2)}, u32[]{:S(2)}) collective-permute-start(f32[256,512]{1,0:T(8,128)} %pad_maximum_fusion.12), channel_id=1, source_target_pairs={{0,8},{8,0},{16,24},{24,16},{1,9},{9,1},{17,25},{25,17},{2,10},{10... | collective-permute-start | bytes 1572872 | tf_op jit(solution)/shard_map/ppermute | solution.py:143
  470.2 7.4 %copy-start.9 = (f32[4,512,256]{2,1,0:T(8,128)S(1)}, f32[4,512,256]{2,1,0:T(8,128)}, u32[]{:S(2)}) copy-start(f32[4,512,256]{2,1,0:T(8,128)} %shard_map.60) | copy-start | bytes 6291460
  477.0 56.5 %collective-permute-start.37 = (f32[4,512,256]{2,1,0:T(8,128)}, f32[4,512,256]{2,1,0:T(8,128)S(1)}, u32[]{:S(2)}, u32[]{:S(2)}) collective-permute-start(f32[4,512,256]{2,1,0:T(8,128)} %shard_map.64), channel_id=1, source_target_pairs={{0,8},{8,0},{16,24},{24,16},{1,9},{9,1},{17,25},{25,17},{2,10},{10... | collective-permute-start | bytes 6291464 | tf_op jit(solution)/shard_map/ppermute | solution.py:143
  480.8 52.7 %collective-permute-start.38 = (f32[4,512,256]{2,1,0:T(8,128)}, f32[4,512,256]{2,1,0:T(8,128)}, u32[]{:S(2)}, u32[]{:S(2)}) collective-permute-start(f32[4,512,256]{2,1,0:T(8,128)} %add.489), channel_id=1, source_target_pairs={{0,16},{8,24},{16,0},{24,8},{1,17},{9,25},{17,1},{25,9},{2,18},{10... | collective-permute-start | bytes 6291464 | tf_op jit(solution)/shard_map/ppermute | solution.py:143
  504.8 26.9 %collective-permute-start.36 = (f32[512,512]{1,0:T(8,128)S(1)}, f32[512,512]{1,0:T(8,128)S(1)}, u32[]{:S(2)}, u32[]{:S(2)}) collective-permute-start(f32[512,512]{1,0:T(8,128)S(1)} %add_add_fusion), channel_id=1, source_target_pairs={{0,1},{1,0},{2,3},{3,2},{4,5},{5,4},{6,7},{7,6},{8,9},{9,8},{10,11... | collective-permute-start | bytes 3145736 | tf_op jit(solution)/shard_map/ppermute | solution.py:269
  518.6 16.2 %copy-start = (f32[1024,512]{1,0:T(8,128)S(1)}, f32[1024,512]{1,0:T(8,128)}, u32[]{:S(2)}) copy-start(f32[1024,512]{1,0:T(8,128)} %parent_ref.1) | copy-start | bytes 6291460
  519.7 22.7 %copy-start.1 = (f32[512,512]{1,0:T(8,128)}, f32[512,512]{1,0:T(8,128)S(1)}, u32[]{:S(2)}) copy-start(f32[512,512]{1,0:T(8,128)S(1)} %fusion.21.mine_ref) | copy-start | bytes 3145732
  533.5 1.4 copy-start.10

commit v11 on v9

--- a/solution.py
+++ b/solution.py
@@ -356,7 +356,7 @@
     pivots = jnp.concatenate(pivots, axis=1) if pivot_devices > 1 else pivots[0]
 
     for k in far[:EARLY]:
-        row, _ = lax.optimization_barrier((rows[k], (steps[-1], corner)))
+        row, _ = lax.optimization_barrier((rows[k], (steps[-1], corner, beside)))
         received[k] = moved(k, row)
     others = lax.optimization_barrier((jnp.stack(line[1:]), corner))[0]
     others = [from_beside(others, "col", ny, j) for j in near]
@@ -391,9 +391,8 @@
     first = join(halve(first, "branch", steps), "branch", steps)
 
     head = jnp.concatenate([factor_columns(u) for u in range(pivot_units)], axis=1)
-    head, _ = lax.optimization_barrier((head, received[far[-2]]))
     corner = corner - halve(product(head, head, 0, 0), "branch")
-    corner, _ = lax.optimization_barrier((corner, received[far[-1]]))
+    corner, _ = lax.optimization_barrier((corner, received[far[-2]]))
     corner = join(corner, "branch")
 
     owned = units_total // branches

time: 498 us -> 488 us (0.980)
  starting transfers between devices: 67.3 us -> 60.3 us
  waiting for transfers between devices: 234 us -> 227 us
    ppermute x7, waiting for transfers between devices: 136 us -> 120 us  [moved(): return lax.ppermute(rows, 'col', pairs)]
    ppermute x19, waiting for transfers between devices: 62 us -> 69.7 us  [flip(): return lax.ppermute(x, axis, [(i, i ^ bit) for i in range(n)])]
    ppermute x19, starting transfers between devices: 23.1 us -> 16.8 us  [flip(): return lax.ppermute(x, axis, [(i, i ^ bit) for i in range(n)])]
  transfers between devices with their start and end apart: 39 -> 39, of which waited for: 16 -> 15; matrix products, arithmetic and copies ran while one was open for 12% -> 14% of each run, Pallas kernels for 14% -> 14%
where the time goes in v11:
time: 488 us; the launch traced here: 480 us
  waiting for transfers between devices  227 us (47%)
  Pallas kernels  81.6 us (17%)
  starting transfers between devices  60.3 us (12%)
  other arithmetic  39 us (8%)
  local copies, waits for them, and re-layouts  28.2 us (6%)
  between operations  27.6 us (6%)
  matrix products  17 us (3%)
    ppermute x7, waiting for transfers between devices, moved(): return lax.ppermute(rows, 'col', pairs)  120 us
    ppermute x19, waiting for transfers between devices, flip(): return lax.ppermute(x, axis, [(i, i ^ bit) for i in range(n)])  69.7 us
    pallas_call x2, Pallas kernels, inverse_factor(): pl.pallas_call(inverse_factor_kernel, out_shape=jax.ShapeDtypeStruct((n,...  43.1 us
    pallas_call x5, Pallas kernels, spread_update(): pl.pallas_call(spread_kernel, grid_spec=pltpu.PrefetchScalarGridSpec(num_...  31 us
    ppermute x3, waiting for transfers between devices, line_gather(): lax.ppermute(ends[1], axis, [(c, c - ny) for c in range(n) if 0 < c // ny...  24.9 us
    dot_general x11, matrix products, product(): lax.dot_general(a, b, (((ca,), (cb,)), ((), ())), precision=precision)  17 us
    ppermute x19, starting transfers between devices, flip(): return lax.ppermute(x, axis, [(i, i ^ bit) for i in range(n)])  16.8 us
    ppermute x1, waiting for transfers between devices, share_beside(): shares.append(lax.ppermute(got, 'col', pairs))  12 us
  transfers between devices with their start and end apart: 39, of which 15 were waited for; matrix products, arithmetic and copies ran while one was open for 14% of the time, Pallas kernels for 14%

profile of v11, /device:TPU:0, one launch (start us, length us, event | category | flops | bytes accessed | tf_op | source)
XLA Modules:
  0.0 480.2 jit_solution(5749570838980015582)
XLA Ops:
  0.6 2.4 slice_bitcast_fusion.6
  3.0 5.9 %collective-permute-start = (f32[512,512]{1,0:T(8,128)}, f32[512,512]{1,0:T(8,128)}, u32[]{:S(2)}, u32[]{:S(2)}) collective-permute-start(f32[512,512]{1,0:T(8,128)} %slice_bitcast_fusion.6), channel_id=1, source_target_pairs={{0,2},{1,3},{2,4},{3,5},{4,6},{5,7},{8,10},{9,11},{10,12},{11,13},... | collective-permute-start | bytes 3145736 | tf_op jit(solution)/shard_map/ppermute | solution.py:241
  19.1 1.6 constant_dynamic-slice_fusion.14
  33.1 5.6 %dynamic-slice_bitcast_fusion.1 = (f32[256,512]{1,0:T(8,128)S(1)}, f32[256,512]{1,0:T(8,128)S(1)}, f32[256,512]{1,0:T(8,128)S(1)}, f32[256,512]{1,0:T(8,128)S(1)...) fusion(f32[1,4096,512]{2,1,0:T(8,128)} %param.3, ...), kind=kLoop, calls=%fused_computation.65 | loop fusion | bytes 16777280 | tf_op jit(solution)/shard_map/dynamic_slice | solution.py:304
  38.7 1.5 pad_maximum_fusion.6
  42.4 1.5 collective-permute-start.3
  45.0 1.6 pad_maximum_fusion.3
  46.6 4.6 collective-permute-done.3
  51.3 1.3 collective-permute-start.4
  52.6 1.6 collective-permute-start.6
  54.2 24.9 %collective-permute-done.4 = f32[512,512]{1,0:T(8,128)S(1)} collective-permute-done((f32[512,512]{1,0:T(8,128)}, f32[512,512]{1,0:T(8,128)S(1)}, u32[]{:S(2)}, u32[]{:S(2)}) %collective-permute-start.4) | collective-permute-done | bytes 1048608 | tf_op jit(solution)/shard_map/ppermute | solution.py:242
  80.4 1.7 collective-permute-start.7
  82.2 1.6 collective-permute-start.9
  84.3 7.2 %collective-permute-done.9 = f32[64,512]{0,1:T(8,128)S(1)} collective-permute-done((f32[64,512]{0,1:T(8,128)S(1)}, f32[64,512]{0,1:T(8,128)S(1)}, u32[]{:S(2)}, u32[]{:S(2)}) %collective-permute-start.9) | collective-permute-done | bytes 131104 | tf_op jit(solution)/shard_map/ppermute | solution.py:143
  91.8 3.7 collective-permute-start.10
  97.9 13.0 %collective-permute-done.10 = f32[32,512]{0,1:T(8,128)S(1)} collective-permute-done((f32[32,512]{0,1:T(8,128)S(1)}, f32[32,512]{0,1:T(8,128)S(1)}, u32[]{:S(2)}, u32[]{:S(2)}) %collective-permute-start.10) | collective-permute-done | bytes 65568 | tf_op jit(solution)/shard_map/ppermute | solution.py:143
  111.2 2.8 collective-permute-start.11
  114.0 10.4 %collective-permute-done.11 = f32[16,512]{0,1:T(8,128)S(1)} collective-permute-done((f32[16,512]{0,1:T(8,128)S(1)}, f32[16,512]{0,1:T(8,128)S(1)}, u32[]{:S(2)}, u32[]{:S(2)}) %collective-permute-start.11) | collective-permute-done | bytes 32800 | tf_op jit(solution)/shard_map/ppermute | solution.py:143
  125.3 12.3 %collective-permute-done.12 = f32[16,512]{0,1:T(8,128)S(1)} collective-permute-done((f32[16,512]{0,1:T(8,128)S(1)}, f32[16,512]{0,1:T(8,128)S(1)}, u32[]{:S(2)}, u32[]{:S(2)}) %collective-permute-start.12) | collective-permute-done | bytes 32800 | tf_op jit(solution)/shard_map/ppermute | solution.py:143
  138.6 3.6 collective-permute-done.13
  142.2 1.6 collective-permute-start.14
  143.8 5.1 %select_add_fusion.3 = (f32[512,512]{1,0:T(8,128)}, f32[512,512]{1,0:T(8,128)S(1)}, f32[512,512]{1,0:T(8,128)S(1)}, f32[512,512]{1,0:T(8,128)S(1)}) fusion(pred[]{:T(512)S(6)} %eq.104, pred[]{:T(512)S(6)} %eq.103, pred[]{:T(512)S(6)} %eq.96, pred[]{:T(512)S(6)} %eq.95, f32[1,4096,512]{2,1,0:T(8,128)} %param.3, f32[512,512]{1,0:T(8,128)} %collective-permute-done, ...), kind=kLoop, calls=%fused_computation.57 | loop fusion | flops 2621440 | bytes 11534340 | tf_op jit(solution)/shard_map/add | solution.py:350
  149.4 1.3 collective-permute-start.18
  152.0 1.5 collective-permute-start.16
  165.2 1.5 fusion.13
  166.7 1.4 bitcast_dynamic-update-slice_fusion.6
  168.4 7.5 %collective-permute-start.19 = (f32[3,512,512]{2,1,0:T(8,128)S(1)}, f32[3,512,512]{2,1,0:T(8,128)S(1)}, u32[]{:S(2)}, u32[]{:S(2)}) collective-permute-start(f32[3,512,512]{2,1,0:T(8,128)S(1)} %pad_maximum_fusion), channel_id=1, source_target_pairs={{0,1},{1,0},{2,3},{3,2},{4,5},{5,4},{6,7},{7,6},{8,9},{9,8},{10,11... | collective-permute-start | bytes 9437192 | tf_op jit(solution)/shard_map/ppermute | solution.py:248
  175.9 1.5 select_add_fusion.2.a_ref
  177.4 21.7 %shard_map.58 = f32[512,512]{1,0:T(8,128)S(1)} custom-call(f32[512,512]{1,0:T(8,128)S(1)} %select_add_fusion.2.a_ref), custom_call_target="tpu_custom_call" | custom-call | flops 134217728 | bytes 2097152 | tf_op jit(solution)/shard_map/pallas_call | solution.py:86
  199.1 1.3 collective-permute-start.26
  200.4 42.7 %collective-permute-done.18 = f32[512,512]{1,0:T(8,128)} collective-permute-done((f32[512,512]{1,0:T(8,128)}, f32[512,512]{1,0:T(8,128)}, u32[]{:S(2)}, u32[]{:S(2)}) %collective-permute-start.18) | collective-permute-done | bytes 1048608 | tf_op jit(solution)/shard_map/ppermute | solution.py:334
  245.7 2.2 fusion.7
  248.0 2.2 fusion.6
  252.2 2.2 fusion.3
  254.5 10.1 %collective-permute-done.26 = f32[512,512]{1,0:T(8,128)S(1)} collective-permute-done((f32[512,512]{1,0:T(8,128)S(1)}, f32[512,512]{1,0:T(8,128)S(1)}, u32[]{:S(2)}, u32[]{:S(2)}) %collective-permute-start.26) | collective-permute-done | bytes 1048608 | tf_op jit(solution)/shard_map/ppermute | solution.py:334
  264.7 22.3 %collective-permute-done.22 = f32[512,512]{1,0:T(8,128)S(1)} collective-permute-done((f32[512,512]{1,0:T(8,128)S(1)}, f32[512,512]{1,0:T(8,128)S(1)}, u32[]{:S(2)}, u32[]{:S(2)}) %collective-permute-start.22) | collective-permute-done | bytes 1048608 | tf_op jit(solution)/shard_map/ppermute | solution.py:334
  287.1 44.8 %collective-permute-done.27 = f32[512,512]{1,0:T(8,128)S(1)} collective-permute-done((f32[512,512]{1,0:T(8,128)S(1)}, f32[512,512]{1,0:T(8,128)S(1)}, u32[]{:S(2)}, u32[]{:S(2)}) %collective-permute-start.27) | collective-permute-done | bytes 1048608 | tf_op jit(solution)/shard_map/ppermute | solution.py:334
  332.1 1.4 bitcast_dynamic-update-slice_fusion.2
  333.4 1.4 bitcast_dynamic-update-slice_fusion.1
  334.8 1.4 bitcast_dynamic-update-slice_fusion.piece_ref
  339.3 3.3 copy-done.2
  343.9 1.6 copy.90.left_ref
  345.6 4.6 shard_map.59
  356.0 1.6 collective-permute-start.29
  358.8 6.5 %shard_map.61 = f32[4,512,256]{2,1,0:T(8,128)} custom-call(s32[4]{0:T(128)} %dynamic_slice.356.slot_ref, s32[4]{0:T(128)} %get-tuple-element.154.place_ref, s32[4]{0:T(128)} %get-tuple-element.106.part_ref, s32[4]{0:T(128)} %get-tuple-element.102.keep_ref, bf16[512,1536]{1,0:T(8,128)(2,1)} %copy.90.left_ref, f32[8,512,512]{2,1,0:T(8,128)} %copy-done.2, ...), custom_call_target="tpu_custom_call" | custom-call | flops 1610612736 | bytes 6291456 | tf_op jit(solution)/shard_map/pallas_call | solution.py:117
  366.1 1.6 collective-permute-start.21
  367.6 6.9 %collective-permute-done.31 = f32[128,512]{1,0:T(8,128)S(1)} collective-permute-done((f32[128,512]{1,0:T(8,128)S(1)}, f32[128,512]{1,0:T(8,128)S(1)}, u32[]{:S(2)}, u32[]{:S(2)}) %collective-permute-start.31) | collective-permute-done | bytes 262176 | tf_op jit(solution)/shard_map/ppermute | solution.py:143
  375.4 4.3 collective-permute-done.21
  380.4 7.4 %collective-permute-done.23 = f32[128,512]{1,0:T(8,128)S(1)} collective-permute-done((f32[128,512]{1,0:T(8,128)S(1)}, f32[128,512]{1,0:T(8,128)S(1)}, u32[]{:S(2)}, u32[]{:S(2)}) %collective-permute-start.23) | collective-permute-done | bytes 262176 | tf_op jit(solution)/shard_map/ppermute | solution.py:143
  390.1 2.3 collective-permute-start.33
  392.3 2.3 collective-permute-start.34
  394.6 2.3 collective-permute-start.35
  398.2 6.5 %shard_map.60 = f32[4,512,256]{2,1,0:T(8,128)} custom-call(s32[4]{0:T(128)} %dynamic_slice.352.slot_ref, s32[4]{0:T(128)} %get-tuple-element.153.place_ref, s32[4]{0:T(128)} %get-tuple-element.107.part_ref, s32[4]{0:T(128)} %get-tuple-element.103.keep_ref, bf16[512,1536]{1,0:T(8,128)(2,1)} %copy.90.left_ref, f32[8,512,512]{2,1,0:T(8,128)} %copy-done.2, ...), custom_call_target="tpu_custom_call" | custom-call | flops 1610612736 | bytes 6291456 | tf_op jit(solution)/shard_map/pallas_call | solution.py:117
  405.3 6.8 %shard_map.64 = f32[4,512,256]{2,1,0:T(8,128)} custom-call(s32[4]{0:T(128)} %dynamic_slice.364.slot_ref, s32[4]{0:T(128)} %get-tuple-element.156.place_ref, s32[4]{0:T(128)} %get-tuple-element.104.part_ref, s32[4]{0:T(128)} %get-tuple-element.100.keep_ref, bf16[512,1536]{1,0:T(8,128)(2,1)} %copy.90.left_ref, f32[8,512,512]{2,1,0:T(8,128)} %copy-done.2, ...), custom_call_target="tpu_custom_call" | custom-call | flops 1610612736 | bytes 6291456 | tf_op jit(solution)/shard_map/pallas_call | solution.py:117
  412.7 3.2 add.489
  416.2 21.5 %shard_map.62.inverse_ref = f32[512,512]{1,0:T(8,128)S(1)} custom-call(f32[512,512]{1,0:T(8,128)S(1)} %pad_maximum_fusion.9.a_ref), custom_call_target="tpu_custom_call" | custom-call | flops 134217728 | bytes 2097152 | tf_op jit(solution)/shard_map/pallas_call | solution.py:86
  437.7 2.4 add_add_fusion
  440.0 5.9 %collective-permute-start.36 = (f32[512,512]{1,0:T(8,128)S(1)}, f32[512,512]{1,0:T(8,128)S(1)}, u32[]{:S(2)}, u32[]{:S(2)}) collective-permute-start(f32[512,512]{1,0:T(8,128)S(1)} %add_add_fusion), channel_id=1, source_target_pairs={{0,1},{1,0},{2,3},{3,2},{4,5},{5,4},{6,7},{7,6},{8,9},{9,8},{10,11... | collective-permute-start | bytes 3145736 | tf_op jit(solution)/shard_map/ppermute | solution.py:269
  445.9 3.2 convolution_bitcast_fusion.8
  449.7 6.5 %shard_map.63.rest_0_ = f32[4,512,256]{2,1,0:T(8,128)} custom-call(s32[4]{0:T(128)} %dynamic_slice.360.slot_ref, s32[4]{0:T(128)} %get-tuple-element.155.place_ref, s32[4]{0:T(128)} %get-tuple-element.105.part_ref, s32[4]{0:T(128)} %get-tuple-element.101.keep_ref, bf16[512,1536]{1,0:T(8,128)(2,1)} %copy.90.left_ref, f32[8,512,512]{2,1,0:T(8,128)} %copy-done.2, ...), custom_call_target="tpu_custom_call" | custom-call | flops 1610612736 | bytes 6291456 | tf_op jit(solution)/shard_map/pallas_call | solution.py:117
  457.3 12.0 %collective-permute-done.36 = f32[512,512]{1,0:T(8,128)S(1)} collective-permute-done((f32[512,512]{1,0:T(8,128)S(1)}, f32[512,512]{1,0:T(8,128)S(1)}, u32[]{:S(2)}, u32[]{:S(2)}) %collective-permute-start.36) | collective-permute-done | bytes 1048608 | tf_op jit(solution)/shard_map/ppermute | solution.py:269
  469.6 1.5 pad_maximum_fusion.1
  471.1 1.4 copy-done.8
  472.5 7.5 %shard_map.65 = f32[1024,512]{1,0:T(8,128)} custom-call(f32[1024,512]{1,0:T(8,128)S(1)} %copy-done, f32[4,256,512]{2,1,0:T(8,128)} %bitcast.175, f32[512,512]{1,0:T(8,128)S(1)} %shard_map.62.inverse_ref, f32[512,512]{1,0:T(8,128)S(1)} %fusion.21.mine_ref, f32[4,512,256]{2,1,0:T(8,128)} %shard_map.63.rest_0_, f32[4,512,256]{2,1,0:T(8,128)} %copy-done.8, ...), custom_call_target="tpu_custom_call" | custom-call | flops 3221225472 | bytes 16777216 | tf_op jit(solution)/shard_map/pallas_call | solution.py:216
  (169 shorter events, 46.0 us)
Async XLA Ops:
  0.6 20.6 %slice-start = ((f32[1024,512]{1,0:T(8,128)}), f32[512,512]{1,0:T(8,128)S(1)}, s32[]{:S(2)}) async-start(f32[1024,512]{1,0:T(8,128)} %parent_ref.1), calls=%async_computation | async-start | bytes 2097152 | tf_op jit(solution)/shard_map/slice | solution.py:326
  3.0 48.3 %collective-permute-start = (f32[512,512]{1,0:T(8,128)}, f32[512,512]{1,0:T(8,128)}, u32[]{:S(2)}, u32[]{:S(2)}) collective-permute-start(f32[512,512]{1,0:T(8,128)} %slice_bitcast_fusion.6), channel_id=1, source_target_pairs={{0,2},{1,3},{2,4},{3,5},{4,6},{5,7},{8,10},{9,11},{10,12},{11,13},... | collective-permute-start | bytes 3145736 | tf_op jit(solution)/shard_map/ppermute | solution.py:241
  8.9 42.4 %collective-permute-start.1 = (f32[512,512]{1,0:T(8,128)}, f32[512,512]{1,0:T(8,128)}, u32[]{:S(2)}, u32[]{:S(2)}) collective-permute-start(f32[512,512]{1,0:T(8,128)} %slice_bitcast_fusion.6), channel_id=1, source_target_pairs={{2,0},{3,1},{4,2},{5,3},{6,4},{7,5},{10,8},{11,9},{12,10},{13,11},... | collective-permute-start | bytes 3145736 | tf_op jit(solution)/shard_map/ppermute | solution.py:242
  17.1 136.4 %copy-start.16 = (s32[16]{0:T(128)}, s32[16]{0:T(128)S(1)}, u32[]{:S(2)}) copy-start(s32[16]{0:T(128)S(1)} %gather_fusion.1) | copy-start | bytes 196
  21.6 17.1 %copy-start.5 = (f32[512,512]{0,1:T(8,128)}, f32[512,512]{0,1:T(8,128)S(1)}, u32[]{:S(2)}) copy-start(f32[512,512]{0,1:T(8,128)S(1)} %copy.108) | copy-start | bytes 3145732
  22.8 18.5 %collective-permute-start.2 = (f32[256,512]{0,1:T(8,128)}, f32[256,512]{0,1:T(8,128)}, u32[]{:S(2)}, u32[]{:S(2)}) collective-permute-start(f32[256,512]{0,1:T(8,128)} %constant_dynamic-slice_fusion.10), channel_id=1, source_target_pairs={{0,8},{8,0},{16,24},{24,16},{1,9},{9,1},{17,25},{25,17},{2,10},{10... | collective-permute-start | bytes 1572872 | tf_op jit(solution)/shard_map/ppermute | solution.py:143
  42.4 8.8 %collective-permute-start.3 = (f32[128,512]{0,1:T(8,128)S(1)}, f32[128,512]{0,1:T(8,128)S(1)}, u32[]{:S(2)}, u32[]{:S(2)}) collective-permute-start(f32[128,512]{0,1:T(8,128)S(1)} %constant_dynamic-slice_fusion.9), channel_id=1, source_target_pairs={{0,16},{8,24},{16,0},{24,8},{1,17},{9,25},{17,1},{25,9},{2,18},{10... | collective-permute-start | bytes 786440 | tf_op jit(solution)/shard_map/ppermute | solution.py:143
  51.3 27.8 %collective-permute-start.4 = (f32[512,512]{1,0:T(8,128)}, f32[512,512]{1,0:T(8,128)S(1)}, u32[]{:S(2)}, u32[]{:S(2)}) collective-permute-start(f32[512,512]{1,0:T(8,128)} %collective-permute-done.1), channel_id=1, source_target_pairs={{2,0},{3,1},{4,2},{5,3},{10,8},{11,9},{12,10},{13,11},{18,16},{19,... | collective-permute-start | bytes 3145736 | tf_op jit(solution)/shard_map/ppermute | solution.py:242
  52.6 27.8 %collective-permute-start.6 = (f32[512,512]{1,0:T(8,128)}, f32[512,512]{1,0:T(8,128)}, u32[]{:S(2)}, u32[]{:S(2)}) collective-permute-start(f32[512,512]{1,0:T(8,128)} %collective-permute-done), channel_id=1, source_target_pairs={{2,4},{3,5},{4,6},{5,7},{10,12},{11,13},{12,14},{13,15},{18,20},{1... | collective-permute-start | bytes 3145736 | tf_op jit(solution)/shard_map/ppermute | solution.py:241
  79.1 63.1 %copy-start.10 = (f32[512,512]{1,0:T(8,128)}, f32[512,512]{1,0:T(8,128)S(1)}, u32[]{:S(2)}) copy-start(f32[512,512]{1,0:T(8,128)S(1)} %collective-permute-done.4) | copy-start | bytes 3145732
  79.1 31.9 %collective-permute-start.5 = (f32[512,512]{1,0:T(8,128)S(1)}, f32[512,512]{1,0:T(8,128)}, u32[]{:S(2)}, u32[]{:S(2)}) collective-permute-start(f32[512,512]{1,0:T(8,128)S(1)} %collective-permute-done.4), channel_id=1, source_target_pairs={{2,0},{3,1},{10,8},{11,9},{18,16},{19,17},{26,24},{27,25}} | collective-permute-start | bytes 3145736 | tf_op jit(solution)/shard_map/ppermute | solution.py:242
  80.4 30.6 %collective-permute-start.7 = (f32[512,512]{1,0:T(8,128)}, f32[512,512]{1,0:T(8,128)}, u32[]{:S(2)}, u32[]{:S(2)}) collective-permute-start(f32[512,512]{1,0:T(8,128)} %collective-permute-done.6), channel_id=1, source_target_pairs={{4,6},{5,7},{12,14},{13,15},{20,22},{21,23},{28,30},{29,31}} | collective-permute-start | bytes 3145736 | tf_op jit(solution)/shard_map/ppermute | solution.py:241
  82.2 9.3 %collective-permute-start.9 = (f32[64,512]{0,1:T(8,128)S(1)}, f32[64,512]{0,1:T(8,128)S(1)}, u32[]{:S(2)}, u32[]{:S(2)}) collective-permute-start(f32[64,512]{0,1:T(8,128)S(1)} %constant_dynamic-slice_fusion.8), channel_id=1, source_target_pairs={{0,1},{1,0},{2,3},{3,2},{4,5},{5,4},{6,7},{7,6},{8,9},{9,8},{10,11... | collective-permute-start | bytes 393224 | tf_op jit(solution)/shard_map/ppermute | solution.py:143
  83.8 65.6 %collective-permute-start.15 = (f32[512,512]{1,0:T(8,128)}, f32[512,512]{1,0:T(8,128)}, u32[]{:S(2)}, u32[]{:S(2)}) collective-permute-start(f32[512,512]{1,0:T(8,128)} %slice_bitcast_fusion.6), channel_id=1, source_target_pairs={{0,1},{1,0},{2,3},{3,2},{4,5},{5,4},{6,7},{7,6},{8,9},{9,8},{10,11... | collective-permute-start | bytes 3145736 | tf_op jit(solution)/shard_map/ppermute | solution.py:248
  91.8 19.1 %collective-permute-start.10 = (f32[32,512]{0,1:T(8,128)S(1)}, f32[32,512]{0,1:T(8,128)S(1)}, u32[]{:S(2)}, u32[]{:S(2)}) collective-permute-start(f32[32,512]{0,1:T(8,128)S(1)} %constant_dynamic-slice_fusion.7), channel_id=1, source_target_pairs={{0,2},{1,3},{2,0},{3,1},{4,6},{5,7},{6,4},{7,5},{8,10},{9,11},{10,... | collective-permute-start | bytes 196616 | tf_op jit(solution)/shard_map/ppermute | solution.py:143
  96.6 70.1 %collective-permute-start.25 = (f32[512,512]{1,0:T(8,128)}, f32[512,512]{1,0:T(8,128)}, u32[]{:S(2)}, u32[]{:S(2)}) collective-permute-start(f32[512,512]{1,0:T(8,128)} %pad_maximum_fusion.10), channel_id=1, source_target_pairs={{1,0},{2,3},{3,2},{4,5},{5,4},{6,7},{7,6},{9,8},{10,11},{11,10},{1... | collective-permute-start | bytes 3145736 | tf_op jit(solution)/shard_map/ppermute | solution.py:334
  111.2 13.2 %collective-permute-start.11 = (f32[16,512]{0,1:T(8,128)S(1)}, f32[16,512]{0,1:T(8,128)S(1)}, u32[]{:S(2)}, u32[]{:S(2)}) collective-permute-start(f32[16,512]{0,1:T(8,128)S(1)} %constant_dynamic-slice_fusion.6), channel_id=1, source_target_pairs={{0,4},{1,5},{2,6},{3,7},{4,0},{5,1},{6,2},{7,3},{8,12},{9,13},{10,... | collective-permute-start | bytes 98312 | tf_op jit(solution)/shard_map/ppermute | solution.py:143
  114.0 52.7 %copy-start.14 = (s32[16]{0:T(128)}, s32[16]{0:T(128)S(1)}, u32[]{:S(2)}) copy-start(s32[16]{0:T(128)S(1)} %get-tuple-element.143) | copy-start | bytes 196
  114.0 52.7 %copy-start.19 = (s32[16]{0:T(128)}, s32[16]{0:T(128)S(1)}, u32[]{:S(2)}) copy-start(s32[16]{0:T(128)S(1)} %get-tuple-element.48) | copy-start | bytes 196
  124.5 13.1 %collective-permute-start.12 = (f32[16,512]{0,1:T(8,128)S(1)}, f32[16,512]{0,1:T(8,128)S(1)}, u32[]{:S(2)}, u32[]{:S(2)}) collective-permute-start(f32[16,512]{0,1:T(8,128)S(1)} %dynamic-slice_add_fusion.4), channel_id=1, source_target_pairs={{0,4},{1,5},{2,6},{3,7},{4,0},{5,1},{6,2},{7,3},{8,12},{9,13},{10,... | collective-permute-start | bytes 98312 | tf_op jit(solution)/shard_map/ppermute | solution.py:143
  137.8 4.3 collective-permute-start.13
  142.2 7.2 %collective-permute-start.14 = (f32[64,512]{1,0:T(8,128)S(1)}, f32[64,512]{1,0:T(8,128)S(1)}, u32[]{:S(2)}, u32[]{:S(2)}) collective-permute-start(f32[64,512]{1,0:T(8,128)S(1)} %pad_maximum_fusion.15), channel_id=1, source_target_pairs={{0,1},{1,0},{2,3},{3,2},{4,5},{5,4},{6,7},{7,6},{8,9},{9,8},{10,11... | collective-permute-start | bytes 393224 | tf_op jit(solution)/shard_map/ppermute | solution.py:143
  148.9 27.0 %copy-start.4 = (f32[512,512]{1,0:T(8,128)}, f32[512,512]{1,0:T(8,128)S(1)}, u32[]{:S(2)}) copy-start(f32[512,512]{1,0:T(8,128)S(1)} %get-tuple-element.53) | copy-start | bytes 3145732
  148.9 27.0 %collective-permute-start.8 = (f32[512,512]{1,0:T(8,128)}, f32[512,512]{1,0:T(8,128)}, u32[]{:S(2)}, u32[]{:S(2)}) collective-permute-start(f32[512,512]{1,0:T(8,128)} %get-tuple-element.52), channel_id=1, source_target_pairs={{0,1},{1,0},{2,3},{3,2},{4,5},{5,4},{6,7},{7,6},{8,9},{9,8},{10,11... | collective-permute-start | bytes 3145736 | tf_op jit(solution)/shard_map/ppermute | solution.py:248
  149.4 93.7 %collective-permute-start.18 = (f32[512,512]{1,0:T(8,128)}, f32[512,512]{1,0:T(8,128)}, u32[]{:S(2)}, u32[]{:S(2)}) collective-permute-start(f32[512,512]{1,0:T(8,128)} %pad_maximum_fusion.5), channel_id=1, source_target_pairs={{1,4},{2,7},{3,6},{4,1},{5,0},{6,3},{7,2},{9,12},{10,15},{11,14},{... | collective-permute-start | bytes 3145736 | tf_op jit(solution)/shard_map/ppermute | solution.py:334
  150.7 93.7 %collective-permute-start.17 = (f32[512,512]{1,0:T(8,128)}, f32[512,512]{1,0:T(8,128)}, u32[]{:S(2)}, u32[]{:S(2)}) collective-permute-start(f32[512,512]{1,0:T(8,128)} %get-tuple-element.31), channel_id=1, source_target_pairs={{1,7},{2,4},{3,5},{4,2},{5,3},{6,0},{7,1},{9,15},{10,12},{11,13},{... | collective-permute-start | bytes 3145736 | tf_op jit(solution)/shard_map/ppermute | solution.py:334
  152.0 93.7 %collective-permute-start.16 = (f32[512,512]{1,0:T(8,128)}, f32[512,512]{1,0:T(8,128)}, u32[]{:S(2)}, u32[]{:S(2)}) collective-permute-start(f32[512,512]{1,0:T(8,128)} %get-tuple-element.30), channel_id=1, source_target_pairs={{1,6},{2,5},{3,4},{4,3},{5,2},{6,1},{7,0},{9,14},{10,13},{11,12},{... | collective-permute-start | bytes 3145736 | tf_op jit(solution)/shard_map/ppermute | solution.py:334
  165.1 33.9 %copy-start.11 = (f32[512,512]{1,0:T(8,128)S(1)}, f32[512,512]{1,0:T(8,128)}, u32[]{:S(2)}) copy-start(f32[512,512]{1,0:T(8,128)} %pad_maximum_fusion.8) | copy-start | bytes 3145732
  165.2 78.0 %copy-start.13 = (f32[512,512]{1,0:T(8,128)S(1)}, f32[512,512]{1,0:T(8,128)}, u32[]{:S(2)}) copy-start(f32[512,512]{1,0:T(8,128)} %get-tuple-element.35) | copy-start | bytes 3145732
  165.2 79.2 %copy-start.12 = (f32[512,512]{1,0:T(8,128)S(1)}, f32[512,512]{1,0:T(8,128)}, u32[]{:S(2)}) copy-start(f32[512,512]{1,0:T(8,128)} %get-tuple-element.38) | copy-start | bytes 3145732
  168.4 167.8 %collective-permute-start.19 = (f32[3,512,512]{2,1,0:T(8,128)S(1)}, f32[3,512,512]{2,1,0:T(8,128)S(1)}, u32[]{:S(2)}, u32[]{:S(2)}) collective-permute-start(f32[3,512,512]{2,1,0:T(8,128)S(1)} %pad_maximum_fusion), channel_id=1, source_target_pairs={{0,1},{1,0},{2,3},{3,2},{4,5},{5,4},{6,7},{7,6},{8,9},{9,8},{10,11... | collective-permute-start | bytes 9437192 | tf_op jit(solution)/shard_map/ppermute | solution.py:248
  199.1 65.5 %collective-permute-start.26 = (f32[512,512]{1,0:T(8,128)S(1)}, f32[512,512]{1,0:T(8,128)S(1)}, u32[]{:S(2)}, u32[]{:S(2)}) collective-permute-start(f32[512,512]{1,0:T(8,128)S(1)} %copy-done.11), channel_id=1, source_target_pairs={{1,3},{2,0},{3,1},{4,6},{5,7},{6,4},{7,5},{9,11},{10,8},{11,9},{12... | collective-permute-start | bytes 3145736 | tf_op jit(solution)/shard_map/ppermute | solution.py:334
  243.1 43.9 %collective-permute-start.22 = (f32[512,512]{1,0:T(8,128)S(1)}, f32[512,512]{1,0:T(8,128)S(1)}, u32[]{:S(2)}, u32[]{:S(2)}) collective-permute-start(f32[512,512]{1,0:T(8,128)S(1)} %copy-done.13), channel_id=1, source_target_pairs={{1,2},{2,1},{3,0},{4,7},{5,6},{6,5},{7,4},{9,10},{10,9},{11,8},{12... | collective-permute-start | bytes 3145736 | tf_op jit(solution)/shard_map/ppermute | solution.py:334
  244.4 87.5 %collective-permute-start.27 = (f32[512,512]{1,0:T(8,128)S(1)}, f32[512,512]{1,0:T(8,128)S(1)}, u32[]{:S(2)}, u32[]{:S(2)}) collective-permute-start(f32[512,512]{1,0:T(8,128)S(1)} %copy-done.12), channel_id=1, source_target_pairs={{1,5},{2,6},{3,7},{4,0},{5,1},{6,2},{7,3},{9,13},{10,14},{11,15},{... | collective-permute-start | bytes 3145736 | tf_op jit(solution)/shard_map/ppermute | solution.py:334
  336.2 7.5 %copy-start.3 = (f32[8,512,512]{2,1,0:T(8,128)}, f32[8,512,512]{2,1,0:T(8,128)S(1)}, u32[]{:S(2)}) copy-start(f32[8,512,512]{2,1,0:T(8,128)S(1)} %bitcast_dynamic-update-slice_fusion.piece_ref) | copy-start | bytes 25165828
  339.3 3.3 copy-start.2
  345.6 5.9 %copy-start.6 = (f32[512,512]{0,1:T(8,128)S(1)}, f32[512,512]{0,1:T(8,128)}, u32[]{:S(2)}) copy-start(f32[512,512]{0,1:T(8,128)} %copy-done.5) | copy-start | bytes 3145732
  345.6 6.9 %copy-start.17 = (s32[16]{0:T(128)S(1)}, s32[16]{0:T(128)}, u32[]{:S(2)}) copy-start(s32[16]{0:T(128)} %copy-done.16) | copy-start | bytes 196
  345.6 6.9 %copy-start.18 = (s32[16]{0:T(128)S(1)}, s32[16]{0:T(128)}, u32[]{:S(2)}) copy-start(s32[16]{0:T(128)} %get-tuple-element.49) | copy-start | bytes 196
  345.6 7.6 %copy-start.9 = (f32[512,256]{1,0:T(8,128)S(1)}, f32[512,256]{1,0:T(8,128)}, u32[]{:S(2)}) copy-start(f32[512,256]{1,0:T(8,128)} %get-tuple-element.75) | copy-start | bytes 1572868
  350.2 7.3 %copy-start.15 = (s32[16]{0:T(128)S(1)}, s32[16]{0:T(128)}, u32[]{:S(2)}) copy-start(s32[16]{0:T(128)} %copy-done.14) | copy-start | bytes 196
  350.2 8.0 %copy-start.20 = (s32[16]{0:T(128)S(1)}, s32[16]{0:T(128)}, u32[]{:S(2)}) copy-start(s32[16]{0:T(128)} %copy-done.19) | copy-start | bytes 196
  352.5 2.3 collective-permute-start.28
  354.3 11.7 %collective-permute-start.20 = (f32[256,512]{1,0:T(8,128)S(1)}, f32[256,512]{1,0:T(8,128)S(1)}, u32[]{:S(2)}, u32[]{:S(2)}) collective-permute-start(f32[256,512]{1,0:T(8,128)S(1)} %constant_dynamic-slice_fusion.5), channel_id=1, source_target_pairs={{0,8},{8,0},{16,24},{24,16},{1,9},{9,1},{17,25},{25,17},{2,10},{10... | collective-permute-start | bytes 1572872 | tf_op jit(solution)/shard_map/ppermute | solution.py:143
  356.0 9.3 %collective-permute-start.29 = (f32[128,512]{1,0:T(8,128)S(1)}, f32[128,512]{1,0:T(8,128)S(1)}, u32[]{:S(2)}, u32[]{:S(2)}) collective-permute-start(f32[128,512]{1,0:T(8,128)S(1)} %constant_dynamic-slice_fusion), channel_id=1, source_target_pairs={{0,16},{8,24},{16,0},{24,8},{1,17},{9,25},{17,1},{25,9},{2,18},{10... | collective-permute-start | bytes 786440 | tf_op jit(solution)/shard_map/ppermute | solution.py:143
  365.3 46.8 %collective-permute-start.30 = (f32[4,512,256]{2,1,0:T(8,128)}, f32[4,512,256]{2,1,0:T(8,128)}, u32[]{:S(2)}, u32[]{:S(2)}) collective-permute-start(f32[4,512,256]{2,1,0:T(8,128)} %shard_map.61), channel_id=1, source_target_pairs={{0,8},{8,0},{16,24},{24,16},{1,9},{9,1},{17,25},{25,17},{2,10},{10... | collective-permute-start | bytes 6291464 | tf_op jit(solution)/shard_map/ppermute | solution.py:143
  365.4 9.2 %collective-permute-start.31 = (f32[128,512]{1,0:T(8,128)S(1)}, f32[128,512]{1,0:T(8,128)S(1)}, u32[]{:S(2)}, u32[]{:S(2)}) collective-permute-start(f32[128,512]{1,0:T(8,128)S(1)} %dynamic-slice_add_fusion.3), channel_id=1, source_target_pairs={{0,16},{8,24},{16,0},{24,8},{1,17},{9,25},{17,1},{25,9},{2,18},{10... | collective-permute-start | bytes 786440 | tf_op jit(solution)/shard_map/ppermute | solution.py:143
  366.1 13.7 %collective-permute-start.21 = (f32[128,512]{1,0:T(8,128)S(1)}, f32[128,512]{1,0:T(8,128)S(1)}, u32[]{:S(2)}, u32[]{:S(2)}) collective-permute-start(f32[128,512]{1,0:T(8,128)S(1)} %constant_dynamic-slice_fusion.4), channel_id=1, source_target_pairs={{0,16},{8,24},{16,0},{24,8},{1,17},{9,25},{17,1},{25,9},{2,18},{10... | collective-permute-start | bytes 786440 | tf_op jit(solution)/shard_map/ppermute | solution.py:143
  375.4 12.4 %collective-permute-start.32 = (f32[256,512]{1,0:T(8,128)}, f32[256,512]{1,0:T(8,128)}, u32[]{:S(2)}, u32[]{:S(2)}) collective-permute-start(f32[256,512]{1,0:T(8,128)} %pad_maximum_fusion.13), channel_id=1, source_target_pairs={{0,8},{8,0},{16,24},{24,16},{1,9},{9,1},{17,25},{25,17},{2,10},{10... | collective-permute-start | bytes 1572872 | tf_op jit(solution)/shard_map/ppermute | solution.py:143
  379.8 8.0 %collective-permute-start.23 = (f32[128,512]{1,0:T(8,128)S(1)}, f32[128,512]{1,0:T(8,128)S(1)}, u32[]{:S(2)}, u32[]{:S(2)}) collective-permute-start(f32[128,512]{1,0:T(8,128)S(1)} %add_subtract_fusion), channel_id=1, source_target_pairs={{0,16},{8,24},{16,0},{24,8},{1,17},{9,25},{17,1},{25,9},{2,18},{10... | collective-permute-start | bytes 786440 | tf_op jit(solution)/shard_map/ppermute | solution.py:143
  390.1 47.6 %collective-permute-start.33 = (f32[512,512]{1,0:T(8,128)}, f32[512,512]{1,0:T(8,128)}, u32[]{:S(2)}, u32[]{:S(2)}) collective-permute-start(f32[512,512]{1,0:T(8,128)} %pad_maximum_fusion.11), channel_id=1, source_target_pairs={{0,2},{1,3},{10,12},{11,13},{20,22},{21,23},{30,24},{31,25}} | collective-permute-start | bytes 3145736 | tf_op jit(solution)/shard_map/ppermute | solution.py:259
  392.3 45.3 %collective-permute-start.34 = (f32[512,512]{1,0:T(8,128)}, f32[512,512]{1,0:T(8,128)}, u32[]{:S(2)}, u32[]{:S(2)}) collective-permute-start(f32[512,512]{1,0:T(8,128)} %pad_maximum_fusion.11), channel_id=1, source_target_pairs={{0,4},{1,5},{10,14},{11,15},{20,16},{21,17},{30,26},{31,27}} | collective-permute-start | bytes 3145736 | tf_op jit(solution)/shard_map/ppermute | solution.py:259
  394.6 43.1 %collective-permute-start.35 = (f32[512,512]{1,0:T(8,128)}, f32[512,512]{1,0:T(8,128)}, u32[]{:S(2)}, u32[]{:S(2)}) collective-permute-start(f32[512,512]{1,0:T(8,128)} %pad_maximum_fusion.11), channel_id=1, source_target_pairs={{0,6},{1,7},{10,8},{11,9},{20,18},{21,19},{30,28},{31,29}} | collective-permute-start | bytes 3145736 | tf_op jit(solution)/shard_map/ppermute | solution.py:259
  397.7 18.3 %collective-permute-start.24 = (f32[256,512]{1,0:T(8,128)}, f32[256,512]{1,0:T(8,128)S(1)}, u32[]{:S(2)}, u32[]{:S(2)}) collective-permute-start(f32[256,512]{1,0:T(8,128)} %pad_maximum_fusion.12), channel_id=1, source_target_pairs={{0,8},{8,0},{16,24},{24,16},{1,9},{9,1},{17,25},{25,17},{2,10},{10... | collective-permute-start | bytes 1572872 | tf_op jit(solution)/shard_map/ppermute | solution.py:143
  405.3 7.4 %copy-start.7 = (f32[4,512,256]{2,1,0:T(8,128)S(1)}, f32[4,512,256]{2,1,0:T(8,128)}, u32[]{:S(2)}) copy-start(f32[4,512,256]{2,1,0:T(8,128)} %shard_map.60) | copy-start | bytes 6291460
  412.2 59.0 %collective-permute-start.37 = (f32[4,512,256]{2,1,0:T(8,128)}, f32[4,512,256]{2,1,0:T(8,128)S(1)}, u32[]{:S(2)}, u32[]{:S(2)}) collective-permute-start(f32[4,512,256]{2,1,0:T(8,128)} %shard_map.64), channel_id=1, source_target_pairs={{0,8},{8,0},{16,24},{24,16},{1,9},{9,1},{17,25},{25,17},{2,10},{10... | collective-permute-start | bytes 6291464 | tf_op jit(solution)/shard_map/ppermute | solution.py:143
  416.0 55.2 %collective-permute-start.38 = (f32[4,512,256]{2,1,0:T(8,128)}, f32[4,512,256]{2,1,0:T(8,128)}, u32[]{:S(2)}, u32[]{:S(2)}) collective-permute-start(f32[4,512,256]{2,1,0:T(8,128)} %add.489), channel_id=1, source_target_pairs={{0,16},{8,24},{16,0},{24,8},{1,17},{9,25},{17,1},{25,9},{2,18},{10... | collective-permute-start | bytes 6291464 | tf_op jit(solution)/shard_map/ppermute | solution.py:143
  440.0 29.3 %collective-permute-start.36 = (f32[512,512]{1,0:T(8,128)S(1)}, f32[512,512]{1,0:T(8,128)S(1)}, u32[]{:S(2)}, u32[]{:S(2)}) collective-permute-start(f32[512,512]{1,0:T(8,128)S(1)} %add_add_fusion), channel_id=1, source_target_pairs={{0,1},{1,0},{2,3},{3,2},{4,5},{5,4},{6,7},{7,6},{8,9},{9,8},{10,11... | collective-permute-start | bytes 3145736 | tf_op jit(solution)/shard_map/ppermute | solution.py:269
  456.2 16.2 %copy-start = (f32[1024,512]{1,0:T(8,128)S(1)}, f32[1024,512]{1,0:T(8,128)}, u32[]{:S(2)}) copy-start(f32[1024,512]{1,0:T(8,128)} %parent_ref.1) | copy-start | bytes 6291460
  457.3 22.7 %copy-start.1 = (f32[512,512]{1,0:T(8,128)}, f32[512,512]{1,0:T(8,128)S(1)}, u32[]{:S(2)}) copy-start(f32[512,512]{1,0:T(8,128)S(1)} %fusion.21.mine_ref) | copy-start | bytes 3145732
  471.1 1.4 copy-start.8

commit v12 on v11

--- a/solution.py
+++ b/solution.py
@@ -370,9 +370,9 @@
     places = col ^ source
     child_mine = product(inverse, front[:P_SIZE], 1, 0)
 
-    early = [received[k] for k in far[:EARLY]]
+    early = [received[k] for k in far[:EARLY - 1]]
     inverse, early = lax.optimization_barrier((inverse, early))
-    received.update(zip(far[:EARLY], early))
+    received.update(zip(far, early))
     factor = jnp.stack([product(inverse, x, 1, 0) for x in gathered])
 
     def factor_columns(u):
@@ -383,17 +383,16 @@
     mine_keep = jnp.repeat(lax.dynamic_slice_in_dim(keeps, col * per, per), width)[:, None] > 0
     pieces = jnp.stack([jnp.where(mine_keep, received[k], 0.0) for k in range(groups)])
     left = three_part(mine)
+    head = jnp.concatenate([factor_columns(u) for u in range(pivot_units)], axis=1)
+    corner = corner - halve(product(head, head, 0, 0), "branch")
+    left, _ = lax.optimization_barrier((left, corner))
+    corner = join(corner, "branch")
     n = pivot_units
     first = spread_update(slots[:n], places[:n], parts[:n], keeps[:n], left, factor, pieces, width)
     first = jnp.concatenate([first[u] for u in range(n)], axis=1)
     steps = []
     first = first + jnp.where(branch == 0, parent_front[:PP].T, 0.0)
     first = join(halve(first, "branch", steps), "branch", steps)
-
-    head = jnp.concatenate([factor_columns(u) for u in range(pivot_units)], axis=1)
-    corner = corner - halve(product(head, head, 0, 0), "branch")
-    corner, _ = lax.optimization_barrier((corner, received[far[-2]]))
-    corner = join(corner, "branch")
 
     owned = units_total // branches
     spread = [None] * branches

time: 488 us -> 507 us (1.039)
  starting transfers between devices: 60.3 us -> 77.3 us
    ppermute x1, starting transfers between devices: 5.93 us -> 21.4 us  [share_beside(): shares.append(lax.ppermute(got, 'col', pairs))]
    unnamed x7, other arithmetic: 6 us -> 11.7 us
  transfers between devices with their start and end apart: 39 -> 39, of which waited for: 15 -> 15; matrix products, arithmetic and copies ran while one was open for 14% -> 15% of each run, Pallas kernels for 14% -> 14%
where the time goes in v12:
time: 507 us; the launch traced here: 499 us
  waiting for transfers between devices  225 us (44%)
  Pallas kernels  81.6 us (16%)
  starting transfers between devices  77.3 us (15%)
  other arithmetic  43.6 us (9%)
  local copies, waits for them, and re-layouts  27.4 us (5%)
  between operations  26.7 us (5%)
  matrix products  17 us (3%)
    ppermute x7, waiting for transfers between devices, moved(): return lax.ppermute(rows, 'col', pairs)  116 us
    ppermute x19, waiting for transfers between devices, flip(): return lax.ppermute(x, axis, [(i, i ^ bit) for i in range(n)])  72.4 us
    pallas_call x2, Pallas kernels, inverse_factor(): pl.pallas_call(inverse_factor_kernel, out_shape=jax.ShapeDtypeStruct((n,...  43.1 us
    pallas_call x5, Pallas kernels, spread_update(): pl.pallas_call(spread_kernel, grid_spec=pltpu.PrefetchScalarGridSpec(num_...  31 us
    ppermute x3, waiting for transfers between devices, line_gather(): lax.ppermute(ends[1], axis, [(c, c - ny) for c in range(n) if 0 < c // ny...  24.9 us
    ppermute x1, starting transfers between devices, share_beside(): shares.append(lax.ppermute(got, 'col', pairs))  21.4 us
    ppermute x19, starting transfers between devices, flip(): return lax.ppermute(x, axis, [(i, i ^ bit) for i in range(n)])  18.4 us
    dot_general x11, matrix products, product(): lax.dot_general(a, b, (((ca,), (cb,)), ((), ())), precision=precision)  17 us
  transfers between devices with their start and end apart: 39, of which 15 were waited for; matrix products, arithmetic and copies ran while one was open for 15% of the time, Pallas kernels for 14%

profile of v12, /device:TPU:0, one launch (start us, length us, event | category | flops | bytes accessed | tf_op | source)
XLA Modules:
  0.0 498.7 jit_solution(4544066606734244632)
XLA Ops:
  0.6 2.4 slice_bitcast_fusion.6
  3.0 5.9 %collective-permute-start = (f32[512,512]{1,0:T(8,128)}, f32[512,512]{1,0:T(8,128)}, u32[]{:S(2)}, u32[]{:S(2)}) collective-permute-start(f32[512,512]{1,0:T(8,128)} %slice_bitcast_fusion.6), channel_id=1, source_target_pairs={{0,2},{1,3},{2,4},{3,5},{4,6},{5,7},{8,10},{9,11},{10,12},{11,13},... | collective-permute-start | bytes 3145736 | tf_op jit(solution)/shard_map/ppermute | solution.py:241
  19.1 1.6 constant_dynamic-slice_fusion.14
  32.7 5.6 %dynamic-slice_bitcast_fusion.1 = (f32[256,512]{1,0:T(8,128)S(1)}, f32[256,512]{1,0:T(8,128)S(1)}, f32[256,512]{1,0:T(8,128)S(1)}, f32[256,512]{1,0:T(8,128)S(1)...) fusion(f32[1,4096,512]{2,1,0:T(8,128)} %param.3, ...), kind=kLoop, calls=%fused_computation.65 | loop fusion | bytes 16777280 | tf_op jit(solution)/shard_map/dynamic_slice | solution.py:304
  38.3 1.5 pad_maximum_fusion.6
  42.1 1.6 collective-permute-start.3
  44.7 1.5 pad_maximum_fusion.3
  46.3 4.7 collective-permute-done.3
  51.0 1.3 collective-permute-start.4
  52.3 1.6 collective-permute-start.6
  54.0 24.9 %collective-permute-done.4 = f32[512,512]{1,0:T(8,128)S(1)} collective-permute-done((f32[512,512]{1,0:T(8,128)}, f32[512,512]{1,0:T(8,128)S(1)}, u32[]{:S(2)}, u32[]{:S(2)}) %collective-permute-start.4) | collective-permute-done | bytes 1048608 | tf_op jit(solution)/shard_map/ppermute | solution.py:242
  80.1 1.7 collective-permute-start.7
  81.9 1.6 collective-permute-start.9
  84.0 7.2 %collective-permute-done.9 = f32[64,512]{0,1:T(8,128)S(1)} collective-permute-done((f32[64,512]{0,1:T(8,128)S(1)}, f32[64,512]{0,1:T(8,128)S(1)}, u32[]{:S(2)}, u32[]{:S(2)}) %collective-permute-start.9) | collective-permute-done | bytes 131104 | tf_op jit(solution)/shard_map/ppermute | solution.py:143
  91.5 3.7 collective-permute-start.10
  97.6 13.0 %collective-permute-done.10 = f32[32,512]{0,1:T(8,128)S(1)} collective-permute-done((f32[32,512]{0,1:T(8,128)S(1)}, f32[32,512]{0,1:T(8,128)S(1)}, u32[]{:S(2)}, u32[]{:S(2)}) %collective-permute-start.10) | collective-permute-done | bytes 65568 | tf_op jit(solution)/shard_map/ppermute | solution.py:143
  110.8 2.8 collective-permute-start.11
  113.6 10.3 %collective-permute-done.11 = f32[16,512]{0,1:T(8,128)S(1)} collective-permute-done((f32[16,512]{0,1:T(8,128)S(1)}, f32[16,512]{0,1:T(8,128)S(1)}, u32[]{:S(2)}, u32[]{:S(2)}) %collective-permute-start.11) | collective-permute-done | bytes 32800 | tf_op jit(solution)/shard_map/ppermute | solution.py:143
  124.8 12.3 %collective-permute-done.12 = f32[16,512]{0,1:T(8,128)S(1)} collective-permute-done((f32[16,512]{0,1:T(8,128)S(1)}, f32[16,512]{0,1:T(8,128)S(1)}, u32[]{:S(2)}, u32[]{:S(2)}) %collective-permute-start.12) | collective-permute-done | bytes 32800 | tf_op jit(solution)/shard_map/ppermute | solution.py:143
  138.2 3.6 collective-permute-done.13
  141.8 1.7 collective-permute-start.14
  143.5 5.1 %select_add_fusion.3 = (f32[512,512]{1,0:T(8,128)}, f32[512,512]{1,0:T(8,128)S(1)}, f32[512,512]{1,0:T(8,128)S(1)}, f32[512,512]{1,0:T(8,128)S(1)}) fusion(pred[]{:T(512)S(6)} %eq.104, pred[]{:T(512)S(6)} %eq.103, pred[]{:T(512)S(6)} %eq.96, pred[]{:T(512)S(6)} %eq.95, f32[1,4096,512]{2,1,0:T(8,128)} %param.3, f32[512,512]{1,0:T(8,128)} %collective-permute-done, ...), kind=kLoop, calls=%fused_computation.57 | loop fusion | flops 2621440 | bytes 11534340 | tf_op jit(solution)/shard_map/add | solution.py:350
  151.0 1.3 collective-permute-start.16
  163.4 2.5 fusion.13
  166.2 7.5 %collective-permute-start.18 = (f32[3,512,512]{2,1,0:T(8,128)S(1)}, f32[3,512,512]{2,1,0:T(8,128)S(1)}, u32[]{:S(2)}, u32[]{:S(2)}) collective-permute-start(f32[3,512,512]{2,1,0:T(8,128)S(1)} %pad_maximum_fusion), channel_id=1, source_target_pairs={{0,1},{1,0},{2,3},{3,2},{4,5},{5,4},{6,7},{7,6},{8,9},{9,8},{10,11... | collective-permute-start | bytes 9437192 | tf_op jit(solution)/shard_map/ppermute | solution.py:248
  173.7 2.3 bitcast_dynamic-update-slice_fusion.6
  176.1 1.5 collective-permute-start.27
  177.5 1.5 select_add_fusion.2.a_ref
  179.0 21.7 %shard_map.58 = f32[512,512]{1,0:T(8,128)S(1)} custom-call(f32[512,512]{1,0:T(8,128)S(1)} %select_add_fusion.2.a_ref), custom_call_target="tpu_custom_call" | custom-call | flops 134217728 | bytes 2097152 | tf_op jit(solution)/shard_map/pallas_call | solution.py:86
  202.0 1.3 collective-permute-start.25
  204.6 2.2 fusion.7
  206.9 2.2 fusion.6
  211.1 2.2 fusion.3
  213.4 11.6 %collective-permute-done.24 = f32[512,512]{1,0:T(8,128)S(1)} collective-permute-done((f32[512,512]{1,0:T(8,128)S(1)}, f32[512,512]{1,0:T(8,128)S(1)}, u32[]{:S(2)}, u32[]{:S(2)}) %collective-permute-start.24) | collective-permute-done | bytes 1048608 | tf_op jit(solution)/shard_map/ppermute | solution.py:334
  226.1 40.6 %collective-permute-done.25 = f32[512,512]{1,0:T(8,128)S(1)} collective-permute-done((f32[512,512]{1,0:T(8,128)S(1)}, f32[512,512]{1,0:T(8,128)S(1)}, u32[]{:S(2)}, u32[]{:S(2)}) %collective-permute-start.25) | collective-permute-done | bytes 1048608 | tf_op jit(solution)/shard_map/ppermute | solution.py:334
  267.8 63.5 %collective-permute-done.26 = f32[512,512]{1,0:T(8,128)S(1)} collective-permute-done((f32[512,512]{1,0:T(8,128)S(1)}, f32[512,512]{1,0:T(8,128)S(1)}, u32[]{:S(2)}, u32[]{:S(2)}) %collective-permute-start.26) | collective-permute-done | bytes 1048608 | tf_op jit(solution)/shard_map/ppermute | solution.py:334
  336.6 3.3 copy-done.2
  341.4 2.4 bitcast_dynamic-update-slice_fusion.1
  343.8 2.3 bitcast_dynamic-update-slice_fusion.piece_ref
  346.4 1.7 collective-permute-start.20
  348.3 6.9 %collective-permute-done.20 = f32[128,512]{1,0:T(8,128)S(1)} collective-permute-done((f32[128,512]{1,0:T(8,128)S(1)}, f32[128,512]{1,0:T(8,128)S(1)}, u32[]{:S(2)}, u32[]{:S(2)}) %collective-permute-start.20) | collective-permute-done | bytes 262176 | tf_op jit(solution)/shard_map/ppermute | solution.py:143
  355.3 1.6 copy.90.left_ref
  356.9 4.6 shard_map.59
  363.1 1.9 collective-permute-done.28
  365.2 1.7 collective-permute-start.29
  368.8 4.7 collective-permute-done.29
  373.6 1.7 collective-permute-start.31
  375.3 6.5 %shard_map.61 = f32[4,512,256]{2,1,0:T(8,128)} custom-call(s32[4]{0:T(128)} %dynamic_slice.356.slot_ref, s32[4]{0:T(128)} %get-tuple-element.152.place_ref, s32[4]{0:T(128)} %get-tuple-element.104.part_ref, s32[4]{0:T(128)} %get-tuple-element.100.keep_ref, bf16[512,1536]{1,0:T(8,128)(2,1)} %copy.90.left_ref, f32[8,512,512]{2,1,0:T(8,128)} %copy-done.2, ...), custom_call_target="tpu_custom_call" | custom-call | flops 1610612736 | bytes 6291456 | tf_op jit(solution)/shard_map/pallas_call | solution.py:117
  383.1 7.7 %collective-permute-done.21 = f32[128,512]{1,0:T(8,128)S(1)} collective-permute-done((f32[128,512]{1,0:T(8,128)S(1)}, f32[128,512]{1,0:T(8,128)S(1)}, u32[]{:S(2)}, u32[]{:S(2)}) %collective-permute-start.21) | collective-permute-done | bytes 262176 | tf_op jit(solution)/shard_map/ppermute | solution.py:143
  393.0 2.3 collective-permute-start.33
  395.3 2.3 collective-permute-start.34
  397.6 2.3 collective-permute-start.35
  401.2 6.5 %shard_map.60 = f32[4,512,256]{2,1,0:T(8,128)} custom-call(s32[4]{0:T(128)} %dynamic_slice.352.slot_ref, s32[4]{0:T(128)} %get-tuple-element.151.place_ref, s32[4]{0:T(128)} %get-tuple-element.105.part_ref, s32[4]{0:T(128)} %get-tuple-element.101.keep_ref, bf16[512,1536]{1,0:T(8,128)(2,1)} %copy.90.left_ref, f32[8,512,512]{2,1,0:T(8,128)} %copy-done.2, ...), custom_call_target="tpu_custom_call" | custom-call | flops 1610612736 | bytes 6291456 | tf_op jit(solution)/shard_map/pallas_call | solution.py:117
  408.3 6.8 %shard_map.64 = f32[4,512,256]{2,1,0:T(8,128)} custom-call(s32[4]{0:T(128)} %dynamic_slice.364.slot_ref, s32[4]{0:T(128)} %get-tuple-element.154.place_ref, s32[4]{0:T(128)} %get-tuple-element.102.part_ref, s32[4]{0:T(128)} %get-tuple-element.98.keep_ref, bf16[512,1536]{1,0:T(8,128)(2,1)} %copy.90.left_ref, f32[8,512,512]{2,1,0:T(8,128)} %copy-done.2, ...), custom_call_target="tpu_custom_call" | custom-call | flops 1610612736 | bytes 6291456 | tf_op jit(solution)/shard_map/pallas_call | solution.py:117
  415.7 3.2 add.489
  419.1 21.5 %shard_map.62.inverse_ref = f32[512,512]{1,0:T(8,128)S(1)} custom-call(f32[512,512]{1,0:T(8,128)S(1)} %pad_maximum_fusion.9.a_ref), custom_call_target="tpu_custom_call" | custom-call | flops 134217728 | bytes 2097152 | tf_op jit(solution)/shard_map/pallas_call | solution.py:86
  440.6 2.4 add_add_fusion
  443.0 21.4 %collective-permute-start.36 = (f32[512,512]{1,0:T(8,128)S(1)}, f32[512,512]{1,0:T(8,128)S(1)}, u32[]{:S(2)}, u32[]{:S(2)}) collective-permute-start(f32[512,512]{1,0:T(8,128)S(1)} %add_add_fusion), channel_id=1, source_target_pairs={{0,1},{1,0},{2,3},{3,2},{4,5},{5,4},{6,7},{7,6},{8,9},{9,8},{10,11... | collective-permute-start | bytes 3145736 | tf_op jit(solution)/shard_map/ppermute | solution.py:269
  464.4 3.2 convolution_bitcast_fusion.8
  468.2 6.5 %shard_map.63.rest_0_ = f32[4,512,256]{2,1,0:T(8,128)} custom-call(s32[4]{0:T(128)} %dynamic_slice.360.slot_ref, s32[4]{0:T(128)} %get-tuple-element.153.place_ref, s32[4]{0:T(128)} %get-tuple-element.103.part_ref, s32[4]{0:T(128)} %get-tuple-element.99.keep_ref, bf16[512,1536]{1,0:T(8,128)(2,1)} %copy.90.left_ref, f32[8,512,512]{2,1,0:T(8,128)} %copy-done.2, ...), custom_call_target="tpu_custom_call" | custom-call | flops 1610612736 | bytes 6291456 | tf_op jit(solution)/shard_map/pallas_call | solution.py:117
  475.7 12.0 %collective-permute-done.36 = f32[512,512]{1,0:T(8,128)S(1)} collective-permute-done((f32[512,512]{1,0:T(8,128)S(1)}, f32[512,512]{1,0:T(8,128)S(1)}, u32[]{:S(2)}, u32[]{:S(2)}) %collective-permute-start.36) | collective-permute-done | bytes 1048608 | tf_op jit(solution)/shard_map/ppermute | solution.py:269
  488.1 1.5 pad_maximum_fusion.1
  489.6 1.4 copy-done.7
  490.9 7.5 %shard_map.65 = f32[1024,512]{1,0:T(8,128)} custom-call(f32[1024,512]{1,0:T(8,128)S(1)} %copy-done, f32[4,256,512]{2,1,0:T(8,128)} %bitcast.175, f32[512,512]{1,0:T(8,128)S(1)} %shard_map.62.inverse_ref, f32[512,512]{1,0:T(8,128)S(1)} %fusion.21.mine_ref, f32[4,512,256]{2,1,0:T(8,128)} %shard_map.63.rest_0_, f32[4,512,256]{2,1,0:T(8,128)} %copy-done.7, ...), custom_call_target="tpu_custom_call" | custom-call | flops 3221225472 | bytes 16777216 | tf_op jit(solution)/shard_map/pallas_call | solution.py:216
  (169 shorter events, 46.8 us)
Async XLA Ops:
  0.6 20.5 %slice-start = ((f32[1024,512]{1,0:T(8,128)}), f32[512,512]{1,0:T(8,128)S(1)}, s32[]{:S(2)}) async-start(f32[1024,512]{1,0:T(8,128)} %parent_ref.1), calls=%async_computation | async-start | bytes 2097152 | tf_op jit(solution)/shard_map/slice | solution.py:326
  3.0 48.0 %collective-permute-start = (f32[512,512]{1,0:T(8,128)}, f32[512,512]{1,0:T(8,128)}, u32[]{:S(2)}, u32[]{:S(2)}) collective-permute-start(f32[512,512]{1,0:T(8,128)} %slice_bitcast_fusion.6), channel_id=1, source_target_pairs={{0,2},{1,3},{2,4},{3,5},{4,6},{5,7},{8,10},{9,11},{10,12},{11,13},... | collective-permute-start | bytes 3145736 | tf_op jit(solution)/shard_map/ppermute | solution.py:241
  8.9 42.1 %collective-permute-start.1 = (f32[512,512]{1,0:T(8,128)}, f32[512,512]{1,0:T(8,128)}, u32[]{:S(2)}, u32[]{:S(2)}) collective-permute-start(f32[512,512]{1,0:T(8,128)} %slice_bitcast_fusion.6), channel_id=1, source_target_pairs={{2,0},{3,1},{4,2},{5,3},{6,4},{7,5},{10,8},{11,9},{12,10},{13,11},... | collective-permute-start | bytes 3145736 | tf_op jit(solution)/shard_map/ppermute | solution.py:242
  17.1 135.2 %copy-start.16 = (s32[16]{0:T(128)}, s32[16]{0:T(128)S(1)}, u32[]{:S(2)}) copy-start(s32[16]{0:T(128)S(1)} %gather_fusion.1) | copy-start | bytes 196
  21.5 16.8 %copy-start.4 = (f32[512,512]{0,1:T(8,128)}, f32[512,512]{0,1:T(8,128)S(1)}, u32[]{:S(2)}) copy-start(f32[512,512]{0,1:T(8,128)S(1)} %copy.108) | copy-start | bytes 3145732
  22.7 18.3 %collective-permute-start.2 = (f32[256,512]{0,1:T(8,128)}, f32[256,512]{0,1:T(8,128)}, u32[]{:S(2)}, u32[]{:S(2)}) collective-permute-start(f32[256,512]{0,1:T(8,128)} %constant_dynamic-slice_fusion.10), channel_id=1, source_target_pairs={{0,8},{8,0},{16,24},{24,16},{1,9},{9,1},{17,25},{25,17},{2,10},{10... | collective-permute-start | bytes 1572872 | tf_op jit(solution)/shard_map/ppermute | solution.py:143
  42.1 8.8 %collective-permute-start.3 = (f32[128,512]{0,1:T(8,128)S(1)}, f32[128,512]{0,1:T(8,128)S(1)}, u32[]{:S(2)}, u32[]{:S(2)}) collective-permute-start(f32[128,512]{0,1:T(8,128)S(1)} %constant_dynamic-slice_fusion.9), channel_id=1, source_target_pairs={{0,16},{8,24},{16,0},{24,8},{1,17},{9,25},{17,1},{25,9},{2,18},{10... | collective-permute-start | bytes 786440 | tf_op jit(solution)/shard_map/ppermute | solution.py:143
  51.0 27.8 %collective-permute-start.4 = (f32[512,512]{1,0:T(8,128)}, f32[512,512]{1,0:T(8,128)S(1)}, u32[]{:S(2)}, u32[]{:S(2)}) collective-permute-start(f32[512,512]{1,0:T(8,128)} %collective-permute-done.1), channel_id=1, source_target_pairs={{2,0},{3,1},{4,2},{5,3},{10,8},{11,9},{12,10},{13,11},{18,16},{19,... | collective-permute-start | bytes 3145736 | tf_op jit(solution)/shard_map/ppermute | solution.py:242
  52.3 27.8 %collective-permute-start.6 = (f32[512,512]{1,0:T(8,128)}, f32[512,512]{1,0:T(8,128)}, u32[]{:S(2)}, u32[]{:S(2)}) collective-permute-start(f32[512,512]{1,0:T(8,128)} %collective-permute-done), channel_id=1, source_target_pairs={{2,4},{3,5},{4,6},{5,7},{10,12},{11,13},{12,14},{13,15},{18,20},{1... | collective-permute-start | bytes 3145736 | tf_op jit(solution)/shard_map/ppermute | solution.py:241
  78.8 63.0 %copy-start.8 = (f32[512,512]{1,0:T(8,128)}, f32[512,512]{1,0:T(8,128)S(1)}, u32[]{:S(2)}) copy-start(f32[512,512]{1,0:T(8,128)S(1)} %collective-permute-done.4) | copy-start | bytes 3145732
  78.8 31.9 %collective-permute-start.5 = (f32[512,512]{1,0:T(8,128)S(1)}, f32[512,512]{1,0:T(8,128)}, u32[]{:S(2)}, u32[]{:S(2)}) collective-permute-start(f32[512,512]{1,0:T(8,128)S(1)} %collective-permute-done.4), channel_id=1, source_target_pairs={{2,0},{3,1},{10,8},{11,9},{18,16},{19,17},{26,24},{27,25}} | collective-permute-start | bytes 3145736 | tf_op jit(solution)/shard_map/ppermute | solution.py:242
  80.1 30.6 %collective-permute-start.7 = (f32[512,512]{1,0:T(8,128)}, f32[512,512]{1,0:T(8,128)}, u32[]{:S(2)}, u32[]{:S(2)}) collective-permute-start(f32[512,512]{1,0:T(8,128)} %collective-permute-done.6), channel_id=1, source_target_pairs={{4,6},{5,7},{12,14},{13,15},{20,22},{21,23},{28,30},{29,31}} | collective-permute-start | bytes 3145736 | tf_op jit(solution)/shard_map/ppermute | solution.py:241
  81.9 9.3 %collective-permute-start.9 = (f32[64,512]{0,1:T(8,128)S(1)}, f32[64,512]{0,1:T(8,128)S(1)}, u32[]{:S(2)}, u32[]{:S(2)}) collective-permute-start(f32[64,512]{0,1:T(8,128)S(1)} %constant_dynamic-slice_fusion.8), channel_id=1, source_target_pairs={{0,1},{1,0},{2,3},{3,2},{4,5},{5,4},{6,7},{7,6},{8,9},{9,8},{10,11... | collective-permute-start | bytes 393224 | tf_op jit(solution)/shard_map/ppermute | solution.py:143
  83.5 66.2 %collective-permute-start.15 = (f32[512,512]{1,0:T(8,128)}, f32[512,512]{1,0:T(8,128)}, u32[]{:S(2)}, u32[]{:S(2)}) collective-permute-start(f32[512,512]{1,0:T(8,128)} %slice_bitcast_fusion.6), channel_id=1, source_target_pairs={{0,1},{1,0},{2,3},{3,2},{4,5},{5,4},{6,7},{7,6},{8,9},{9,8},{10,11... | collective-permute-start | bytes 3145736 | tf_op jit(solution)/shard_map/ppermute | solution.py:248
  91.5 19.0 %collective-permute-start.10 = (f32[32,512]{0,1:T(8,128)S(1)}, f32[32,512]{0,1:T(8,128)S(1)}, u32[]{:S(2)}, u32[]{:S(2)}) collective-permute-start(f32[32,512]{0,1:T(8,128)S(1)} %constant_dynamic-slice_fusion.7), channel_id=1, source_target_pairs={{0,2},{1,3},{2,0},{3,1},{4,6},{5,7},{6,4},{7,5},{8,10},{9,11},{10,... | collective-permute-start | bytes 196616 | tf_op jit(solution)/shard_map/ppermute | solution.py:143
  96.2 77.5 %collective-permute-start.23 = (f32[512,512]{1,0:T(8,128)}, f32[512,512]{1,0:T(8,128)}, u32[]{:S(2)}, u32[]{:S(2)}) collective-permute-start(f32[512,512]{1,0:T(8,128)} %pad_maximum_fusion.10), channel_id=1, source_target_pairs={{1,0},{2,3},{3,2},{4,5},{5,4},{6,7},{7,6},{9,8},{10,11},{11,10},{1... | collective-permute-start | bytes 3145736 | tf_op jit(solution)/shard_map/ppermute | solution.py:334
  110.8 13.1 %collective-permute-start.11 = (f32[16,512]{0,1:T(8,128)S(1)}, f32[16,512]{0,1:T(8,128)S(1)}, u32[]{:S(2)}, u32[]{:S(2)}) collective-permute-start(f32[16,512]{0,1:T(8,128)S(1)} %constant_dynamic-slice_fusion.6), channel_id=1, source_target_pairs={{0,4},{1,5},{2,6},{3,7},{4,0},{5,1},{6,2},{7,3},{8,12},{9,13},{10,... | collective-permute-start | bytes 98312 | tf_op jit(solution)/shard_map/ppermute | solution.py:143
  113.6 52.2 %copy-start.14 = (s32[16]{0:T(128)}, s32[16]{0:T(128)S(1)}, u32[]{:S(2)}) copy-start(s32[16]{0:T(128)S(1)} %get-tuple-element.141) | copy-start | bytes 196
  113.6 52.2 %copy-start.19 = (s32[16]{0:T(128)}, s32[16]{0:T(128)S(1)}, u32[]{:S(2)}) copy-start(s32[16]{0:T(128)S(1)} %get-tuple-element.46) | copy-start | bytes 196
  124.1 13.1 %collective-permute-start.12 = (f32[16,512]{0,1:T(8,128)S(1)}, f32[16,512]{0,1:T(8,128)S(1)}, u32[]{:S(2)}, u32[]{:S(2)}) collective-permute-start(f32[16,512]{0,1:T(8,128)S(1)} %dynamic-slice_add_fusion.4), channel_id=1, source_target_pairs={{0,4},{1,5},{2,6},{3,7},{4,0},{5,1},{6,2},{7,3},{8,12},{9,13},{10,... | collective-permute-start | bytes 98312 | tf_op jit(solution)/shard_map/ppermute | solution.py:143
  137.4 4.3 collective-permute-start.13
  141.8 7.2 %collective-permute-start.14 = (f32[64,512]{1,0:T(8,128)S(1)}, f32[64,512]{1,0:T(8,128)S(1)}, u32[]{:S(2)}, u32[]{:S(2)}) collective-permute-start(f32[64,512]{1,0:T(8,128)S(1)} %pad_maximum_fusion.15), channel_id=1, source_target_pairs={{0,1},{1,0},{2,3},{3,2},{4,5},{5,4},{6,7},{7,6},{8,9},{9,8},{10,11... | collective-permute-start | bytes 393224 | tf_op jit(solution)/shard_map/ppermute | solution.py:143
  148.6 28.9 %copy-start.3 = (f32[512,512]{1,0:T(8,128)}, f32[512,512]{1,0:T(8,128)S(1)}, u32[]{:S(2)}) copy-start(f32[512,512]{1,0:T(8,128)S(1)} %get-tuple-element.51) | copy-start | bytes 3145732
  148.6 28.9 %collective-permute-start.8 = (f32[512,512]{1,0:T(8,128)}, f32[512,512]{1,0:T(8,128)}, u32[]{:S(2)}, u32[]{:S(2)}) collective-permute-start(f32[512,512]{1,0:T(8,128)} %get-tuple-element.50), channel_id=1, source_target_pairs={{0,1},{1,0},{2,3},{3,2},{4,5},{5,4},{6,7},{7,6},{8,9},{9,8},{10,11... | collective-permute-start | bytes 3145736 | tf_op jit(solution)/shard_map/ppermute | solution.py:248
  149.7 52.3 %collective-permute-start.17 = (f32[512,512]{1,0:T(8,128)}, f32[512,512]{1,0:T(8,128)}, u32[]{:S(2)}, u32[]{:S(2)}) collective-permute-start(f32[512,512]{1,0:T(8,128)} %get-tuple-element.30), channel_id=1, source_target_pairs={{1,7},{2,4},{3,5},{4,2},{5,3},{6,0},{7,1},{9,15},{10,12},{11,13},{... | collective-permute-start | bytes 3145736 | tf_op jit(solution)/shard_map/ppermute | solution.py:334
  151.0 52.4 %collective-permute-start.16 = (f32[512,512]{1,0:T(8,128)}, f32[512,512]{1,0:T(8,128)}, u32[]{:S(2)}, u32[]{:S(2)}) collective-permute-start(f32[512,512]{1,0:T(8,128)} %get-tuple-element.29), channel_id=1, source_target_pairs={{1,6},{2,5},{3,4},{4,3},{5,2},{6,1},{7,0},{9,14},{10,13},{11,12},{... | collective-permute-start | bytes 3145736 | tf_op jit(solution)/shard_map/ppermute | solution.py:334
  163.3 12.7 %copy-start.9 = (f32[512,512]{1,0:T(8,128)S(1)}, f32[512,512]{1,0:T(8,128)}, u32[]{:S(2)}) copy-start(f32[512,512]{1,0:T(8,128)} %pad_maximum_fusion.5) | copy-start | bytes 3145732
  163.3 37.4 %copy-start.10 = (f32[512,512]{1,0:T(8,128)S(1)}, f32[512,512]{1,0:T(8,128)}, u32[]{:S(2)}) copy-start(f32[512,512]{1,0:T(8,128)} %pad_maximum_fusion.8) | copy-start | bytes 3145732
  163.3 38.7 %copy-start.12 = (f32[512,512]{1,0:T(8,128)S(1)}, f32[512,512]{1,0:T(8,128)}, u32[]{:S(2)}) copy-start(f32[512,512]{1,0:T(8,128)} %get-tuple-element.35) | copy-start | bytes 3145732
  163.3 40.0 %copy-start.11 = (f32[512,512]{1,0:T(8,128)S(1)}, f32[512,512]{1,0:T(8,128)}, u32[]{:S(2)}) copy-start(f32[512,512]{1,0:T(8,128)} %get-tuple-element.36) | copy-start | bytes 3145732
  166.2 167.4 %collective-permute-start.18 = (f32[3,512,512]{2,1,0:T(8,128)S(1)}, f32[3,512,512]{2,1,0:T(8,128)S(1)}, u32[]{:S(2)}, u32[]{:S(2)}) collective-permute-start(f32[3,512,512]{2,1,0:T(8,128)S(1)} %pad_maximum_fusion), channel_id=1, source_target_pairs={{0,1},{1,0},{2,3},{3,2},{4,5},{5,4},{6,7},{7,6},{8,9},{9,8},{10,11... | collective-permute-start | bytes 9437192 | tf_op jit(solution)/shard_map/ppermute | solution.py:248
  176.1 156.4 %collective-permute-start.27 = (f32[512,512]{1,0:T(8,128)S(1)}, f32[512,512]{1,0:T(8,128)S(1)}, u32[]{:S(2)}, u32[]{:S(2)}) collective-permute-start(f32[512,512]{1,0:T(8,128)S(1)} %copy-done.9), channel_id=1, source_target_pairs={{1,4},{2,7},{3,6},{4,1},{5,0},{6,3},{7,2},{9,12},{10,15},{11,14},{... | collective-permute-start | bytes 3145736 | tf_op jit(solution)/shard_map/ppermute | solution.py:334
  200.7 24.3 %collective-permute-start.24 = (f32[512,512]{1,0:T(8,128)S(1)}, f32[512,512]{1,0:T(8,128)S(1)}, u32[]{:S(2)}, u32[]{:S(2)}) collective-permute-start(f32[512,512]{1,0:T(8,128)S(1)} %copy-done.10), channel_id=1, source_target_pairs={{1,3},{2,0},{3,1},{4,6},{5,7},{6,4},{7,5},{9,11},{10,8},{11,9},{12... | collective-permute-start | bytes 3145736 | tf_op jit(solution)/shard_map/ppermute | solution.py:334
  202.0 64.7 %collective-permute-start.25 = (f32[512,512]{1,0:T(8,128)S(1)}, f32[512,512]{1,0:T(8,128)S(1)}, u32[]{:S(2)}, u32[]{:S(2)}) collective-permute-start(f32[512,512]{1,0:T(8,128)S(1)} %copy-done.12), channel_id=1, source_target_pairs={{1,2},{2,1},{3,0},{4,7},{5,6},{6,5},{7,4},{9,10},{10,9},{11,8},{12... | collective-permute-start | bytes 3145736 | tf_op jit(solution)/shard_map/ppermute | solution.py:334
  203.4 128.0 %collective-permute-start.26 = (f32[512,512]{1,0:T(8,128)S(1)}, f32[512,512]{1,0:T(8,128)S(1)}, u32[]{:S(2)}, u32[]{:S(2)}) collective-permute-start(f32[512,512]{1,0:T(8,128)S(1)} %copy-done.11), channel_id=1, source_target_pairs={{1,5},{2,6},{3,7},{4,0},{5,1},{6,2},{7,3},{9,13},{10,14},{11,15},{... | collective-permute-start | bytes 3145736 | tf_op jit(solution)/shard_map/ppermute | solution.py:334
  336.6 3.3 copy-start.2
  340.0 15.2 %copy-start.13 = (f32[64,512]{1,0:T(8,128)S(1)}, f32[64,512]{1,0:T(8,128)}, u32[]{:S(2)}) copy-start(f32[64,512]{1,0:T(8,128)} %get-tuple-element.95) | copy-start | bytes 393220
  341.4 4.9 collective-permute-start.19
  346.4 8.8 %collective-permute-start.20 = (f32[128,512]{1,0:T(8,128)S(1)}, f32[128,512]{1,0:T(8,128)S(1)}, u32[]{:S(2)}, u32[]{:S(2)}) collective-permute-start(f32[128,512]{1,0:T(8,128)S(1)} %constant_dynamic-slice_fusion.4), channel_id=1, source_target_pairs={{0,16},{8,24},{16,0},{24,8},{1,17},{9,25},{17,1},{25,9},{2,18},{10... | collective-permute-start | bytes 786440 | tf_op jit(solution)/shard_map/ppermute | solution.py:143
  356.9 5.9 %copy-start.5 = (f32[512,512]{0,1:T(8,128)S(1)}, f32[512,512]{0,1:T(8,128)}, u32[]{:S(2)}) copy-start(f32[512,512]{0,1:T(8,128)} %copy-done.4) | copy-start | bytes 3145732
  361.5 5.3 %copy-start.15 = (s32[16]{0:T(128)S(1)}, s32[16]{0:T(128)}, u32[]{:S(2)}) copy-start(s32[16]{0:T(128)} %copy-done.14) | copy-start | bytes 196
  361.5 6.0 %copy-start.17 = (s32[16]{0:T(128)S(1)}, s32[16]{0:T(128)}, u32[]{:S(2)}) copy-start(s32[16]{0:T(128)} %copy-done.16) | copy-start | bytes 196
  361.5 6.0 %copy-start.18 = (s32[16]{0:T(128)S(1)}, s32[16]{0:T(128)}, u32[]{:S(2)}) copy-start(s32[16]{0:T(128)} %get-tuple-element.47) | copy-start | bytes 196
  361.5 6.6 %copy-start.20 = (s32[16]{0:T(128)S(1)}, s32[16]{0:T(128)}, u32[]{:S(2)}) copy-start(s32[16]{0:T(128)} %copy-done.19) | copy-start | bytes 196
  363.1 2.0 collective-permute-start.28
  365.2 8.4 %collective-permute-start.29 = (f32[128,512]{1,0:T(8,128)S(1)}, f32[128,512]{1,0:T(8,128)S(1)}, u32[]{:S(2)}, u32[]{:S(2)}) collective-permute-start(f32[128,512]{1,0:T(8,128)S(1)} %constant_dynamic-slice_fusion), channel_id=1, source_target_pairs={{0,16},{8,24},{16,0},{24,8},{1,17},{9,25},{17,1},{25,9},{2,18},{10... | collective-permute-start | bytes 786440 | tf_op jit(solution)/shard_map/ppermute | solution.py:143
  373.6 8.2 %collective-permute-start.31 = (f32[128,512]{1,0:T(8,128)S(1)}, f32[128,512]{1,0:T(8,128)S(1)}, u32[]{:S(2)}, u32[]{:S(2)}) collective-permute-start(f32[128,512]{1,0:T(8,128)S(1)} %dynamic-slice_add_fusion.3), channel_id=1, source_target_pairs={{0,16},{8,24},{16,0},{24,8},{1,17},{9,25},{17,1},{25,9},{2,18},{10... | collective-permute-start | bytes 786440 | tf_op jit(solution)/shard_map/ppermute | solution.py:143
  381.8 33.3 %collective-permute-start.30 = (f32[4,512,256]{2,1,0:T(8,128)}, f32[4,512,256]{2,1,0:T(8,128)}, u32[]{:S(2)}, u32[]{:S(2)}) collective-permute-start(f32[4,512,256]{2,1,0:T(8,128)} %shard_map.61), channel_id=1, source_target_pairs={{0,8},{8,0},{16,24},{24,16},{1,9},{9,1},{17,25},{25,17},{2,10},{10... | collective-permute-start | bytes 6291464 | tf_op jit(solution)/shard_map/ppermute | solution.py:143
  381.9 8.9 %collective-permute-start.32 = (f32[256,512]{1,0:T(8,128)S(1)}, f32[256,512]{1,0:T(8,128)}, u32[]{:S(2)}, u32[]{:S(2)}) collective-permute-start(f32[256,512]{1,0:T(8,128)S(1)} %pad_maximum_fusion.13), channel_id=1, source_target_pairs={{0,8},{8,0},{16,24},{24,16},{1,9},{9,1},{17,25},{25,17},{2,10},{10... | collective-permute-start | bytes 1572872 | tf_op jit(solution)/shard_map/ppermute | solution.py:143
  382.5 8.3 %collective-permute-start.21 = (f32[128,512]{1,0:T(8,128)S(1)}, f32[128,512]{1,0:T(8,128)S(1)}, u32[]{:S(2)}, u32[]{:S(2)}) collective-permute-start(f32[128,512]{1,0:T(8,128)S(1)} %add_subtract_fusion), channel_id=1, source_target_pairs={{0,16},{8,24},{16,0},{24,8},{1,17},{9,25},{17,1},{25,9},{2,18},{10... | collective-permute-start | bytes 786440 | tf_op jit(solution)/shard_map/ppermute | solution.py:143
  393.0 47.5 %collective-permute-start.33 = (f32[512,512]{1,0:T(8,128)}, f32[512,512]{1,0:T(8,128)}, u32[]{:S(2)}, u32[]{:S(2)}) collective-permute-start(f32[512,512]{1,0:T(8,128)} %pad_maximum_fusion.11), channel_id=1, source_target_pairs={{0,2},{1,3},{10,12},{11,13},{20,22},{21,23},{30,24},{31,25}} | collective-permute-start | bytes 3145736 | tf_op jit(solution)/shard_map/ppermute | solution.py:259
  395.3 45.3 %collective-permute-start.34 = (f32[512,512]{1,0:T(8,128)}, f32[512,512]{1,0:T(8,128)}, u32[]{:S(2)}, u32[]{:S(2)}) collective-permute-start(f32[512,512]{1,0:T(8,128)} %pad_maximum_fusion.11), channel_id=1, source_target_pairs={{0,4},{1,5},{10,14},{11,15},{20,16},{21,17},{30,26},{31,27}} | collective-permute-start | bytes 3145736 | tf_op jit(solution)/shard_map/ppermute | solution.py:259
  397.6 43.0 %collective-permute-start.35 = (f32[512,512]{1,0:T(8,128)}, f32[512,512]{1,0:T(8,128)}, u32[]{:S(2)}, u32[]{:S(2)}) collective-permute-start(f32[512,512]{1,0:T(8,128)} %pad_maximum_fusion.11), channel_id=1, source_target_pairs={{0,6},{1,7},{10,8},{11,9},{20,18},{21,19},{30,28},{31,29}} | collective-permute-start | bytes 3145736 | tf_op jit(solution)/shard_map/ppermute | solution.py:259
  400.6 18.3 %collective-permute-start.22 = (f32[256,512]{1,0:T(8,128)}, f32[256,512]{1,0:T(8,128)S(1)}, u32[]{:S(2)}, u32[]{:S(2)}) collective-permute-start(f32[256,512]{1,0:T(8,128)} %pad_maximum_fusion.12), channel_id=1, source_target_pairs={{0,8},{8,0},{16,24},{24,16},{1,9},{9,1},{17,25},{25,17},{2,10},{10... | collective-permute-start | bytes 1572872 | tf_op jit(solution)/shard_map/ppermute | solution.py:143
  408.3 7.4 %copy-start.6 = (f32[4,512,256]{2,1,0:T(8,128)S(1)}, f32[4,512,256]{2,1,0:T(8,128)}, u32[]{:S(2)}) copy-start(f32[4,512,256]{2,1,0:T(8,128)} %shard_map.60) | copy-start | bytes 6291460
  415.2 74.4 %collective-permute-start.37 = (f32[4,512,256]{2,1,0:T(8,128)}, f32[4,512,256]{2,1,0:T(8,128)S(1)}, u32[]{:S(2)}, u32[]{:S(2)}) collective-permute-start(f32[4,512,256]{2,1,0:T(8,128)} %shard_map.64), channel_id=1, source_target_pairs={{0,8},{8,0},{16,24},{24,16},{1,9},{9,1},{17,25},{25,17},{2,10},{10... | collective-permute-start | bytes 6291464 | tf_op jit(solution)/shard_map/ppermute | solution.py:143
  418.9 70.7 %collective-permute-start.38 = (f32[4,512,256]{2,1,0:T(8,128)}, f32[4,512,256]{2,1,0:T(8,128)}, u32[]{:S(2)}, u32[]{:S(2)}) collective-permute-start(f32[4,512,256]{2,1,0:T(8,128)} %add.489), channel_id=1, source_target_pairs={{0,16},{8,24},{16,0},{24,8},{1,17},{9,25},{17,1},{25,9},{2,18},{10... | collective-permute-start | bytes 6291464 | tf_op jit(solution)/shard_map/ppermute | solution.py:143
  443.0 44.8 %collective-permute-start.36 = (f32[512,512]{1,0:T(8,128)S(1)}, f32[512,512]{1,0:T(8,128)S(1)}, u32[]{:S(2)}, u32[]{:S(2)}) collective-permute-start(f32[512,512]{1,0:T(8,128)S(1)} %add_add_fusion), channel_id=1, source_target_pairs={{0,1},{1,0},{2,3},{3,2},{4,5},{5,4},{6,7},{7,6},{8,9},{9,8},{10,11... | collective-permute-start | bytes 3145736 | tf_op jit(solution)/shard_map/ppermute | solution.py:269
  474.7 16.2 %copy-start = (f32[1024,512]{1,0:T(8,128)S(1)}, f32[1024,512]{1,0:T(8,128)}, u32[]{:S(2)}) copy-start(f32[1024,512]{1,0:T(8,128)} %parent_ref.1) | copy-start | bytes 6291460
  475.7 22.7 %copy-start.1 = (f32[512,512]{1,0:T(8,128)}, f32[512,512]{1,0:T(8,128)S(1)}, u32[]{:S(2)}) copy-start(f32[512,512]{1,0:T(8,128)S(1)} %fusion.21.mine_ref) | copy-start | bytes 3145732
  489.6 1.4 copy-start.7

commit v13 on v11

--- a/solution.py
+++ b/solution.py
@@ -9,7 +9,7 @@
 P_SIZE = 512
 NP = 4096
 PP = 512
-EARLY = 3
+EARLY = 4
 
 SUB = 8
 LANES = 128
@@ -370,9 +370,9 @@
     places = col ^ source
     child_mine = product(inverse, front[:P_SIZE], 1, 0)
 
-    early = [received[k] for k in far[:EARLY]]
+    early = [received[k] for k in far[:EARLY - 1]]
     inverse, early = lax.optimization_barrier((inverse, early))
-    received.update(zip(far[:EARLY], early))
+    received.update(zip(far, early))
     factor = jnp.stack([product(inverse, x, 1, 0) for x in gathered])
 
     def factor_columns(u):

time: 488 us -> 502 us (1.029)
  starting transfers between devices: 60.3 us -> 85.3 us
  waiting for transfers between devices: 227 us -> 216 us
    ppermute x3, starting transfers between devices: 6.76 us -> 19.1 us  [share_line(): got = got + lax.ppermute(x, ('branch', 'col'), pairs)]
    ppermute x1, starting transfers between devices: 5.93 us -> 13.4 us  [share_beside(): shares.append(lax.ppermute(got, 'col', pairs))]
    ppermute x19, waiting for transfers between devices: 69.7 us -> 62.6 us  [flip(): return lax.ppermute(x, axis, [(i, i ^ bit) for i in range(n)])]
  transfers between devices with their start and end apart: 39 -> 39, of which waited for: 15 -> 16; matrix products, arithmetic and copies ran while one was open for 14% -> 13% of each run, Pallas kernels for 14% -> 14%
where the time goes in v13:
time: 502 us; the launch traced here: 494 us
  waiting for transfers between devices  216 us (43%)
  starting transfers between devices  85.3 us (17%)
  Pallas kernels  81.6 us (16%)
  other arithmetic  38.2 us (8%)
  local copies, waits for them, and re-layouts  28.3 us (6%)
  between operations  27.5 us (5%)
  matrix products  17 us (3%)
    ppermute x7, waiting for transfers between devices, moved(): return lax.ppermute(rows, 'col', pairs)  115 us
    ppermute x19, waiting for transfers between devices, flip(): return lax.ppermute(x, axis, [(i, i ^ bit) for i in range(n)])  62.6 us
    pallas_call x2, Pallas kernels, inverse_factor(): pl.pallas_call(inverse_factor_kernel, out_shape=jax.ShapeDtypeStruct((n,...  43.1 us
    pallas_call x5, Pallas kernels, spread_update(): pl.pallas_call(spread_kernel, grid_spec=pltpu.PrefetchScalarGridSpec(num_...  31 us
    ppermute x3, waiting for transfers between devices, line_gather(): lax.ppermute(ends[1], axis, [(c, c - ny) for c in range(n) if 0 < c // ny...  24 us
    ppermute x19, starting transfers between devices, flip(): return lax.ppermute(x, axis, [(i, i ^ bit) for i in range(n)])  21.2 us
    ppermute x3, starting transfers between devices, share_line(): got = got + lax.ppermute(x, ('branch', 'col'), pairs)  19.1 us
    dot_general x11, matrix products, product(): lax.dot_general(a, b, (((ca,), (cb,)), ((), ())), precision=precision)  17 us
  transfers between devices with their start and end apart: 39, of which 16 were waited for; matrix products, arithmetic and copies ran while one was open for 13% of the time, Pallas kernels for 14%

profile of v13, /device:TPU:0, one launch (start us, length us, event | category | flops | bytes accessed | tf_op | source)
XLA Modules:
  0.0 494.0 jit_solution(3922505632577528630)
XLA Ops:
  9.6 1.8 constant_dynamic-slice_fusion.14
  13.6 2.3 slice_bitcast_fusion.6
  15.9 5.8 %collective-permute-start = (f32[512,512]{1,0:T(8,128)}, f32[512,512]{1,0:T(8,128)}, u32[]{:S(2)}, u32[]{:S(2)}) collective-permute-start(f32[512,512]{1,0:T(8,128)} %slice_bitcast_fusion.6), channel_id=1, source_target_pairs={{0,2},{1,3},{2,4},{3,5},{4,6},{5,7},{8,10},{9,11},{10,12},{11,13},... | collective-permute-start | bytes 3145736 | tf_op jit(solution)/shard_map/ppermute | solution.py:241
  33.3 5.6 %dynamic-slice_bitcast_fusion.1 = (f32[256,512]{1,0:T(8,128)S(1)}, f32[256,512]{1,0:T(8,128)S(1)}, f32[256,512]{1,0:T(8,128)S(1)}, f32[256,512]{1,0:T(8,128)S(1)...) fusion(f32[1,4096,512]{2,1,0:T(8,128)} %param.3, ...), kind=kLoop, calls=%fused_computation.65 | loop fusion | bytes 16777280 | tf_op jit(solution)/shard_map/dynamic_slice | solution.py:304
  38.9 1.5 pad_maximum_fusion.7
  41.6 1.4 collective-permute-start.3
  43.0 1.5 pad_maximum_fusion.5
  44.5 1.5 pad_maximum_fusion.3
  46.0 4.1 collective-permute-done.3
  50.2 1.3 collective-permute-start.4
  51.5 1.6 collective-permute-start.6
  53.1 24.0 %collective-permute-done.4 = f32[512,512]{1,0:T(8,128)S(1)} collective-permute-done((f32[512,512]{1,0:T(8,128)}, f32[512,512]{1,0:T(8,128)S(1)}, u32[]{:S(2)}, u32[]{:S(2)}) %collective-permute-start.4) | collective-permute-done | bytes 1048608 | tf_op jit(solution)/shard_map/ppermute | solution.py:242
  78.4 1.7 collective-permute-start.7
  80.2 1.6 collective-permute-start.9
  82.3 7.2 %collective-permute-done.9 = f32[64,512]{0,1:T(8,128)S(1)} collective-permute-done((f32[64,512]{0,1:T(8,128)S(1)}, f32[64,512]{0,1:T(8,128)S(1)}, u32[]{:S(2)}, u32[]{:S(2)}) %collective-permute-start.9) | collective-permute-done | bytes 131104 | tf_op jit(solution)/shard_map/ppermute | solution.py:143
  89.8 3.7 collective-permute-start.10
  95.9 12.3 %collective-permute-done.10 = f32[32,512]{0,1:T(8,128)S(1)} collective-permute-done((f32[32,512]{0,1:T(8,128)S(1)}, f32[32,512]{0,1:T(8,128)S(1)}, u32[]{:S(2)}, u32[]{:S(2)}) %collective-permute-start.10) | collective-permute-done | bytes 65568 | tf_op jit(solution)/shard_map/ppermute | solution.py:143
  108.5 2.8 collective-permute-start.11
  111.3 9.6 %collective-permute-done.11 = f32[16,512]{0,1:T(8,128)S(1)} collective-permute-done((f32[16,512]{0,1:T(8,128)S(1)}, f32[16,512]{0,1:T(8,128)S(1)}, u32[]{:S(2)}, u32[]{:S(2)}) %collective-permute-start.11) | collective-permute-done | bytes 32800 | tf_op jit(solution)/shard_map/ppermute | solution.py:143
  121.8 9.4 %collective-permute-done.12 = f32[16,512]{0,1:T(8,128)S(1)} collective-permute-done((f32[16,512]{0,1:T(8,128)S(1)}, f32[16,512]{0,1:T(8,128)S(1)}, u32[]{:S(2)}, u32[]{:S(2)}) %collective-permute-start.12) | collective-permute-done | bytes 32800 | tf_op jit(solution)/shard_map/ppermute | solution.py:143
  131.5 4.4 collective-permute-start.13
  136.6 1.6 collective-permute-done.13
  138.2 1.6 collective-permute-start.14
  139.8 5.1 %select_add_fusion.3 = (f32[512,512]{1,0:T(8,128)}, f32[512,512]{1,0:T(8,128)S(1)}, f32[512,512]{1,0:T(8,128)S(1)}, f32[512,512]{1,0:T(8,128)S(1)}) fusion(pred[]{:T(512)S(6)} %eq.104, pred[]{:T(512)S(6)} %eq.103, pred[]{:T(512)S(6)} %eq.96, pred[]{:T(512)S(6)} %eq.95, f32[1,4096,512]{2,1,0:T(8,128)} %param.3, f32[512,512]{1,0:T(8,128)} %collective-permute-done, ...), kind=kLoop, calls=%fused_computation.57 | loop fusion | flops 2621440 | bytes 11534340 | tf_op jit(solution)/shard_map/add | solution.py:350
  145.4 1.3 collective-permute-start.18
  160.9 1.5 fusion.13
  162.4 1.4 bitcast_dynamic-update-slice_fusion.6
  164.1 1.5 collective-permute-start.27
  165.6 2.4 collective-permute-done.8
  168.0 8.4 %collective-permute-start.19 = (f32[3,512,512]{2,1,0:T(8,128)S(1)}, f32[3,512,512]{2,1,0:T(8,128)S(1)}, u32[]{:S(2)}, u32[]{:S(2)}) collective-permute-start(f32[3,512,512]{2,1,0:T(8,128)S(1)} %pad_maximum_fusion), channel_id=1, source_target_pairs={{0,1},{1,0},{2,3},{3,2},{4,5},{5,4},{6,7},{7,6},{8,9},{9,8},{10,11... | collective-permute-start | bytes 9437192 | tf_op jit(solution)/shard_map/ppermute | solution.py:248
  176.4 1.5 select_add_fusion.2.a_ref
  177.9 21.7 %shard_map.58 = f32[512,512]{1,0:T(8,128)S(1)} custom-call(f32[512,512]{1,0:T(8,128)S(1)} %select_add_fusion.2.a_ref), custom_call_target="tpu_custom_call" | custom-call | flops 134217728 | bytes 2097152 | tf_op jit(solution)/shard_map/pallas_call | solution.py:86
  199.5 61.5 %collective-permute-done.18 = f32[512,512]{1,0:T(8,128)} collective-permute-done((f32[512,512]{1,0:T(8,128)}, f32[512,512]{1,0:T(8,128)}, u32[]{:S(2)}, u32[]{:S(2)}) %collective-permute-start.18) | collective-permute-done | bytes 1048608 | tf_op jit(solution)/shard_map/ppermute | solution.py:334
  263.7 2.2 fusion.7
  265.9 2.2 fusion.6
  270.2 2.2 fusion.3
  272.4 11.3 %collective-permute-done.26 = f32[512,512]{1,0:T(8,128)S(1)} collective-permute-done((f32[512,512]{1,0:T(8,128)S(1)}, f32[512,512]{1,0:T(8,128)S(1)}, u32[]{:S(2)}, u32[]{:S(2)}) %collective-permute-start.26) | collective-permute-done | bytes 1048608 | tf_op jit(solution)/shard_map/ppermute | solution.py:334
  283.8 24.3 %collective-permute-done.22 = f32[512,512]{1,0:T(8,128)S(1)} collective-permute-done((f32[512,512]{1,0:T(8,128)S(1)}, f32[512,512]{1,0:T(8,128)S(1)}, u32[]{:S(2)}, u32[]{:S(2)}) %collective-permute-start.22) | collective-permute-done | bytes 1048608 | tf_op jit(solution)/shard_map/ppermute | solution.py:334
  308.2 18.0 %collective-permute-done.27 = f32[512,512]{1,0:T(8,128)S(1)} collective-permute-done((f32[512,512]{1,0:T(8,128)S(1)}, f32[512,512]{1,0:T(8,128)S(1)}, u32[]{:S(2)}, u32[]{:S(2)}) %collective-permute-start.27) | collective-permute-done | bytes 1048608 | tf_op jit(solution)/shard_map/ppermute | solution.py:334
  326.4 1.4 bitcast_dynamic-update-slice_fusion.2
  327.8 1.4 bitcast_dynamic-update-slice_fusion.1
  329.2 1.4 bitcast_dynamic-update-slice_fusion.piece_ref
  333.6 3.3 copy-done.2
  338.3 1.6 copy.90.left_ref
  339.9 4.6 shard_map.59
  352.7 6.5 %shard_map.61 = f32[4,512,256]{2,1,0:T(8,128)} custom-call(s32[4]{0:T(128)} %dynamic_slice.356.slot_ref, s32[4]{0:T(128)} %get-tuple-element.156.place_ref, s32[4]{0:T(128)} %get-tuple-element.106.part_ref, s32[4]{0:T(128)} %get-tuple-element.102.keep_ref, bf16[512,1536]{1,0:T(8,128)(2,1)} %copy.90.left_ref, f32[8,512,512]{2,1,0:T(8,128)} %copy-done.2, ...), custom_call_target="tpu_custom_call" | custom-call | flops 1610612736 | bytes 6291456 | tf_op jit(solution)/shard_map/pallas_call | solution.py:117
  361.6 6.9 %collective-permute-done.31 = f32[128,512]{1,0:T(8,128)S(1)} collective-permute-done((f32[128,512]{1,0:T(8,128)S(1)}, f32[128,512]{1,0:T(8,128)S(1)}, u32[]{:S(2)}, u32[]{:S(2)}) %collective-permute-start.31) | collective-permute-done | bytes 262176 | tf_op jit(solution)/shard_map/ppermute | solution.py:143
  369.4 4.3 collective-permute-done.21
  374.7 7.1 %collective-permute-done.23 = f32[128,512]{1,0:T(8,128)S(1)} collective-permute-done((f32[128,512]{1,0:T(8,128)S(1)}, f32[128,512]{1,0:T(8,128)S(1)}, u32[]{:S(2)}, u32[]{:S(2)}) %collective-permute-start.23) | collective-permute-done | bytes 262176 | tf_op jit(solution)/shard_map/ppermute | solution.py:143
  384.0 8.9 %collective-permute-start.33 = (f32[512,512]{1,0:T(8,128)}, f32[512,512]{1,0:T(8,128)}, u32[]{:S(2)}, u32[]{:S(2)}) collective-permute-start(f32[512,512]{1,0:T(8,128)} %pad_maximum_fusion.11), channel_id=1, source_target_pairs={{0,2},{1,3},{10,12},{11,13},{20,22},{21,23},{30,24},{31,25}} | collective-permute-start | bytes 3145736 | tf_op jit(solution)/shard_map/ppermute | solution.py:259
  392.9 8.0 %collective-permute-start.34 = (f32[512,512]{1,0:T(8,128)}, f32[512,512]{1,0:T(8,128)}, u32[]{:S(2)}, u32[]{:S(2)}) collective-permute-start(f32[512,512]{1,0:T(8,128)} %pad_maximum_fusion.11), channel_id=1, source_target_pairs={{0,4},{1,5},{10,14},{11,15},{20,16},{21,17},{30,26},{31,27}} | collective-permute-start | bytes 3145736 | tf_op jit(solution)/shard_map/ppermute | solution.py:259
  400.9 2.2 collective-permute-start.35
  404.6 6.5 %shard_map.60 = f32[4,512,256]{2,1,0:T(8,128)} custom-call(s32[4]{0:T(128)} %dynamic_slice.352.slot_ref, s32[4]{0:T(128)} %get-tuple-element.155.place_ref, s32[4]{0:T(128)} %get-tuple-element.107.part_ref, s32[4]{0:T(128)} %get-tuple-element.103.keep_ref, bf16[512,1536]{1,0:T(8,128)(2,1)} %copy.90.left_ref, f32[8,512,512]{2,1,0:T(8,128)} %copy-done.2, ...), custom_call_target="tpu_custom_call" | custom-call | flops 1610612736 | bytes 6291456 | tf_op jit(solution)/shard_map/pallas_call | solution.py:117
  411.7 6.8 %shard_map.64 = f32[4,512,256]{2,1,0:T(8,128)} custom-call(s32[4]{0:T(128)} %dynamic_slice.364.slot_ref, s32[4]{0:T(128)} %get-tuple-element.158.place_ref, s32[4]{0:T(128)} %get-tuple-element.104.part_ref, s32[4]{0:T(128)} %get-tuple-element.100.keep_ref, bf16[512,1536]{1,0:T(8,128)(2,1)} %copy.90.left_ref, f32[8,512,512]{2,1,0:T(8,128)} %copy-done.2, ...), custom_call_target="tpu_custom_call" | custom-call | flops 1610612736 | bytes 6291456 | tf_op jit(solution)/shard_map/pallas_call | solution.py:117
  419.1 3.2 add.489
  422.5 21.5 %shard_map.62.inverse_ref = f32[512,512]{1,0:T(8,128)S(1)} custom-call(f32[512,512]{1,0:T(8,128)S(1)} %pad_maximum_fusion.9.a_ref), custom_call_target="tpu_custom_call" | custom-call | flops 134217728 | bytes 2097152 | tf_op jit(solution)/shard_map/pallas_call | solution.py:86
  444.0 2.4 add_add_fusion
  446.4 13.4 %collective-permute-start.36 = (f32[512,512]{1,0:T(8,128)S(1)}, f32[512,512]{1,0:T(8,128)S(1)}, u32[]{:S(2)}, u32[]{:S(2)}) collective-permute-start(f32[512,512]{1,0:T(8,128)S(1)} %add_add_fusion), channel_id=1, source_target_pairs={{0,1},{1,0},{2,3},{3,2},{4,5},{5,4},{6,7},{7,6},{8,9},{9,8},{10,11... | collective-permute-start | bytes 3145736 | tf_op jit(solution)/shard_map/ppermute | solution.py:269
  459.8 3.2 convolution_bitcast_fusion.8
  463.5 6.5 %shard_map.63.rest_0_ = f32[4,512,256]{2,1,0:T(8,128)} custom-call(s32[4]{0:T(128)} %dynamic_slice.360.slot_ref, s32[4]{0:T(128)} %get-tuple-element.157.place_ref, s32[4]{0:T(128)} %get-tuple-element.105.part_ref, s32[4]{0:T(128)} %get-tuple-element.101.keep_ref, bf16[512,1536]{1,0:T(8,128)(2,1)} %copy.90.left_ref, f32[8,512,512]{2,1,0:T(8,128)} %copy-done.2, ...), custom_call_target="tpu_custom_call" | custom-call | flops 1610612736 | bytes 6291456 | tf_op jit(solution)/shard_map/pallas_call | solution.py:117
  471.1 12.0 %collective-permute-done.36 = f32[512,512]{1,0:T(8,128)S(1)} collective-permute-done((f32[512,512]{1,0:T(8,128)S(1)}, f32[512,512]{1,0:T(8,128)S(1)}, u32[]{:S(2)}, u32[]{:S(2)}) %collective-permute-start.36) | collective-permute-done | bytes 1048608 | tf_op jit(solution)/shard_map/ppermute | solution.py:269
  483.4 1.5 pad_maximum_fusion.1
  484.9 1.4 copy-done.8
  486.3 7.5 %shard_map.65 = f32[1024,512]{1,0:T(8,128)} custom-call(f32[1024,512]{1,0:T(8,128)S(1)} %copy-done, f32[4,256,512]{2,1,0:T(8,128)} %bitcast.175, f32[512,512]{1,0:T(8,128)S(1)} %shard_map.62.inverse_ref, f32[512,512]{1,0:T(8,128)S(1)} %fusion.21.mine_ref, f32[4,512,256]{2,1,0:T(8,128)} %shard_map.63.rest_0_, f32[4,512,256]{2,1,0:T(8,128)} %copy-done.8, ...), custom_call_target="tpu_custom_call" | custom-call | flops 3221225472 | bytes 16777216 | tf_op jit(solution)/shard_map/pallas_call | solution.py:216
  (168 shorter events, 48.3 us)
Async XLA Ops:
  0.6 11.3 %slice-start = ((f32[1024,512]{1,0:T(8,128)}), f32[512,512]{1,0:T(8,128)S(1)}, s32[]{:S(2)}) async-start(f32[1024,512]{1,0:T(8,128)} %parent_ref.1), calls=%async_computation | async-start | bytes 2097152 | tf_op jit(solution)/shard_map/slice | solution.py:326
  7.5 141.8 %copy-start.16 = (s32[16]{0:T(128)}, s32[16]{0:T(128)S(1)}, u32[]{:S(2)}) copy-start(s32[16]{0:T(128)S(1)} %gather_fusion.1) | copy-start | bytes 196
  12.3 26.6 %copy-start.5 = (f32[512,512]{0,1:T(8,128)}, f32[512,512]{0,1:T(8,128)S(1)}, u32[]{:S(2)}) copy-start(f32[512,512]{0,1:T(8,128)S(1)} %copy.108) | copy-start | bytes 3145732
  13.4 27.0 %collective-permute-start.2 = (f32[256,512]{0,1:T(8,128)}, f32[256,512]{0,1:T(8,128)}, u32[]{:S(2)}, u32[]{:S(2)}) collective-permute-start(f32[256,512]{0,1:T(8,128)} %constant_dynamic-slice_fusion.10), channel_id=1, source_target_pairs={{0,8},{8,0},{16,24},{24,16},{1,9},{9,1},{17,25},{25,17},{2,10},{10... | collective-permute-start | bytes 1572872 | tf_op jit(solution)/shard_map/ppermute | solution.py:143
  15.9 34.3 %collective-permute-start = (f32[512,512]{1,0:T(8,128)}, f32[512,512]{1,0:T(8,128)}, u32[]{:S(2)}, u32[]{:S(2)}) collective-permute-start(f32[512,512]{1,0:T(8,128)} %slice_bitcast_fusion.6), channel_id=1, source_target_pairs={{0,2},{1,3},{2,4},{3,5},{4,6},{5,7},{8,10},{9,11},{10,12},{11,13},... | collective-permute-start | bytes 3145736 | tf_op jit(solution)/shard_map/ppermute | solution.py:241
  21.7 28.5 %collective-permute-start.1 = (f32[512,512]{1,0:T(8,128)}, f32[512,512]{1,0:T(8,128)}, u32[]{:S(2)}, u32[]{:S(2)}) collective-permute-start(f32[512,512]{1,0:T(8,128)} %slice_bitcast_fusion.6), channel_id=1, source_target_pairs={{2,0},{3,1},{4,2},{5,3},{6,4},{7,5},{10,8},{11,9},{12,10},{13,11},... | collective-permute-start | bytes 3145736 | tf_op jit(solution)/shard_map/ppermute | solution.py:242
  41.6 8.6 %collective-permute-start.3 = (f32[128,512]{0,1:T(8,128)S(1)}, f32[128,512]{0,1:T(8,128)S(1)}, u32[]{:S(2)}, u32[]{:S(2)}) collective-permute-start(f32[128,512]{0,1:T(8,128)S(1)} %constant_dynamic-slice_fusion.9), channel_id=1, source_target_pairs={{0,16},{8,24},{16,0},{24,8},{1,17},{9,25},{17,1},{25,9},{2,18},{10... | collective-permute-start | bytes 786440 | tf_op jit(solution)/shard_map/ppermute | solution.py:143
  50.2 26.9 %collective-permute-start.4 = (f32[512,512]{1,0:T(8,128)}, f32[512,512]{1,0:T(8,128)S(1)}, u32[]{:S(2)}, u32[]{:S(2)}) collective-permute-start(f32[512,512]{1,0:T(8,128)} %collective-permute-done.1), channel_id=1, source_target_pairs={{2,0},{3,1},{4,2},{5,3},{10,8},{11,9},{12,10},{13,11},{18,16},{19,... | collective-permute-start | bytes 3145736 | tf_op jit(solution)/shard_map/ppermute | solution.py:242
  51.5 26.9 %collective-permute-start.6 = (f32[512,512]{1,0:T(8,128)}, f32[512,512]{1,0:T(8,128)}, u32[]{:S(2)}, u32[]{:S(2)}) collective-permute-start(f32[512,512]{1,0:T(8,128)} %collective-permute-done), channel_id=1, source_target_pairs={{2,4},{3,5},{4,6},{5,7},{10,12},{11,13},{12,14},{13,15},{18,20},{1... | collective-permute-start | bytes 3145736 | tf_op jit(solution)/shard_map/ppermute | solution.py:241
  77.1 61.1 %copy-start.10 = (f32[512,512]{1,0:T(8,128)}, f32[512,512]{1,0:T(8,128)S(1)}, u32[]{:S(2)}) copy-start(f32[512,512]{1,0:T(8,128)S(1)} %collective-permute-done.4) | copy-start | bytes 3145732
  77.1 31.2 %collective-permute-start.5 = (f32[512,512]{1,0:T(8,128)S(1)}, f32[512,512]{1,0:T(8,128)}, u32[]{:S(2)}, u32[]{:S(2)}) collective-permute-start(f32[512,512]{1,0:T(8,128)S(1)} %collective-permute-done.4), channel_id=1, source_target_pairs={{2,0},{3,1},{10,8},{11,9},{18,16},{19,17},{26,24},{27,25}} | collective-permute-start | bytes 3145736 | tf_op jit(solution)/shard_map/ppermute | solution.py:242
  78.4 29.9 %collective-permute-start.7 = (f32[512,512]{1,0:T(8,128)}, f32[512,512]{1,0:T(8,128)}, u32[]{:S(2)}, u32[]{:S(2)}) collective-permute-start(f32[512,512]{1,0:T(8,128)} %collective-permute-done.6), channel_id=1, source_target_pairs={{4,6},{5,7},{12,14},{13,15},{20,22},{21,23},{28,30},{29,31}} | collective-permute-start | bytes 3145736 | tf_op jit(solution)/shard_map/ppermute | solution.py:241
  80.2 9.3 %collective-permute-start.9 = (f32[64,512]{0,1:T(8,128)S(1)}, f32[64,512]{0,1:T(8,128)S(1)}, u32[]{:S(2)}, u32[]{:S(2)}) collective-permute-start(f32[64,512]{0,1:T(8,128)S(1)} %constant_dynamic-slice_fusion.8), channel_id=1, source_target_pairs={{0,1},{1,0},{2,3},{3,2},{4,5},{5,4},{6,7},{7,6},{8,9},{9,8},{10,11... | collective-permute-start | bytes 393224 | tf_op jit(solution)/shard_map/ppermute | solution.py:143
  81.8 63.6 %collective-permute-start.15 = (f32[512,512]{1,0:T(8,128)}, f32[512,512]{1,0:T(8,128)}, u32[]{:S(2)}, u32[]{:S(2)}) collective-permute-start(f32[512,512]{1,0:T(8,128)} %slice_bitcast_fusion.6), channel_id=1, source_target_pairs={{0,1},{1,0},{2,3},{3,2},{4,5},{5,4},{6,7},{7,6},{8,9},{9,8},{10,11... | collective-permute-start | bytes 3145736 | tf_op jit(solution)/shard_map/ppermute | solution.py:248
  89.8 18.4 %collective-permute-start.10 = (f32[32,512]{0,1:T(8,128)S(1)}, f32[32,512]{0,1:T(8,128)S(1)}, u32[]{:S(2)}, u32[]{:S(2)}) collective-permute-start(f32[32,512]{0,1:T(8,128)S(1)} %constant_dynamic-slice_fusion.7), channel_id=1, source_target_pairs={{0,2},{1,3},{2,0},{3,1},{4,6},{5,7},{6,4},{7,5},{8,10},{9,11},{10,... | collective-permute-start | bytes 196616 | tf_op jit(solution)/shard_map/ppermute | solution.py:143
  94.5 67.9 %collective-permute-start.25 = (f32[512,512]{1,0:T(8,128)}, f32[512,512]{1,0:T(8,128)}, u32[]{:S(2)}, u32[]{:S(2)}) collective-permute-start(f32[512,512]{1,0:T(8,128)} %pad_maximum_fusion.10), channel_id=1, source_target_pairs={{1,0},{2,3},{3,2},{4,5},{5,4},{6,7},{7,6},{9,8},{10,11},{11,10},{1... | collective-permute-start | bytes 3145736 | tf_op jit(solution)/shard_map/ppermute | solution.py:334
  108.5 12.5 %collective-permute-start.11 = (f32[16,512]{0,1:T(8,128)S(1)}, f32[16,512]{0,1:T(8,128)S(1)}, u32[]{:S(2)}, u32[]{:S(2)}) collective-permute-start(f32[16,512]{0,1:T(8,128)S(1)} %constant_dynamic-slice_fusion.6), channel_id=1, source_target_pairs={{0,4},{1,5},{2,6},{3,7},{4,0},{5,1},{6,2},{7,3},{8,12},{9,13},{10,... | collective-permute-start | bytes 98312 | tf_op jit(solution)/shard_map/ppermute | solution.py:143
  111.3 51.1 %copy-start.14 = (s32[16]{0:T(128)}, s32[16]{0:T(128)S(1)}, u32[]{:S(2)}) copy-start(s32[16]{0:T(128)S(1)} %get-tuple-element.143) | copy-start | bytes 196
  111.3 51.1 %copy-start.19 = (s32[16]{0:T(128)}, s32[16]{0:T(128)S(1)}, u32[]{:S(2)}) copy-start(s32[16]{0:T(128)S(1)} %get-tuple-element.48) | copy-start | bytes 196
  121.0 10.2 %collective-permute-start.12 = (f32[16,512]{0,1:T(8,128)S(1)}, f32[16,512]{0,1:T(8,128)S(1)}, u32[]{:S(2)}, u32[]{:S(2)}) collective-permute-start(f32[16,512]{0,1:T(8,128)S(1)} %dynamic-slice_add_fusion.4), channel_id=1, source_target_pairs={{0,4},{1,5},{2,6},{3,7},{4,0},{5,1},{6,2},{7,3},{8,12},{9,13},{10,... | collective-permute-start | bytes 98312 | tf_op jit(solution)/shard_map/ppermute | solution.py:143
  131.5 6.7 %collective-permute-start.13 = (f32[32,512]{1,0:T(8,128)S(1)}, f32[32,512]{1,0:T(8,128)S(1)}, u32[]{:S(2)}, u32[]{:S(2)}) collective-permute-start(f32[32,512]{1,0:T(8,128)S(1)} %pad_maximum_fusion.16), channel_id=1, source_target_pairs={{0,2},{1,3},{2,0},{3,1},{4,6},{5,7},{6,4},{7,5},{8,10},{9,11},{10,... | collective-permute-start | bytes 196616 | tf_op jit(solution)/shard_map/ppermute | solution.py:143
  138.2 7.2 %collective-permute-start.14 = (f32[64,512]{1,0:T(8,128)S(1)}, f32[64,512]{1,0:T(8,128)S(1)}, u32[]{:S(2)}, u32[]{:S(2)}) collective-permute-start(f32[64,512]{1,0:T(8,128)S(1)} %pad_maximum_fusion.15), channel_id=1, source_target_pairs={{0,1},{1,0},{2,3},{3,2},{4,5},{5,4},{6,7},{7,6},{8,9},{9,8},{10,11... | collective-permute-start | bytes 393224 | tf_op jit(solution)/shard_map/ppermute | solution.py:143
  144.9 31.5 %copy-start.4 = (f32[512,512]{1,0:T(8,128)}, f32[512,512]{1,0:T(8,128)S(1)}, u32[]{:S(2)}) copy-start(f32[512,512]{1,0:T(8,128)S(1)} %get-tuple-element.53) | copy-start | bytes 3145732
  144.9 23.1 %collective-permute-start.8 = (f32[512,512]{1,0:T(8,128)}, f32[512,512]{1,0:T(8,128)}, u32[]{:S(2)}, u32[]{:S(2)}) collective-permute-start(f32[512,512]{1,0:T(8,128)} %get-tuple-element.52), channel_id=1, source_target_pairs={{0,1},{1,0},{2,3},{3,2},{4,5},{5,4},{6,7},{7,6},{8,9},{9,8},{10,11... | collective-permute-start | bytes 3145736 | tf_op jit(solution)/shard_map/ppermute | solution.py:248
  145.4 115.6 %collective-permute-start.18 = (f32[512,512]{1,0:T(8,128)}, f32[512,512]{1,0:T(8,128)}, u32[]{:S(2)}, u32[]{:S(2)}) collective-permute-start(f32[512,512]{1,0:T(8,128)} %get-tuple-element.32), channel_id=1, source_target_pairs={{1,4},{2,7},{3,6},{4,1},{5,0},{6,3},{7,2},{9,12},{10,15},{11,14},{... | collective-permute-start | bytes 3145736 | tf_op jit(solution)/shard_map/ppermute | solution.py:334
  146.7 115.6 %collective-permute-start.17 = (f32[512,512]{1,0:T(8,128)}, f32[512,512]{1,0:T(8,128)}, u32[]{:S(2)}, u32[]{:S(2)}) collective-permute-start(f32[512,512]{1,0:T(8,128)} %get-tuple-element.31), channel_id=1, source_target_pairs={{1,7},{2,4},{3,5},{4,2},{5,3},{6,0},{7,1},{9,15},{10,12},{11,13},{... | collective-permute-start | bytes 3145736 | tf_op jit(solution)/shard_map/ppermute | solution.py:334
  148.0 115.6 %collective-permute-start.16 = (f32[512,512]{1,0:T(8,128)}, f32[512,512]{1,0:T(8,128)}, u32[]{:S(2)}, u32[]{:S(2)}) collective-permute-start(f32[512,512]{1,0:T(8,128)} %get-tuple-element.30), channel_id=1, source_target_pairs={{1,6},{2,5},{3,4},{4,3},{5,2},{6,1},{7,0},{9,14},{10,13},{11,12},{... | collective-permute-start | bytes 3145736 | tf_op jit(solution)/shard_map/ppermute | solution.py:334
  160.9 3.2 copy-start.13
  160.9 100.2 %copy-start.12 = (f32[512,512]{1,0:T(8,128)S(1)}, f32[512,512]{1,0:T(8,128)}, u32[]{:S(2)}) copy-start(f32[512,512]{1,0:T(8,128)} %get-tuple-element.37) | copy-start | bytes 3145732
  160.9 101.5 %copy-start.11 = (f32[512,512]{1,0:T(8,128)S(1)}, f32[512,512]{1,0:T(8,128)}, u32[]{:S(2)}) copy-start(f32[512,512]{1,0:T(8,128)} %get-tuple-element.35) | copy-start | bytes 3145732
  164.1 162.2 %collective-permute-start.27 = (f32[512,512]{1,0:T(8,128)S(1)}, f32[512,512]{1,0:T(8,128)S(1)}, u32[]{:S(2)}, u32[]{:S(2)}) collective-permute-start(f32[512,512]{1,0:T(8,128)S(1)} %copy-done.13), channel_id=1, source_target_pairs={{1,5},{2,6},{3,7},{4,0},{5,1},{6,2},{7,3},{9,13},{10,14},{11,15},{... | collective-permute-start | bytes 3145736 | tf_op jit(solution)/shard_map/ppermute | solution.py:334
  168.0 162.6 %collective-permute-start.19 = (f32[3,512,512]{2,1,0:T(8,128)S(1)}, f32[3,512,512]{2,1,0:T(8,128)S(1)}, u32[]{:S(2)}, u32[]{:S(2)}) collective-permute-start(f32[3,512,512]{2,1,0:T(8,128)S(1)} %pad_maximum_fusion), channel_id=1, source_target_pairs={{0,1},{1,0},{2,3},{3,2},{4,5},{5,4},{6,7},{7,6},{8,9},{9,8},{10,11... | collective-permute-start | bytes 9437192 | tf_op jit(solution)/shard_map/ppermute | solution.py:248
  261.0 22.7 %collective-permute-start.26 = (f32[512,512]{1,0:T(8,128)S(1)}, f32[512,512]{1,0:T(8,128)S(1)}, u32[]{:S(2)}, u32[]{:S(2)}) collective-permute-start(f32[512,512]{1,0:T(8,128)S(1)} %copy-done.12), channel_id=1, source_target_pairs={{1,3},{2,0},{3,1},{4,6},{5,7},{6,4},{7,5},{9,11},{10,8},{11,9},{12... | collective-permute-start | bytes 3145736 | tf_op jit(solution)/shard_map/ppermute | solution.py:334
  262.4 45.7 %collective-permute-start.22 = (f32[512,512]{1,0:T(8,128)S(1)}, f32[512,512]{1,0:T(8,128)S(1)}, u32[]{:S(2)}, u32[]{:S(2)}) collective-permute-start(f32[512,512]{1,0:T(8,128)S(1)} %copy-done.11), channel_id=1, source_target_pairs={{1,2},{2,1},{3,0},{4,7},{5,6},{6,5},{7,4},{9,10},{10,9},{11,8},{12... | collective-permute-start | bytes 3145736 | tf_op jit(solution)/shard_map/ppermute | solution.py:334
  330.5 7.5 %copy-start.3 = (f32[8,512,512]{2,1,0:T(8,128)}, f32[8,512,512]{2,1,0:T(8,128)S(1)}, u32[]{:S(2)}) copy-start(f32[8,512,512]{2,1,0:T(8,128)S(1)} %bitcast_dynamic-update-slice_fusion.piece_ref) | copy-start | bytes 25165828
  333.6 3.3 copy-start.2
  339.9 5.9 %copy-start.6 = (f32[512,512]{0,1:T(8,128)S(1)}, f32[512,512]{0,1:T(8,128)}, u32[]{:S(2)}) copy-start(f32[512,512]{0,1:T(8,128)} %copy-done.5) | copy-start | bytes 3145732
  339.9 6.9 %copy-start.17 = (s32[16]{0:T(128)S(1)}, s32[16]{0:T(128)}, u32[]{:S(2)}) copy-start(s32[16]{0:T(128)} %copy-done.16) | copy-start | bytes 196
  339.9 6.9 %copy-start.18 = (s32[16]{0:T(128)S(1)}, s32[16]{0:T(128)}, u32[]{:S(2)}) copy-start(s32[16]{0:T(128)} %get-tuple-element.49) | copy-start | bytes 196
  339.9 7.6 %copy-start.9 = (f32[512,256]{1,0:T(8,128)S(1)}, f32[512,256]{1,0:T(8,128)}, u32[]{:S(2)}) copy-start(f32[512,256]{1,0:T(8,128)} %get-tuple-element.75) | copy-start | bytes 1572868
  344.5 7.0 %copy-start.15 = (s32[16]{0:T(128)S(1)}, s32[16]{0:T(128)}, u32[]{:S(2)}) copy-start(s32[16]{0:T(128)} %copy-done.14) | copy-start | bytes 196
  344.5 7.6 %copy-start.20 = (s32[16]{0:T(128)S(1)}, s32[16]{0:T(128)}, u32[]{:S(2)}) copy-start(s32[16]{0:T(128)} %copy-done.19) | copy-start | bytes 196
  346.8 2.3 collective-permute-start.28
  348.6 11.6 %collective-permute-start.20 = (f32[256,512]{1,0:T(8,128)S(1)}, f32[256,512]{1,0:T(8,128)S(1)}, u32[]{:S(2)}, u32[]{:S(2)}) collective-permute-start(f32[256,512]{1,0:T(8,128)S(1)} %constant_dynamic-slice_fusion.5), channel_id=1, source_target_pairs={{0,8},{8,0},{16,24},{24,16},{1,9},{9,1},{17,25},{25,17},{2,10},{10... | collective-permute-start | bytes 1572872 | tf_op jit(solution)/shard_map/ppermute | solution.py:143
  350.3 8.9 %collective-permute-start.29 = (f32[128,512]{1,0:T(8,128)S(1)}, f32[128,512]{1,0:T(8,128)S(1)}, u32[]{:S(2)}, u32[]{:S(2)}) collective-permute-start(f32[128,512]{1,0:T(8,128)S(1)} %constant_dynamic-slice_fusion), channel_id=1, source_target_pairs={{0,16},{8,24},{16,0},{24,8},{1,17},{9,25},{17,1},{25,9},{2,18},{10... | collective-permute-start | bytes 786440 | tf_op jit(solution)/shard_map/ppermute | solution.py:143
  359.3 59.3 %collective-permute-start.30 = (f32[4,512,256]{2,1,0:T(8,128)}, f32[4,512,256]{2,1,0:T(8,128)}, u32[]{:S(2)}, u32[]{:S(2)}) collective-permute-start(f32[4,512,256]{2,1,0:T(8,128)} %shard_map.61), channel_id=1, source_target_pairs={{0,8},{8,0},{16,24},{24,16},{1,9},{9,1},{17,25},{25,17},{2,10},{10... | collective-permute-start | bytes 6291464 | tf_op jit(solution)/shard_map/ppermute | solution.py:143
  359.3 9.2 %collective-permute-start.31 = (f32[128,512]{1,0:T(8,128)S(1)}, f32[128,512]{1,0:T(8,128)S(1)}, u32[]{:S(2)}, u32[]{:S(2)}) collective-permute-start(f32[128,512]{1,0:T(8,128)S(1)} %dynamic-slice_add_fusion.3), channel_id=1, source_target_pairs={{0,16},{8,24},{16,0},{24,8},{1,17},{9,25},{17,1},{25,9},{2,18},{10... | collective-permute-start | bytes 786440 | tf_op jit(solution)/shard_map/ppermute | solution.py:143
  360.4 13.4 %collective-permute-start.21 = (f32[128,512]{1,0:T(8,128)S(1)}, f32[128,512]{1,0:T(8,128)S(1)}, u32[]{:S(2)}, u32[]{:S(2)}) collective-permute-start(f32[128,512]{1,0:T(8,128)S(1)} %constant_dynamic-slice_fusion.4), channel_id=1, source_target_pairs={{0,16},{8,24},{16,0},{24,8},{1,17},{9,25},{17,1},{25,9},{2,18},{10... | collective-permute-start | bytes 786440 | tf_op jit(solution)/shard_map/ppermute | solution.py:143
  369.4 12.4 %collective-permute-start.32 = (f32[256,512]{1,0:T(8,128)}, f32[256,512]{1,0:T(8,128)}, u32[]{:S(2)}, u32[]{:S(2)}) collective-permute-start(f32[256,512]{1,0:T(8,128)} %pad_maximum_fusion.13), channel_id=1, source_target_pairs={{0,8},{8,0},{16,24},{24,16},{1,9},{9,1},{17,25},{25,17},{2,10},{10... | collective-permute-start | bytes 1572872 | tf_op jit(solution)/shard_map/ppermute | solution.py:143
  373.8 8.0 %collective-permute-start.23 = (f32[128,512]{1,0:T(8,128)S(1)}, f32[128,512]{1,0:T(8,128)S(1)}, u32[]{:S(2)}, u32[]{:S(2)}) collective-permute-start(f32[128,512]{1,0:T(8,128)S(1)} %add_subtract_fusion), channel_id=1, source_target_pairs={{0,16},{8,24},{16,0},{24,8},{1,17},{9,25},{17,1},{25,9},{2,18},{10... | collective-permute-start | bytes 786440 | tf_op jit(solution)/shard_map/ppermute | solution.py:143
  384.0 60.0 %collective-permute-start.33 = (f32[512,512]{1,0:T(8,128)}, f32[512,512]{1,0:T(8,128)}, u32[]{:S(2)}, u32[]{:S(2)}) collective-permute-start(f32[512,512]{1,0:T(8,128)} %pad_maximum_fusion.11), channel_id=1, source_target_pairs={{0,2},{1,3},{10,12},{11,13},{20,22},{21,23},{30,24},{31,25}} | collective-permute-start | bytes 3145736 | tf_op jit(solution)/shard_map/ppermute | solution.py:259
  392.9 51.1 %collective-permute-start.34 = (f32[512,512]{1,0:T(8,128)}, f32[512,512]{1,0:T(8,128)}, u32[]{:S(2)}, u32[]{:S(2)}) collective-permute-start(f32[512,512]{1,0:T(8,128)} %pad_maximum_fusion.11), channel_id=1, source_target_pairs={{0,4},{1,5},{10,14},{11,15},{20,16},{21,17},{30,26},{31,27}} | collective-permute-start | bytes 3145736 | tf_op jit(solution)/shard_map/ppermute | solution.py:259
  400.9 43.1 %collective-permute-start.35 = (f32[512,512]{1,0:T(8,128)}, f32[512,512]{1,0:T(8,128)}, u32[]{:S(2)}, u32[]{:S(2)}) collective-permute-start(f32[512,512]{1,0:T(8,128)} %pad_maximum_fusion.11), channel_id=1, source_target_pairs={{0,6},{1,7},{10,8},{11,9},{20,18},{21,19},{30,28},{31,29}} | collective-permute-start | bytes 3145736 | tf_op jit(solution)/shard_map/ppermute | solution.py:259
  404.0 18.3 %collective-permute-start.24 = (f32[256,512]{1,0:T(8,128)}, f32[256,512]{1,0:T(8,128)S(1)}, u32[]{:S(2)}, u32[]{:S(2)}) collective-permute-start(f32[256,512]{1,0:T(8,128)} %pad_maximum_fusion.12), channel_id=1, source_target_pairs={{0,8},{8,0},{16,24},{24,16},{1,9},{9,1},{17,25},{25,17},{2,10},{10... | collective-permute-start | bytes 1572872 | tf_op jit(solution)/shard_map/ppermute | solution.py:143
  411.7 7.4 %copy-start.7 = (f32[4,512,256]{2,1,0:T(8,128)S(1)}, f32[4,512,256]{2,1,0:T(8,128)}, u32[]{:S(2)}) copy-start(f32[4,512,256]{2,1,0:T(8,128)} %shard_map.60) | copy-start | bytes 6291460
  418.5 66.4 %collective-permute-start.37 = (f32[4,512,256]{2,1,0:T(8,128)}, f32[4,512,256]{2,1,0:T(8,128)S(1)}, u32[]{:S(2)}, u32[]{:S(2)}) collective-permute-start(f32[4,512,256]{2,1,0:T(8,128)} %shard_map.64), channel_id=1, source_target_pairs={{0,8},{8,0},{16,24},{24,16},{1,9},{9,1},{17,25},{25,17},{2,10},{10... | collective-permute-start | bytes 6291464 | tf_op jit(solution)/shard_map/ppermute | solution.py:143
  422.3 62.6 %collective-permute-start.38 = (f32[4,512,256]{2,1,0:T(8,128)}, f32[4,512,256]{2,1,0:T(8,128)}, u32[]{:S(2)}, u32[]{:S(2)}) collective-permute-start(f32[4,512,256]{2,1,0:T(8,128)} %add.489), channel_id=1, source_target_pairs={{0,16},{8,24},{16,0},{24,8},{1,17},{9,25},{17,1},{25,9},{2,18},{10... | collective-permute-start | bytes 6291464 | tf_op jit(solution)/shard_map/ppermute | solution.py:143
  446.4 36.7 %collective-permute-start.36 = (f32[512,512]{1,0:T(8,128)S(1)}, f32[512,512]{1,0:T(8,128)S(1)}, u32[]{:S(2)}, u32[]{:S(2)}) collective-permute-start(f32[512,512]{1,0:T(8,128)S(1)} %add_add_fusion), channel_id=1, source_target_pairs={{0,1},{1,0},{2,3},{3,2},{4,5},{5,4},{6,7},{7,6},{8,9},{9,8},{10,11... | collective-permute-start | bytes 3145736 | tf_op jit(solution)/shard_map/ppermute | solution.py:269
  470.1 16.2 %copy-start = (f32[1024,512]{1,0:T(8,128)S(1)}, f32[1024,512]{1,0:T(8,128)}, u32[]{:S(2)}) copy-start(f32[1024,512]{1,0:T(8,128)} %parent_ref.1) | copy-start | bytes 6291460
  471.1 22.7 %copy-start.1 = (f32[512,512]{1,0:T(8,128)}, f32[512,512]{1,0:T(8,128)S(1)}, u32[]{:S(2)}) copy-start(f32[512,512]{1,0:T(8,128)S(1)} %fusion.21.mine_ref) | copy-start | bytes 3145732
  484.9 1.4 copy-start.8

commit v14 on v10

--- a/solution.py
+++ b/solution.py
@@ -358,20 +358,21 @@
     for k in far[:EARLY]:
         row, _ = lax.optimization_barrier((rows[k], (steps[-1], halved, beside)))
         received[k] = moved(k, row)
-    others = lax.optimization_barrier((jnp.stack(line[1:]), pivots))[0]
+    others, corner = lax.optimization_barrier((jnp.stack(line[1:]), corner))
+    pivots, corner = lax.optimization_barrier((pivots, corner))
     others = [from_beside(others, "col", ny, j) for j in near]
     gathered = line + [x for j in range(ny - 1) for x in [beside[j]] + [others[j][k] for k in range(len(line) - 1)]]
     slots = (source % ny - y) % ny * len(line) + (z - source // ny) % len(line)
 
     inverse = inverse_factor(pivots)
     for k in far[EARLY:]:
-        row, _ = lax.optimization_barrier((rows[k], pivots if k == far[EARLY] else others))
+        row, _ = lax.optimization_barrier((rows[k], inverse))
         received[k] = moved(k, row)
     places = col ^ source
     child_mine = product(inverse, front[:P_SIZE], 1, 0)
 
     early = [received[k] for k in far[:EARLY]]
-    inverse, early, corner = lax.optimization_barrier((inverse, early, corner))
+    inverse, early = lax.optimization_barrier((inverse, early))
     received.update(zip(far[:EARLY], early))
     factor = jnp.stack([product(inverse, x, 1, 0) for x in gathered])
 

time: 552 us -> 490 us (0.89)
  waiting for transfers between devices: 258 us -> 210 us
  other arithmetic: 56.8 us -> 42.6 us
  Pallas kernels: 81.6 us -> 92.3 us
    ppermute x19, waiting for transfers between devices: 116 us -> 59.3 us  [flip(): return lax.ppermute(x, axis, [(i, i ^ bit) for i in range(n)])]
    ppermute x7, waiting for transfers between devices: 97.5 us -> 119 us  [moved(): return lax.ppermute(rows, 'col', pairs)]
    pallas_call x2, Pallas kernels: 43.1 us -> 53.8 us  [inverse_factor(): pl.pallas_call(inverse_factor_kernel, out_shape=jax.ShapeDtypeStruct((n,...]
    ppermute x3, waiting for transfers between devices: 8.48 us -> 0.01 us  [from_beside(): lax.ppermute(x, axis, [(c, c // ny * ny + (c % ny - j) % ny) for c in ran...]
    unnamed x7, other arithmetic: 16.5 us -> 9.28 us
  transfers between devices with their start and end apart: 39 -> 39, of which waited for: 13 -> 14; matrix products, arithmetic and copies ran while one was open for 16% -> 15% of each run, Pallas kernels for 13% -> 17%
where the time goes in v14:
time: 490 us; the launch traced here: 482 us
  waiting for transfers between devices  210 us (43%)
  Pallas kernels  92.3 us (19%)
  starting transfers between devices  62.6 us (13%)
  other arithmetic  42.6 us (9%)
  local copies, waits for them, and re-layouts  30 us (6%)
  between operations  27.8 us (6%)
  matrix products  17 us (3%)
    ppermute x7, waiting for transfers between devices, moved(): return lax.ppermute(rows, 'col', pairs)  119 us
    ppermute x19, waiting for transfers between devices, flip(): return lax.ppermute(x, axis, [(i, i ^ bit) for i in range(n)])  59.3 us
    pallas_call x2, Pallas kernels, inverse_factor(): pl.pallas_call(inverse_factor_kernel, out_shape=jax.ShapeDtypeStruct((n,...  53.8 us
    pallas_call x5, Pallas kernels, spread_update(): pl.pallas_call(spread_kernel, grid_spec=pltpu.PrefetchScalarGridSpec(num_...  31 us
    ppermute x19, starting transfers between devices, flip(): return lax.ppermute(x, axis, [(i, i ^ bit) for i in range(n)])  26.1 us
    ppermute x3, waiting for transfers between devices, line_gather(): lax.ppermute(ends[1], axis, [(c, c - ny) for c in range(n) if 0 < c // ny...  19.6 us
    dot_general x11, matrix products, product(): lax.dot_general(a, b, (((ca,), (cb,)), ((), ())), precision=precision)  17 us
    ppermute x1, waiting for transfers between devices, share_beside(): shares.append(lax.ppermute(got, 'col', pairs))  12 us
  transfers between devices with their start and end apart: 39, of which 14 were waited for; matrix products, arithmetic and copies ran while one was open for 15% of the time, Pallas kernels for 17%

profile of v14, /device:TPU:0, one launch (start us, length us, event | category | flops | bytes accessed | tf_op | source)
XLA Modules:
  0.0 482.2 jit_solution(15935540529128433458)
XLA Ops:
  0.6 2.4 slice_bitcast_fusion.6
  3.0 5.9 %collective-permute-start = (f32[512,512]{1,0:T(8,128)}, f32[512,512]{1,0:T(8,128)}, u32[]{:S(2)}, u32[]{:S(2)}) collective-permute-start(f32[512,512]{1,0:T(8,128)} %slice_bitcast_fusion.6), channel_id=1, source_target_pairs={{0,2},{1,3},{2,4},{3,5},{4,6},{5,7},{8,10},{9,11},{10,12},{11,13},... | collective-permute-start | bytes 3145736 | tf_op jit(solution)/shard_map/ppermute | solution.py:241
  18.8 1.6 constant_dynamic-slice_fusion.14
  32.9 4.5 dynamic-slice_bitcast_fusion.1
  37.4 1.5 pad_maximum_fusion.6
  41.2 1.6 collective-permute-start.3
  43.9 1.6 pad_maximum_fusion.3
  45.5 4.6 collective-permute-done.3
  50.1 1.3 collective-permute-start.4
  51.4 1.7 collective-permute-start.6
  53.1 1.5 collective-permute-start.15
  58.3 19.6 %collective-permute-done.4 = f32[512,512]{1,0:T(8,128)S(1)} collective-permute-done((f32[512,512]{1,0:T(8,128)}, f32[512,512]{1,0:T(8,128)S(1)}, u32[]{:S(2)}, u32[]{:S(2)}) %collective-permute-start.4) | collective-permute-done | bytes 1048608 | tf_op jit(solution)/shard_map/ppermute | solution.py:242
  78.0 1.3 collective-permute-start.5
  80.1 1.6 collective-permute-start.9
  81.8 24.4 %collective-permute-done.9 = f32[64,512]{0,1:T(8,128)S(1)} collective-permute-done((f32[64,512]{0,1:T(8,128)S(1)}, f32[64,512]{0,1:T(8,128)S(1)}, u32[]{:S(2)}, u32[]{:S(2)}) %collective-permute-start.9) | collective-permute-done | bytes 131104 | tf_op jit(solution)/shard_map/ppermute | solution.py:143
  106.5 6.1 %collective-permute-start.10 = (f32[32,512]{0,1:T(8,128)S(1)}, f32[32,512]{0,1:T(8,128)S(1)}, u32[]{:S(2)}, u32[]{:S(2)}) collective-permute-start(f32[32,512]{0,1:T(8,128)S(1)} %constant_dynamic-slice_fusion.7), channel_id=1, source_target_pairs={{0,2},{1,3},{2,0},{3,1},{4,6},{5,7},{6,4},{7,5},{8,10},{9,11},{10,... | collective-permute-start | bytes 196616 | tf_op jit(solution)/shard_map/ppermute | solution.py:143
  113.3 4.1 collective-permute-done.10
  132.8 2.1 collective-permute-start.12
  134.9 5.1 %select_add_fusion.3 = (f32[512,512]{1,0:T(8,128)}, f32[512,512]{1,0:T(8,128)S(1)}, f32[512,512]{1,0:T(8,128)S(1)}, f32[512,512]{1,0:T(8,128)S(1)}) fusion(pred[]{:T(512)S(6)} %eq.104, pred[]{:T(512)S(6)} %eq.103, pred[]{:T(512)S(6)} %eq.96, pred[]{:T(512)S(6)} %eq.95, f32[1,4096,512]{2,1,0:T(8,128)} %param.3, f32[512,512]{1,0:T(8,128)} %collective-permute-done, ...), kind=kLoop, calls=%fused_computation.57 | loop fusion | flops 2621440 | bytes 11534340 | tf_op jit(solution)/shard_map/add | solution.py:350
  140.1 1.6 collective-permute-start.8
  141.6 3.7 collective-permute-done.12
  147.3 2.5 bitcast_dynamic-update-slice_fusion.6
  149.8 1.3 collective-permute-start.18
  151.1 1.3 collective-permute-start.17
  152.4 1.5 collective-permute-start.16
  154.0 8.1 %collective-permute-start.14 = (f32[64,512]{1,0:T(8,128)S(1)}, f32[64,512]{1,0:T(8,128)S(1)}, u32[]{:S(2)}, u32[]{:S(2)}) collective-permute-start(f32[64,512]{1,0:T(8,128)S(1)} %pad_maximum_fusion.15), channel_id=1, source_target_pairs={{0,1},{1,0},{2,3},{3,2},{4,5},{5,4},{6,7},{7,6},{8,9},{9,8},{10,11... | collective-permute-start | bytes 393224 | tf_op jit(solution)/shard_map/ppermute | solution.py:143
  162.4 3.9 collective-permute-done.14
  166.4 1.7 collective-permute-start.19
  168.1 1.5 select_add_fusion.2.a_ref
  169.5 32.3 %shard_map.58 = f32[512,512]{1,0:T(8,128)S(1)} custom-call(f32[512,512]{1,0:T(8,128)S(1)} %select_add_fusion.2.a_ref), custom_call_target="tpu_custom_call" | custom-call | flops 134217728 | bytes 2097152 | tf_op jit(solution)/shard_map/pallas_call | solution.py:86
  201.9 1.3 collective-permute-start.26
  203.2 43.8 %collective-permute-done.18 = f32[512,512]{1,0:T(8,128)S(1)} collective-permute-done((f32[512,512]{1,0:T(8,128)}, f32[512,512]{1,0:T(8,128)S(1)}, u32[]{:S(2)}, u32[]{:S(2)}) %collective-permute-start.18) | collective-permute-done | bytes 1048608 | tf_op jit(solution)/shard_map/ppermute | solution.py:334
  247.0 1.3 collective-permute-start.22
  248.3 1.3 collective-permute-start.27
  249.6 2.2 fusion.7
  251.9 2.2 fusion.6
  256.1 2.2 fusion.3
  258.4 10.2 %collective-permute-done.26 = f32[512,512]{1,0:T(8,128)S(1)} collective-permute-done((f32[512,512]{1,0:T(8,128)S(1)}, f32[512,512]{1,0:T(8,128)S(1)}, u32[]{:S(2)}, u32[]{:S(2)}) %collective-permute-start.26) | collective-permute-done | bytes 1048608 | tf_op jit(solution)/shard_map/ppermute | solution.py:334
  269.7 21.1 %collective-permute-done.22 = f32[512,512]{1,0:T(8,128)S(1)} collective-permute-done((f32[512,512]{1,0:T(8,128)S(1)}, f32[512,512]{1,0:T(8,128)S(1)}, u32[]{:S(2)}, u32[]{:S(2)}) %collective-permute-start.22) | collective-permute-done | bytes 1048608 | tf_op jit(solution)/shard_map/ppermute | solution.py:334
  292.0 43.9 %collective-permute-done.27 = f32[512,512]{1,0:T(8,128)S(1)} collective-permute-done((f32[512,512]{1,0:T(8,128)S(1)}, f32[512,512]{1,0:T(8,128)S(1)}, u32[]{:S(2)}, u32[]{:S(2)}) %collective-permute-start.27) | collective-permute-done | bytes 1048608 | tf_op jit(solution)/shard_map/ppermute | solution.py:334
  343.5 3.3 copy-done.2
  348.1 1.6 copy.90.left_ref
  349.8 4.6 shard_map.59
  360.2 1.6 collective-permute-start.29
  362.9 6.5 %shard_map.61 = f32[4,512,256]{2,1,0:T(8,128)} custom-call(s32[4]{0:T(128)} %dynamic_slice.356.slot_ref, s32[4]{0:T(128)} %get-tuple-element.160.place_ref, s32[4]{0:T(128)} %get-tuple-element.112.part_ref, s32[4]{0:T(128)} %get-tuple-element.108.keep_ref, bf16[512,1536]{1,0:T(8,128)(2,1)} %copy.90.left_ref, f32[8,512,512]{2,1,0:T(8,128)} %copy-done.2, ...), custom_call_target="tpu_custom_call" | custom-call | flops 1610612736 | bytes 6291456 | tf_op jit(solution)/shard_map/pallas_call | solution.py:117
  370.3 1.5 collective-permute-start.21
  371.7 6.9 %collective-permute-done.31 = f32[128,512]{1,0:T(8,128)S(1)} collective-permute-done((f32[128,512]{1,0:T(8,128)S(1)}, f32[128,512]{1,0:T(8,128)S(1)}, u32[]{:S(2)}, u32[]{:S(2)}) %collective-permute-start.31) | collective-permute-done | bytes 262176 | tf_op jit(solution)/shard_map/ppermute | solution.py:143
  379.5 4.3 collective-permute-done.21
  384.6 7.3 %collective-permute-done.23 = f32[128,512]{1,0:T(8,128)S(1)} collective-permute-done((f32[128,512]{1,0:T(8,128)S(1)}, f32[128,512]{1,0:T(8,128)S(1)}, u32[]{:S(2)}, u32[]{:S(2)}) %collective-permute-start.23) | collective-permute-done | bytes 262176 | tf_op jit(solution)/shard_map/ppermute | solution.py:143
  394.2 2.2 collective-permute-start.33
  396.4 2.2 collective-permute-start.34
  398.6 2.2 collective-permute-start.35
  402.3 6.5 %shard_map.60 = f32[4,512,256]{2,1,0:T(8,128)} custom-call(s32[4]{0:T(128)} %dynamic_slice.352.slot_ref, s32[4]{0:T(128)} %get-tuple-element.159.place_ref, s32[4]{0:T(128)} %get-tuple-element.113.part_ref, s32[4]{0:T(128)} %get-tuple-element.109.keep_ref, bf16[512,1536]{1,0:T(8,128)(2,1)} %copy.90.left_ref, f32[8,512,512]{2,1,0:T(8,128)} %copy-done.2, ...), custom_call_target="tpu_custom_call" | custom-call | flops 1610612736 | bytes 6291456 | tf_op jit(solution)/shard_map/pallas_call | solution.py:117
  409.4 6.8 %shard_map.64 = f32[4,512,256]{2,1,0:T(8,128)} custom-call(s32[4]{0:T(128)} %dynamic_slice.364.slot_ref, s32[4]{0:T(128)} %get-tuple-element.162.place_ref, s32[4]{0:T(128)} %get-tuple-element.110.part_ref, s32[4]{0:T(128)} %get-tuple-element.106.keep_ref, bf16[512,1536]{1,0:T(8,128)(2,1)} %copy.90.left_ref, f32[8,512,512]{2,1,0:T(8,128)} %copy-done.2, ...), custom_call_target="tpu_custom_call" | custom-call | flops 1610612736 | bytes 6291456 | tf_op jit(solution)/shard_map/pallas_call | solution.py:117
  416.9 3.2 add.489
  420.3 21.5 %shard_map.62.inverse_ref = f32[512,512]{1,0:T(8,128)S(1)} custom-call(f32[512,512]{1,0:T(8,128)S(1)} %pad_maximum_fusion.9.a_ref), custom_call_target="tpu_custom_call" | custom-call | flops 134217728 | bytes 2097152 | tf_op jit(solution)/shard_map/pallas_call | solution.py:86
  441.8 2.4 add_add_fusion
  444.2 3.6 collective-permute-start.36
  447.8 3.2 convolution_bitcast_fusion.8
  451.5 6.5 %shard_map.63.rest_0_ = f32[4,512,256]{2,1,0:T(8,128)} custom-call(s32[4]{0:T(128)} %dynamic_slice.360.slot_ref, s32[4]{0:T(128)} %get-tuple-element.161.place_ref, s32[4]{0:T(128)} %get-tuple-element.111.part_ref, s32[4]{0:T(128)} %get-tuple-element.107.keep_ref, bf16[512,1536]{1,0:T(8,128)(2,1)} %copy.90.left_ref, f32[8,512,512]{2,1,0:T(8,128)} %copy-done.2, ...), custom_call_target="tpu_custom_call" | custom-call | flops 1610612736 | bytes 6291456 | tf_op jit(solution)/shard_map/pallas_call | solution.py:117
  459.1 12.0 %collective-permute-done.36 = f32[512,512]{1,0:T(8,128)S(1)} collective-permute-done((f32[512,512]{1,0:T(8,128)S(1)}, f32[512,512]{1,0:T(8,128)S(1)}, u32[]{:S(2)}, u32[]{:S(2)}) %collective-permute-start.36) | collective-permute-done | bytes 1048608 | tf_op jit(solution)/shard_map/ppermute | solution.py:269
  471.4 1.5 pad_maximum_fusion.1
  472.9 1.4 copy-done.7
  474.3 7.5 %shard_map.65 = f32[1024,512]{1,0:T(8,128)} custom-call(f32[1024,512]{1,0:T(8,128)S(1)} %copy-done, f32[4,256,512]{2,1,0:T(8,128)} %bitcast.175, f32[512,512]{1,0:T(8,128)S(1)} %shard_map.62.inverse_ref, f32[512,512]{1,0:T(8,128)S(1)} %fusion.21.mine_ref, f32[4,512,256]{2,1,0:T(8,128)} %shard_map.63.rest_0_, f32[4,512,256]{2,1,0:T(8,128)} %copy-done.7, ...), custom_call_target="tpu_custom_call" | custom-call | flops 3221225472 | bytes 16777216 | tf_op jit(solution)/shard_map/pallas_call | solution.py:216
  (172 shorter events, 52.6 us)
Async XLA Ops:
  0.6 20.3 %slice-start = ((f32[1024,512]{1,0:T(8,128)}), f32[512,512]{1,0:T(8,128)S(1)}, s32[]{:S(2)}) async-start(f32[1024,512]{1,0:T(8,128)} %parent_ref.1), calls=%async_computation | async-start | bytes 2097152 | tf_op jit(solution)/shard_map/slice | solution.py:326
  3.0 47.1 %collective-permute-start = (f32[512,512]{1,0:T(8,128)}, f32[512,512]{1,0:T(8,128)}, u32[]{:S(2)}, u32[]{:S(2)}) collective-permute-start(f32[512,512]{1,0:T(8,128)} %slice_bitcast_fusion.6), channel_id=1, source_target_pairs={{0,2},{1,3},{2,4},{3,5},{4,6},{5,7},{8,10},{9,11},{10,12},{11,13},... | collective-permute-start | bytes 3145736 | tf_op jit(solution)/shard_map/ppermute | solution.py:241
  8.9 41.2 %collective-permute-start.1 = (f32[512,512]{1,0:T(8,128)}, f32[512,512]{1,0:T(8,128)}, u32[]{:S(2)}, u32[]{:S(2)}) collective-permute-start(f32[512,512]{1,0:T(8,128)} %slice_bitcast_fusion.6), channel_id=1, source_target_pairs={{2,0},{3,1},{4,2},{5,3},{6,4},{7,5},{10,8},{11,9},{12,10},{13,11},... | collective-permute-start | bytes 3145736 | tf_op jit(solution)/shard_map/ppermute | solution.py:242
  16.8 40.2 %copy-start.17 = (s32[16]{0:T(128)}, s32[16]{0:T(128)S(1)}, u32[]{:S(2)}) copy-start(s32[16]{0:T(128)S(1)} %gather_fusion.1) | copy-start | bytes 196
  21.3 16.1 %copy-start.4 = (f32[512,512]{0,1:T(8,128)}, f32[512,512]{0,1:T(8,128)S(1)}, u32[]{:S(2)}) copy-start(f32[512,512]{0,1:T(8,128)S(1)} %copy.108) | copy-start | bytes 3145732
  22.5 17.6 %collective-permute-start.2 = (f32[256,512]{0,1:T(8,128)}, f32[256,512]{0,1:T(8,128)}, u32[]{:S(2)}, u32[]{:S(2)}) collective-permute-start(f32[256,512]{0,1:T(8,128)} %constant_dynamic-slice_fusion.10), channel_id=1, source_target_pairs={{0,8},{8,0},{16,24},{24,16},{1,9},{9,1},{17,25},{25,17},{2,10},{10... | collective-permute-start | bytes 1572872 | tf_op jit(solution)/shard_map/ppermute | solution.py:143
  41.2 8.8 %collective-permute-start.3 = (f32[128,512]{0,1:T(8,128)S(1)}, f32[128,512]{0,1:T(8,128)S(1)}, u32[]{:S(2)}, u32[]{:S(2)}) collective-permute-start(f32[128,512]{0,1:T(8,128)S(1)} %constant_dynamic-slice_fusion.9), channel_id=1, source_target_pairs={{0,16},{8,24},{16,0},{24,8},{1,17},{9,25},{17,1},{25,9},{2,18},{10... | collective-permute-start | bytes 786440 | tf_op jit(solution)/shard_map/ppermute | solution.py:143
  50.1 27.8 %collective-permute-start.4 = (f32[512,512]{1,0:T(8,128)}, f32[512,512]{1,0:T(8,128)S(1)}, u32[]{:S(2)}, u32[]{:S(2)}) collective-permute-start(f32[512,512]{1,0:T(8,128)} %collective-permute-done.1), channel_id=1, source_target_pairs={{2,0},{3,1},{4,2},{5,3},{10,8},{11,9},{12,10},{13,11},{18,16},{19,... | collective-permute-start | bytes 3145736 | tf_op jit(solution)/shard_map/ppermute | solution.py:242
  51.4 27.8 %collective-permute-start.6 = (f32[512,512]{1,0:T(8,128)}, f32[512,512]{1,0:T(8,128)}, u32[]{:S(2)}, u32[]{:S(2)}) collective-permute-start(f32[512,512]{1,0:T(8,128)} %collective-permute-done), channel_id=1, source_target_pairs={{2,4},{3,5},{4,6},{5,7},{10,12},{11,13},{12,14},{13,15},{18,20},{1... | collective-permute-start | bytes 3145736 | tf_op jit(solution)/shard_map/ppermute | solution.py:241
  53.1 96.7 %collective-permute-start.15 = (f32[512,512]{1,0:T(8,128)}, f32[512,512]{1,0:T(8,128)}, u32[]{:S(2)}, u32[]{:S(2)}) collective-permute-start(f32[512,512]{1,0:T(8,128)} %slice_bitcast_fusion.6), channel_id=1, source_target_pairs={{0,1},{1,0},{2,3},{3,2},{4,5},{5,4},{6,7},{7,6},{8,9},{9,8},{10,11... | collective-permute-start | bytes 3145736 | tf_op jit(solution)/shard_map/ppermute | solution.py:248
  55.6 91.7 %collective-permute-start.25 = (f32[512,512]{1,0:T(8,128)}, f32[512,512]{1,0:T(8,128)}, u32[]{:S(2)}, u32[]{:S(2)}) collective-permute-start(f32[512,512]{1,0:T(8,128)} %pad_maximum_fusion.10), channel_id=1, source_target_pairs={{1,0},{2,3},{3,2},{4,5},{5,4},{6,7},{7,6},{9,8},{10,11},{11,10},{1... | collective-permute-start | bytes 3145736 | tf_op jit(solution)/shard_map/ppermute | solution.py:334
  78.0 54.9 %copy-start.9 = (f32[512,512]{1,0:T(8,128)}, f32[512,512]{1,0:T(8,128)S(1)}, u32[]{:S(2)}) copy-start(f32[512,512]{1,0:T(8,128)S(1)} %collective-permute-done.4) | copy-start | bytes 3145732
  78.0 39.5 %collective-permute-start.5 = (f32[512,512]{1,0:T(8,128)S(1)}, f32[512,512]{1,0:T(8,128)S(1)}, u32[]{:S(2)}, u32[]{:S(2)}) collective-permute-start(f32[512,512]{1,0:T(8,128)S(1)} %collective-permute-done.4), channel_id=1, source_target_pairs={{2,0},{3,1},{10,8},{11,9},{18,16},{19,17},{26,24},{27,25}} | collective-permute-start | bytes 3145736 | tf_op jit(solution)/shard_map/ppermute | solution.py:242
  79.3 39.2 %collective-permute-start.7 = (f32[512,512]{1,0:T(8,128)}, f32[512,512]{1,0:T(8,128)S(1)}, u32[]{:S(2)}, u32[]{:S(2)}) collective-permute-start(f32[512,512]{1,0:T(8,128)} %collective-permute-done.6), channel_id=1, source_target_pairs={{4,6},{5,7},{12,14},{13,15},{20,22},{21,23},{28,30},{29,31}} | collective-permute-start | bytes 3145736 | tf_op jit(solution)/shard_map/ppermute | solution.py:241
  80.1 26.1 %collective-permute-start.9 = (f32[64,512]{0,1:T(8,128)S(1)}, f32[64,512]{0,1:T(8,128)S(1)}, u32[]{:S(2)}, u32[]{:S(2)}) collective-permute-start(f32[64,512]{0,1:T(8,128)S(1)} %constant_dynamic-slice_fusion.8), channel_id=1, source_target_pairs={{0,1},{1,0},{2,3},{3,2},{4,5},{5,4},{6,7},{7,6},{8,9},{9,8},{10,11... | collective-permute-start | bytes 393224 | tf_op jit(solution)/shard_map/ppermute | solution.py:143
  81.8 65.4 %copy-start.15 = (s32[16]{0:T(128)}, s32[16]{0:T(128)S(1)}, u32[]{:S(2)}) copy-start(s32[16]{0:T(128)S(1)} %get-tuple-element.149) | copy-start | bytes 196
  81.8 65.4 %copy-start.20 = (s32[16]{0:T(128)}, s32[16]{0:T(128)S(1)}, u32[]{:S(2)}) copy-start(s32[16]{0:T(128)S(1)} %get-tuple-element.54) | copy-start | bytes 196
  106.5 10.8 %collective-permute-start.10 = (f32[32,512]{0,1:T(8,128)S(1)}, f32[32,512]{0,1:T(8,128)S(1)}, u32[]{:S(2)}, u32[]{:S(2)}) collective-permute-start(f32[32,512]{0,1:T(8,128)S(1)} %constant_dynamic-slice_fusion.7), channel_id=1, source_target_pairs={{0,2},{1,3},{2,0},{3,1},{4,6},{5,7},{6,4},{7,5},{8,10},{9,11},{10,... | collective-permute-start | bytes 196616 | tf_op jit(solution)/shard_map/ppermute | solution.py:143
  117.5 1.0 copy-start.10
  118.5 1.0 copy-start.11
  119.6 13.1 %collective-permute-start.11 = (f32[16,512]{0,1:T(8,128)S(1)}, f32[16,512]{0,1:T(8,128)S(1)}, u32[]{:S(2)}, u32[]{:S(2)}) collective-permute-start(f32[16,512]{0,1:T(8,128)S(1)} %constant_dynamic-slice_fusion.6), channel_id=1, source_target_pairs={{0,4},{1,5},{2,6},{3,7},{4,0},{5,1},{6,2},{7,3},{8,12},{9,13},{10,... | collective-permute-start | bytes 98312 | tf_op jit(solution)/shard_map/ppermute | solution.py:143
  132.8 12.5 %collective-permute-start.12 = (f32[16,512]{0,1:T(8,128)S(1)}, f32[16,512]{0,1:T(8,128)S(1)}, u32[]{:S(2)}, u32[]{:S(2)}) collective-permute-start(f32[16,512]{0,1:T(8,128)S(1)} %dynamic-slice_add_fusion.4), channel_id=1, source_target_pairs={{0,4},{1,5},{2,6},{3,7},{4,0},{5,1},{6,2},{7,3},{8,12},{9,13},{10,... | collective-permute-start | bytes 98312 | tf_op jit(solution)/shard_map/ppermute | solution.py:143
  140.0 28.0 %copy-start.3 = (f32[512,512]{1,0:T(8,128)}, f32[512,512]{1,0:T(8,128)S(1)}, u32[]{:S(2)}) copy-start(f32[512,512]{1,0:T(8,128)S(1)} %get-tuple-element.59) | copy-start | bytes 3145732
  140.1 28.0 %collective-permute-start.8 = (f32[512,512]{1,0:T(8,128)}, f32[512,512]{1,0:T(8,128)}, u32[]{:S(2)}, u32[]{:S(2)}) collective-permute-start(f32[512,512]{1,0:T(8,128)} %get-tuple-element.58), channel_id=1, source_target_pairs={{0,1},{1,0},{2,3},{3,2},{4,5},{5,4},{6,7},{7,6},{8,9},{9,8},{10,11... | collective-permute-start | bytes 3145736 | tf_op jit(solution)/shard_map/ppermute | solution.py:248
  147.2 54.7 %copy-start.12 = (f32[512,512]{1,0:T(8,128)S(1)}, f32[512,512]{1,0:T(8,128)}, u32[]{:S(2)}) copy-start(f32[512,512]{1,0:T(8,128)} %pad_maximum_fusion.8) | copy-start | bytes 3145732
  147.2 99.8 %copy-start.14 = (f32[512,512]{1,0:T(8,128)S(1)}, f32[512,512]{1,0:T(8,128)}, u32[]{:S(2)}) copy-start(f32[512,512]{1,0:T(8,128)} %get-tuple-element.41) | copy-start | bytes 3145732
  147.2 101.1 %copy-start.13 = (f32[512,512]{1,0:T(8,128)S(1)}, f32[512,512]{1,0:T(8,128)}, u32[]{:S(2)}) copy-start(f32[512,512]{1,0:T(8,128)} %get-tuple-element.44) | copy-start | bytes 3145732
  147.2 6.7 %collective-permute-start.13 = (f32[32,512]{1,0:T(8,128)S(1)}, f32[32,512]{1,0:T(8,128)S(1)}, u32[]{:S(2)}, u32[]{:S(2)}) collective-permute-start(f32[32,512]{1,0:T(8,128)S(1)} %pad_maximum_fusion.16), channel_id=1, source_target_pairs={{0,2},{1,3},{2,0},{3,1},{4,6},{5,7},{6,4},{7,5},{8,10},{9,11},{10,... | collective-permute-start | bytes 196616 | tf_op jit(solution)/shard_map/ppermute | solution.py:143
  149.8 97.2 %collective-permute-start.18 = (f32[512,512]{1,0:T(8,128)}, f32[512,512]{1,0:T(8,128)S(1)}, u32[]{:S(2)}, u32[]{:S(2)}) collective-permute-start(f32[512,512]{1,0:T(8,128)} %pad_maximum_fusion.5), channel_id=1, source_target_pairs={{1,4},{2,7},{3,6},{4,1},{5,0},{6,3},{7,2},{9,12},{10,15},{11,14},{... | collective-permute-start | bytes 3145736 | tf_op jit(solution)/shard_map/ppermute | solution.py:334
  151.1 97.2 %collective-permute-start.17 = (f32[512,512]{1,0:T(8,128)}, f32[512,512]{1,0:T(8,128)S(1)}, u32[]{:S(2)}, u32[]{:S(2)}) collective-permute-start(f32[512,512]{1,0:T(8,128)} %get-tuple-element.37), channel_id=1, source_target_pairs={{1,7},{2,4},{3,5},{4,2},{5,3},{6,0},{7,1},{9,15},{10,12},{11,13},{... | collective-permute-start | bytes 3145736 | tf_op jit(solution)/shard_map/ppermute | solution.py:334
  152.4 97.2 %collective-permute-start.16 = (f32[512,512]{1,0:T(8,128)}, f32[512,512]{1,0:T(8,128)S(1)}, u32[]{:S(2)}, u32[]{:S(2)}) collective-permute-start(f32[512,512]{1,0:T(8,128)} %get-tuple-element.36), channel_id=1, source_target_pairs={{1,6},{2,5},{3,4},{4,3},{5,2},{6,1},{7,0},{9,14},{10,13},{11,12},{... | collective-permute-start | bytes 3145736 | tf_op jit(solution)/shard_map/ppermute | solution.py:334
  154.0 12.3 %collective-permute-start.14 = (f32[64,512]{1,0:T(8,128)S(1)}, f32[64,512]{1,0:T(8,128)S(1)}, u32[]{:S(2)}, u32[]{:S(2)}) collective-permute-start(f32[64,512]{1,0:T(8,128)S(1)} %pad_maximum_fusion.15), channel_id=1, source_target_pairs={{0,1},{1,0},{2,3},{3,2},{4,5},{5,4},{6,7},{7,6},{8,9},{9,8},{10,11... | collective-permute-start | bytes 393224 | tf_op jit(solution)/shard_map/ppermute | solution.py:143
  166.4 174.0 %collective-permute-start.19 = (f32[3,512,512]{2,1,0:T(8,128)S(1)}, f32[3,512,512]{2,1,0:T(8,128)S(1)}, u32[]{:S(2)}, u32[]{:S(2)}) collective-permute-start(f32[3,512,512]{2,1,0:T(8,128)S(1)} %pad_maximum_fusion), channel_id=1, source_target_pairs={{0,1},{1,0},{2,3},{3,2},{4,5},{5,4},{6,7},{7,6},{8,9},{9,8},{10,11... | collective-permute-start | bytes 9437192 | tf_op jit(solution)/shard_map/ppermute | solution.py:248
  201.9 66.7 %collective-permute-start.26 = (f32[512,512]{1,0:T(8,128)S(1)}, f32[512,512]{1,0:T(8,128)S(1)}, u32[]{:S(2)}, u32[]{:S(2)}) collective-permute-start(f32[512,512]{1,0:T(8,128)S(1)} %copy-done.12), channel_id=1, source_target_pairs={{1,3},{2,0},{3,1},{4,6},{5,7},{6,4},{7,5},{9,11},{10,8},{11,9},{12... | collective-permute-start | bytes 3145736 | tf_op jit(solution)/shard_map/ppermute | solution.py:334
  247.0 43.8 %collective-permute-start.22 = (f32[512,512]{1,0:T(8,128)S(1)}, f32[512,512]{1,0:T(8,128)S(1)}, u32[]{:S(2)}, u32[]{:S(2)}) collective-permute-start(f32[512,512]{1,0:T(8,128)S(1)} %copy-done.14), channel_id=1, source_target_pairs={{1,2},{2,1},{3,0},{4,7},{5,6},{6,5},{7,4},{9,10},{10,9},{11,8},{12... | collective-permute-start | bytes 3145736 | tf_op jit(solution)/shard_map/ppermute | solution.py:334
  248.3 87.6 %collective-permute-start.27 = (f32[512,512]{1,0:T(8,128)S(1)}, f32[512,512]{1,0:T(8,128)S(1)}, u32[]{:S(2)}, u32[]{:S(2)}) collective-permute-start(f32[512,512]{1,0:T(8,128)S(1)} %copy-done.13), channel_id=1, source_target_pairs={{1,5},{2,6},{3,7},{4,0},{5,1},{6,2},{7,3},{9,13},{10,14},{11,15},{... | collective-permute-start | bytes 3145736 | tf_op jit(solution)/shard_map/ppermute | solution.py:334
  343.5 3.3 copy-start.2
  349.8 5.9 %copy-start.5 = (f32[512,512]{0,1:T(8,128)S(1)}, f32[512,512]{0,1:T(8,128)}, u32[]{:S(2)}) copy-start(f32[512,512]{0,1:T(8,128)} %copy-done.4) | copy-start | bytes 3145732
  349.8 6.9 %copy-start.18 = (s32[16]{0:T(128)S(1)}, s32[16]{0:T(128)}, u32[]{:S(2)}) copy-start(s32[16]{0:T(128)} %copy-done.17) | copy-start | bytes 196
  349.8 6.9 %copy-start.19 = (s32[16]{0:T(128)S(1)}, s32[16]{0:T(128)}, u32[]{:S(2)}) copy-start(s32[16]{0:T(128)} %get-tuple-element.55) | copy-start | bytes 196
  349.8 7.6 %copy-start.8 = (f32[512,256]{1,0:T(8,128)S(1)}, f32[512,256]{1,0:T(8,128)}, u32[]{:S(2)}) copy-start(f32[512,256]{1,0:T(8,128)} %get-tuple-element.81) | copy-start | bytes 1572868
  354.4 7.4 %copy-start.16 = (s32[16]{0:T(128)S(1)}, s32[16]{0:T(128)}, u32[]{:S(2)}) copy-start(s32[16]{0:T(128)} %copy-done.15) | copy-start | bytes 196
  354.4 8.0 %copy-start.21 = (s32[16]{0:T(128)S(1)}, s32[16]{0:T(128)}, u32[]{:S(2)}) copy-start(s32[16]{0:T(128)} %copy-done.20) | copy-start | bytes 196
  356.7 2.3 collective-permute-start.28
  358.5 11.7 %collective-permute-start.20 = (f32[256,512]{1,0:T(8,128)S(1)}, f32[256,512]{1,0:T(8,128)S(1)}, u32[]{:S(2)}, u32[]{:S(2)}) collective-permute-start(f32[256,512]{1,0:T(8,128)S(1)} %constant_dynamic-slice_fusion.5), channel_id=1, source_target_pairs={{0,8},{8,0},{16,24},{24,16},{1,9},{9,1},{17,25},{25,17},{2,10},{10... | collective-permute-start | bytes 1572872 | tf_op jit(solution)/shard_map/ppermute | solution.py:143
  360.2 9.2 %collective-permute-start.29 = (f32[128,512]{1,0:T(8,128)S(1)}, f32[128,512]{1,0:T(8,128)S(1)}, u32[]{:S(2)}, u32[]{:S(2)}) collective-permute-start(f32[128,512]{1,0:T(8,128)S(1)} %constant_dynamic-slice_fusion), channel_id=1, source_target_pairs={{0,16},{8,24},{16,0},{24,8},{1,17},{9,25},{17,1},{25,9},{2,18},{10... | collective-permute-start | bytes 786440 | tf_op jit(solution)/shard_map/ppermute | solution.py:143
  369.4 46.9 %collective-permute-start.30 = (f32[4,512,256]{2,1,0:T(8,128)}, f32[4,512,256]{2,1,0:T(8,128)}, u32[]{:S(2)}, u32[]{:S(2)}) collective-permute-start(f32[4,512,256]{2,1,0:T(8,128)} %shard_map.61), channel_id=1, source_target_pairs={{0,8},{8,0},{16,24},{24,16},{1,9},{9,1},{17,25},{25,17},{2,10},{10... | collective-permute-start | bytes 6291464 | tf_op jit(solution)/shard_map/ppermute | solution.py:143
  369.5 9.2 %collective-permute-start.31 = (f32[128,512]{1,0:T(8,128)S(1)}, f32[128,512]{1,0:T(8,128)S(1)}, u32[]{:S(2)}, u32[]{:S(2)}) collective-permute-start(f32[128,512]{1,0:T(8,128)S(1)} %dynamic-slice_add_fusion.3), channel_id=1, source_target_pairs={{0,16},{8,24},{16,0},{24,8},{1,17},{9,25},{17,1},{25,9},{2,18},{10... | collective-permute-start | bytes 786440 | tf_op jit(solution)/shard_map/ppermute | solution.py:143
  370.3 13.6 %collective-permute-start.21 = (f32[128,512]{1,0:T(8,128)S(1)}, f32[128,512]{1,0:T(8,128)S(1)}, u32[]{:S(2)}, u32[]{:S(2)}) collective-permute-start(f32[128,512]{1,0:T(8,128)S(1)} %constant_dynamic-slice_fusion.4), channel_id=1, source_target_pairs={{0,16},{8,24},{16,0},{24,8},{1,17},{9,25},{17,1},{25,9},{2,18},{10... | collective-permute-start | bytes 786440 | tf_op jit(solution)/shard_map/ppermute | solution.py:143
  379.5 12.5 %collective-permute-start.32 = (f32[256,512]{1,0:T(8,128)}, f32[256,512]{1,0:T(8,128)}, u32[]{:S(2)}, u32[]{:S(2)}) collective-permute-start(f32[256,512]{1,0:T(8,128)} %pad_maximum_fusion.13), channel_id=1, source_target_pairs={{0,8},{8,0},{16,24},{24,16},{1,9},{9,1},{17,25},{25,17},{2,10},{10... | collective-permute-start | bytes 1572872 | tf_op jit(solution)/shard_map/ppermute | solution.py:143
  383.9 8.0 %collective-permute-start.23 = (f32[128,512]{1,0:T(8,128)S(1)}, f32[128,512]{1,0:T(8,128)S(1)}, u32[]{:S(2)}, u32[]{:S(2)}) collective-permute-start(f32[128,512]{1,0:T(8,128)S(1)} %add_subtract_fusion), channel_id=1, source_target_pairs={{0,16},{8,24},{16,0},{24,8},{1,17},{9,25},{17,1},{25,9},{2,18},{10... | collective-permute-start | bytes 786440 | tf_op jit(solution)/shard_map/ppermute | solution.py:143
  394.2 47.7 %collective-permute-start.33 = (f32[512,512]{1,0:T(8,128)}, f32[512,512]{1,0:T(8,128)}, u32[]{:S(2)}, u32[]{:S(2)}) collective-permute-start(f32[512,512]{1,0:T(8,128)} %pad_maximum_fusion.11), channel_id=1, source_target_pairs={{0,2},{1,3},{10,12},{11,13},{20,22},{21,23},{30,24},{31,25}} | collective-permute-start | bytes 3145736 | tf_op jit(solution)/shard_map/ppermute | solution.py:259
  396.4 45.4 %collective-permute-start.34 = (f32[512,512]{1,0:T(8,128)}, f32[512,512]{1,0:T(8,128)}, u32[]{:S(2)}, u32[]{:S(2)}) collective-permute-start(f32[512,512]{1,0:T(8,128)} %pad_maximum_fusion.11), channel_id=1, source_target_pairs={{0,4},{1,5},{10,14},{11,15},{20,16},{21,17},{30,26},{31,27}} | collective-permute-start | bytes 3145736 | tf_op jit(solution)/shard_map/ppermute | solution.py:259
  398.6 43.2 %collective-permute-start.35 = (f32[512,512]{1,0:T(8,128)}, f32[512,512]{1,0:T(8,128)}, u32[]{:S(2)}, u32[]{:S(2)}) collective-permute-start(f32[512,512]{1,0:T(8,128)} %pad_maximum_fusion.11), channel_id=1, source_target_pairs={{0,6},{1,7},{10,8},{11,9},{20,18},{21,19},{30,28},{31,29}} | collective-permute-start | bytes 3145736 | tf_op jit(solution)/shard_map/ppermute | solution.py:259
  401.7 18.4 %collective-permute-start.24 = (f32[256,512]{1,0:T(8,128)}, f32[256,512]{1,0:T(8,128)S(1)}, u32[]{:S(2)}, u32[]{:S(2)}) collective-permute-start(f32[256,512]{1,0:T(8,128)} %pad_maximum_fusion.12), channel_id=1, source_target_pairs={{0,8},{8,0},{16,24},{24,16},{1,9},{9,1},{17,25},{25,17},{2,10},{10... | collective-permute-start | bytes 1572872 | tf_op jit(solution)/shard_map/ppermute | solution.py:143
  409.4 7.4 %copy-start.6 = (f32[4,512,256]{2,1,0:T(8,128)S(1)}, f32[4,512,256]{2,1,0:T(8,128)}, u32[]{:S(2)}) copy-start(f32[4,512,256]{2,1,0:T(8,128)} %shard_map.60) | copy-start | bytes 6291460
  416.3 56.6 %collective-permute-start.37 = (f32[4,512,256]{2,1,0:T(8,128)}, f32[4,512,256]{2,1,0:T(8,128)S(1)}, u32[]{:S(2)}, u32[]{:S(2)}) collective-permute-start(f32[4,512,256]{2,1,0:T(8,128)} %shard_map.64), channel_id=1, source_target_pairs={{0,8},{8,0},{16,24},{24,16},{1,9},{9,1},{17,25},{25,17},{2,10},{10... | collective-permute-start | bytes 6291464 | tf_op jit(solution)/shard_map/ppermute | solution.py:143
  420.1 52.8 %collective-permute-start.38 = (f32[4,512,256]{2,1,0:T(8,128)}, f32[4,512,256]{2,1,0:T(8,128)}, u32[]{:S(2)}, u32[]{:S(2)}) collective-permute-start(f32[4,512,256]{2,1,0:T(8,128)} %add.489), channel_id=1, source_target_pairs={{0,16},{8,24},{16,0},{24,8},{1,17},{9,25},{17,1},{25,9},{2,18},{10... | collective-permute-start | bytes 6291464 | tf_op jit(solution)/shard_map/ppermute | solution.py:143
  444.2 26.9 %collective-permute-start.36 = (f32[512,512]{1,0:T(8,128)S(1)}, f32[512,512]{1,0:T(8,128)S(1)}, u32[]{:S(2)}, u32[]{:S(2)}) collective-permute-start(f32[512,512]{1,0:T(8,128)S(1)} %add_add_fusion), channel_id=1, source_target_pairs={{0,1},{1,0},{2,3},{3,2},{4,5},{5,4},{6,7},{7,6},{8,9},{9,8},{10,11... | collective-permute-start | bytes 3145736 | tf_op jit(solution)/shard_map/ppermute | solution.py:269
  458.1 16.2 %copy-start = (f32[1024,512]{1,0:T(8,128)S(1)}, f32[1024,512]{1,0:T(8,128)}, u32[]{:S(2)}) copy-start(f32[1024,512]{1,0:T(8,128)} %parent_ref.1) | copy-start | bytes 6291460
  459.1 22.7 %copy-start.1 = (f32[512,512]{1,0:T(8,128)}, f32[512,512]{1,0:T(8,128)S(1)}, u32[]{:S(2)}) copy-start(f32[512,512]{1,0:T(8,128)S(1)} %fusion.21.mine_ref) | copy-start | bytes 3145732
  472.9 1.4 copy-start.7

commit v15 on v11

--- a/solution.py
+++ b/solution.py
@@ -407,8 +407,7 @@
 
     parent_mine = product(parent_inverse, first, 1, 1)
     if groups // ny == branches:
-        line, parent_inverse = lax.optimization_barrier((share_line(first, ny), parent_inverse))
-        sides = jnp.concatenate(share_beside(line, ny), axis=0)
+        sides = jnp.concatenate(share_beside(share_line(first, ny), ny), axis=0)
     else:
         sides = lax.dynamic_slice_in_dim(
             lax.all_gather(first, "col"), branch * groups // branches, groups // branches, 0).reshape(nrows, PP)

time: 488 us -> 492 us (level)
  the two profiles are of different devices: /device:TPU:0 before, /device:TPU:10 now
where the time goes in v15:
time: 492 us; the launch traced here: 484 us
  waiting for transfers between devices  182 us (37%)
  starting transfers between devices  105 us (21%)
  Pallas kernels  81.5 us (17%)
  other arithmetic  41 us (8%)
  local copies, waits for them, and re-layouts  30.7 us (6%)
  between operations  27.7 us (6%)
  matrix products  17 us (3%)
    ppermute x7, waiting for transfers between devices, moved(): return lax.ppermute(rows, 'col', pairs)  64.2 us
    ppermute x19, waiting for transfers between devices, flip(): return lax.ppermute(x, axis, [(i, i ^ bit) for i in range(n)])  51.4 us
    ppermute x7, starting transfers between devices, moved(): return lax.ppermute(rows, 'col', pairs)  43.3 us
    pallas_call x2, Pallas kernels, inverse_factor(): pl.pallas_call(inverse_factor_kernel, out_shape=jax.ShapeDtypeStruct((n,...  43 us
    ppermute x19, starting transfers between devices, flip(): return lax.ppermute(x, axis, [(i, i ^ bit) for i in range(n)])  33.6 us
    pallas_call x5, Pallas kernels, spread_update(): pl.pallas_call(spread_kernel, grid_spec=pltpu.PrefetchScalarGridSpec(num_...  31 us
    ppermute x3, waiting for transfers between devices, share_line(): got = got + lax.ppermute(x, ('branch', 'col'), pairs)  25 us
    ppermute x3, waiting for transfers between devices, from_beside(): lax.ppermute(x, axis, [(c, c // ny * ny + (c % ny - j) % ny) for c in ran...  21 us
  transfers between devices with their start and end apart: 39, of which 15 were waited for; matrix products, arithmetic and copies ran while one was open for 14% of the time, Pallas kernels for 14%

profile of v15, /device:TPU:10, one launch (start us, length us, event | category | flops | bytes accessed | tf_op | source)
XLA Modules:
  0.0 484.1 jit_solution(6342364277289465521)
XLA Ops:
  0.6 2.4 slice_bitcast_fusion.6
  3.0 3.5 collective-permute-start
  6.5 3.3 collective-permute-start.1
  18.7 1.7 constant_dynamic-slice_fusion.14
  32.6 5.6 %dynamic-slice_bitcast_fusion.1 = (f32[256,512]{1,0:T(8,128)S(1)}, f32[256,512]{1,0:T(8,128)S(1)}, f32[256,512]{1,0:T(8,128)S(1)}, f32[256,512]{1,0:T(8,128)S(1)...) fusion(f32[1,4096,512]{2,1,0:T(8,128)} %param.3, ...), kind=kLoop, calls=%fused_computation.65 | loop fusion | bytes 16777280 | tf_op jit(solution)/shard_map/dynamic_slice | solution.py:304
  38.2 1.5 pad_maximum_fusion.6
  43.6 1.6 pad_maximum_fusion.3
  45.2 5.6 %collective-permute-done.3 = f32[128,512]{0,1:T(8,128)S(1)} collective-permute-done((f32[128,512]{0,1:T(8,128)S(1)}, f32[128,512]{0,1:T(8,128)S(1)}, u32[]{:S(2)}, u32[]{:S(2)}) %collective-permute-start.3) | collective-permute-done | bytes 262176 | tf_op jit(solution)/shard_map/ppermute | solution.py:143
  50.8 1.9 collective-permute-start.4
  52.7 5.0 %collective-permute-start.6 = (f32[512,512]{1,0:T(8,128)}, f32[512,512]{1,0:T(8,128)}, u32[]{:S(2)}, u32[]{:S(2)}) collective-permute-start(f32[512,512]{1,0:T(8,128)} %collective-permute-done), channel_id=1, source_target_pairs={{2,4},{3,5},{4,6},{5,7},{10,12},{11,13},{12,14},{13,15},{18,20},{1... | collective-permute-start | bytes 3145736 | tf_op jit(solution)/shard_map/ppermute | solution.py:241
  57.6 20.0 %collective-permute-done.4 = f32[512,512]{1,0:T(8,128)S(1)} collective-permute-done((f32[512,512]{1,0:T(8,128)}, f32[512,512]{1,0:T(8,128)S(1)}, u32[]{:S(2)}, u32[]{:S(2)}) %collective-permute-start.4) | collective-permute-done | bytes 1048608 | tf_op jit(solution)/shard_map/ppermute | solution.py:242
  77.7 3.2 collective-permute-start.5
  80.9 1.6 collective-permute-start.7
  82.7 1.6 collective-permute-start.9
  84.8 7.2 %collective-permute-done.9 = f32[64,512]{0,1:T(8,128)S(1)} collective-permute-done((f32[64,512]{0,1:T(8,128)S(1)}, f32[64,512]{0,1:T(8,128)S(1)}, u32[]{:S(2)}, u32[]{:S(2)}) %collective-permute-start.9) | collective-permute-done | bytes 131104 | tf_op jit(solution)/shard_map/ppermute | solution.py:143
  93.4 3.4 collective-permute-start.25
  96.9 10.4 %collective-permute-done.10 = f32[32,512]{0,1:T(8,128)S(1)} collective-permute-done((f32[32,512]{0,1:T(8,128)S(1)}, f32[32,512]{0,1:T(8,128)S(1)}, u32[]{:S(2)}, u32[]{:S(2)}) %collective-permute-start.10) | collective-permute-done | bytes 65568 | tf_op jit(solution)/shard_map/ppermute | solution.py:143
  107.6 5.7 %collective-permute-start.11 = (f32[16,512]{0,1:T(8,128)S(1)}, f32[16,512]{0,1:T(8,128)S(1)}, u32[]{:S(2)}, u32[]{:S(2)}) collective-permute-start(f32[16,512]{0,1:T(8,128)S(1)} %constant_dynamic-slice_fusion.6), channel_id=1, source_target_pairs={{0,4},{1,5},{2,6},{3,7},{4,0},{5,1},{6,2},{7,3},{8,12},{9,13},{10,... | collective-permute-start | bytes 98312 | tf_op jit(solution)/shard_map/ppermute | solution.py:143
  113.3 8.2 %collective-permute-done.11 = f32[16,512]{0,1:T(8,128)S(1)} collective-permute-done((f32[16,512]{0,1:T(8,128)S(1)}, f32[16,512]{0,1:T(8,128)S(1)}, u32[]{:S(2)}, u32[]{:S(2)}) %collective-permute-start.11) | collective-permute-done | bytes 32800 | tf_op jit(solution)/shard_map/ppermute | solution.py:143
  121.7 3.5 collective-permute-start.12
  125.8 7.0 %collective-permute-done.12 = f32[16,512]{0,1:T(8,128)S(1)} collective-permute-done((f32[16,512]{0,1:T(8,128)S(1)}, f32[16,512]{0,1:T(8,128)S(1)}, u32[]{:S(2)}, u32[]{:S(2)}) %collective-permute-start.12) | collective-permute-done | bytes 32800 | tf_op jit(solution)/shard_map/ppermute | solution.py:143
  133.0 3.7 collective-permute-start.13
  137.4 1.6 collective-permute-done.13
  139.0 1.6 collective-permute-start.14
  140.6 5.1 %select_add_fusion.3 = (f32[512,512]{1,0:T(8,128)}, f32[512,512]{1,0:T(8,128)S(1)}, f32[512,512]{1,0:T(8,128)S(1)}, f32[512,512]{1,0:T(8,128)S(1)}) fusion(pred[]{:T(512)S(6)} %eq.104, pred[]{:T(512)S(6)} %eq.103, pred[]{:T(512)S(6)} %eq.96, pred[]{:T(512)S(6)} %eq.95, f32[1,4096,512]{2,1,0:T(8,128)} %param.3, f32[512,512]{1,0:T(8,128)} %collective-permute-done, ...), kind=kLoop, calls=%fused_computation.57 | loop fusion | flops 2621440 | bytes 11534340 | tf_op jit(solution)/shard_map/add | solution.py:350
  146.3 4.6 collective-permute-start.18
  150.9 3.6 collective-permute-start.17
  154.5 3.4 collective-permute-start.16
  169.5 1.5 fusion.13
  173.6 21.0 %collective-permute-done.8 = f32[512,512]{1,0:T(8,128)} collective-permute-done((f32[512,512]{1,0:T(8,128)}, f32[512,512]{1,0:T(8,128)}, u32[]{:S(2)}, u32[]{:S(2)}) %collective-permute-start.8) | collective-permute-done | bytes 1048608 | tf_op jit(solution)/shard_map/ppermute | solution.py:248
  194.6 1.5 select_add_fusion.2.a_ref
  196.1 21.4 %shard_map.58 = f32[512,512]{1,0:T(8,128)S(1)} custom-call(f32[512,512]{1,0:T(8,128)S(1)} %select_add_fusion.2.a_ref), custom_call_target="tpu_custom_call" | custom-call | flops 134217728 | bytes 2097152 | tf_op jit(solution)/shard_map/pallas_call | solution.py:86
  218.9 25.0 %collective-permute-start.22 = (f32[512,512]{1,0:T(8,128)S(1)}, f32[512,512]{1,0:T(8,128)S(1)}, u32[]{:S(2)}, u32[]{:S(2)}) collective-permute-start(f32[512,512]{1,0:T(8,128)S(1)} %copy-done.14), channel_id=1, source_target_pairs={{1,2},{2,1},{3,0},{4,7},{5,6},{6,5},{7,4},{9,10},{10,9},{11,8},{12... | collective-permute-start | bytes 3145736 | tf_op jit(solution)/shard_map/ppermute | solution.py:334
  244.0 18.2 %collective-permute-done.17 = f32[512,512]{1,0:T(8,128)} collective-permute-done((f32[512,512]{1,0:T(8,128)}, f32[512,512]{1,0:T(8,128)}, u32[]{:S(2)}, u32[]{:S(2)}) %collective-permute-start.17) | collective-permute-done | bytes 1048608 | tf_op jit(solution)/shard_map/ppermute | solution.py:334
  262.2 1.9 collective-permute-start.27
  264.1 45.9 %collective-permute-done.16 = f32[512,512]{1,0:T(8,128)} collective-permute-done((f32[512,512]{1,0:T(8,128)}, f32[512,512]{1,0:T(8,128)}, u32[]{:S(2)}, u32[]{:S(2)}) %collective-permute-start.16) | collective-permute-done | bytes 1048608 | tf_op jit(solution)/shard_map/ppermute | solution.py:334
  310.0 2.2 fusion.7
  312.3 2.2 fusion.6
  316.5 2.2 fusion.3
  319.2 1.4 bitcast_dynamic-update-slice_fusion.2
  320.6 1.4 bitcast_dynamic-update-slice_fusion.1
  326.4 3.3 copy-done.2
  331.1 1.8 copy.90.left_ref
  332.9 4.6 shard_map.59
  339.9 2.2 collective-permute-done.28
  348.2 5.2 %collective-permute-done.29 = f32[128,512]{1,0:T(8,128)} collective-permute-done((f32[128,512]{1,0:T(8,128)}, f32[128,512]{1,0:T(8,128)}, u32[]{:S(2)}, u32[]{:S(2)}) %collective-permute-start.29) | collective-permute-done | bytes 262176 | tf_op jit(solution)/shard_map/ppermute | solution.py:143
  355.1 6.5 %shard_map.61 = f32[4,512,256]{2,1,0:T(8,128)} custom-call(s32[4]{0:T(128)} %dynamic_slice.356.slot_ref, s32[4]{0:T(128)} %get-tuple-element.150.place_ref, s32[4]{0:T(128)} %get-tuple-element.102.part_ref, s32[4]{0:T(128)} %get-tuple-element.98.keep_ref, bf16[512,1536]{1,0:T(8,128)(2,1)} %copy.90.left_ref, f32[8,512,512]{2,1,0:T(8,128)} %copy-done.2, ...), custom_call_target="tpu_custom_call" | custom-call | flops 1610612736 | bytes 6291456 | tf_op jit(solution)/shard_map/pallas_call | solution.py:117
  363.1 3.9 collective-permute-done.20
  368.9 1.5 collective-permute-start.21
  372.6 1.6 collective-permute-start.33
  374.2 1.6 collective-permute-start.34
  378.8 1.6 collective-permute-start.23
  380.4 6.5 %shard_map.60 = f32[4,512,256]{2,1,0:T(8,128)} custom-call(s32[4]{0:T(128)} %dynamic_slice.352.slot_ref, s32[4]{0:T(128)} %get-tuple-element.149.place_ref, s32[4]{0:T(128)} %get-tuple-element.103.part_ref, s32[4]{0:T(128)} %get-tuple-element.99.keep_ref, bf16[512,1536]{1,0:T(8,128)(2,1)} %copy.90.left_ref, f32[8,512,512]{2,1,0:T(8,128)} %copy-done.2, ...), custom_call_target="tpu_custom_call" | custom-call | flops 1610612736 | bytes 6291456 | tf_op jit(solution)/shard_map/pallas_call | solution.py:117
  387.5 6.6 %shard_map.64 = f32[4,512,256]{2,1,0:T(8,128)} custom-call(s32[4]{0:T(128)} %dynamic_slice.364.slot_ref, s32[4]{0:T(128)} %get-tuple-element.152.place_ref, s32[4]{0:T(128)} %get-tuple-element.100.part_ref, s32[4]{0:T(128)} %get-tuple-element.96.keep_ref, bf16[512,1536]{1,0:T(8,128)(2,1)} %copy.90.left_ref, f32[8,512,512]{2,1,0:T(8,128)} %copy-done.2, ...), custom_call_target="tpu_custom_call" | custom-call | flops 1610612736 | bytes 6291456 | tf_op jit(solution)/shard_map/pallas_call | solution.py:117
  394.1 11.8 %collective-permute-start.37 = (f32[4,512,256]{2,1,0:T(8,128)}, f32[4,512,256]{2,1,0:T(8,128)S(1)}, u32[]{:S(2)}, u32[]{:S(2)}) collective-permute-start(f32[4,512,256]{2,1,0:T(8,128)} %shard_map.64), channel_id=1, source_target_pairs={{0,8},{8,0},{16,24},{24,16},{1,9},{9,1},{17,25},{25,17},{2,10},{10... | collective-permute-start | bytes 6291464 | tf_op jit(solution)/shard_map/ppermute | solution.py:143
  405.9 3.2 add.489
  409.5 25.0 %collective-permute-done.35 = f32[512,512]{1,0:T(8,128)} collective-permute-done((f32[512,512]{1,0:T(8,128)}, f32[512,512]{1,0:T(8,128)}, u32[]{:S(2)}, u32[]{:S(2)}) %collective-permute-start.35) | collective-permute-done | bytes 1048608 | tf_op jit(solution)/shard_map/ppermute | solution.py:259
  434.5 2.3 add_add_fusion
  436.8 2.7 collective-permute-start.36
  439.5 3.2 convolution_bitcast_fusion.8
  443.5 6.8 %shard_map.63.rest_0_ = f32[4,512,256]{2,1,0:T(8,128)} custom-call(s32[4]{0:T(128)} %dynamic_slice.360.slot_ref, s32[4]{0:T(128)} %get-tuple-element.151.place_ref, s32[4]{0:T(128)} %get-tuple-element.101.part_ref, s32[4]{0:T(128)} %get-tuple-element.97.keep_ref, bf16[512,1536]{1,0:T(8,128)(2,1)} %copy.90.left_ref, f32[8,512,512]{2,1,0:T(8,128)} %copy-done.2, ...), custom_call_target="tpu_custom_call" | custom-call | flops 1610612736 | bytes 6291456 | tf_op jit(solution)/shard_map/pallas_call | solution.py:117
  450.2 21.6 %shard_map.62.inverse_ref = f32[512,512]{1,0:T(8,128)S(1)} custom-call(f32[512,512]{1,0:T(8,128)S(1)} %pad_maximum_fusion.9.a_ref), custom_call_target="tpu_custom_call" | custom-call | flops 134217728 | bytes 2097152 | tf_op jit(solution)/shard_map/pallas_call | solution.py:86
  473.2 1.5 pad_maximum_fusion.1
  476.1 7.5 %shard_map.65 = f32[1024,512]{1,0:T(8,128)} custom-call(f32[1024,512]{1,0:T(8,128)S(1)} %copy-done, f32[4,256,512]{2,1,0:T(8,128)} %bitcast.175, f32[512,512]{1,0:T(8,128)S(1)} %shard_map.62.inverse_ref, f32[512,512]{1,0:T(8,128)S(1)} %fusion.21.mine_ref, f32[4,512,256]{2,1,0:T(8,128)} %shard_map.63.rest_0_, f32[4,512,256]{2,1,0:T(8,128)} %copy-done.8, ...), custom_call_target="tpu_custom_call" | custom-call | flops 3221225472 | bytes 16777216 | tf_op jit(solution)/shard_map/pallas_call | solution.py:216
  (171 shorter events, 50.5 us)
Async XLA Ops:
  0.6 20.3 %slice-start = ((f32[1024,512]{1,0:T(8,128)}), f32[512,512]{1,0:T(8,128)S(1)}, s32[]{:S(2)}) async-start(f32[1024,512]{1,0:T(8,128)} %parent_ref.1), calls=%async_computation | async-start | bytes 2097152 | tf_op jit(solution)/shard_map/slice | solution.py:326
  3.0 47.8 %collective-permute-start = (f32[512,512]{1,0:T(8,128)}, f32[512,512]{1,0:T(8,128)}, u32[]{:S(2)}, u32[]{:S(2)}) collective-permute-start(f32[512,512]{1,0:T(8,128)} %slice_bitcast_fusion.6), channel_id=1, source_target_pairs={{0,2},{1,3},{2,4},{3,5},{4,6},{5,7},{8,10},{9,11},{10,12},{11,13},... | collective-permute-start | bytes 3145736 | tf_op jit(solution)/shard_map/ppermute | solution.py:241
  6.5 44.3 %collective-permute-start.1 = (f32[512,512]{1,0:T(8,128)}, f32[512,512]{1,0:T(8,128)}, u32[]{:S(2)}, u32[]{:S(2)}) collective-permute-start(f32[512,512]{1,0:T(8,128)} %slice_bitcast_fusion.6), channel_id=1, source_target_pairs={{2,0},{3,1},{4,2},{5,3},{6,4},{7,5},{10,8},{11,9},{12,10},{13,11},... | collective-permute-start | bytes 3145736 | tf_op jit(solution)/shard_map/ppermute | solution.py:242
  16.6 141.3 %copy-start.17 = (s32[16]{0:T(128)}, s32[16]{0:T(128)S(1)}, u32[]{:S(2)}) copy-start(s32[16]{0:T(128)S(1)} %gather_fusion.1) | copy-start | bytes 196
  21.2 16.9 %copy-start.5 = (f32[512,512]{0,1:T(8,128)}, f32[512,512]{0,1:T(8,128)S(1)}, u32[]{:S(2)}) copy-start(f32[512,512]{0,1:T(8,128)S(1)} %copy.108) | copy-start | bytes 3145732
  22.4 18.3 %collective-permute-start.2 = (f32[256,512]{0,1:T(8,128)}, f32[256,512]{0,1:T(8,128)}, u32[]{:S(2)}, u32[]{:S(2)}) collective-permute-start(f32[256,512]{0,1:T(8,128)} %constant_dynamic-slice_fusion.10), channel_id=1, source_target_pairs={{0,8},{8,0},{16,24},{24,16},{1,9},{9,1},{17,25},{25,17},{2,10},{10... | collective-permute-start | bytes 1572872 | tf_op jit(solution)/shard_map/ppermute | solution.py:143
  41.9 8.8 %collective-permute-start.3 = (f32[128,512]{0,1:T(8,128)S(1)}, f32[128,512]{0,1:T(8,128)S(1)}, u32[]{:S(2)}, u32[]{:S(2)}) collective-permute-start(f32[128,512]{0,1:T(8,128)S(1)} %constant_dynamic-slice_fusion.9), channel_id=1, source_target_pairs={{0,16},{8,24},{16,0},{24,8},{1,17},{9,25},{17,1},{25,9},{2,18},{10... | collective-permute-start | bytes 786440 | tf_op jit(solution)/shard_map/ppermute | solution.py:143
  50.8 26.9 %collective-permute-start.4 = (f32[512,512]{1,0:T(8,128)}, f32[512,512]{1,0:T(8,128)S(1)}, u32[]{:S(2)}, u32[]{:S(2)}) collective-permute-start(f32[512,512]{1,0:T(8,128)} %collective-permute-done.1), channel_id=1, source_target_pairs={{2,0},{3,1},{4,2},{5,3},{10,8},{11,9},{12,10},{13,11},{18,16},{19,... | collective-permute-start | bytes 3145736 | tf_op jit(solution)/shard_map/ppermute | solution.py:242
  52.7 28.2 %collective-permute-start.6 = (f32[512,512]{1,0:T(8,128)}, f32[512,512]{1,0:T(8,128)}, u32[]{:S(2)}, u32[]{:S(2)}) collective-permute-start(f32[512,512]{1,0:T(8,128)} %collective-permute-done), channel_id=1, source_target_pairs={{2,4},{3,5},{4,6},{5,7},{10,12},{11,13},{12,14},{13,15},{18,20},{1... | collective-permute-start | bytes 3145736 | tf_op jit(solution)/shard_map/ppermute | solution.py:241
  77.7 61.3 %copy-start.11 = (f32[512,512]{1,0:T(8,128)}, f32[512,512]{1,0:T(8,128)S(1)}, u32[]{:S(2)}) copy-start(f32[512,512]{1,0:T(8,128)S(1)} %collective-permute-done.4) | copy-start | bytes 3145732
  77.7 29.7 %collective-permute-start.5 = (f32[512,512]{1,0:T(8,128)S(1)}, f32[512,512]{1,0:T(8,128)}, u32[]{:S(2)}, u32[]{:S(2)}) collective-permute-start(f32[512,512]{1,0:T(8,128)S(1)} %collective-permute-done.4), channel_id=1, source_target_pairs={{2,0},{3,1},{10,8},{11,9},{18,16},{19,17},{26,24},{27,25}} | collective-permute-start | bytes 3145736 | tf_op jit(solution)/shard_map/ppermute | solution.py:242
  80.9 26.5 %collective-permute-start.7 = (f32[512,512]{1,0:T(8,128)}, f32[512,512]{1,0:T(8,128)}, u32[]{:S(2)}, u32[]{:S(2)}) collective-permute-start(f32[512,512]{1,0:T(8,128)} %collective-permute-done.6), channel_id=1, source_target_pairs={{4,6},{5,7},{12,14},{13,15},{20,22},{21,23},{28,30},{29,31}} | collective-permute-start | bytes 3145736 | tf_op jit(solution)/shard_map/ppermute | solution.py:241
  82.7 9.3 %collective-permute-start.9 = (f32[64,512]{0,1:T(8,128)S(1)}, f32[64,512]{0,1:T(8,128)S(1)}, u32[]{:S(2)}, u32[]{:S(2)}) collective-permute-start(f32[64,512]{0,1:T(8,128)S(1)} %constant_dynamic-slice_fusion.8), channel_id=1, source_target_pairs={{0,1},{1,0},{2,3},{3,2},{4,5},{5,4},{6,7},{7,6},{8,9},{9,8},{10,11... | collective-permute-start | bytes 393224 | tf_op jit(solution)/shard_map/ppermute | solution.py:143
  84.3 62.0 %collective-permute-start.15 = (f32[512,512]{1,0:T(8,128)}, f32[512,512]{1,0:T(8,128)}, u32[]{:S(2)}, u32[]{:S(2)}) collective-permute-start(f32[512,512]{1,0:T(8,128)} %slice_bitcast_fusion.6), channel_id=1, source_target_pairs={{0,1},{1,0},{2,3},{3,2},{4,5},{5,4},{6,7},{7,6},{8,9},{9,8},{10,11... | collective-permute-start | bytes 3145736 | tf_op jit(solution)/shard_map/ppermute | solution.py:248
  92.3 15.0 %collective-permute-start.10 = (f32[32,512]{0,1:T(8,128)S(1)}, f32[32,512]{0,1:T(8,128)S(1)}, u32[]{:S(2)}, u32[]{:S(2)}) collective-permute-start(f32[32,512]{0,1:T(8,128)S(1)} %constant_dynamic-slice_fusion.7), channel_id=1, source_target_pairs={{0,2},{1,3},{2,0},{3,1},{4,6},{5,7},{6,4},{7,5},{8,10},{9,11},{10,... | collective-permute-start | bytes 196616 | tf_op jit(solution)/shard_map/ppermute | solution.py:143
  93.4 77.6 %collective-permute-start.25 = (f32[512,512]{1,0:T(8,128)}, f32[512,512]{1,0:T(8,128)}, u32[]{:S(2)}, u32[]{:S(2)}) collective-permute-start(f32[512,512]{1,0:T(8,128)} %pad_maximum_fusion.10), channel_id=1, source_target_pairs={{1,0},{2,3},{3,2},{4,5},{5,4},{6,7},{7,6},{9,8},{10,11},{11,10},{1... | collective-permute-start | bytes 3145736 | tf_op jit(solution)/shard_map/ppermute | solution.py:334
  107.6 14.0 %collective-permute-start.11 = (f32[16,512]{0,1:T(8,128)S(1)}, f32[16,512]{0,1:T(8,128)S(1)}, u32[]{:S(2)}, u32[]{:S(2)}) collective-permute-start(f32[16,512]{0,1:T(8,128)S(1)} %constant_dynamic-slice_fusion.6), channel_id=1, source_target_pairs={{0,4},{1,5},{2,6},{3,7},{4,0},{5,1},{6,2},{7,3},{8,12},{9,13},{10,... | collective-permute-start | bytes 98312 | tf_op jit(solution)/shard_map/ppermute | solution.py:143
  113.3 57.7 %copy-start.15 = (s32[16]{0:T(128)}, s32[16]{0:T(128)S(1)}, u32[]{:S(2)}) copy-start(s32[16]{0:T(128)S(1)} %get-tuple-element.139) | copy-start | bytes 196
  113.3 57.7 %copy-start.20 = (s32[16]{0:T(128)}, s32[16]{0:T(128)S(1)}, u32[]{:S(2)}) copy-start(s32[16]{0:T(128)S(1)} %get-tuple-element.44) | copy-start | bytes 196
  121.7 11.1 %collective-permute-start.12 = (f32[16,512]{0,1:T(8,128)S(1)}, f32[16,512]{0,1:T(8,128)S(1)}, u32[]{:S(2)}, u32[]{:S(2)}) collective-permute-start(f32[16,512]{0,1:T(8,128)S(1)} %dynamic-slice_add_fusion.4), channel_id=1, source_target_pairs={{0,4},{1,5},{2,6},{3,7},{4,0},{5,1},{6,2},{7,3},{8,12},{9,13},{10,... | collective-permute-start | bytes 98312 | tf_op jit(solution)/shard_map/ppermute | solution.py:143
  133.0 6.0 %collective-permute-start.13 = (f32[32,512]{1,0:T(8,128)S(1)}, f32[32,512]{1,0:T(8,128)S(1)}, u32[]{:S(2)}, u32[]{:S(2)}) collective-permute-start(f32[32,512]{1,0:T(8,128)S(1)} %pad_maximum_fusion.16), channel_id=1, source_target_pairs={{0,2},{1,3},{2,0},{3,1},{4,6},{5,7},{6,4},{7,5},{8,10},{9,11},{10,... | collective-permute-start | bytes 196616 | tf_op jit(solution)/shard_map/ppermute | solution.py:143
  139.0 7.2 %collective-permute-start.14 = (f32[64,512]{1,0:T(8,128)S(1)}, f32[64,512]{1,0:T(8,128)S(1)}, u32[]{:S(2)}, u32[]{:S(2)}) collective-permute-start(f32[64,512]{1,0:T(8,128)S(1)} %pad_maximum_fusion.15), channel_id=1, source_target_pairs={{0,1},{1,0},{2,3},{3,2},{4,5},{5,4},{6,7},{7,6},{8,9},{9,8},{10,11... | collective-permute-start | bytes 393224 | tf_op jit(solution)/shard_map/ppermute | solution.py:143
  145.7 48.9 %copy-start.4 = (f32[512,512]{1,0:T(8,128)}, f32[512,512]{1,0:T(8,128)S(1)}, u32[]{:S(2)}) copy-start(f32[512,512]{1,0:T(8,128)S(1)} %get-tuple-element.49) | copy-start | bytes 3145732
  145.7 48.9 %collective-permute-start.8 = (f32[512,512]{1,0:T(8,128)}, f32[512,512]{1,0:T(8,128)}, u32[]{:S(2)}, u32[]{:S(2)}) collective-permute-start(f32[512,512]{1,0:T(8,128)} %get-tuple-element.48), channel_id=1, source_target_pairs={{0,1},{1,0},{2,3},{3,2},{4,5},{5,4},{6,7},{7,6},{8,9},{9,8},{10,11... | collective-permute-start | bytes 3145736 | tf_op jit(solution)/shard_map/ppermute | solution.py:248
  146.3 72.6 %collective-permute-start.18 = (f32[512,512]{1,0:T(8,128)}, f32[512,512]{1,0:T(8,128)}, u32[]{:S(2)}, u32[]{:S(2)}) collective-permute-start(f32[512,512]{1,0:T(8,128)} %pad_maximum_fusion.5), channel_id=1, source_target_pairs={{1,4},{2,7},{3,6},{4,1},{5,0},{6,3},{7,2},{9,12},{10,15},{11,14},{... | collective-permute-start | bytes 3145736 | tf_op jit(solution)/shard_map/ppermute | solution.py:334
  150.9 111.3 %collective-permute-start.17 = (f32[512,512]{1,0:T(8,128)}, f32[512,512]{1,0:T(8,128)}, u32[]{:S(2)}, u32[]{:S(2)}) collective-permute-start(f32[512,512]{1,0:T(8,128)} %get-tuple-element.29), channel_id=1, source_target_pairs={{1,7},{2,4},{3,5},{4,2},{5,3},{6,0},{7,1},{9,15},{10,12},{11,13},{... | collective-permute-start | bytes 3145736 | tf_op jit(solution)/shard_map/ppermute | solution.py:334
  154.5 155.5 %collective-permute-start.16 = (f32[512,512]{1,0:T(8,128)}, f32[512,512]{1,0:T(8,128)}, u32[]{:S(2)}, u32[]{:S(2)}) collective-permute-start(f32[512,512]{1,0:T(8,128)} %get-tuple-element.28), channel_id=1, source_target_pairs={{1,6},{2,5},{3,4},{4,3},{5,2},{6,1},{7,0},{9,14},{10,13},{11,12},{... | collective-permute-start | bytes 3145736 | tf_op jit(solution)/shard_map/ppermute | solution.py:334
  169.5 48.1 %copy-start.12 = (f32[512,512]{1,0:T(8,128)S(1)}, f32[512,512]{1,0:T(8,128)}, u32[]{:S(2)}) copy-start(f32[512,512]{1,0:T(8,128)} %pad_maximum_fusion.8) | copy-start | bytes 3145732
  169.5 49.5 %copy-start.14 = (f32[512,512]{1,0:T(8,128)S(1)}, f32[512,512]{1,0:T(8,128)}, u32[]{:S(2)}) copy-start(f32[512,512]{1,0:T(8,128)} %get-tuple-element.33) | copy-start | bytes 3145732
  169.5 92.7 %copy-start.13 = (f32[512,512]{1,0:T(8,128)S(1)}, f32[512,512]{1,0:T(8,128)}, u32[]{:S(2)}) copy-start(f32[512,512]{1,0:T(8,128)} %get-tuple-element.36) | copy-start | bytes 3145732
  172.7 150.6 %collective-permute-start.19 = (f32[3,512,512]{2,1,0:T(8,128)S(1)}, f32[3,512,512]{2,1,0:T(8,128)S(1)}, u32[]{:S(2)}, u32[]{:S(2)}) collective-permute-start(f32[3,512,512]{2,1,0:T(8,128)S(1)} %pad_maximum_fusion), channel_id=1, source_target_pairs={{0,1},{1,0},{2,3},{3,2},{4,5},{5,4},{6,7},{7,6},{8,9},{9,8},{10,11... | collective-permute-start | bytes 9437192 | tf_op jit(solution)/shard_map/ppermute | solution.py:248
  217.5 101.2 %collective-permute-start.26 = (f32[512,512]{1,0:T(8,128)S(1)}, f32[512,512]{1,0:T(8,128)S(1)}, u32[]{:S(2)}, u32[]{:S(2)}) collective-permute-start(f32[512,512]{1,0:T(8,128)S(1)} %copy-done.12), channel_id=1, source_target_pairs={{1,3},{2,0},{3,1},{4,6},{5,7},{6,4},{7,5},{9,11},{10,8},{11,9},{12... | collective-permute-start | bytes 3145736 | tf_op jit(solution)/shard_map/ppermute | solution.py:334
  218.9 100.0 %collective-permute-start.22 = (f32[512,512]{1,0:T(8,128)S(1)}, f32[512,512]{1,0:T(8,128)S(1)}, u32[]{:S(2)}, u32[]{:S(2)}) collective-permute-start(f32[512,512]{1,0:T(8,128)S(1)} %copy-done.14), channel_id=1, source_target_pairs={{1,2},{2,1},{3,0},{4,7},{5,6},{6,5},{7,4},{9,10},{10,9},{11,8},{12... | collective-permute-start | bytes 3145736 | tf_op jit(solution)/shard_map/ppermute | solution.py:334
  262.2 56.9 %collective-permute-start.27 = (f32[512,512]{1,0:T(8,128)S(1)}, f32[512,512]{1,0:T(8,128)S(1)}, u32[]{:S(2)}, u32[]{:S(2)}) collective-permute-start(f32[512,512]{1,0:T(8,128)S(1)} %copy-done.13), channel_id=1, source_target_pairs={{1,5},{2,6},{3,7},{4,0},{5,1},{6,2},{7,3},{9,13},{10,14},{11,15},{... | collective-permute-start | bytes 3145736 | tf_op jit(solution)/shard_map/ppermute | solution.py:334
  323.3 7.5 %copy-start.3 = (f32[8,512,512]{2,1,0:T(8,128)}, f32[8,512,512]{2,1,0:T(8,128)S(1)}, u32[]{:S(2)}) copy-start(f32[8,512,512]{2,1,0:T(8,128)S(1)} %bitcast_dynamic-update-slice_fusion.piece_ref) | copy-start | bytes 25165828
  326.4 3.3 copy-start.2
  332.9 6.0 %copy-start.6 = (f32[512,512]{0,1:T(8,128)S(1)}, f32[512,512]{0,1:T(8,128)}, u32[]{:S(2)}) copy-start(f32[512,512]{0,1:T(8,128)} %copy-done.5) | copy-start | bytes 3145732
  337.5 7.8 %copy-start.16 = (s32[16]{0:T(128)S(1)}, s32[16]{0:T(128)}, u32[]{:S(2)}) copy-start(s32[16]{0:T(128)} %copy-done.15) | copy-start | bytes 196
  337.5 8.4 %copy-start.18 = (s32[16]{0:T(128)S(1)}, s32[16]{0:T(128)}, u32[]{:S(2)}) copy-start(s32[16]{0:T(128)} %copy-done.17) | copy-start | bytes 196
  337.5 8.4 %copy-start.19 = (s32[16]{0:T(128)S(1)}, s32[16]{0:T(128)}, u32[]{:S(2)}) copy-start(s32[16]{0:T(128)} %get-tuple-element.45) | copy-start | bytes 196
  337.5 9.1 %copy-start.9 = (f32[512,256]{1,0:T(8,128)S(1)}, f32[512,256]{1,0:T(8,128)}, u32[]{:S(2)}) copy-start(f32[512,256]{1,0:T(8,128)} %get-tuple-element.71) | copy-start | bytes 1572868
  337.5 10.1 %copy-start.21 = (s32[16]{0:T(128)S(1)}, s32[16]{0:T(128)}, u32[]{:S(2)}) copy-start(s32[16]{0:T(128)} %copy-done.20) | copy-start | bytes 196
  339.9 2.3 collective-permute-start.28
  343.3 0.8 copy-start.10
  344.8 8.7 %collective-permute-start.29 = (f32[128,512]{1,0:T(8,128)}, f32[128,512]{1,0:T(8,128)}, u32[]{:S(2)}, u32[]{:S(2)}) collective-permute-start(f32[128,512]{1,0:T(8,128)} %constant_dynamic-slice_fusion), channel_id=1, source_target_pairs={{0,16},{8,24},{16,0},{24,8},{1,17},{9,25},{17,1},{25,9},{2,18},{10... | collective-permute-start | bytes 786440 | tf_op jit(solution)/shard_map/ppermute | solution.py:143
  354.5 7.7 %collective-permute-start.31 = (f32[128,512]{1,0:T(8,128)S(1)}, f32[128,512]{1,0:T(8,128)S(1)}, u32[]{:S(2)}, u32[]{:S(2)}) collective-permute-start(f32[128,512]{1,0:T(8,128)S(1)} %dynamic-slice_add_fusion.3), channel_id=1, source_target_pairs={{0,16},{8,24},{16,0},{24,8},{1,17},{9,25},{17,1},{25,9},{2,18},{10... | collective-permute-start | bytes 786440 | tf_op jit(solution)/shard_map/ppermute | solution.py:143
  361.6 32.5 %collective-permute-start.30 = (f32[4,512,256]{2,1,0:T(8,128)}, f32[4,512,256]{2,1,0:T(8,128)}, u32[]{:S(2)}, u32[]{:S(2)}) collective-permute-start(f32[4,512,256]{2,1,0:T(8,128)} %shard_map.61), channel_id=1, source_target_pairs={{0,8},{8,0},{16,24},{24,16},{1,9},{9,1},{17,25},{25,17},{2,10},{10... | collective-permute-start | bytes 6291464 | tf_op jit(solution)/shard_map/ppermute | solution.py:143
  361.7 5.4 %collective-permute-start.20 = (f32[256,512]{1,0:T(8,128)S(1)}, f32[256,512]{1,0:T(8,128)}, u32[]{:S(2)}, u32[]{:S(2)}) collective-permute-start(f32[256,512]{1,0:T(8,128)S(1)} %constant_dynamic-slice_fusion.5), channel_id=1, source_target_pairs={{0,8},{8,0},{16,24},{24,16},{1,9},{9,1},{17,25},{25,17},{2,10},{10... | collective-permute-start | bytes 1572872 | tf_op jit(solution)/shard_map/ppermute | solution.py:143
  363.1 7.3 %collective-permute-start.32 = (f32[256,512]{1,0:T(8,128)}, f32[256,512]{1,0:T(8,128)}, u32[]{:S(2)}, u32[]{:S(2)}) collective-permute-start(f32[256,512]{1,0:T(8,128)} %pad_maximum_fusion.13), channel_id=1, source_target_pairs={{0,8},{8,0},{16,24},{24,16},{1,9},{9,1},{17,25},{25,17},{2,10},{10... | collective-permute-start | bytes 1572872 | tf_op jit(solution)/shard_map/ppermute | solution.py:143
  368.9 8.9 %collective-permute-start.21 = (f32[128,512]{1,0:T(8,128)}, f32[128,512]{1,0:T(8,128)}, u32[]{:S(2)}, u32[]{:S(2)}) collective-permute-start(f32[128,512]{1,0:T(8,128)} %constant_dynamic-slice_fusion.4), channel_id=1, source_target_pairs={{0,16},{8,24},{16,0},{24,8},{1,17},{9,25},{17,1},{25,9},{2,18},{10... | collective-permute-start | bytes 786440 | tf_op jit(solution)/shard_map/ppermute | solution.py:143
  372.6 36.8 %collective-permute-start.33 = (f32[512,512]{1,0:T(8,128)}, f32[512,512]{1,0:T(8,128)}, u32[]{:S(2)}, u32[]{:S(2)}) collective-permute-start(f32[512,512]{1,0:T(8,128)} %pad_maximum_fusion.11), channel_id=1, source_target_pairs={{0,2},{1,3},{10,12},{11,13},{20,22},{21,23},{30,24},{31,25}} | collective-permute-start | bytes 3145736 | tf_op jit(solution)/shard_map/ppermute | solution.py:259
  374.2 35.3 %collective-permute-start.34 = (f32[512,512]{1,0:T(8,128)}, f32[512,512]{1,0:T(8,128)}, u32[]{:S(2)}, u32[]{:S(2)}) collective-permute-start(f32[512,512]{1,0:T(8,128)} %pad_maximum_fusion.11), channel_id=1, source_target_pairs={{0,4},{1,5},{10,14},{11,15},{20,16},{21,17},{30,26},{31,27}} | collective-permute-start | bytes 3145736 | tf_op jit(solution)/shard_map/ppermute | solution.py:259
  375.8 58.6 %collective-permute-start.35 = (f32[512,512]{1,0:T(8,128)}, f32[512,512]{1,0:T(8,128)}, u32[]{:S(2)}, u32[]{:S(2)}) collective-permute-start(f32[512,512]{1,0:T(8,128)} %pad_maximum_fusion.11), channel_id=1, source_target_pairs={{0,6},{1,7},{10,8},{11,9},{20,18},{21,19},{30,28},{31,29}} | collective-permute-start | bytes 3145736 | tf_op jit(solution)/shard_map/ppermute | solution.py:259
  378.8 30.2 %collective-permute-start.23 = (f32[128,512]{1,0:T(8,128)S(1)}, f32[128,512]{1,0:T(8,128)S(1)}, u32[]{:S(2)}, u32[]{:S(2)}) collective-permute-start(f32[128,512]{1,0:T(8,128)S(1)} %add_subtract_fusion), channel_id=1, source_target_pairs={{0,16},{8,24},{16,0},{24,8},{1,17},{9,25},{17,1},{25,9},{2,18},{10... | collective-permute-start | bytes 786440 | tf_op jit(solution)/shard_map/ppermute | solution.py:143
  387.5 18.4 %copy-start.7 = (f32[4,512,256]{2,1,0:T(8,128)S(1)}, f32[4,512,256]{2,1,0:T(8,128)}, u32[]{:S(2)}) copy-start(f32[4,512,256]{2,1,0:T(8,128)} %shard_map.60) | copy-start | bytes 6291460
  394.1 80.6 %collective-permute-start.37 = (f32[4,512,256]{2,1,0:T(8,128)}, f32[4,512,256]{2,1,0:T(8,128)S(1)}, u32[]{:S(2)}, u32[]{:S(2)}) collective-permute-start(f32[4,512,256]{2,1,0:T(8,128)} %shard_map.64), channel_id=1, source_target_pairs={{0,8},{8,0},{16,24},{24,16},{1,9},{9,1},{17,25},{25,17},{2,10},{10... | collective-permute-start | bytes 6291464 | tf_op jit(solution)/shard_map/ppermute | solution.py:143
  409.0 65.7 %collective-permute-start.38 = (f32[4,512,256]{2,1,0:T(8,128)}, f32[4,512,256]{2,1,0:T(8,128)}, u32[]{:S(2)}, u32[]{:S(2)}) collective-permute-start(f32[4,512,256]{2,1,0:T(8,128)} %add.489), channel_id=1, source_target_pairs={{0,16},{8,24},{16,0},{24,8},{1,17},{9,25},{17,1},{25,9},{2,18},{10... | collective-permute-start | bytes 6291464 | tf_op jit(solution)/shard_map/ppermute | solution.py:143
  409.4 33.9 %collective-permute-start.24 = (f32[256,512]{1,0:T(8,128)S(1)}, f32[256,512]{1,0:T(8,128)S(1)}, u32[]{:S(2)}, u32[]{:S(2)}) collective-permute-start(f32[256,512]{1,0:T(8,128)S(1)} %pad_maximum_fusion.12), channel_id=1, source_target_pairs={{0,8},{8,0},{16,24},{24,16},{1,9},{9,1},{17,25},{25,17},{2,10},{10... | collective-permute-start | bytes 1572872 | tf_op jit(solution)/shard_map/ppermute | solution.py:143
  436.8 36.0 %collective-permute-start.36 = (f32[512,512]{1,0:T(8,128)S(1)}, f32[512,512]{1,0:T(8,128)S(1)}, u32[]{:S(2)}, u32[]{:S(2)}) collective-permute-start(f32[512,512]{1,0:T(8,128)S(1)} %add_add_fusion), channel_id=1, source_target_pairs={{0,1},{1,0},{2,3},{3,2},{4,5},{5,4},{6,7},{7,6},{8,9},{9,8},{10,11... | collective-permute-start | bytes 3145736 | tf_op jit(solution)/shard_map/ppermute | solution.py:269
  450.2 25.8 %copy-start = (f32[1024,512]{1,0:T(8,128)S(1)}, f32[1024,512]{1,0:T(8,128)}, u32[]{:S(2)}) copy-start(f32[1024,512]{1,0:T(8,128)} %parent_ref.1) | copy-start | bytes 6291460
  472.8 10.7 %copy-start.1 = (f32[512,512]{1,0:T(8,128)}, f32[512,512]{1,0:T(8,128)S(1)}, u32[]{:S(2)}) copy-start(f32[512,512]{1,0:T(8,128)S(1)} %fusion.21.mine_ref) | copy-start | bytes 3145732
  474.7 1.4 copy-start.8
